TPU v7x, 128 devices: a whole 4x4x4 slice. The times are simulated.
128 devices in a mesh: section: 2 (over z_hi), seq: 4 (over x), mp: 16 (over z_lo, y, core).
Axes of the slice: x: 4, y: 4, z: 4 (z_hi: 2, z_lo: 2; z = z_hi * 2 + z_lo), core: 2. Of those that a mesh axis runs over, the one named last changes fastest.
Arguments:
- hidden_states: bfloat16 [2, 1024, 4096], P(None, 'seq', 'mp'), may hold values from -6 to 6
- neighbour_ids: int32 [64, 128], replicated, may hold values from 0 to 63999
- neighbour_table: int32 [2, 16, 2], P(None, 'seq'), may hold values from 0 to 63
- enc_embed: bfloat16 [64000, 1024], P('mp'), may hold values from -6 to 6
- enc_norms: float32 [2, 1024], replicated, may hold values from 0.1 to 1.9
- enc_qkv: bfloat16 [1024, 3, 1024], P('mp'), may hold values from -0.1875 to 0.1875
- enc_out: bfloat16 [1024, 1024], P('mp'), may hold values from -0.1875 to 0.1875
- enc_up: bfloat16 [1024, 4096], P('mp'), may hold values from -0.1875 to 0.1875
- enc_down: bfloat16 [4096, 1024], P('mp'), may hold values from -0.09375 to 0.09375
- dec_norms: float32 [2, 2, 4096], P('section'), may hold values from 0.1 to 1.9
- dec_qkv: bfloat16 [2, 4096, 3, 4096], P('section', None, None, 'mp'), may hold values from -0.09375 to 0.09375
- dec_out: bfloat16 [2, 4096, 4096], P('section', 'mp'), may hold values from -0.09375 to 0.09375
- cross_query: bfloat16 [2, 4096, 4096], P('section', None, 'mp'), may hold values from -0.09375 to 0.09375
- cross_pair: bfloat16 [2, 1024, 2, 4096], P('section', None, None, 'mp'), may hold values from -0.1875 to 0.1875
- cross_out: bfloat16 [2, 4096, 4096], P('section', 'mp'), may hold values from -0.09375 to 0.09375
Outputs:
- block_states: bfloat16 [2, 1024, 4096], P('section', 'seq', 'mp')
All inputs are finite; a program needn't handle non-finite values.
Results may differ from a plain program's by a relative error of at most 0.035.
Values may be sent and summed in bfloat16 or wider, within the bound.
No kernel may reach another device: no remote copies, remote signals or barrier semaphores. Data moves between devices by JAX's collectives and lax.ppermute only.
A program may use at most 192 MiB of HBM per device.

v0:
```python
import jax
import jax.numpy as jnp
from jax import lax
from jax.sharding import PartitionSpec as P

D = 4096
HEAD = 128
ENC_D = 1024
ENC_HEADS = 16
ENC_HEAD = 64
BLOCK = 64
NB_LEN = 128
NEIGH = 2
BATCH = 2


epsilon = 1e-05


def shifted(value, axis, steps):
    count = lax.axis_size(axis)
    pairs = [(source, (source + steps) % count) for source in range(count)]
    return lax.ppermute(value, axis, pairs)


def passed_along(block, axis, distance):
    devices = range(lax.axis_size(axis))
    route = [(i - distance, i) for i in devices if i - distance in devices]
    return lax.ppermute(block, axis, route)


def project(local, gains, weight):
    widened = lax.all_gather(local, "mp", axis=1, tiled=True).astype(jnp.float32)
    scaled = (widened * gains).astype(jnp.bfloat16)
    summed = jnp.dot(scaled, weight, preferred_element_type=jnp.float32)
    return (summed, jnp.sum(widened * widened, axis=1))


def normalize(summed, squares, width):
    return summed / jnp.sqrt(squares / width + epsilon)[:, None]


def row_product(left, weight_rows):
    return jnp.dot(
        left,
        lax.all_gather(weight_rows, "mp", axis=0, tiled=True),
        preferred_element_type=jnp.float32,
    )


def row_scale(values):
    widened = values.astype(jnp.float32)
    return (widened, jnp.sqrt(jnp.mean(widened * widened, axis=1) + epsilon)[:, None])


def handoff(states):
    return shifted(states, "section", 1)


def attend(queries, keys, values, scaling):
    scores = (
        jnp.einsum("gqhd,gkhd->ghqk", queries, keys, preferred_element_type=jnp.float32) * scaling
    )
    weights = jnp.exp(scores)
    numer = jnp.einsum(
        "ghqk,gkhd->gqhd", weights.astype(jnp.bfloat16), values, preferred_element_type=jnp.float32
    )
    denom = jnp.transpose(jnp.sum(weights, axis=3), (0, 2, 1))
    return (numer / denom[..., None]).astype(jnp.bfloat16)


def causal(queries, keys, values, first_row):
    length = queries.shape[0]
    scaling = HEAD ** (-0.5)
    asked_pos = first_row + jnp.arange(length, dtype=jnp.int32)
    piece_keys = lax.all_gather(keys, "seq", axis=0, tiled=True)
    piece_values = lax.all_gather(values, "seq", axis=0, tiled=True)
    scores = (
        jnp.einsum("qhd,khd->hqk", queries, piece_keys, preferred_element_type=jnp.float32)
        * scaling
    )
    key_pos = jnp.arange(piece_keys.shape[0], dtype=jnp.int32)
    weights = jnp.where(key_pos[None, None, :] <= asked_pos[None, :, None], jnp.exp(scores), 0.0)
    numer = jnp.einsum(
        "hqk,khd->qhd",
        weights.astype(jnp.bfloat16),
        piece_values,
        preferred_element_type=jnp.float32,
    )
    numer, denom = (numer, jnp.transpose(jnp.sum(weights, axis=2)))
    return (numer / denom[..., None]).astype(jnp.bfloat16)


def encode_rows(flat_ids, enc_embed, enc_norms, enc_qkv, enc_out, enc_up, enc_down):
    vocab_here = enc_embed.shape[0]
    vocab_start = lax.axis_index("mp") * vocab_here
    wanted = flat_ids - vocab_start
    inside = (wanted >= 0) & (wanted < vocab_here)
    picked = enc_embed[jnp.clip(wanted, 0, vocab_here - 1)].astype(jnp.float32)
    embedded = lax.psum_scatter(
        jnp.where(inside[:, None], picked, 0.0).astype(jnp.bfloat16),
        "mp",
        scatter_dimension=0,
        tiled=True,
    )
    widened, scale = row_scale(embedded)
    scaled = (widened * enc_norms[0]).astype(jnp.bfloat16)
    triple = (row_product(scaled, enc_qkv.reshape(enc_qkv.shape[0], -1)) / scale).astype(
        jnp.bfloat16
    )
    shaped = triple.reshape(-1, NB_LEN, 3, ENC_HEADS, ENC_HEAD)
    mixed = attend(shaped[:, :, 0], shaped[:, :, 1], shaped[:, :, 2], ENC_HEAD ** (-0.5)).reshape(
        -1, ENC_D
    )
    inner = (widened + row_product(mixed, enc_out)).astype(jnp.bfloat16)
    widened, scale = row_scale(inner)
    scaled = (widened * enc_norms[1]).astype(jnp.bfloat16)
    hidden = jax.nn.gelu(row_product(scaled, enc_up) / scale, approximate=True).astype(jnp.bfloat16)
    outer = widened + row_product(hidden, enc_down)
    return outer.astype(jnp.bfloat16)


def decoder_layer(states, pairs_here, weights):
    norms, triple_w, out_w, query_w, back_w = weights
    length, local_width = states.shape
    heads_here = local_width // HEAD
    summed, squares = project(states, norms[0], triple_w.reshape(D, 3 * local_width))
    triple = normalize(summed, squares, D).astype(jnp.bfloat16).reshape(length, 3, heads_here, HEAD)
    mixed = causal(
        triple[:, 0], triple[:, 1], triple[:, 2], lax.axis_index("seq") * length
    ).reshape(length, local_width)
    partial_value = jnp.dot(mixed, out_w, preferred_element_type=jnp.float32)
    middle = (
        states.astype(jnp.float32)
        + lax.psum_scatter(
            partial_value.astype(jnp.bfloat16), "mp", scatter_dimension=1, tiled=True
        ).astype(jnp.float32)
    ).astype(jnp.bfloat16)
    summed, squares = project(middle, norms[1], query_w)
    asked = normalize(summed, squares, D).astype(jnp.bfloat16)
    groups = pairs_here.shape[0]
    padded = jnp.concatenate(
        [
            jnp.zeros((1, local_width), jnp.bfloat16),
            asked,
            jnp.zeros((BLOCK - 1, local_width), jnp.bfloat16),
        ],
        axis=0,
    )
    crossed = attend(
        padded.reshape(groups, BLOCK, heads_here, HEAD),
        pairs_here[:, :, 0],
        pairs_here[:, :, 1],
        HEAD ** (-0.5),
    )
    crossed = crossed.reshape(groups * BLOCK, local_width)[1 : 1 + length]
    back_term = jnp.dot(crossed, back_w, preferred_element_type=jnp.float32)
    result = middle.astype(jnp.float32) + lax.psum_scatter(
        back_term.astype(jnp.bfloat16), "mp", scatter_dimension=1, tiled=True
    ).astype(jnp.float32)
    return result.astype(jnp.bfloat16)


def on_device(
    hidden_states,
    neighbour_ids,
    neighbour_table,
    enc_embed,
    enc_norms,
    enc_qkv,
    enc_out,
    enc_up,
    enc_down,
    dec_norms,
    dec_qkv,
    dec_out,
    cross_query,
    cross_pair,
    cross_out,
):
    blocks_here = neighbour_table.shape[1]
    slot_ids = neighbour_ids[neighbour_table.reshape(-1)]
    encoded_own = encode_rows(
        slot_ids.reshape(-1), enc_embed, enc_norms, enc_qkv, enc_out, enc_up, enc_down
    )
    slots = lax.all_gather(encoded_own.reshape(-1, NB_LEN, ENC_D), "mp", axis=0, tiled=True)
    encoded = slots.reshape(BATCH, blocks_here, NEIGH * NB_LEN, ENC_D)
    local_width = hidden_states.shape[2]
    heads_here = local_width // HEAD
    pair_w = cross_pair[0].reshape(ENC_D, 2 * local_width)
    previous = passed_along(encoded[:, -1], "seq", 1)
    extended = jnp.concatenate([previous[:, None], encoded], axis=1)
    pairs = jnp.dot(extended.reshape(-1, ENC_D), pair_w, preferred_element_type=jnp.float32).astype(
        jnp.bfloat16
    )
    pairs = pairs.reshape(BATCH, blocks_here + 1, NEIGH * NB_LEN, 2, heads_here, HEAD)
    first_section = lax.axis_index("section") == 0
    weights = (dec_norms[0], dec_qkv[0], dec_out[0], cross_query[0], cross_out[0])

    def step_layer(states, which):
        pairs_here = lax.dynamic_index_in_dim(pairs, which, 0, keepdims=False)
        return decoder_layer(states, pairs_here, weights)

    out_first = step_layer(hidden_states[0], 0)
    received = handoff(out_first)
    second_in = jnp.where(first_section, hidden_states[1], received)
    out_second = step_layer(second_in, jnp.where(first_section, 1, 0))
    received = handoff(out_second)
    out_third = step_layer(received, 1)
    return jnp.where(first_section, received, out_third)[None]


def solution(mesh):
    return jax.shard_map(
        on_device,
        mesh=mesh,
        in_specs=(
            P(None, "seq", "mp"),
            P(),
            P(None, "seq", None),
            P("mp", None),
            P(),
            P("mp", None, None),
            P("mp", None),
            P("mp", None),
            P("mp", None),
            P("section", None, None),
            P("section", None, None, "mp"),
            P("section", "mp", None),
            P("section", None, "mp"),
            P("section", None, None, "mp"),
            P("section", "mp", None),
        ),
        out_specs=P("section", "seq", "mp"),
        check_vma=False,
    )
```

profile of v0, /device:TPU:0, one launch (start us, length us, event | category | flops | bytes accessed | tf_op | source)
XLA Modules:
  0.0 1076.0 jit_solution(6783091776715894768)
XLA Ops:
  10.6 15.3 %gather_fusion.1 = bf16[2048,1024]{1,0:T(8,128)(2,1)} fusion(bf16[4000,1024]{1,0:T(8,128)(2,1)} %param.18, s32[2048]{0:T(1024)S(1)} %broadcast_clamp_fusion), kind=kCustom, calls=%fused_computation.1 | custom fusion | bytes 8396800 | tf_op jit(solution)/shard_map/gather | solution.py:99
  25.9 4.0 select_convert_fusion
  33.6 8.7 copy.39
  42.6 6.2 all-gather.38.cloned.1.call-done
  51.1 4.6 fusion.74
  56.3 13.1 %all-gather.2 = bf16[1024,1,2,128]{3,0,2,1:T(8,128)(2,1)S(1)} all-gather(bf16[256,1,2,128]{3,0,2,1:T(8,128)(2,1)S(1)} %copy.68), channel_id=4, replica_groups=mesh['section'=2,'seq'=4,'mp'=16] {'seq'}, dimensions={0}, use_global_device_ids=true | all-gather | bytes 655360 | tf_op jit(solution)/shard_map/all_gather | solution.py:76
  69.4 13.4 %all-gather.1 = bf16[1024,1,2,128]{0,3,2,1:T(8,128)(2,1)S(1)} all-gather(bf16[256,1,2,128]{0,3,2,1:T(8,128)(2,1)S(1)} %copy.66), channel_id=3, replica_groups=mesh['section'=2,'seq'=4,'mp'=16] {'seq'}, dimensions={0}, use_global_device_ids=true | all-gather | bytes 655360 | tf_op jit(solution)/shard_map/all_gather | solution.py:77
  87.0 31.3 %reduce-scatter.10.cloned.1.call-done = bf16[128,1024]{1,0:T(8,128)(2,1)} async-done(((bf16[2048,1024]{1,0:T(8,128)(2,1)}), bf16[128,1024]{1,0:T(8,128)(2,1)}) %reduce-scatter.10.cloned.1.call-update) | async-done | bytes 262160 | tf_op jit(solution)/shard_map/reduce_scatter | solution.py:100
  119.4 41.6 %all-gather.20.cloned.1.call-done = bf16[1024,3072]{1,0:T(8,128)(2,1)} async-done(((bf16[64,3072]{1,0:T(8,128)(2,1)}), bf16[1024,3072]{1,0:T(8,128)(2,1)}) %all-gather.20.cloned.1.call-update) | async-done | bytes 6291472 | tf_op jit(solution)/shard_map/all_gather | solution.py:46
  161.0 4.8 fusion.12
  168.0 29.2 %all-gather.22.cloned.1.call-done = bf16[1024,1024]{1,0:T(8,128)(2,1)} async-done(((bf16[64,1024]{1,0:T(8,128)(2,1)}), bf16[1024,1024]{1,0:T(8,128)(2,1)}) %all-gather.22.cloned.1.call-update) | async-done | bytes 2097168 | tf_op jit(solution)/shard_map/all_gather | solution.py:46
  197.2 2.9 multiply_reduce_fusion
  200.1 51.1 %all-gather.24.cloned.1.call-done = bf16[1024,4096]{1,0:T(8,128)(2,1)} async-done(((bf16[64,4096]{1,0:T(8,128)(2,1)}), bf16[1024,4096]{1,0:T(8,128)(2,1)}) %all-gather.24.cloned.1.call-update) | async-done | bytes 8388624 | tf_op jit(solution)/shard_map/all_gather | solution.py:46
  251.2 54.6 %all-gather.26.cloned.1.call-done = bf16[4096,1024]{1,0:T(8,128)(2,1)} async-done(((bf16[256,1024]{1,0:T(8,128)(2,1)}), bf16[4096,1024]{1,0:T(8,128)(2,1)}) %all-gather.26.cloned.1.call-update) | async-done | bytes 8388624 | tf_op jit(solution)/shard_map/all_gather | solution.py:46
  305.7 9.5 fusion.79
  315.3 57.1 %reduce-scatter.8.cloned.1.call-done = bf16[256,256]{1,0:T(8,128)(2,1)} async-done(((bf16[256,4096]{1,0:T(8,128)(2,1)}), bf16[256,256]{1,0:T(8,128)(2,1)}) %reduce-scatter.8.cloned.1.call-update) | async-done | bytes 131088 | tf_op jit(solution)/shard_map/reduce_scatter | solution.py:135
  375.4 34.7 %all-gather.40.cloned.1.call-done = bf16[2048,1024]{1,0:T(8,128)(2,1)} async-done(((bf16[128,1024]{1,0:T(8,128)(2,1)}), bf16[2048,1024]{1,0:T(8,128)(2,1)}) %all-gather.40.cloned.1.call-update) | async-done | bytes 4194320 | tf_op jit(solution)/shard_map/all_gather | solution.py:186
  410.1 2.4 slice_bitcast_fusion
  412.5 4.0 collective-permute-start
  416.4 32.7 %all-gather.28.cloned.1.call-done = bf16[256,4096]{1,0:T(8,128)(2,1)} async-done(((bf16[256,256]{1,0:T(8,128)(2,1)}), bf16[256,4096]{1,0:T(8,128)(2,1)}) %all-gather.28.cloned.1.call-update) | async-done | bytes 2097168 | tf_op jit(solution)/shard_map/all_gather | solution.py:33
  451.4 2.3 fusion.97
  454.7 2.7 pad_maximum_fusion
  457.4 3.1 convolution_convert_fusion.6
  462.4 4.0 squeeze.85
  466.4 2.4 fusion.182
  472.5 63.6 %reduce-scatter.12.cloned.1.call-done = bf16[256,256]{1,0:T(8,128)(2,1)} async-done(((bf16[256,4096]{1,0:T(8,128)(2,1)}), bf16[256,256]{1,0:T(8,128)(2,1)}) %reduce-scatter.12.cloned.1.call-update) | async-done | bytes 131088 | tf_op jit(solution)/shard_map/reduce_scatter | solution.py:158
  537.7 2.9 collective-permute-start.1
  540.6 3.8 collective-permute-done.1
  546.1 36.0 %all-gather.30.cloned.1.call-done = bf16[256,4096]{1,0:T(8,128)(2,1)} async-done(((bf16[256,256]{1,0:T(8,128)(2,1)}), bf16[256,4096]{1,0:T(8,128)(2,1)}) %all-gather.30.cloned.1.call-update) | async-done | bytes 2097168 | tf_op jit(solution)/shard_map/all_gather | solution.py:33
  584.3 5.4 fusion.62
  593.5 13.8 %all-gather.5 = bf16[1024,1,2,128]{3,0,2,1:T(8,128)(2,1)} all-gather(bf16[256,1,2,128]{3,0,2,1:T(8,128)(2,1)S(1)} %copy.74), channel_id=7, replica_groups=mesh['section'=2,'seq'=4,'mp'=16] {'seq'}, dimensions={0}, use_global_device_ids=true | all-gather | bytes 655360 | tf_op jit(solution)/shard_map/all_gather | solution.py:76
  608.4 13.2 %all-gather.4 = bf16[1024,1,2,128]{0,3,2,1:T(8,128)(2,1)S(1)} all-gather(bf16[256,1,2,128]{0,3,2,1:T(8,128)(2,1)S(1)} %copy.72), channel_id=6, replica_groups=mesh['section'=2,'seq'=4,'mp'=16] {'seq'}, dimensions={0}, use_global_device_ids=true | all-gather | bytes 655360 | tf_op jit(solution)/shard_map/all_gather | solution.py:77
  626.5 62.8 %reduce-scatter.14.cloned.1.call-done = bf16[256,256]{1,0:T(8,128)(2,1)} async-done(((bf16[256,4096]{1,0:T(8,128)(2,1)}), bf16[256,256]{1,0:T(8,128)(2,1)}) %reduce-scatter.14.cloned.1.call-update) | async-done | bytes 131088 | tf_op jit(solution)/shard_map/reduce_scatter | solution.py:135
  691.0 4.9 reshape.249
  699.5 27.6 %all-gather.32.cloned.1.call-done = bf16[256,4096]{1,0:T(8,128)(2,1)} async-done(((bf16[256,256]{1,0:T(8,128)(2,1)}), bf16[256,4096]{1,0:T(8,128)(2,1)}) %all-gather.32.cloned.1.call-update) | async-done | bytes 2097168 | tf_op jit(solution)/shard_map/all_gather | solution.py:33
  729.3 2.3 fusion.107
  739.6 63.7 %reduce-scatter.16.cloned.1.call-done = bf16[256,256]{1,0:T(8,128)(2,1)} async-done(((bf16[256,4096]{1,0:T(8,128)(2,1)}), bf16[256,256]{1,0:T(8,128)(2,1)}) %reduce-scatter.16.cloned.1.call-update) | async-done | bytes 131088 | tf_op jit(solution)/shard_map/reduce_scatter | solution.py:158
  804.2 2.9 collective-permute-start.2
  807.1 3.6 collective-permute-done.2
  811.5 36.0 %all-gather.34.cloned.1.call-done = bf16[256,4096]{1,0:T(8,128)(2,1)} async-done(((bf16[256,256]{1,0:T(8,128)(2,1)}), bf16[256,4096]{1,0:T(8,128)(2,1)}) %all-gather.34.cloned.1.call-update) | async-done | bytes 2097168 | tf_op jit(solution)/shard_map/all_gather | solution.py:33
  849.7 5.4 fusion.68
  858.9 13.8 %all-gather.7 = bf16[1024,1,2,128]{3,0,2,1:T(8,128)(2,1)} all-gather(bf16[256,1,2,128]{3,0,2,1:T(8,128)(2,1)S(1)} %copy.77), channel_id=9, replica_groups=mesh['section'=2,'seq'=4,'mp'=16] {'seq'}, dimensions={0}, use_global_device_ids=true | all-gather | bytes 655360 | tf_op jit(solution)/shard_map/all_gather | solution.py:76
  873.8 13.2 %all-gather.6 = bf16[1024,1,2,128]{0,3,2,1:T(8,128)(2,1)S(1)} all-gather(bf16[256,1,2,128]{0,3,2,1:T(8,128)(2,1)S(1)} %copy.75), channel_id=8, replica_groups=mesh['section'=2,'seq'=4,'mp'=16] {'seq'}, dimensions={0}, use_global_device_ids=true | all-gather | bytes 655360 | tf_op jit(solution)/shard_map/all_gather | solution.py:77
  891.7 63.0 %reduce-scatter.18.cloned.1.call-done = bf16[256,256]{1,0:T(8,128)(2,1)} async-done(((bf16[256,4096]{1,0:T(8,128)(2,1)}), bf16[256,256]{1,0:T(8,128)(2,1)}) %reduce-scatter.18.cloned.1.call-update) | async-done | bytes 131088 | tf_op jit(solution)/shard_map/reduce_scatter | solution.py:135
  957.9 2.3 fusion.181
  960.2 32.3 %all-gather.36.cloned.1.call-done = bf16[256,4096]{1,0:T(8,128)(2,1)} async-done(((bf16[256,256]{1,0:T(8,128)(2,1)}), bf16[256,4096]{1,0:T(8,128)(2,1)}) %all-gather.36.cloned.1.call-update) | async-done | bytes 2097168 | tf_op jit(solution)/shard_map/all_gather | solution.py:33
  994.7 2.3 fusion.117
  1003.6 63.7 %reduce-scatter.20.cloned.1.call-done = bf16[256,256]{1,0:T(8,128)(2,1)} async-done(((bf16[256,4096]{1,0:T(8,128)(2,1)}), bf16[256,256]{1,0:T(8,128)(2,1)}) %reduce-scatter.20.cloned.1.call-update) | async-done | bytes 131088 | tf_op jit(solution)/shard_map/reduce_scatter | solution.py:158
  (191 shorter events, 87.1 us)
Async XLA Ops:
  6.5 77.7 %copy-start = (bf16[1,256,4096]{2,1,0:T(8,128)(2,1)S(1)}, bf16[1,256,4096]{2,1,0:T(8,128)(2,1)}, u32[]{:S(2)}) copy-start(bf16[1,256,4096]{2,1,0:T(8,128)(2,1)} %param.26) | copy-start | bytes 6291460
  6.5 42.3 %all-gather.38.cloned.1.call-start = ((), (), s32[]{:S(2)}) async-start(), calls=%async_computation.23 | async-start | bytes 2228224 | tf_op jit(solution)/shard_map/all_gather | solution.py:33
  8.3 110.0 %reduce-scatter.10.cloned.1.call-start = ((), (), s32[]{:S(2)}) async-start(), calls=%async_computation.8 | async-start | bytes 4456448 | tf_op jit(solution)/shard_map/reduce_scatter | solution.py:100
  30.0 131.0 %all-gather.20.cloned.1.call-start = ((), (), s32[]{:S(2)}) async-start(), calls=%async_computation.9 | async-start | bytes 6684672 | tf_op jit(solution)/shard_map/all_gather | solution.py:46
  31.8 165.4 %all-gather.22.cloned.1.call-start = ((), (), s32[]{:S(2)}) async-start(), calls=%async_computation.10 | async-start | bytes 2228224 | tf_op jit(solution)/shard_map/all_gather | solution.py:46
  32.4 218.8 %all-gather.24.cloned.1.call-start = ((), (), s32[]{:S(2)}) async-start(), calls=%async_computation.11 | async-start | bytes 8912896 | tf_op jit(solution)/shard_map/all_gather | solution.py:46
  32.9 272.8 %all-gather.26.cloned.1.call-start = ((), (), s32[]{:S(2)}) async-start(), calls=%async_computation.12 | async-start | bytes 8912896 | tf_op jit(solution)/shard_map/all_gather | solution.py:46
  33.5 9.0 copy-start.26
  33.5 338.9 %reduce-scatter.8.cloned.1.call-start = ((), (), s32[]{:S(2)}) async-start(), calls=%async_computation.7 | async-start | bytes 2228224 | tf_op jit(solution)/shard_map/reduce_scatter | solution.py:135
  42.6 41.1 %copy-start.22 = (pred[256,1024]{1,0:T(8,128)(4,1)}, pred[256,1024]{1,0:T(8,128)(4,1)S(1)}, u32[]{:S(2)}) copy-start(pred[256,1024]{1,0:T(8,128)(4,1)S(1)} %iota_compare_fusion) | copy-start | bytes 786436
  42.6 13.1 %copy-start.29 = (f32[1,1,4096]{2,1,0:T(1,128)}, f32[1,1,4096]{2,1,0:T(1,128)S(1)}, u32[]{:S(2)}) copy-start(f32[1,1,4096]{2,1,0:T(1,128)S(1)} %get-tuple-element.21) | copy-start | bytes 49156
  42.6 408.8 %copy-start.27 = (f32[1,1,4096]{2,1,0:T(1,128)}, f32[1,1,4096]{2,1,0:T(1,128)S(1)}, u32[]{:S(2)}) copy-start(f32[1,1,4096]{2,1,0:T(1,128)S(1)} %get-tuple-element.20) | copy-start | bytes 49156
  48.9 2.2 copy-start.5
  86.3 323.8 %all-gather.40.cloned.1.call-start = ((), (), s32[]{:S(2)}) async-start(), calls=%async_computation.24 | async-start | bytes 4456448 | tf_op jit(solution)/shard_map/all_gather | solution.py:186
  167.3 29.9 %copy-start.19 = (bf16[128,1024]{1,0:T(8,128)(2,1)S(1)}, bf16[128,1024]{1,0:T(8,128)(2,1)}, u32[]{:S(2)}) copy-start(bf16[128,1024]{1,0:T(8,128)(2,1)} %reduce-scatter.10.cloned.1.call-done) | copy-start | bytes 786436
  305.7 66.7 %copy-start.20 = (bf16[2,256,256]{2,1,0:T(8,128)(2,1)S(1)}, bf16[2,256,256]{2,1,0:T(8,128)(2,1)}, u32[]{:S(2)}) copy-start(bf16[2,256,256]{2,1,0:T(8,128)(2,1)} %param.15) | copy-start | bytes 786436
  305.7 68.4 %copy-start.17 = (bf16[1,1024,2,256]{3,2,1,0:T(2,128)(2,1)S(1)}, bf16[1,1024,2,256]{3,2,1,0:T(2,128)(2,1)}, u32[]{:S(2)}) copy-start(bf16[1,1024,2,256]{3,2,1,0:T(2,128)(2,1)} %param.28) | copy-start | bytes 3145732
  315.3 133.9 %all-gather.28.cloned.1.call-start = ((), (), s32[]{:S(2)}) async-start(), calls=%async_computation.13 | async-start | bytes 2228224 | tf_op jit(solution)/shard_map/all_gather | solution.py:33
  374.1 162.1 %reduce-scatter.12.cloned.1.call-start = ((), (), s32[]{:S(2)}) async-start(), calls=%async_computation.14 | async-start | bytes 2228224 | tf_op jit(solution)/shard_map/reduce_scatter | solution.py:158
  412.5 42.2 %collective-permute-start = (bf16[2,256,1024]{2,1,0:T(8,128)(2,1)}, bf16[2,256,1024]{2,1,0:T(8,128)(2,1)S(1)}, u32[]{:S(2)}, u32[]{:S(2)}) collective-permute-start(bf16[2,256,1024]{2,1,0:T(8,128)(2,1)} %slice_bitcast_fusion), channel_id=1, source_target_pairs={{0,16},{16,32},{32,48},{1,17},{17,33},{33,49},{2,18},{18,34},{34,5... | collective-permute-start | bytes 3145736 | tf_op jit(solution)/shard_map/ppermute | solution.py:29
  449.2 2.3 copy-start.6
  454.7 2.7 copy-start.18
  466.4 2.4 copy-start.25
  472.5 63.7 %copy-start.13 = (bf16[256,256]{1,0:T(8,128)(2,1)S(1)}, bf16[256,256]{1,0:T(8,128)(2,1)}, u32[]{:S(2)}) copy-start(bf16[256,256]{1,0:T(8,128)(2,1)} %fusion.157) | copy-start | bytes 393220
  472.5 109.6 %all-gather.30.cloned.1.call-start = ((), (), s32[]{:S(2)}) async-start(), calls=%async_computation.15 | async-start | bytes 2228224 | tf_op jit(solution)/shard_map/all_gather | solution.py:33
  537.7 6.7 collective-permute-start.1
  546.0 38.3 %copy-start.30 = (f32[1,1,4096]{2,1,0:T(1,128)S(1)}, f32[1,1,4096]{2,1,0:T(1,128)}, u32[]{:S(2)}) copy-start(f32[1,1,4096]{2,1,0:T(1,128)} %copy-done.29) | copy-start | bytes 49156
  546.0 143.3 %reduce-scatter.14.cloned.1.call-start = ((), (), s32[]{:S(2)}) async-start(), calls=%async_computation.16 | async-start | bytes 2228224 | tf_op jit(solution)/shard_map/reduce_scatter | solution.py:135
  582.0 2.3 copy-start.10
  608.4 15.2 %copy-start.23 = (pred[256,1024]{1,0:T(8,128)(4,1)S(1)}, pred[256,1024]{1,0:T(8,128)(4,1)}, u32[]{:S(2)}) copy-start(pred[256,1024]{1,0:T(8,128)(4,1)} %copy-done.22) | copy-start | bytes 786436
  626.2 63.1 %copy-start.16 = (bf16[256,256]{1,0:T(8,128)(2,1)S(1)}, bf16[256,256]{1,0:T(8,128)(2,1)}, u32[]{:S(2)}) copy-start(bf16[256,256]{1,0:T(8,128)(2,1)} %bitcast_select_fusion) | copy-start | bytes 393220
  626.2 100.8 %all-gather.32.cloned.1.call-start = ((), (), s32[]{:S(2)}) async-start(), calls=%async_computation.17 | async-start | bytes 2228224 | tf_op jit(solution)/shard_map/all_gather | solution.py:33
  690.9 112.3 %reduce-scatter.16.cloned.1.call-start = ((), (), s32[]{:S(2)}) async-start(), calls=%async_computation.18 | async-start | bytes 2228224 | tf_op jit(solution)/shard_map/reduce_scatter | solution.py:158
  698.1 31.2 %copy-start.28 = (f32[1,1,4096]{2,1,0:T(1,128)S(1)}, f32[1,1,4096]{2,1,0:T(1,128)}, u32[]{:S(2)}) copy-start(f32[1,1,4096]{2,1,0:T(1,128)} %copy-done.27) | copy-start | bytes 49156
  727.0 2.3 copy-start.7
  734.1 3.3 copy-start.2
  739.5 63.7 %copy-start.15 = (bf16[256,256]{1,0:T(8,128)(2,1)S(1)}, bf16[256,256]{1,0:T(8,128)(2,1)}, u32[]{:S(2)}) copy-start(bf16[256,256]{1,0:T(8,128)(2,1)} %add_convert_fusion.3) | copy-start | bytes 393220
  739.5 107.9 %all-gather.34.cloned.1.call-start = ((), (), s32[]{:S(2)}) async-start(), calls=%async_computation.19 | async-start | bytes 2228224 | tf_op jit(solution)/shard_map/all_gather | solution.py:33
  804.2 6.6 collective-permute-start.2
  811.4 143.3 %reduce-scatter.18.cloned.1.call-start = ((), (), s32[]{:S(2)}) async-start(), calls=%async_computation.20 | async-start | bytes 2228224 | tf_op jit(solution)/shard_map/reduce_scatter | solution.py:135
  847.5 2.2 copy-start.9
  873.8 15.2 %copy-start.24 = (pred[256,1024]{1,0:T(8,128)(4,1)S(1)}, pred[256,1024]{1,0:T(8,128)(4,1)}, u32[]{:S(2)}) copy-start(pred[256,1024]{1,0:T(8,128)(4,1)} %copy-done.22) | copy-start | bytes 786436
  891.7 63.1 %copy-start.12 = (bf16[256,256]{1,0:T(8,128)(2,1)S(1)}, bf16[256,256]{1,0:T(8,128)(2,1)}, u32[]{:S(2)}) copy-start(bf16[256,256]{1,0:T(8,128)(2,1)} %copy-done.11) | copy-start | bytes 393220
  891.7 100.8 %all-gather.36.cloned.1.call-start = ((), (), s32[]{:S(2)}) async-start(), calls=%async_computation.21 | async-start | bytes 2228224 | tf_op jit(solution)/shard_map/all_gather | solution.py:33
  956.4 111.0 %reduce-scatter.20.cloned.1.call-start = ((), (), s32[]{:S(2)}) async-start(), calls=%async_computation.22 | async-start | bytes 2228224 | tf_op jit(solution)/shard_map/reduce_scatter | solution.py:158
  992.5 2.2 copy-start.8
  999.5 2.0 copy-start.3
  1003.6 63.7 %copy-start.14 = (bf16[256,256]{1,0:T(8,128)(2,1)S(1)}, bf16[256,256]{1,0:T(8,128)(2,1)}, u32[]{:S(2)}) copy-start(bf16[256,256]{1,0:T(8,128)(2,1)} %add_convert_fusion.1) | copy-start | bytes 393220
  (5 other events, 5.8 us)
Sparse Core Ops, SparseCore 0:
  9.0 39.8 all-gather.37
  51.3 67.0 reduce-scatter.9
  120.0 40.9 all-gather.19
  162.6 34.5 all-gather.21
  198.7 52.3 all-gather.23
  252.7 52.9 all-gather.25
  308.1 64.2 reduce-scatter.7
  374.1 35.9 all-gather.39
  411.7 37.4 all-gather.27
  472.6 63.4 reduce-scatter.11
  546.1 35.8 all-gather.29
  626.4 62.8 reduce-scatter.13
  691.0 35.9 all-gather.31
  739.6 63.5 reduce-scatter.15
  811.5 35.8 all-gather.33
  891.8 62.8 reduce-scatter.17
  956.5 35.9 all-gather.35
  1003.7 63.5 reduce-scatter.19
where the time goes:
time: 1080 us
  waiting for transfers between devices  796 us (74%)
  blocking collectives  80.6 us (7%)
  local copies, waits for them, and re-layouts  71.7 us (7%)
  matrix products  67.8 us (6%)
  other arithmetic  33.9 us (3%)
  between operations  14.4 us (1%)
  starting transfers between devices  11.1 us (1%)
    reduce_scatter x3, waiting for transfers between devices, decoder_layer(): lax.psum_scatter(back_term.astype(jnp.bfloat16), 'mp', scatter_dimension=...  191 us
    reduce_scatter x3, waiting for transfers between devices, decoder_layer(): lax.psum_scatter(partial_value.astype(jnp.bfloat16), 'mp', scatter_dimens...  183 us
    all_gather x4, waiting for transfers between devices, row_product(): lax.all_gather(weight_rows, 'mp', axis=0, tiled=True)  176 us
    all_gather x6, waiting for transfers between devices, project(): lax.all_gather(local, 'mp', axis=1, tiled=True).astype(jnp.float32)  171 us
    all_gather x3, blocking collectives, causal(): piece_keys = lax.all_gather(keys, 'seq', axis=0, tiled=True)  40.7 us
    all_gather x3, blocking collectives, causal(): piece_values = lax.all_gather(values, 'seq', axis=0, tiled=True)  39.9 us
    all_gather x1, waiting for transfers between devices, on_device(): lax.all_gather(encoded_own.reshape(-1, NB_LEN, ENC_D), 'mp', axis=0, tile...  34.7 us
    reduce_scatter x1, waiting for transfers between devices, encode_rows(): lax.psum_scatter(jnp.where(inside[:, None], picked, 0.0).astype(jnp.bfloa...  31.3 us
  transfers between devices with their start and end apart: 21, of which 20 were waited for; matrix products, arithmetic and copies ran while one was open for 8% of the time, Pallas kernels for 0%

commit v1 on v0

v1 whole, which is shorter than its diff:
```python
import functools

import jax
import jax.numpy as jnp
from jax import lax
from jax.experimental import pallas as pl
from jax.experimental.pallas import tpu as pltpu
from jax.sharding import Mesh, PartitionSpec as P

D = 4096
HEAD = 128
ENC_D = 1024
ENC_HEADS = 16
ENC_HEAD = 64
BLOCK = 64
NB_LEN = 128
NEIGH = 2
BATCH = 2
CHIPS = 8
ROWS = 256
WIDTH = 256
UNITS = 4
HALF = ROWS // 2
MP = ("z", "y", "core")
KEYS = NEIGH * NB_LEN
VMEM_LIMIT = 48 * 1024 * 1024

epsilon = 1e-05
f32 = jnp.float32
bf16 = jnp.bfloat16


def params():
    return pltpu.CompilerParams(vmem_limit_bytes=VMEM_LIMIT)


def whole(shape):
    return pl.BlockSpec(shape, lambda *_: (0,) * len(shape))


SCALAR = pl.BlockSpec(memory_space=pltpu.SMEM)


def core_swap(value):
    return lax.ppermute(value, "core", [(0, 1), (1, 0)])


def section_swap(value):
    return lax.ppermute(value, "section", [(0, 1), (1, 0)])


def chips_to_chips(value):
    return lax.all_to_all(value, ("z", "y"), 0, 0, tiled=True)


def gather_rows(local):
    same = chips_to_chips(jnp.broadcast_to(local[None], (CHIPS,) + local.shape))
    return same, core_swap(same)


def scatter_sum(own, other):
    paired = (own.astype(f32) + core_swap(other).astype(f32)).astype(bf16)
    return jnp.sum(chips_to_chips(paired).astype(f32), axis=0)


def project_kernel(units, core_ref, same_ref, swap_ref, gain_ref, w_ref, out_ref, acc_ref, sq_ref):
    step = pl.program_id(0)
    core = core_ref[0]
    parts = w_ref.shape[0]

    @pl.when(step == 0)
    def _():
        acc_ref[...] = jnp.zeros_like(acc_ref)
        sq_ref[...] = jnp.zeros_like(sq_ref)

    for ref, at in ((same_ref, core), (swap_ref, 1 - core)):
        wide = ref[0].astype(f32)
        squares = wide * wide
        sq_ref[...] += squares[:, :128] + squares[:, 128:]
        scaled = (wide * gain_ref[0, pl.ds(at, 1), :]).astype(bf16)
        rows = pl.ds(pl.multiple_of(at * WIDTH, WIDTH), WIDTH)
        for part in range(parts):
            acc_ref[part] += jnp.dot(scaled, w_ref[part, rows, :], preferred_element_type=f32)

    @pl.when(step == CHIPS - 1)
    def _():
        mean = jnp.sum(sq_ref[...], axis=1, keepdims=True) / D
        root = jnp.sqrt(mean + epsilon)
        for part in range(parts):
            done = (acc_ref[part] / root).astype(bf16)
            if not units:
                out_ref[...] = done
                continue
            for unit in range(UNITS):
                h, half = divmod(unit, 2)
                cols = slice(h * HEAD, (h + 1) * HEAD)
                if part == 0:
                    out_ref[unit, :HALF, :] = done[half * HALF : (half + 1) * HALF, cols]
                else:
                    at = HALF + (part - 1) * ROWS
                    out_ref[unit, at : at + ROWS, :] = done[:, cols]


def project(core, same, swap, gains, weight, units):
    parts = weight.shape[0]
    out = (UNITS, HALF + 2 * ROWS, HEAD) if units else (ROWS, WIDTH)
    block = pl.BlockSpec((1, ROWS, WIDTH), lambda s: (s, 0, 0))
    return pl.pallas_call(
        functools.partial(project_kernel, units),
        grid=(CHIPS,),
        in_specs=[
            SCALAR,
            block,
            block,
            pl.BlockSpec((1, 2, WIDTH), lambda s: (s, 0, 0)),
            pl.BlockSpec((parts, 2 * WIDTH, WIDTH), lambda s: (0, s, 0)),
        ],
        out_specs=whole(out),
        out_shape=jax.ShapeDtypeStruct(out, bf16),
        scratch_shapes=[pltpu.VMEM((parts, ROWS, WIDTH), f32), pltpu.VMEM((ROWS, 128), f32)],
        compiler_params=params(),
    )(core, same, swap, gains.reshape(CHIPS, 2, WIDTH), weight)


def causal_kernel(half_ref, triple_ref, out_ref):
    scaling = HEAD ** (-0.5)
    row = lax.broadcasted_iota(jnp.int32, (HALF, ROWS), 0) + half_ref[0] * HALF
    col = lax.broadcasted_iota(jnp.int32, (HALF, ROWS), 1)
    for i in range(UNITS):
        queries = triple_ref[i, :HALF, :]
        numer = jnp.zeros((HALF, HEAD), f32)
        denom = jnp.zeros((HALF, 1), f32)
        for j in range(i + 1):
            keys = triple_ref[j, HALF : HALF + ROWS, :]
            values = triple_ref[j, HALF + ROWS :, :]
            scores = lax.dot_general(
                queries, keys, (((1,), (1,)), ((), ())), preferred_element_type=f32
            )
            weights = jnp.exp(scores * scaling)
            if i == j:
                weights = jnp.where(col <= row, weights, 0.0)
            denom += jnp.sum(weights, axis=1, keepdims=True)
            numer += jnp.dot(weights.astype(bf16), values, preferred_element_type=f32)
        out_ref[i] = (numer / denom).astype(bf16)


def causal(half, triple):
    out = (UNITS, HALF, HEAD)
    return pl.pallas_call(
        causal_kernel,
        in_specs=[SCALAR, whole(triple.shape)],
        out_specs=whole(out),
        grid=(1,),
        out_shape=jax.ShapeDtypeStruct(out, bf16),
        compiler_params=params(),
    )(half, triple)


def crossed_kernel(asked_ref, prev_ref, pairs_ref, out_ref):
    scaling = HEAD ** (-0.5)
    row = lax.broadcasted_iota(jnp.int32, (BLOCK, 2 * KEYS), 0)
    col = lax.broadcasted_iota(jnp.int32, (BLOCK, 2 * KEYS), 1)
    allowed = (row < BLOCK - 1) == (col < KEYS)
    for h in range(2):
        kcols = slice(h * HEAD, (h + 1) * HEAD)
        vcols = slice((2 + h) * HEAD, (3 + h) * HEAD)
        for i in range(ROWS // BLOCK):
            queries = asked_ref[i * BLOCK : (i + 1) * BLOCK, kcols]
            if i == 0:
                keys = jnp.concatenate([prev_ref[:, kcols], pairs_ref[0, :, kcols]], axis=0)
                values = jnp.concatenate([prev_ref[:, vcols], pairs_ref[0, :, vcols]], axis=0)
            else:
                keys = pairs_ref[i - 1 : i + 1, :, kcols].reshape(2 * KEYS, HEAD)
                values = pairs_ref[i - 1 : i + 1, :, vcols].reshape(2 * KEYS, HEAD)
            scores = lax.dot_general(
                queries, keys, (((1,), (1,)), ((), ())), preferred_element_type=f32
            )
            weights = jnp.where(allowed, jnp.exp(scores * scaling), 0.0)
            denom = jnp.sum(weights, axis=1, keepdims=True)
            numer = jnp.dot(weights.astype(bf16), values, preferred_element_type=f32)
            half, at = divmod(i, 2)
            out_ref[h * 2 + half, at * BLOCK : (at + 1) * BLOCK, :] = (numer / denom).astype(bf16)


def cross(asked, prev, pairs):
    out = (UNITS, HALF, HEAD)
    return pl.pallas_call(
        crossed_kernel,
        out_shape=jax.ShapeDtypeStruct(out, bf16),
        compiler_params=params(),
    )(asked, prev, pairs)


def terms_kernel(core_ref, mixed_ref, w_ref, own_ref, other_ref, left_ref):
    core = core_ref[0]

    @pl.when(pl.program_id(0) == 0)
    def _():
        for unit in range(UNITS):
            h, half = divmod(unit, 2)
            left_ref[half * HALF : (half + 1) * HALF, h * HEAD : (h + 1) * HEAD] = mixed_ref[unit]

    product = jnp.dot(left_ref[...], w_ref[...], preferred_element_type=f32).astype(bf16)

    @pl.when(core == 0)
    def _():
        for at in range(2):
            own_ref[at] = product[:, 2 * at * WIDTH : (2 * at + 1) * WIDTH]
            other_ref[at] = product[:, (2 * at + 1) * WIDTH : (2 * at + 2) * WIDTH]

    @pl.when(core == 1)
    def _():
        for at in range(2):
            other_ref[at] = product[:, 2 * at * WIDTH : (2 * at + 1) * WIDTH]
            own_ref[at] = product[:, (2 * at + 1) * WIDTH : (2 * at + 2) * WIDTH]


def terms(core, mixed, weight):
    block = pl.BlockSpec((2, ROWS, WIDTH), lambda s: (s, 0, 0))
    out = jax.ShapeDtypeStruct((CHIPS, ROWS, WIDTH), bf16)
    return pl.pallas_call(
        terms_kernel,
        grid=(CHIPS // 2,),
        in_specs=[
            SCALAR,
            whole((UNITS, HALF, HEAD)),
            pl.BlockSpec((WIDTH, 4 * WIDTH), lambda s: (0, s)),
        ],
        out_specs=[block, block],
        out_shape=[out, out],
        scratch_shapes=[pltpu.VMEM((ROWS, WIDTH), bf16)],
        compiler_params=params(),
    )(core, mixed, weight)


def look_up(ids, enc_embed, core, section):
    vocab_here = enc_embed.shape[0]
    mine = lax.dynamic_slice_in_dim(ids, section * (NB_LEN // 2), NB_LEN // 2, axis=1)
    wanted = mine.reshape(CHIPS, 2, NB_LEN // 2) - lax.axis_index(MP) * vocab_here

    def rows(at):
        picks = lax.dynamic_index_in_dim(wanted, at, 1, keepdims=False).reshape(-1)
        inside = (picks >= 0) & (picks < vocab_here)
        found = enc_embed[jnp.clip(picks, 0, vocab_here - 1)]
        found = jnp.where(inside[:, None], found, jnp.zeros((), bf16))
        return found.reshape(CHIPS, NB_LEN // 2, ENC_D)

    paired = core_swap(rows(1 - core)) + rows(core)
    half = jnp.sum(chips_to_chips(paired).astype(f32), axis=0).astype(bf16)
    far = section_swap(half)
    return jnp.where(
        section == 0, jnp.concatenate([half, far], axis=0), jnp.concatenate([far, half], axis=0)
    )


def weight_pieces(section, enc_qkv, enc_out, enc_up, enc_down):
    width = ENC_D // 2
    triple = lax.dynamic_slice_in_dim(enc_qkv, section * width, width, axis=2)
    up = enc_up.reshape(64, 16, 2, 2, 64)
    up = lax.dynamic_index_in_dim(up, section, 2, keepdims=False)
    up = jnp.transpose(up, (2, 0, 1, 3)).reshape(2, 64, 2, width)
    down = lax.dynamic_slice_in_dim(enc_down, section * 128, 128, axis=0)
    down = down.reshape(2, 64, 2, width)
    local = jnp.concatenate(
        [
            jnp.transpose(up, (0, 2, 1, 3)).reshape(4, 64, width),
            jnp.transpose(down, (0, 2, 1, 3)).reshape(4, 64, width),
            jnp.transpose(triple, (1, 0, 2)),
            jnp.transpose(enc_out.reshape(64, 2, width), (1, 0, 2)),
        ],
        axis=0,
    )
    return lax.all_gather(local, MP, axis=1, tiled=True)


def scaled_rows(values, gain):
    wide = values.astype(f32)
    root = jnp.sqrt(jnp.mean(wide * wide, axis=1, keepdims=True) + epsilon)
    return (wide * gain).astype(bf16), root


def enc_mix_kernel(section_ref, x_ref, gain_ref, q_ref, k_ref, v_ref, o0_ref, o1_ref, out_ref, mix_ref):
    scaled, root = scaled_rows(x_ref[...], gain_ref[...])
    triple = [
        (jnp.dot(scaled, ref[0], preferred_element_type=f32) / root).astype(bf16)
        for ref in (q_ref, k_ref, v_ref)
    ]
    for head in range(ENC_HEADS // 2):
        cols = slice(head * ENC_HEAD, (head + 1) * ENC_HEAD)
        scores = lax.dot_general(
            triple[0][:, cols],
            triple[1][:, cols],
            (((1,), (1,)), ((), ())),
            preferred_element_type=f32,
        )
        weights = jnp.exp(scores * ENC_HEAD ** (-0.5))
        denom = jnp.sum(weights, axis=1, keepdims=True)
        numer = jnp.dot(weights.astype(bf16), triple[2][:, cols], preferred_element_type=f32)
        mix_ref[:, cols] = (numer / denom).astype(bf16)
    mixed = mix_ref[...]
    width = ENC_D // 2
    rows = pl.ds(pl.multiple_of(section_ref[0] * width, width), width)
    for at, ref in enumerate((o0_ref, o1_ref)):
        part = jnp.dot(mixed, ref[0, rows, :], preferred_element_type=f32)
        out_ref[:, at * width : (at + 1) * width] = part.astype(bf16)


def enc_feed_kernel(x_ref, gain_ref, w_ref, out_ref):
    scaled, root = scaled_rows(x_ref[...], gain_ref[...])
    width = ENC_D // 2
    hidden = [
        jax.nn.gelu(
            jnp.dot(scaled, w_ref[piece], preferred_element_type=f32) / root, approximate=True
        ).astype(bf16)
        for piece in range(4)
    ]
    for at in range(2):
        part = jnp.zeros((NB_LEN, width), f32)
        for piece in range(4):
            rows = slice((piece % 2) * width, (piece % 2 + 1) * width)
            down = w_ref[4 + 2 * (piece // 2) + at, rows, :]
            part += jnp.dot(hidden[piece], down, preferred_element_type=f32)
        out_ref[:, at * width : (at + 1) * width] = part.astype(bf16)


def encode(embedded, enc_norms, pieces, section):
    out = jax.ShapeDtypeStruct((NB_LEN, ENC_D), bf16)
    width = ENC_D // 2
    full = whole((NB_LEN, ENC_D))
    gain = whole((1, ENC_D))

    def piece(at):
        return pl.BlockSpec((1, ENC_D, width), lambda s: (at, 0, 0))

    mixed = pl.pallas_call(
        enc_mix_kernel,
        grid=(1,),
        in_specs=[SCALAR, full, gain] + [piece(8 + at) for at in range(5)],
        out_specs=full,
        out_shape=out,
        scratch_shapes=[pltpu.VMEM((NB_LEN, width), bf16)],
        compiler_params=params(),
    )(section, embedded, enc_norms[:1], *([pieces] * 5))
    inner = (embedded.astype(f32) + (mixed.astype(f32) + section_swap(mixed).astype(f32))).astype(
        bf16
    )
    fed = pl.pallas_call(
        enc_feed_kernel,
        grid=(1,),
        in_specs=[full, gain, pl.BlockSpec((8, ENC_D, width), lambda s: (0, 0, 0))],
        out_specs=full,
        out_shape=out,
        compiler_params=params(),
    )(inner, enc_norms[1:], pieces)
    return (inner.astype(f32) + (fed.astype(f32) + section_swap(fed).astype(f32))).astype(bf16)


def pairs_kernel(core_ref, same_ref, swap_ref, w_ref, out_ref):
    core = core_ref[0]
    for ref, at in ((same_ref, core), (swap_ref, 1 - core)):
        out_ref[at] = jnp.dot(ref[0], w_ref[...], preferred_element_type=f32).astype(bf16)


def make_pairs(core, same, swap, weight):
    block = pl.BlockSpec((1, NB_LEN, ENC_D), lambda s: (s, 0, 0))
    return pl.pallas_call(
        pairs_kernel,
        grid=(CHIPS,),
        in_specs=[SCALAR, block, block, whole((ENC_D, 2 * WIDTH))],
        out_specs=pl.BlockSpec((2, NB_LEN, 2 * WIDTH), lambda s: (s, 0, 0)),
        out_shape=jax.ShapeDtypeStruct((2 * CHIPS, NB_LEN, 2 * WIDTH), bf16),
        compiler_params=params(),
    )(core, same, swap, weight)


def self_part(core, half, states, weights):
    norms, triple_w, out_w, query_w, back_w = weights
    same, swap = gather_rows(states)
    triple = project(core, same, swap, norms[0], triple_w, True)
    triple = lax.all_to_all(triple, "seq", 0, 0, tiled=True)
    mixed = lax.all_to_all(causal(half, triple), "seq", 0, 0, tiled=True)
    middle = (states.astype(f32) + scatter_sum(*terms(core, mixed, out_w))).astype(bf16)
    same, swap = gather_rows(middle)
    return middle, project(core, same, swap, norms[1], query_w[None], False)


def cross_part(core, middle, asked, prev, pairs, weights):
    crossed = cross(asked, prev, pairs)
    return (middle.astype(f32) + scatter_sum(*terms(core, crossed, weights[4]))).astype(bf16)


def on_device(
    hidden_states,
    neighbour_ids,
    neighbour_table,
    enc_embed,
    enc_norms,
    enc_qkv,
    enc_out,
    enc_up,
    enc_down,
    dec_norms,
    dec_qkv,
    dec_out,
    cross_query,
    cross_pair,
    cross_out,
):
    section = lax.axis_index("section").astype(jnp.int32)
    core_at = lax.axis_index("core").astype(jnp.int32)
    core = jnp.reshape(core_at, (1,))
    half = jnp.reshape(lax.axis_index("seq").astype(jnp.int32) % 2, (1,))
    blocks_here = neighbour_table.shape[1]
    pieces = weight_pieces(section, enc_qkv, enc_out, enc_up, enc_down)
    slot_ids = neighbour_ids[neighbour_table.reshape(-1)]
    embedded = look_up(slot_ids, enc_embed, core_at, section)
    encoded = encode(embedded, enc_norms, pieces, jnp.reshape(section, (1,)))
    same, swap = gather_rows(encoded)
    pairs = make_pairs(core, same, swap, cross_pair[0].reshape(ENC_D, 2 * WIDTH))
    pairs = pairs.reshape(BATCH, blocks_here, KEYS, 2 * WIDTH)
    count = lax.axis_size("seq")
    prev = lax.ppermute(pairs[:, -1], "seq", [(i, i + 1) for i in range(count - 1)])
    weights = (
        dec_norms[0],
        jnp.transpose(dec_qkv[0], (1, 0, 2)),
        dec_out[0],
        cross_query[0],
        cross_out[0],
    )

    def layer(states, at):
        middle, asked = self_part(core, half, states, weights)
        return cross_part(core, middle, asked, prev[at], pairs[at], weights)

    second = []
    for at in range(BATCH):
        first = layer(hidden_states[at], at)
        second.append(layer(section_swap(first), at))
    return jnp.where(section == 0, section_swap(second[0]), second[1])[None]


def solution(mesh):
    devices = mesh.devices
    sections, seqs = devices.shape[:2]
    split = Mesh(
        devices.reshape(sections, seqs, 2, 4, 2), ("section", "seq", "z", "y", "core")
    )
    mp = ("z", "y", "core")
    return jax.shard_map(
        on_device,
        mesh=split,
        in_specs=(
            P(None, "seq", mp),
            P(),
            P(None, "seq", None),
            P(mp, None),
            P(),
            P(mp, None, None),
            P(mp, None),
            P(mp, None),
            P(mp, None),
            P("section", None, None),
            P("section", None, None, mp),
            P("section", mp, None),
            P("section", None, mp),
            P("section", None, None, mp),
            P("section", mp, None),
        ),
        out_specs=P("section", "seq", mp),
        check_vma=False,
    )
```

time: 1080 us -> 626 us (0.58)
  waiting for transfers between devices: 796 us -> 238 us
  starting transfers between devices: 11.1 us -> 118 us
  Pallas kernels: 0 us -> 95.3 us
  matrix products: 67.8 us -> 0 us
  local copies, waits for them, and re-layouts: 71.7 us -> 46.4 us
  blocking collectives: 80.6 us -> 65.7 us
    reduce_scatter x7 -> x0, waiting for transfers between devices: 405 us -> none  [the longest x3 191 us: decoder_layer(): lax.psum_scatter(back_term.astype(jnp.bfloat16), 'mp', scatter_dimension=...]
    all_gather x11 -> x1, waiting for transfers between devices: 382 us -> 0.02 us  [weight_pieces(): return lax.all_gather(local, MP, axis=1, tiled=True)]
    all_to_all x0 -> x21, waiting for transfers between devices: none -> 196 us  [the longest x17 191 us: chips_to_chips(): return lax.all_to_all(value, ('z', 'y'), 0, 0, tiled=True)]
    all_to_all x0 -> x21, starting transfers between devices: none -> 96.2 us  [the longest x17 81 us: chips_to_chips(): return lax.all_to_all(value, ('z', 'y'), 0, 0, tiled=True)]
    pallas_call x0 -> x27, Pallas kernels: none -> 95.3 us  [the longest x8 50.2 us: project(): pl.pallas_call(functools.partial(project_kernel, units), grid=(CHIPS,), i...]
    all_gather x6 -> x0, blocking collectives: 80.6 us -> none  [the longest x3 40.7 us: causal(): piece_keys = lax.all_gather(keys, 'seq', axis=0, tiled=True)]
    dot_general x30 -> x0, matrix products: 67.8 us -> none  [the longest x6 22.4 us: project(): summed = jnp.dot(scaled, weight, preferred_element_type=jnp.float32)]
    all_to_all x0 -> x5, blocking collectives: none -> 65.7 us  [the longest x2 30.8 us: self_part(): triple = lax.all_to_all(triple, 'seq', 0, 0, tiled=True)]
  transfers between devices with their start and end apart: 21 -> 47, of which waited for: 20 -> 25; matrix products, arithmetic and copies ran while one was open for 8% -> 9% of each run, Pallas kernels for 0% -> 16%
where the time goes in v1:
time: 626 us; the launch traced here: 614 us
  waiting for transfers between devices  238 us (38%)
  starting transfers between devices  118 us (19%)
  Pallas kernels  95.3 us (15%)
  blocking collectives  65.7 us (10%)
  local copies, waits for them, and re-layouts  46.4 us (7%)
  other arithmetic  35.9 us (6%)
  between operations  14.8 us (2%)
    all_to_all x17, waiting for transfers between devices, chips_to_chips(): return lax.all_to_all(value, ('z', 'y'), 0, 0, tiled=True)  191 us
    all_to_all x17, starting transfers between devices, chips_to_chips(): return lax.all_to_all(value, ('z', 'y'), 0, 0, tiled=True)  81 us
    pallas_call x8, Pallas kernels, project(): pl.pallas_call(functools.partial(project_kernel, units), grid=(CHIPS,), i...  50.2 us
    ppermute x6, waiting for transfers between devices, section_swap(): return lax.ppermute(value, 'section', [(0, 1), (1, 0)])  36.6 us
    all_to_all x2, blocking collectives, self_part(): triple = lax.all_to_all(triple, 'seq', 0, 0, tiled=True)  30.8 us
    all_to_all x1, blocking collectives, chips_to_chips(): return lax.all_to_all(value, ('z', 'y'), 0, 0, tiled=True)  18.2 us
    pallas_call x8, Pallas kernels, terms(): pl.pallas_call(terms_kernel, grid=(CHIPS // 2,), in_specs=[SCALAR, whole(...  17.4 us
    all_to_all x2, blocking collectives, self_part(): mixed = lax.all_to_all(causal(half, triple), 'seq', 0, 0, tiled=True)  16.7 us
  transfers between devices with their start and end apart: 47, of which 25 were waited for; matrix products, arithmetic and copies ran while one was open for 9% of the time, Pallas kernels for 16%

profile of v1, /device:TPU:0, one launch (start us, length us, event | category | flops | bytes accessed | tf_op | source)
XLA Modules:
  0.0 614.3 jit_solution(17349698790594761180)
XLA Ops:
  13.9 5.9 all-to-all-start
  20.9 18.5 %all-to-all-done.same_ref = bf16[8,256,256]{2,1,0:T(8,128)(2,1)S(1)} async-done(((bf16[8,256,256]{2,1,0:T(8,128)(2,1)}), bf16[8,256,256]{2,1,0:T(8,128)(2,1)S(1)}, u32[]{:S(2)}, u32[]{:S(2)}) %all-to-all-start) | async-done | bytes 1048608 | tf_op jit(solution)/shard_map/all_to_all | solution.py:53
  40.4 7.1 %all-to-all-start.14 = ((bf16[8,256,256]{2,1,0:T(8,128)(2,1)}), bf16[8,256,256]{2,1,0:T(8,128)(2,1)S(1)}, u32[]{:S(2)}, u32[]{:S(2)}) async-start(bf16[8,256,256]{2,1,0:T(8,128)(2,1)} %broadcast_in_dim.91), calls=%async_computation.14 | async-start | bytes 2097152 | tf_op jit(solution)/shard_map/all_to_all | solution.py:53
  47.5 8.0 %gather_fusion.1 = bf16[512,1024]{1,0:T(8,128)(2,1)} fusion(bf16[4000,1024]{1,0:T(8,128)(2,1)} %param.18, s32[1024]{0:T(1024)S(1)} %pad_clamp_fusion.1), kind=kCustom, calls=%fused_computation.1 | custom fusion | bytes 2099200 | tf_op jit(solution)/shard_map/gather | solution.py:244
  58.5 7.9 %shard_map.145 = bf16[4,640,128]{2,1,0:T(8,128)(2,1)} custom-call(s32[1]{0:T(128)} %bitcast.1.core_ref, bf16[8,256,256]{2,1,0:T(8,128)(2,1)S(1)} %all-to-all-done.same_ref, bf16[8,256,256]{2,1,0:T(8,128)(2,1)S(1)} %collective-permute-done.swap_ref, f32[8,2,256]{2,1,0:T(2,128)S(1)} %reshape_squeeze.6.gain_ref, bf16[3,4096,256]{2,1,0:T(8,128)(2,1)} %bitcast.99), custom_call_target="tpu_custom_call" | custom-call | tf_op jit(solution)/shard_map/pallas_call | solution.py:108
  69.9 4.3 all-to-all-start.1
  74.2 8.0 %gather_fusion.2 = bf16[512,1024]{1,0:T(8,128)(2,1)} fusion(bf16[4000,1024]{1,0:T(8,128)(2,1)} %param.18, s32[1024]{0:T(1024)S(1)} %pad_clamp_fusion), kind=kCustom, calls=%fused_computation.2 | custom fusion | bytes 2099200 | tf_op jit(solution)/shard_map/gather | solution.py:244
  94.8 7.1 %all-to-all-start.5 = ((bf16[8,64,1024]{2,1,0:T(8,128)(2,1)}), bf16[8,64,1024]{2,1,0:T(8,128)(2,1)}, u32[]{:S(2)}, u32[]{:S(2)}) async-start(bf16[8,64,1024]{2,1,0:T(8,128)(2,1)} %select_add_fusion), calls=%async_computation.5 | async-start | bytes 2097152 | tf_op jit(solution)/shard_map/all_to_all | solution.py:53
  105.8 7.2 %shard_map.160 = bf16[4,640,128]{2,1,0:T(8,128)(2,1)S(1)} custom-call(s32[1]{0:T(128)} %bitcast.1.core_ref, bf16[8,256,256]{2,1,0:T(8,128)(2,1)S(1)} %all-to-all-done.14.same_ref, bf16[8,256,256]{2,1,0:T(8,128)(2,1)} %collective-permute-done.16.swap_ref, f32[8,2,256]{2,1,0:T(2,128)S(1)} %reshape_squeeze.6.gain_ref, bf16[3,4096,256]{2,1,0:T(8,128)(2,1)} %bitcast.100), custom_call_target="tpu_custom_call" | custom-call | tf_op jit(solution)/shard_map/pallas_call | solution.py:108
  113.9 5.2 all-to-all-done.5
  124.0 4.1 collective-permute-start.4
  138.0 4.7 shard_map.149
  149.1 6.0 all-to-all-start.3
  155.3 4.7 shard_map.150
  161.1 12.3 %collective-permute-done.6 = bf16[128,1024]{1,0:T(8,128)(2,1)S(1)} collective-permute-done((bf16[128,1024]{1,0:T(8,128)(2,1)S(1)}, bf16[128,1024]{1,0:T(8,128)(2,1)S(1)}, u32[]{:S(2)}, u32[]{:S(2)}) %collective-permute-start.6) | collective-permute-done | bytes 262176 | tf_op jit(solution)/shard_map/ppermute | solution.py:49
  175.2 4.3 all-to-all-start.6
  185.3 21.0 %all-to-all-done.6.same_ref = bf16[8,128,1024]{2,1,0:T(8,128)(2,1)} async-done(((bf16[8,128,1024]{2,1,0:T(8,128)(2,1)}), bf16[8,128,1024]{2,1,0:T(8,128)(2,1)}, u32[]{:S(2)}, u32[]{:S(2)}) %all-to-all-start.6) | async-done | bytes 2097184 | tf_op jit(solution)/shard_map/all_to_all | solution.py:53
  206.2 6.1 all-to-all-start.17
  213.8 13.3 %all-to-all-done.17 = bf16[8,256,256]{2,1,0:T(8,128)(2,1)S(1)} async-done(((bf16[8,256,256]{2,1,0:T(8,128)(2,1)}), bf16[8,256,256]{2,1,0:T(8,128)(2,1)S(1)}, u32[]{:S(2)}, u32[]{:S(2)}) %all-to-all-start.17) | async-done | bytes 1048608 | tf_op jit(solution)/shard_map/all_to_all | solution.py:53
  228.4 18.2 %all_to_all.130.same_ref = bf16[8,256,256]{2,1,0:T(8,128)(2,1)S(1)} all-to-all(bf16[8,256,256]{2,1,0:T(8,128)(2,1)S(1)} %broadcast_in_dim.44), channel_id=1, replica_groups=mesh['section'=2,'seq'=4,'z'=2,'y'=4,'core'=2] {'z','y'}, dimensions={0} | all-to-all | bytes 2097152 | tf_op jit(solution)/shard_map/all_to_all | solution.py:53
  247.8 4.2 all-to-all-start.18
  253.6 6.7 %shard_map.151 = bf16[16,128,512]{2,1,0:T(8,128)(2,1)S(1)} custom-call(s32[1]{0:T(128)} %bitcast.1.core_ref, bf16[8,128,1024]{2,1,0:T(8,128)(2,1)} %all-to-all-done.6.same_ref, bf16[8,128,1024]{2,1,0:T(8,128)(2,1)} %collective-permute-done.7.swap_ref, bf16[1024,512]{1,0:T(8,128)(2,1)S(1)} %bitcast.98), custom_call_target="tpu_custom_call" | custom-call | tf_op jit(solution)/shard_map/pallas_call | solution.py:366
  270.4 5.2 shard_map.148.asked_ref
  282.4 5.1 shard_map.163.asked_ref
  294.3 5.3 all-to-all-start.7
  302.4 13.2 %all-to-all-done.7 = bf16[8,256,256]{2,1,0:T(8,128)(2,1)} async-done(((bf16[8,256,256]{2,1,0:T(8,128)(2,1)}), bf16[8,256,256]{2,1,0:T(8,128)(2,1)}, u32[]{:S(2)}, u32[]{:S(2)}) %all-to-all-start.7) | async-done | bytes 1048608 | tf_op jit(solution)/shard_map/all_to_all | solution.py:53
  315.6 4.2 all-to-all-start.19
  322.0 13.7 %all-to-all-done.19 = bf16[8,256,256]{2,1,0:T(8,128)(2,1)} async-done(((bf16[8,256,256]{2,1,0:T(8,128)(2,1)}), bf16[8,256,256]{2,1,0:T(8,128)(2,1)}, u32[]{:S(2)}, u32[]{:S(2)}) %all-to-all-start.19) | async-done | bytes 1048608 | tf_op jit(solution)/shard_map/all_to_all | solution.py:53
  340.6 5.1 collective-permute-done.10
  347.4 4.2 all-to-all-start.8
  353.3 14.3 %collective-permute-done.20 = bf16[256,256]{1,0:T(8,128)(2,1)} collective-permute-done((bf16[256,256]{1,0:T(8,128)(2,1)}, bf16[256,256]{1,0:T(8,128)(2,1)}, u32[]{:S(2)}, u32[]{:S(2)}) %collective-permute-start.20) | collective-permute-done | bytes 131104 | tf_op jit(solution)/shard_map/ppermute | solution.py:49
  369.5 4.3 all-to-all-start.20
  373.9 15.4 %all-to-all-done.20.same_ref = bf16[8,256,256]{2,1,0:T(8,128)(2,1)} async-done(((bf16[8,256,256]{2,1,0:T(8,128)(2,1)}), bf16[8,256,256]{2,1,0:T(8,128)(2,1)}, u32[]{:S(2)}, u32[]{:S(2)}) %all-to-all-start.20) | async-done | bytes 1048608 | tf_op jit(solution)/shard_map/all_to_all | solution.py:53
  389.3 7.4 %shard_map.154 = bf16[4,640,128]{2,1,0:T(8,128)(2,1)S(1)} custom-call(s32[1]{0:T(128)} %bitcast.1.core_ref, bf16[8,256,256]{2,1,0:T(8,128)(2,1)} %all-to-all-done.8.same_ref, bf16[8,256,256]{2,1,0:T(8,128)(2,1)} %collective-permute-done.11.swap_ref, f32[8,2,256]{2,1,0:T(2,128)S(1)} %reshape_squeeze.6.gain_ref, bf16[3,4096,256]{2,1,0:T(8,128)(2,1)} %bitcast.101), custom_call_target="tpu_custom_call" | custom-call | tf_op jit(solution)/shard_map/pallas_call | solution.py:108
  396.7 16.6 %all_to_all.131.triple_ref = bf16[4,640,128]{2,1,0:T(8,128)(2,1)S(1)} all-to-all(bf16[4,640,128]{2,1,0:T(8,128)(2,1)S(1)} %shard_map.154), channel_id=1, replica_groups=mesh['section'=2,'seq'=4,'z'=2,'y'=4,'core'=2] {'seq'}, dimensions={0} | all-to-all | bytes 1310720 | tf_op jit(solution)/shard_map/all_to_all | solution.py:380
  414.4 8.4 %all_to_all.132.mixed_ref = bf16[4,128,128]{2,1,0:T(8,128)(2,1)S(1)} all-to-all(bf16[4,128,128]{2,1,0:T(8,128)(2,1)S(1)} %shard_map.155), channel_id=1, replica_groups=mesh['section'=2,'seq'=4,'z'=2,'y'=4,'core'=2] {'seq'}, dimensions={0} | all-to-all | bytes 262144 | tf_op jit(solution)/shard_map/all_to_all | solution.py:381
  424.6 7.2 %shard_map.166 = bf16[4,640,128]{2,1,0:T(8,128)(2,1)S(1)} custom-call(s32[1]{0:T(128)} %bitcast.1.core_ref, bf16[8,256,256]{2,1,0:T(8,128)(2,1)} %all-to-all-done.20.same_ref, bf16[8,256,256]{2,1,0:T(8,128)(2,1)S(1)} %collective-permute-done.21.swap_ref, f32[8,2,256]{2,1,0:T(2,128)S(1)} %reshape_squeeze.6.gain_ref, bf16[3,4096,256]{2,1,0:T(8,128)(2,1)} %bitcast.102), custom_call_target="tpu_custom_call" | custom-call | tf_op jit(solution)/shard_map/pallas_call | solution.py:108
  431.7 14.2 %all_to_all.133.triple_ref = bf16[4,640,128]{2,1,0:T(8,128)(2,1)S(1)} all-to-all(bf16[4,640,128]{2,1,0:T(8,128)(2,1)S(1)} %shard_map.166), channel_id=1, replica_groups=mesh['section'=2,'seq'=4,'z'=2,'y'=4,'core'=2] {'seq'}, dimensions={0} | all-to-all | bytes 1310720 | tf_op jit(solution)/shard_map/all_to_all | solution.py:380
  447.1 8.4 %all_to_all.134.mixed_ref = bf16[4,128,128]{2,1,0:T(8,128)(2,1)S(1)} all-to-all(bf16[4,128,128]{2,1,0:T(8,128)(2,1)S(1)} %shard_map.167), channel_id=1, replica_groups=mesh['section'=2,'seq'=4,'z'=2,'y'=4,'core'=2] {'seq'}, dimensions={0} | all-to-all | bytes 262144 | tf_op jit(solution)/shard_map/all_to_all | solution.py:381
  466.5 14.1 %all-to-all-done.11 = bf16[8,256,256]{2,1,0:T(8,128)(2,1)S(1)} async-done(((bf16[8,256,256]{2,1,0:T(8,128)(2,1)}), bf16[8,256,256]{2,1,0:T(8,128)(2,1)S(1)}, u32[]{:S(2)}, u32[]{:S(2)}) %all-to-all-start.11) | async-done | bytes 1048608 | tf_op jit(solution)/shard_map/all_to_all | solution.py:53
  485.2 14.8 %all-to-all-done.23 = bf16[8,256,256]{2,1,0:T(8,128)(2,1)S(1)} async-done(((bf16[8,256,256]{2,1,0:T(8,128)(2,1)}), bf16[8,256,256]{2,1,0:T(8,128)(2,1)S(1)}, u32[]{:S(2)}, u32[]{:S(2)}) %all-to-all-start.23) | async-done | bytes 1048608 | tf_op jit(solution)/shard_map/all_to_all | solution.py:53
  507.2 13.4 %all-to-all-done.12.same_ref = bf16[8,256,256]{2,1,0:T(8,128)(2,1)S(1)} async-done(((bf16[8,256,256]{2,1,0:T(8,128)(2,1)}), bf16[8,256,256]{2,1,0:T(8,128)(2,1)S(1)}, u32[]{:S(2)}, u32[]{:S(2)}) %all-to-all-start.12) | async-done | bytes 1048608 | tf_op jit(solution)/shard_map/all_to_all | solution.py:53
  521.9 4.2 all-to-all-start.24
  526.3 15.7 %all-to-all-done.24.same_ref = bf16[8,256,256]{2,1,0:T(8,128)(2,1)} async-done(((bf16[8,256,256]{2,1,0:T(8,128)(2,1)}), bf16[8,256,256]{2,1,0:T(8,128)(2,1)}, u32[]{:S(2)}, u32[]{:S(2)}) %all-to-all-start.24) | async-done | bytes 1048608 | tf_op jit(solution)/shard_map/all_to_all | solution.py:53
  545.1 5.2 shard_map.157.asked_ref
  554.0 5.1 shard_map.169.asked_ref
  570.6 14.1 %all-to-all-done.13 = bf16[8,256,256]{2,1,0:T(8,128)(2,1)S(1)} async-done(((bf16[8,256,256]{2,1,0:T(8,128)(2,1)}), bf16[8,256,256]{2,1,0:T(8,128)(2,1)S(1)}, u32[]{:S(2)}, u32[]{:S(2)}) %all-to-all-start.13) | async-done | bytes 1048608 | tf_op jit(solution)/shard_map/all_to_all | solution.py:53
  591.7 12.5 %all-to-all-done.25 = bf16[8,256,256]{2,1,0:T(8,128)(2,1)S(1)} async-done(((bf16[8,256,256]{2,1,0:T(8,128)(2,1)}), bf16[8,256,256]{2,1,0:T(8,128)(2,1)S(1)}, u32[]{:S(2)}, u32[]{:S(2)}) %all-to-all-start.25) | async-done | bytes 1048608 | tf_op jit(solution)/shard_map/all_to_all | solution.py:53
  (230 shorter events, 163.1 us)
Async XLA Ops:
  6.5 131.5 %all-gather.2.cloned.1.call-start = ((), (), s32[]{:S(2)}) async-start(), calls=%async_computation.26 | async-start | bytes 14483456 | tf_op jit(solution)/shard_map/all_gather | solution.py:273
  13.9 25.5 %all-to-all-start = ((bf16[8,256,256]{2,1,0:T(8,128)(2,1)}), bf16[8,256,256]{2,1,0:T(8,128)(2,1)S(1)}, u32[]{:S(2)}, u32[]{:S(2)}) async-start(bf16[8,256,256]{2,1,0:T(8,128)(2,1)} %broadcast_in_dim.42), calls=%async_computation | async-start | bytes 2097152 | tf_op jit(solution)/shard_map/all_to_all | solution.py:53
  40.4 29.5 %all-to-all-start.14 = ((bf16[8,256,256]{2,1,0:T(8,128)(2,1)}), bf16[8,256,256]{2,1,0:T(8,128)(2,1)S(1)}, u32[]{:S(2)}, u32[]{:S(2)}) async-start(bf16[8,256,256]{2,1,0:T(8,128)(2,1)} %broadcast_in_dim.91), calls=%async_computation.14 | async-start | bytes 2097152 | tf_op jit(solution)/shard_map/all_to_all | solution.py:53
  47.5 11.0 %collective-permute-start = (bf16[8,256,256]{2,1,0:T(8,128)(2,1)S(1)}, bf16[8,256,256]{2,1,0:T(8,128)(2,1)S(1)}, u32[]{:S(2)}, u32[]{:S(2)}) collective-permute-start(bf16[8,256,256]{2,1,0:T(8,128)(2,1)S(1)} %all-to-all-done.same_ref), channel_id=1, source_target_pairs={{0,1},{1,0},{2,3},{3,2},{4,5},{5,4},{6,7},{7,6},{8,9},{9,8},{10,11... | collective-permute-start | bytes 3145736 | tf_op jit(solution)/shard_map/ppermute | solution.py:45
  57.9 30.9 %collective-permute-start.3 = (bf16[8,64,1024]{2,1,0:T(8,128)(2,1)}, bf16[8,64,1024]{2,1,0:T(8,128)(2,1)}, u32[]{:S(2)}, u32[]{:S(2)}) collective-permute-start(bf16[8,64,1024]{2,1,0:T(8,128)(2,1)} %broadcast_select_fusion), channel_id=1, source_target_pairs={{0,1},{1,0},{2,3},{3,2},{4,5},{5,4},{6,7},{7,6},{8,9},{9,8},{10,11... | collective-permute-start | bytes 3145736 | tf_op jit(solution)/shard_map/ppermute | solution.py:45
  69.9 13.1 %all-to-all-start.1 = ((bf16[4,640,128]{2,1,0:T(8,128)(2,1)}), bf16[4,640,128]{2,1,0:T(8,128)(2,1)S(1)}, u32[]{:S(2)}, u32[]{:S(2)}) async-start(bf16[4,640,128]{2,1,0:T(8,128)(2,1)} %shard_map.145), calls=%async_computation.1 | async-start | bytes 1310720 | tf_op jit(solution)/shard_map/all_to_all | solution.py:380
  82.2 23.6 %collective-permute-start.16 = (bf16[8,256,256]{2,1,0:T(8,128)(2,1)S(1)}, bf16[8,256,256]{2,1,0:T(8,128)(2,1)}, u32[]{:S(2)}, u32[]{:S(2)}) collective-permute-start(bf16[8,256,256]{2,1,0:T(8,128)(2,1)S(1)} %all-to-all-done.14.same_ref), channel_id=1, source_target_pairs={{0,1},{1,0},{2,3},{3,2},{4,5},{5,4},{6,7},{7,6},{8,9},{9,8},{10,11... | collective-permute-start | bytes 3145736 | tf_op jit(solution)/shard_map/ppermute | solution.py:45
  84.8 10.0 %all-to-all-start.2 = ((bf16[4,128,128]{2,1,0:T(8,128)(2,1)}), bf16[4,128,128]{2,1,0:T(8,128)(2,1)S(1)}, u32[]{:S(2)}, u32[]{:S(2)}) async-start(bf16[4,128,128]{2,1,0:T(8,128)(2,1)} %shard_map.146), calls=%async_computation.2 | async-start | bytes 262144 | tf_op jit(solution)/shard_map/all_to_all | solution.py:381
  94.8 24.3 %all-to-all-start.5 = ((bf16[8,64,1024]{2,1,0:T(8,128)(2,1)}), bf16[8,64,1024]{2,1,0:T(8,128)(2,1)}, u32[]{:S(2)}, u32[]{:S(2)}) async-start(bf16[8,64,1024]{2,1,0:T(8,128)(2,1)} %select_add_fusion), calls=%async_computation.5 | async-start | bytes 2097152 | tf_op jit(solution)/shard_map/all_to_all | solution.py:53
  105.6 41.0 %collective-permute-start.1 = (bf16[8,256,256]{2,1,0:T(8,128)(2,1)}, bf16[8,256,256]{2,1,0:T(8,128)(2,1)}, u32[]{:S(2)}, u32[]{:S(2)}) collective-permute-start(bf16[8,256,256]{2,1,0:T(8,128)(2,1)} %get-tuple-element.22), channel_id=1, source_target_pairs={{0,1},{1,0},{2,3},{3,2},{4,5},{5,4},{6,7},{7,6},{8,9},{9,8},{10,11... | collective-permute-start | bytes 3145736 | tf_op jit(solution)/shard_map/ppermute | solution.py:45
  119.1 13.7 %all-to-all-start.15 = ((bf16[4,640,128]{2,1,0:T(8,128)(2,1)}), bf16[4,640,128]{2,1,0:T(8,128)(2,1)S(1)}, u32[]{:S(2)}, u32[]{:S(2)}) async-start(bf16[4,640,128]{2,1,0:T(8,128)(2,1)} %copy-done.15), calls=%async_computation.15 | async-start | bytes 1310720 | tf_op jit(solution)/shard_map/all_to_all | solution.py:380
  124.0 7.1 %collective-permute-start.4 = (bf16[64,1024]{1,0:T(8,128)(2,1)S(1)}, bf16[64,1024]{1,0:T(8,128)(2,1)S(1)}, u32[]{:S(2)}, u32[]{:S(2)}) collective-permute-start(bf16[64,1024]{1,0:T(8,128)(2,1)S(1)} %reduce_sum.90), channel_id=1, source_target_pairs={{0,64},{64,0},{1,65},{65,1},{2,66},{66,2},{3,67},{67,3},{4,68},{68... | collective-permute-start | bytes 393224 | tf_op jit(solution)/shard_map/ppermute | solution.py:49
  134.6 14.5 %all-to-all-start.16 = ((bf16[4,128,128]{2,1,0:T(8,128)(2,1)}), bf16[4,128,128]{2,1,0:T(8,128)(2,1)S(1)}, u32[]{:S(2)}, u32[]{:S(2)}) async-start(bf16[4,128,128]{2,1,0:T(8,128)(2,1)} %shard_map.161), calls=%async_computation.16 | async-start | bytes 262144 | tf_op jit(solution)/shard_map/all_to_all | solution.py:381
  142.7 12.4 %collective-permute-start.5 = (bf16[128,1024]{1,0:T(8,128)(2,1)S(1)}, bf16[128,1024]{1,0:T(8,128)(2,1)S(1)}, u32[]{:S(2)}, u32[]{:S(2)}) collective-permute-start(bf16[128,1024]{1,0:T(8,128)(2,1)S(1)} %shard_map.149), channel_id=1, source_target_pairs={{0,64},{64,0},{1,65},{65,1},{2,66},{66,2},{3,67},{67,3},{4,68},{68... | collective-permute-start | bytes 786440 | tf_op jit(solution)/shard_map/ppermute | solution.py:49
  149.1 24.4 %all-to-all-start.3 = ((bf16[8,256,256]{2,1,0:T(8,128)(2,1)}), bf16[8,256,256]{2,1,0:T(8,128)(2,1)}, u32[]{:S(2)}, u32[]{:S(2)}) async-start(bf16[8,256,256]{2,1,0:T(8,128)(2,1)} %add_convert_fusion.7), calls=%async_computation.3 | async-start | bytes 2097152 | tf_op jit(solution)/shard_map/all_to_all | solution.py:53
  160.0 13.5 %collective-permute-start.6 = (bf16[128,1024]{1,0:T(8,128)(2,1)S(1)}, bf16[128,1024]{1,0:T(8,128)(2,1)S(1)}, u32[]{:S(2)}, u32[]{:S(2)}) collective-permute-start(bf16[128,1024]{1,0:T(8,128)(2,1)S(1)} %shard_map.150), channel_id=1, source_target_pairs={{0,64},{64,0},{1,65},{65,1},{2,66},{66,2},{3,67},{67,3},{4,68},{68... | collective-permute-start | bytes 786440 | tf_op jit(solution)/shard_map/ppermute | solution.py:49
  175.2 31.0 %all-to-all-start.6 = ((bf16[8,128,1024]{2,1,0:T(8,128)(2,1)}), bf16[8,128,1024]{2,1,0:T(8,128)(2,1)}, u32[]{:S(2)}, u32[]{:S(2)}) async-start(bf16[8,128,1024]{2,1,0:T(8,128)(2,1)} %broadcast_in_dim.88), calls=%async_computation.6 | async-start | bytes 4194304 | tf_op jit(solution)/shard_map/all_to_all | solution.py:53
  181.2 2.7 collective-permute-start.17
  206.2 20.8 %all-to-all-start.17 = ((bf16[8,256,256]{2,1,0:T(8,128)(2,1)}), bf16[8,256,256]{2,1,0:T(8,128)(2,1)S(1)}, u32[]{:S(2)}, u32[]{:S(2)}) async-start(bf16[8,256,256]{2,1,0:T(8,128)(2,1)} %add_convert_fusion.3), calls=%async_computation.17 | async-start | bytes 2097152 | tf_op jit(solution)/shard_map/all_to_all | solution.py:53
  212.3 41.2 %collective-permute-start.7 = (bf16[8,128,1024]{2,1,0:T(8,128)(2,1)}, bf16[8,128,1024]{2,1,0:T(8,128)(2,1)}, u32[]{:S(2)}, u32[]{:S(2)}) collective-permute-start(bf16[8,128,1024]{2,1,0:T(8,128)(2,1)} %all-to-all-done.6.same_ref), channel_id=1, source_target_pairs={{0,1},{1,0},{2,3},{3,2},{4,5},{5,4},{6,7},{7,6},{8,9},{9,8},{10,11... | collective-permute-start | bytes 6291464 | tf_op jit(solution)/shard_map/ppermute | solution.py:45
  246.7 22.1 %collective-permute-start.2 = (bf16[8,256,256]{2,1,0:T(8,128)(2,1)S(1)}, bf16[8,256,256]{2,1,0:T(8,128)(2,1)}, u32[]{:S(2)}, u32[]{:S(2)}) collective-permute-start(bf16[8,256,256]{2,1,0:T(8,128)(2,1)S(1)} %all_to_all.130.same_ref), channel_id=1, source_target_pairs={{0,1},{1,0},{2,3},{3,2},{4,5},{5,4},{6,7},{7,6},{8,9},{9,8},{10,11... | collective-permute-start | bytes 3145736 | tf_op jit(solution)/shard_map/ppermute | solution.py:45
  247.8 20.9 %all-to-all-start.18 = ((bf16[8,256,256]{2,1,0:T(8,128)(2,1)}), bf16[8,256,256]{2,1,0:T(8,128)(2,1)}, u32[]{:S(2)}, u32[]{:S(2)}) async-start(bf16[8,256,256]{2,1,0:T(8,128)(2,1)} %broadcast_in_dim.93), calls=%async_computation.18 | async-start | bytes 2097152 | tf_op jit(solution)/shard_map/all_to_all | solution.py:53
  262.4 15.5 %collective-permute-start.8 = (bf16[2,256,512]{2,1,0:T(8,128)(2,1)}, bf16[2,256,512]{2,1,0:T(8,128)(2,1)}, u32[]{:S(2)}, u32[]{:S(2)}) collective-permute-start(bf16[2,256,512]{2,1,0:T(8,128)(2,1)} %slice_bitcast_fusion), channel_id=1, source_target_pairs={{0,16},{16,32},{32,48},{1,17},{17,33},{33,49},{2,18},{18,34},{34,5... | collective-permute-start | bytes 1572872 | tf_op jit(solution)/shard_map/ppermute | solution.py:422
  268.7 13.6 %collective-permute-start.18 = (bf16[8,256,256]{2,1,0:T(8,128)(2,1)}, bf16[8,256,256]{2,1,0:T(8,128)(2,1)S(1)}, u32[]{:S(2)}, u32[]{:S(2)}) collective-permute-start(bf16[8,256,256]{2,1,0:T(8,128)(2,1)} %all-to-all-done.18.same_ref), channel_id=1, source_target_pairs={{0,1},{1,0},{2,3},{3,2},{4,5},{5,4},{6,7},{7,6},{8,9},{9,8},{10,11... | collective-permute-start | bytes 3145736 | tf_op jit(solution)/shard_map/ppermute | solution.py:45
  282.1 11.0 %collective-permute-start.9 = (bf16[8,256,256]{2,1,0:T(8,128)(2,1)S(1)}, bf16[8,256,256]{2,1,0:T(8,128)(2,1)S(1)}, u32[]{:S(2)}, u32[]{:S(2)}) collective-permute-start(bf16[8,256,256]{2,1,0:T(8,128)(2,1)S(1)} %get-tuple-element.24), channel_id=1, source_target_pairs={{0,1},{1,0},{2,3},{3,2},{4,5},{5,4},{6,7},{7,6},{8,9},{9,8},{10,11... | collective-permute-start | bytes 3145736 | tf_op jit(solution)/shard_map/ppermute | solution.py:45
  292.6 7.0 %collective-permute-start.19 = (bf16[8,256,256]{2,1,0:T(8,128)(2,1)}, bf16[8,256,256]{2,1,0:T(8,128)(2,1)}, u32[]{:S(2)}, u32[]{:S(2)}) collective-permute-start(bf16[8,256,256]{2,1,0:T(8,128)(2,1)} %get-tuple-element.32), channel_id=1, source_target_pairs={{0,1},{1,0},{2,3},{3,2},{4,5},{5,4},{6,7},{7,6},{8,9},{9,8},{10,11... | collective-permute-start | bytes 3145736 | tf_op jit(solution)/shard_map/ppermute | solution.py:45
  294.3 21.3 %all-to-all-start.7 = ((bf16[8,256,256]{2,1,0:T(8,128)(2,1)}), bf16[8,256,256]{2,1,0:T(8,128)(2,1)}, u32[]{:S(2)}, u32[]{:S(2)}) async-start(bf16[8,256,256]{2,1,0:T(8,128)(2,1)} %add_convert_fusion.6), calls=%async_computation.7 | async-start | bytes 2097152 | tf_op jit(solution)/shard_map/all_to_all | solution.py:53
  315.6 20.1 %all-to-all-start.19 = ((bf16[8,256,256]{2,1,0:T(8,128)(2,1)}), bf16[8,256,256]{2,1,0:T(8,128)(2,1)}, u32[]{:S(2)}, u32[]{:S(2)}) async-start(bf16[8,256,256]{2,1,0:T(8,128)(2,1)} %add_convert_fusion.2), calls=%async_computation.19 | async-start | bytes 2097152 | tf_op jit(solution)/shard_map/all_to_all | solution.py:53
  339.1 6.6 %collective-permute-start.10 = (bf16[256,256]{1,0:T(8,128)(2,1)S(1)}, bf16[256,256]{1,0:T(8,128)(2,1)S(1)}, u32[]{:S(2)}, u32[]{:S(2)}) collective-permute-start(bf16[256,256]{1,0:T(8,128)(2,1)S(1)} %get-tuple-element.44), channel_id=1, source_target_pairs={{0,64},{64,0},{1,65},{65,1},{2,66},{66,2},{3,67},{67,3},{4,68},{68... | collective-permute-start | bytes 393224 | tf_op jit(solution)/shard_map/ppermute | solution.py:49
  347.4 20.2 %all-to-all-start.8 = ((bf16[8,256,256]{2,1,0:T(8,128)(2,1)}), bf16[8,256,256]{2,1,0:T(8,128)(2,1)}, u32[]{:S(2)}, u32[]{:S(2)}) async-start(bf16[8,256,256]{2,1,0:T(8,128)(2,1)} %broadcast_in_dim.89), calls=%async_computation.8 | async-start | bytes 2097152 | tf_op jit(solution)/shard_map/all_to_all | solution.py:53
  351.6 15.9 %collective-permute-start.20 = (bf16[256,256]{1,0:T(8,128)(2,1)}, bf16[256,256]{1,0:T(8,128)(2,1)}, u32[]{:S(2)}, u32[]{:S(2)}) collective-permute-start(bf16[256,256]{1,0:T(8,128)(2,1)} %get-tuple-element.43), channel_id=1, source_target_pairs={{0,64},{64,0},{1,65},{65,1},{2,66},{66,2},{3,67},{67,3},{4,68},{68... | collective-permute-start | bytes 393224 | tf_op jit(solution)/shard_map/ppermute | solution.py:49
  369.5 19.8 %all-to-all-start.20 = ((bf16[8,256,256]{2,1,0:T(8,128)(2,1)}), bf16[8,256,256]{2,1,0:T(8,128)(2,1)}, u32[]{:S(2)}, u32[]{:S(2)}) async-start(bf16[8,256,256]{2,1,0:T(8,128)(2,1)} %broadcast_in_dim.94), calls=%async_computation.20 | async-start | bytes 2097152 | tf_op jit(solution)/shard_map/all_to_all | solution.py:53
  373.8 15.5 %collective-permute-start.11 = (bf16[8,256,256]{2,1,0:T(8,128)(2,1)}, bf16[8,256,256]{2,1,0:T(8,128)(2,1)}, u32[]{:S(2)}, u32[]{:S(2)}) collective-permute-start(bf16[8,256,256]{2,1,0:T(8,128)(2,1)} %all-to-all-done.8.same_ref), channel_id=1, source_target_pairs={{0,1},{1,0},{2,3},{3,2},{4,5},{5,4},{6,7},{7,6},{8,9},{9,8},{10,11... | collective-permute-start | bytes 3145736 | tf_op jit(solution)/shard_map/ppermute | solution.py:45
  389.3 35.3 %collective-permute-start.21 = (bf16[8,256,256]{2,1,0:T(8,128)(2,1)}, bf16[8,256,256]{2,1,0:T(8,128)(2,1)S(1)}, u32[]{:S(2)}, u32[]{:S(2)}) collective-permute-start(bf16[8,256,256]{2,1,0:T(8,128)(2,1)} %all-to-all-done.20.same_ref), channel_id=1, source_target_pairs={{0,1},{1,0},{2,3},{3,2},{4,5},{5,4},{6,7},{7,6},{8,9},{9,8},{10,11... | collective-permute-start | bytes 3145736 | tf_op jit(solution)/shard_map/ppermute | solution.py:45
  424.5 34.7 %collective-permute-start.12 = (bf16[8,256,256]{2,1,0:T(8,128)(2,1)S(1)}, bf16[8,256,256]{2,1,0:T(8,128)(2,1)S(1)}, u32[]{:S(2)}, u32[]{:S(2)}) collective-permute-start(bf16[8,256,256]{2,1,0:T(8,128)(2,1)S(1)} %get-tuple-element.26), channel_id=1, source_target_pairs={{0,1},{1,0},{2,3},{3,2},{4,5},{5,4},{6,7},{7,6},{8,9},{9,8},{10,11... | collective-permute-start | bytes 3145736 | tf_op jit(solution)/shard_map/ppermute | solution.py:45
  459.1 4.8 collective-permute-start.22
  460.4 20.2 %all-to-all-start.11 = ((bf16[8,256,256]{2,1,0:T(8,128)(2,1)}), bf16[8,256,256]{2,1,0:T(8,128)(2,1)S(1)}, u32[]{:S(2)}, u32[]{:S(2)}) async-start(bf16[8,256,256]{2,1,0:T(8,128)(2,1)} %add_convert_fusion.5), calls=%async_computation.11 | async-start | bytes 2097152 | tf_op jit(solution)/shard_map/all_to_all | solution.py:53
  480.5 19.4 %all-to-all-start.23 = ((bf16[8,256,256]{2,1,0:T(8,128)(2,1)}), bf16[8,256,256]{2,1,0:T(8,128)(2,1)S(1)}, u32[]{:S(2)}, u32[]{:S(2)}) async-start(bf16[8,256,256]{2,1,0:T(8,128)(2,1)} %add_convert_fusion.1), calls=%async_computation.23 | async-start | bytes 2097152 | tf_op jit(solution)/shard_map/all_to_all | solution.py:53
  501.3 19.4 %all-to-all-start.12 = ((bf16[8,256,256]{2,1,0:T(8,128)(2,1)}), bf16[8,256,256]{2,1,0:T(8,128)(2,1)S(1)}, u32[]{:S(2)}, u32[]{:S(2)}) async-start(bf16[8,256,256]{2,1,0:T(8,128)(2,1)} %broadcast_in_dim.90), calls=%async_computation.12 | async-start | bytes 2097152 | tf_op jit(solution)/shard_map/all_to_all | solution.py:53
  521.9 20.1 %all-to-all-start.24 = ((bf16[8,256,256]{2,1,0:T(8,128)(2,1)}), bf16[8,256,256]{2,1,0:T(8,128)(2,1)}, u32[]{:S(2)}, u32[]{:S(2)}) async-start(bf16[8,256,256]{2,1,0:T(8,128)(2,1)} %broadcast_in_dim.95), calls=%async_computation.24 | async-start | bytes 2097152 | tf_op jit(solution)/shard_map/all_to_all | solution.py:53
  526.2 16.1 %collective-permute-start.13 = (bf16[8,256,256]{2,1,0:T(8,128)(2,1)}, bf16[8,256,256]{2,1,0:T(8,128)(2,1)}, u32[]{:S(2)}, u32[]{:S(2)}) collective-permute-start(bf16[8,256,256]{2,1,0:T(8,128)(2,1)} %copy-done.13), channel_id=1, source_target_pairs={{0,1},{1,0},{2,3},{3,2},{4,5},{5,4},{6,7},{7,6},{8,9},{9,8},{10,11... | collective-permute-start | bytes 3145736 | tf_op jit(solution)/shard_map/ppermute | solution.py:45
  542.0 12.0 %collective-permute-start.23 = (bf16[8,256,256]{2,1,0:T(8,128)(2,1)}, bf16[8,256,256]{2,1,0:T(8,128)(2,1)S(1)}, u32[]{:S(2)}, u32[]{:S(2)}) collective-permute-start(bf16[8,256,256]{2,1,0:T(8,128)(2,1)} %all-to-all-done.24.same_ref), channel_id=1, source_target_pairs={{0,1},{1,0},{2,3},{3,2},{4,5},{5,4},{6,7},{7,6},{8,9},{9,8},{10,11... | collective-permute-start | bytes 3145736 | tf_op jit(solution)/shard_map/ppermute | solution.py:45
  553.5 9.8 %collective-permute-start.14 = (bf16[8,256,256]{2,1,0:T(8,128)(2,1)S(1)}, bf16[8,256,256]{2,1,0:T(8,128)(2,1)S(1)}, u32[]{:S(2)}, u32[]{:S(2)}) collective-permute-start(bf16[8,256,256]{2,1,0:T(8,128)(2,1)S(1)} %get-tuple-element.28), channel_id=1, source_target_pairs={{0,1},{1,0},{2,3},{3,2},{4,5},{5,4},{6,7},{7,6},{8,9},{9,8},{10,11... | collective-permute-start | bytes 3145736 | tf_op jit(solution)/shard_map/ppermute | solution.py:45
  563.3 4.8 collective-permute-start.24
  564.5 20.1 %all-to-all-start.13 = ((bf16[8,256,256]{2,1,0:T(8,128)(2,1)}), bf16[8,256,256]{2,1,0:T(8,128)(2,1)S(1)}, u32[]{:S(2)}, u32[]{:S(2)}) async-start(bf16[8,256,256]{2,1,0:T(8,128)(2,1)} %add_convert_fusion.4), calls=%async_computation.13 | async-start | bytes 2097152 | tf_op jit(solution)/shard_map/all_to_all | solution.py:53
  570.6 35.8 %copy-start.28 = (bf16[256,256]{1,0:T(8,128)(2,1)S(1)}, bf16[256,256]{1,0:T(8,128)(2,1)}, u32[]{:S(2)}) copy-start(bf16[256,256]{1,0:T(8,128)(2,1)} %copy-done.27) | copy-start | bytes 393220
  584.7 19.5 %all-to-all-start.25 = ((bf16[8,256,256]{2,1,0:T(8,128)(2,1)}), bf16[8,256,256]{2,1,0:T(8,128)(2,1)S(1)}, u32[]{:S(2)}, u32[]{:S(2)}) async-start(bf16[8,256,256]{2,1,0:T(8,128)(2,1)} %add_convert_fusion), calls=%async_computation.25 | async-start | bytes 2097152 | tf_op jit(solution)/shard_map/all_to_all | solution.py:53
  588.4 17.9 %collective-permute-start.15 = (bf16[256,256]{1,0:T(8,128)(2,1)S(1)}, bf16[256,256]{1,0:T(8,128)(2,1)S(1)}, u32[]{:S(2)}, u32[]{:S(2)}) collective-permute-start(bf16[256,256]{1,0:T(8,128)(2,1)S(1)} %add_convert_fusion.14), channel_id=1, source_target_pairs={{0,64},{64,0},{1,65},{65,1},{2,66},{66,2},{3,67},{67,3},{4,68},{68... | collective-permute-start | bytes 393224 | tf_op jit(solution)/shard_map/ppermute | solution.py:49
  (37 other events, 243.0 us)
Sparse Core Ops, SparseCore 0:
  12.9 108.9 all-gather.1

commit v2 on v1

v2 whole, which is shorter than its diff:
```python
import functools

import jax
import jax.numpy as jnp
from jax import lax
from jax.experimental import pallas as pl
from jax.experimental.pallas import tpu as pltpu
from jax.sharding import Mesh, PartitionSpec as P

D = 4096
HEAD = 128
ENC_D = 1024
ENC_HEADS = 16
ENC_HEAD = 64
BLOCK = 64
NB_LEN = 128
NEIGH = 2
BATCH = 2
CHIPS = 8
ROWS = 256
WIDTH = 256
UNITS = 4
GROUP = 4
MP = ("z", "y", "core")
KEYS = NEIGH * NB_LEN
VMEM_LIMIT = 48 * 1024 * 1024

epsilon = 1e-05
f32 = jnp.float32
bf16 = jnp.bfloat16


def params():
    return pltpu.CompilerParams(vmem_limit_bytes=VMEM_LIMIT)


def whole(shape):
    return pl.BlockSpec(shape, lambda *_: (0,) * len(shape))


SCALAR = pl.BlockSpec(memory_space=pltpu.SMEM)


def core_swap(value):
    return lax.ppermute(value, "core", [(0, 1), (1, 0)])


def section_swap(value):
    return lax.ppermute(value, "section", [(0, 1), (1, 0)])


def chips_to_chips(value):
    return lax.all_to_all(value, ("z", "y"), 0, 0, tiled=True)


def gather_chips(local):
    return chips_to_chips(jnp.broadcast_to(local[None], (CHIPS,) + local.shape))


def project_kernel(last, units, pick_ref, x_ref, gain_ref, w_ref, *refs):
    if last:
        acc_in, sq_in, out_ref, acc_ref, sq_ref, left_ref = refs
    else:
        acc_ref, sq_ref, left_ref = refs
    step = pl.program_id(0)
    parts = w_ref.shape[0]

    @pl.when(step == 0)
    def _():
        if last:
            acc_ref[...] = acc_in[...]
            sq_ref[...] = sq_in[...]
        else:
            acc_ref[...] = jnp.zeros_like(acc_ref)
            sq_ref[...] = jnp.zeros_like(sq_ref)

    for at in range(GROUP):
        wide = x_ref[at].astype(f32)
        squares = wide * wide
        sq_ref[...] += squares[:, :128] + squares[:, 128:]
        left_ref[:, at * WIDTH : (at + 1) * WIDTH] = (wide * gain_ref[at, 0]).astype(bf16)
    for part in range(parts):
        right = w_ref[part].reshape(GROUP * WIDTH, WIDTH)
        acc_ref[part] += jnp.dot(left_ref[...], right, preferred_element_type=f32)

    if last:

        @pl.when(step == CHIPS // GROUP - 1)
        def _():
            mean = jnp.sum(sq_ref[...], axis=1, keepdims=True) / D
            root = jnp.sqrt(mean + epsilon)
            for part in range(parts):
                done = (acc_ref[part] / root).astype(bf16)
                if units:
                    for unit in range(UNITS):
                        b, h = divmod(unit, 2)
                        out_ref[unit, part] = done[
                            b * ROWS : (b + 1) * ROWS, h * HEAD : (h + 1) * HEAD
                        ]
                else:
                    out_ref[...] = done


def project_half(pick, rows, gains, weight, before, units):
    parts = weight.shape[0]
    count = BATCH * ROWS
    acc = (parts, count, WIDTH)
    sq = (count, 128)
    last = before is not None
    in_specs = [
        pl.BlockSpec((GROUP, count, WIDTH), lambda s, pick: (s, 0, 0)),
        pl.BlockSpec((GROUP, 1, 1, WIDTH), lambda s, pick: (s, pick[0], 0, 0)),
        pl.BlockSpec((parts, GROUP, 1, WIDTH, WIDTH), lambda s, pick: (0, s, pick[0], 0, 0)),
    ]
    scratch = [pltpu.VMEM((count, GROUP * WIDTH), bf16)]
    if last:
        out = (UNITS, parts, ROWS, HEAD) if units else (count, WIDTH)
        in_specs += [whole(acc), whole(sq)]
        out_specs = whole(out)
        out_shape = jax.ShapeDtypeStruct(out, bf16)
        scratch = [pltpu.VMEM(acc, f32), pltpu.VMEM(sq, f32)] + scratch
    else:
        out_specs = [whole(acc), whole(sq)]
        out_shape = [jax.ShapeDtypeStruct(acc, f32), jax.ShapeDtypeStruct(sq, f32)]
    return pl.pallas_call(
        functools.partial(project_kernel, last, units),
        grid_spec=pltpu.PrefetchScalarGridSpec(
            num_scalar_prefetch=1,
            grid=(CHIPS // GROUP,),
            in_specs=in_specs,
            out_specs=out_specs,
            scratch_shapes=scratch,
        ),
        out_shape=out_shape,
        compiler_params=params(),
        cost_estimate=pl.CostEstimate(
            flops=2 * count * (D // 2) * WIDTH * parts,
            bytes_accessed=D * WIDTH * parts + D * count + 4 * count * WIDTH * parts,
            transcendentals=0,
        ),
    )(
        pick,
        rows,
        gains.reshape(CHIPS, 2, 1, WIDTH),
        weight.reshape(parts, CHIPS, 2, WIDTH, WIDTH),
        *(before or ()),
    )


def project(core, local, gains, weight, units):
    same = gather_chips(local)
    swap = core_swap(same)
    before = project_half(core, same, gains, weight, None, units)
    return project_half(1 - core, swap, gains, weight, before, units)


def causal_kernel(triple_ref, out_ref):
    scaling = HEAD ** (-0.5)
    row = lax.broadcasted_iota(jnp.int32, (ROWS, ROWS), 0)
    col = lax.broadcasted_iota(jnp.int32, (ROWS, ROWS), 1)
    for i in range(UNITS):
        queries = triple_ref[i, 0]
        numer = jnp.zeros((ROWS, HEAD), f32)
        denom = jnp.zeros((ROWS, 1), f32)
        for j in range(i + 1):
            scores = lax.dot_general(
                queries, triple_ref[j, 1], (((1,), (1,)), ((), ())), preferred_element_type=f32
            )
            weights = jnp.exp(scores * scaling)
            if i == j:
                weights = jnp.where(col <= row, weights, 0.0)
            denom += jnp.sum(weights, axis=1, keepdims=True)
            numer += jnp.dot(weights.astype(bf16), triple_ref[j, 2], preferred_element_type=f32)
        out_ref[i] = (numer / denom).astype(bf16)


def causal(triple):
    out = (UNITS, ROWS, HEAD)
    return pl.pallas_call(
        causal_kernel,
        out_shape=jax.ShapeDtypeStruct(out, bf16),
        compiler_params=params(),
    )(triple)


def crossed_kernel(asked_ref, prev_ref, pairs_ref, out_ref):
    scaling = HEAD ** (-0.5)
    row = lax.broadcasted_iota(jnp.int32, (BLOCK, 2 * KEYS), 0)
    col = lax.broadcasted_iota(jnp.int32, (BLOCK, 2 * KEYS), 1)
    allowed = (row < BLOCK - 1) == (col < KEYS)
    for unit in range(UNITS):
        b, h = divmod(unit, 2)
        kcols = slice(h * HEAD, (h + 1) * HEAD)
        vcols = slice((2 + h) * HEAD, (3 + h) * HEAD)
        for i in range(ROWS // BLOCK):
            queries = asked_ref[b * ROWS + i * BLOCK : b * ROWS + (i + 1) * BLOCK, kcols]
            if i == 0:
                keys = jnp.concatenate([prev_ref[b, :, kcols], pairs_ref[b, 0, :, kcols]], axis=0)
                values = jnp.concatenate([prev_ref[b, :, vcols], pairs_ref[b, 0, :, vcols]], axis=0)
            else:
                keys = pairs_ref[b, i - 1 : i + 1, :, kcols].reshape(2 * KEYS, HEAD)
                values = pairs_ref[b, i - 1 : i + 1, :, vcols].reshape(2 * KEYS, HEAD)
            scores = lax.dot_general(
                queries, keys, (((1,), (1,)), ((), ())), preferred_element_type=f32
            )
            weights = jnp.where(allowed, jnp.exp(scores * scaling), 0.0)
            denom = jnp.sum(weights, axis=1, keepdims=True)
            numer = jnp.dot(weights.astype(bf16), values, preferred_element_type=f32)
            out_ref[unit, i * BLOCK : (i + 1) * BLOCK, :] = (numer / denom).astype(bf16)


def cross(asked, prev, pairs):
    out = (UNITS, ROWS, HEAD)
    return pl.pallas_call(
        crossed_kernel,
        out_shape=jax.ShapeDtypeStruct(out, bf16),
        compiler_params=params(),
    )(asked, prev, pairs)


def terms_kernel(pick_ref, mixed_ref, *refs):
    *w_refs, out_ref, left_ref = refs

    @pl.when(pl.program_id(0) == 0)
    def _():
        for unit in range(UNITS):
            b, h = divmod(unit, 2)
            left_ref[b * ROWS : (b + 1) * ROWS, h * HEAD : (h + 1) * HEAD] = mixed_ref[unit]

    for at, w_ref in enumerate(w_refs):
        out_ref[at] = jnp.dot(
            left_ref[...], w_ref[...], preferred_element_type=f32
        ).astype(bf16)


def terms(pick, mixed, weight):
    count = BATCH * ROWS

    def columns(at):
        return pl.BlockSpec((WIDTH, WIDTH), lambda s, pick: (0, 2 * (GROUP * s + at) + pick[0]))

    return pl.pallas_call(
        terms_kernel,
        grid_spec=pltpu.PrefetchScalarGridSpec(
            num_scalar_prefetch=1,
            grid=(CHIPS // GROUP,),
            in_specs=[whole((UNITS, ROWS, HEAD))] + [columns(at) for at in range(GROUP)],
            out_specs=pl.BlockSpec((GROUP, count, WIDTH), lambda s, pick: (s, 0, 0)),
            scratch_shapes=[pltpu.VMEM((count, WIDTH), bf16)],
        ),
        out_shape=jax.ShapeDtypeStruct((CHIPS, count, WIDTH), bf16),
        compiler_params=params(),
        cost_estimate=pl.CostEstimate(
            flops=2 * count * WIDTH * D // 2,
            bytes_accessed=D * WIDTH + D * count,
            transcendentals=0,
        ),
    )(pick, mixed, *([weight] * GROUP))


def product_sum(core, mixed, weight):
    far = core_swap(terms(1 - core, mixed, weight))
    paired = (terms(core, mixed, weight).astype(f32) + far.astype(f32)).astype(bf16)
    return jnp.sum(chips_to_chips(paired).astype(f32), axis=0)


def look_up(ids, enc_embed, core, section):
    vocab_here = enc_embed.shape[0]
    mine = lax.dynamic_slice_in_dim(ids, section * (NB_LEN // 2), NB_LEN // 2, axis=1)
    wanted = mine.reshape(CHIPS, 2, NB_LEN // 2) - lax.axis_index(MP) * vocab_here

    def rows(at):
        picks = lax.dynamic_index_in_dim(wanted, at, 1, keepdims=False).reshape(-1)
        inside = (picks >= 0) & (picks < vocab_here)
        found = enc_embed[jnp.clip(picks, 0, vocab_here - 1)]
        found = jnp.where(inside[:, None], found, jnp.zeros((), bf16))
        return found.reshape(CHIPS, NB_LEN // 2, ENC_D)

    paired = core_swap(rows(1 - core)) + rows(core)
    half = jnp.sum(chips_to_chips(paired).astype(f32), axis=0).astype(bf16)
    far = section_swap(half)
    return jnp.where(
        section == 0, jnp.concatenate([half, far], axis=0), jnp.concatenate([far, half], axis=0)
    )


def weight_pieces(section, enc_qkv, enc_out, enc_up, enc_down):
    width = ENC_D // 2
    triple = lax.dynamic_slice_in_dim(enc_qkv, section * width, width, axis=2)
    up = enc_up.reshape(64, 16, 2, 2, 64)
    up = lax.dynamic_index_in_dim(up, section, 2, keepdims=False)
    up = jnp.transpose(up, (2, 0, 1, 3)).reshape(2, 64, 2, width)
    down = lax.dynamic_slice_in_dim(enc_down, section * 128, 128, axis=0)
    down = down.reshape(2, 64, 2, width)
    local = jnp.concatenate(
        [
            jnp.transpose(up, (0, 2, 1, 3)).reshape(4, 64, width),
            jnp.transpose(down, (0, 2, 1, 3)).reshape(4, 64, width),
            jnp.transpose(triple, (1, 0, 2)),
            jnp.transpose(enc_out.reshape(64, 2, width), (1, 0, 2)),
        ],
        axis=0,
    )
    return lax.all_gather(local, MP, axis=1, tiled=True)


def scaled_rows(values, gain):
    wide = values.astype(f32)
    root = jnp.sqrt(jnp.mean(wide * wide, axis=1, keepdims=True) + epsilon)
    return (wide * gain).astype(bf16), root


def enc_mix_kernel(section_ref, x_ref, gain_ref, q_ref, k_ref, v_ref, o0_ref, o1_ref, out_ref, mix_ref):
    scaled, root = scaled_rows(x_ref[...], gain_ref[...])
    triple = [
        (jnp.dot(scaled, ref[0], preferred_element_type=f32) / root).astype(bf16)
        for ref in (q_ref, k_ref, v_ref)
    ]
    for head in range(ENC_HEADS // 2):
        cols = slice(head * ENC_HEAD, (head + 1) * ENC_HEAD)
        scores = lax.dot_general(
            triple[0][:, cols],
            triple[1][:, cols],
            (((1,), (1,)), ((), ())),
            preferred_element_type=f32,
        )
        weights = jnp.exp(scores * ENC_HEAD ** (-0.5))
        denom = jnp.sum(weights, axis=1, keepdims=True)
        numer = jnp.dot(weights.astype(bf16), triple[2][:, cols], preferred_element_type=f32)
        mix_ref[:, cols] = (numer / denom).astype(bf16)
    mixed = mix_ref[...]
    width = ENC_D // 2
    rows = pl.ds(pl.multiple_of(section_ref[0] * width, width), width)
    for at, ref in enumerate((o0_ref, o1_ref)):
        part = jnp.dot(mixed, ref[0, rows, :], preferred_element_type=f32)
        out_ref[:, at * width : (at + 1) * width] = part.astype(bf16)


def enc_feed_kernel(x_ref, gain_ref, w_ref, out_ref):
    scaled, root = scaled_rows(x_ref[...], gain_ref[...])
    width = ENC_D // 2
    hidden = [
        jax.nn.gelu(
            jnp.dot(scaled, w_ref[piece], preferred_element_type=f32) / root, approximate=True
        ).astype(bf16)
        for piece in range(4)
    ]
    for at in range(2):
        part = jnp.zeros((NB_LEN, width), f32)
        for piece in range(4):
            rows = slice((piece % 2) * width, (piece % 2 + 1) * width)
            down = w_ref[4 + 2 * (piece // 2) + at, rows, :]
            part += jnp.dot(hidden[piece], down, preferred_element_type=f32)
        out_ref[:, at * width : (at + 1) * width] = part.astype(bf16)


def encode(embedded, enc_norms, pieces, section):
    out = jax.ShapeDtypeStruct((NB_LEN, ENC_D), bf16)
    width = ENC_D // 2
    full = whole((NB_LEN, ENC_D))
    gain = whole((1, ENC_D))

    def piece(at):
        return pl.BlockSpec((1, ENC_D, width), lambda s: (at, 0, 0))

    mixed = pl.pallas_call(
        enc_mix_kernel,
        grid=(1,),
        in_specs=[SCALAR, full, gain] + [piece(8 + at) for at in range(5)],
        out_specs=full,
        out_shape=out,
        scratch_shapes=[pltpu.VMEM((NB_LEN, width), bf16)],
        compiler_params=params(),
    )(section, embedded, enc_norms[:1], *([pieces] * 5))
    inner = (embedded.astype(f32) + (mixed.astype(f32) + section_swap(mixed).astype(f32))).astype(
        bf16
    )
    fed = pl.pallas_call(
        enc_feed_kernel,
        grid=(1,),
        in_specs=[full, gain, pl.BlockSpec((8, ENC_D, width), lambda s: (0, 0, 0))],
        out_specs=full,
        out_shape=out,
        compiler_params=params(),
    )(inner, enc_norms[1:], pieces)
    return (inner.astype(f32) + (fed.astype(f32) + section_swap(fed).astype(f32))).astype(bf16)


def decoder_layer(core, states, prev, pairs, weights):
    norms, triple_w, out_w, query_w, back_w = weights
    triple = project(core, states, norms[0], triple_w, True)
    triple = lax.all_to_all(triple, "seq", 0, 0, tiled=True)
    mixed = lax.all_to_all(causal(triple), "seq", 0, 0, tiled=True)
    middle = (states.astype(f32) + product_sum(core, mixed, out_w)).astype(bf16)
    asked = project(core, middle, norms[1], query_w[None], False)
    crossed = cross(asked, prev, pairs)
    return (middle.astype(f32) + product_sum(core, crossed, back_w)).astype(bf16)


def on_device(
    hidden_states,
    neighbour_ids,
    neighbour_table,
    enc_embed,
    enc_norms,
    enc_qkv,
    enc_out,
    enc_up,
    enc_down,
    dec_norms,
    dec_qkv,
    dec_out,
    cross_query,
    cross_pair,
    cross_out,
):
    section = lax.axis_index("section").astype(jnp.int32)
    core_at = lax.axis_index("core").astype(jnp.int32)
    core = jnp.reshape(core_at, (1,))
    blocks_here = neighbour_table.shape[1]
    pieces = weight_pieces(section, enc_qkv, enc_out, enc_up, enc_down)
    slot_ids = neighbour_ids[neighbour_table.reshape(-1)]
    embedded = look_up(slot_ids, enc_embed, core_at, section)
    encoded = encode(embedded, enc_norms, pieces, jnp.reshape(section, (1,)))
    encoded = lax.all_gather(encoded, MP, axis=0, tiled=True)
    pairs = jnp.dot(
        encoded, cross_pair[0].reshape(ENC_D, 2 * WIDTH), preferred_element_type=f32
    ).astype(bf16)
    pairs = pairs.reshape(BATCH, blocks_here, KEYS, 2 * WIDTH)
    count = lax.axis_size("seq")
    prev = lax.ppermute(pairs[:, -1], "seq", [(i, i + 1) for i in range(count - 1)])
    weights = (
        dec_norms[0],
        jnp.transpose(dec_qkv[0], (1, 0, 2)),
        dec_out[0],
        cross_query[0],
        cross_out[0],
    )

    states = hidden_states.reshape(BATCH * ROWS, WIDTH)
    first = decoder_layer(core, states, prev, pairs, weights)
    second = decoder_layer(core, section_swap(first), prev, pairs, weights)
    second = second.reshape(BATCH, ROWS, WIDTH)
    return jnp.where(section == 0, section_swap(second[0]), second[1])[None]


def solution(mesh):
    devices = mesh.devices
    sections, seqs = devices.shape[:2]
    split = Mesh(
        devices.reshape(sections, seqs, 2, 4, 2), ("section", "seq", "z", "y", "core")
    )
    mp = ("z", "y", "core")
    return jax.shard_map(
        on_device,
        mesh=split,
        in_specs=(
            P(None, "seq", mp),
            P(),
            P(None, "seq", None),
            P(mp, None),
            P(),
            P(mp, None, None),
            P(mp, None),
            P(mp, None),
            P(mp, None),
            P("section", None, None),
            P("section", None, None, mp),
            P("section", mp, None),
            P("section", None, mp),
            P("section", None, None, mp),
            P("section", mp, None),
        ),
        out_specs=P("section", "seq", mp),
        check_vma=False,
    )
```

time: 626 us -> 525 us (0.84)
  blocking collectives: 65.7 us -> 247 us
  waiting for transfers between devices: 238 us -> 112 us
  starting transfers between devices: 118 us -> 41.1 us
  Pallas kernels: 95.3 us -> 50.9 us
  other arithmetic: 35.9 us -> 13.8 us
  local copies, waits for them, and re-layouts: 46.4 us -> 32.1 us
    all_to_all x1 -> x7, blocking collectives: 18.2 us -> 210 us  [chips_to_chips(): return lax.all_to_all(value, ('z', 'y'), 0, 0, tiled=True)]
    all_to_all x17 -> x2, waiting for transfers between devices: 191 us -> 39.1 us  [chips_to_chips(): return lax.all_to_all(value, ('z', 'y'), 0, 0, tiled=True)]
    all_to_all x17 -> x2, starting transfers between devices: 81 us -> 16.5 us  [chips_to_chips(): return lax.all_to_all(value, ('z', 'y'), 0, 0, tiled=True)]
    pallas_call x21 -> x18, Pallas kernels: 80.2 us -> 35.4 us  [the longest x8 22.9 us: project_half(): pl.pallas_call(functools.partial(project_kernel, last, units), grid_spec=...]
    all_gather x1, waiting for transfers between devices: 0.02 us -> 21.4 us  [weight_pieces(): return lax.all_gather(local, MP, axis=1, tiled=True)]
    convert_element_type x12 -> x8, other arithmetic: 19.1 us -> 2.27 us  [the longest x4 2.03 us: product_sum(): (terms(core, mixed, weight).astype(f32) + far.astype(f32)).astype(bf16)]
    ppermute x6 -> x5, waiting for transfers between devices: 36.6 us -> 19.8 us  [section_swap(): return lax.ppermute(value, 'section', [(0, 1), (1, 0)])]
    ppermute x18 -> x9, waiting for transfers between devices: 2.69 us -> 14.8 us  [core_swap(): return lax.ppermute(value, 'core', [(0, 1), (1, 0)])]
  transfers between devices with their start and end apart: 47 -> 20, of which waited for: 25 -> 14; matrix products, arithmetic and copies ran while one was open for 9% -> 7% of each run, Pallas kernels for 16% -> 7%
where the time goes in v2:
time: 525 us; the launch traced here: 516 us
  blocking collectives  247 us (47%)
  waiting for transfers between devices  112 us (21%)
  Pallas kernels  50.9 us (10%)
  starting transfers between devices  41.1 us (8%)
  local copies, waits for them, and re-layouts  32.1 us (6%)
  between operations  14.4 us (3%)
  other arithmetic  13.8 us (3%)
    all_to_all x7, blocking collectives, chips_to_chips(): return lax.all_to_all(value, ('z', 'y'), 0, 0, tiled=True)  210 us
    all_to_all x2, waiting for transfers between devices, chips_to_chips(): return lax.all_to_all(value, ('z', 'y'), 0, 0, tiled=True)  39.1 us
    pallas_call x8, Pallas kernels, project_half(): pl.pallas_call(functools.partial(project_kernel, last, units), grid_spec=...  22.9 us
    all_gather x1, waiting for transfers between devices, weight_pieces(): return lax.all_gather(local, MP, axis=1, tiled=True)  21.4 us
    ppermute x5, waiting for transfers between devices, section_swap(): return lax.ppermute(value, 'section', [(0, 1), (1, 0)])  19.8 us
    all_to_all x1, blocking collectives, decoder_layer(): triple = lax.all_to_all(triple, 'seq', 0, 0, tiled=True)  18.3 us
    all_to_all x2, blocking collectives, decoder_layer(): mixed = lax.all_to_all(causal(triple), 'seq', 0, 0, tiled=True)  18.1 us
    all_to_all x2, starting transfers between devices, chips_to_chips(): return lax.all_to_all(value, ('z', 'y'), 0, 0, tiled=True)  16.5 us
  transfers between devices with their start and end apart: 20, of which 14 were waited for; matrix products, arithmetic and copies ran while one was open for 7% of the time, Pallas kernels for 7%

profile of v2, /device:TPU:0, one launch (start us, length us, event | category | flops | bytes accessed | tf_op | source)
XLA Modules:
  0.0 515.5 jit_solution(9976751359442783959)
XLA Ops:
  7.8 2.7 reshape.188
  14.2 6.0 %all-to-all-start = ((bf16[8,512,256]{2,1,0:T(8,128)(2,1)}), bf16[8,512,256]{2,1,0:T(8,128)(2,1)S(1)}, u32[]{:S(2)}, u32[]{:S(2)}) async-start(bf16[8,512,256]{2,1,0:T(8,128)(2,1)} %broadcast_in_dim.28), calls=%async_computation | async-start | bytes 4194304 | tf_op jit(solution)/shard_map/all_to_all | solution.py:53
  21.3 7.9 %gather_fusion.1 = bf16[512,1024]{1,0:T(8,128)(2,1)} fusion(bf16[4000,1024]{1,0:T(8,128)(2,1)} %param.18, s32[1024]{0:T(1024)S(1)} %pad_clamp_fusion.1), kind=kCustom, calls=%fused_computation.1 | custom fusion | bytes 2099200 | tf_op jit(solution)/shard_map/gather | solution.py:275
  29.2 2.3 broadcast_select_fusion
  31.5 8.0 %gather_fusion.2 = bf16[512,1024]{1,0:T(8,128)(2,1)} fusion(bf16[4000,1024]{1,0:T(8,128)(2,1)} %param.18, s32[1024]{0:T(1024)S(1)} %pad_clamp_fusion), kind=kCustom, calls=%fused_computation.2 | custom fusion | bytes 2099200 | tf_op jit(solution)/shard_map/gather | solution.py:275
  39.6 2.7 select_add_fusion
  42.3 17.1 %all-to-all-done.x_ref = bf16[8,512,256]{2,1,0:T(8,128)(2,1)S(1)} async-done(((bf16[8,512,256]{2,1,0:T(8,128)(2,1)}), bf16[8,512,256]{2,1,0:T(8,128)(2,1)S(1)}, u32[]{:S(2)}, u32[]{:S(2)}) %all-to-all-start) | async-done | bytes 2097184 | tf_op jit(solution)/shard_map/all_to_all | solution.py:53
  59.3 10.5 %all-to-all-start.5 = ((bf16[8,64,1024]{2,1,0:T(8,128)(2,1)}), bf16[8,64,1024]{2,1,0:T(8,128)(2,1)}, u32[]{:S(2)}, u32[]{:S(2)}) async-start(bf16[8,64,1024]{2,1,0:T(8,128)(2,1)} %select_add_fusion), calls=%async_computation.5 | async-start | bytes 2097152 | tf_op jit(solution)/shard_map/all_to_all | solution.py:53
  69.8 22.1 %all-to-all-done.5 = bf16[8,64,1024]{2,1,0:T(8,128)(2,1)} async-done(((bf16[8,64,1024]{2,1,0:T(8,128)(2,1)}), bf16[8,64,1024]{2,1,0:T(8,128)(2,1)}, u32[]{:S(2)}, u32[]{:S(2)}) %all-to-all-start.5) | async-done | bytes 1048608 | tf_op jit(solution)/shard_map/all_to_all | solution.py:53
  93.3 4.4 collective-permute-start.4
  97.7 5.7 %collective-permute-done.4 = bf16[64,1024]{1,0:T(8,128)(2,1)S(1)} collective-permute-done((bf16[64,1024]{1,0:T(8,128)(2,1)S(1)}, bf16[64,1024]{1,0:T(8,128)(2,1)S(1)}, u32[]{:S(2)}, u32[]{:S(2)}) %collective-permute-start.4) | collective-permute-done | bytes 131104 | tf_op jit(solution)/shard_map/ppermute | solution.py:49
  103.5 21.4 %all-gather.3.cloned.1.call-done.q_ref.k_ref.v_ref.o0_ref.o1_ref.w_ref = bf16[13,1024,512]{2,1,0:T(8,128)(2,1)} async-done(((bf16[13,64,512]{2,1,0:T(8,128)(2,1)}), bf16[13,1024,512]{2,1,0:T(8,128)(2,1)}) %all-gather.3.cloned.1.call-update) | async-done | bytes 13631504 | tf_op jit(solution)/shard_map/all_gather | solution.py:304
  124.8 4.6 shard_map.152
  129.5 3.8 collective-permute-start.5
  133.3 3.6 shard_map.145
  137.0 3.0 collective-permute-done.5
  140.2 5.5 %shard_map.153 = bf16[128,1024]{1,0:T(8,128)(2,1)} custom-call(bf16[128,1024]{1,0:T(8,128)(2,1)S(1)} %add_convert_fusion.8.x_ref, f32[1,1024]{1,0:T(1,128)S(1)} %get-tuple-element.23.gain_ref, bf16[13,1024,512]{2,1,0:T(8,128)(2,1)} %all-gather.3.cloned.1.call-done.q_ref.k_ref.v_ref.o0_ref.o1_ref.w_ref), custom_call_target="tpu_custom_call" | custom-call | tf_op jit(solution)/shard_map/pallas_call | solution.py:378
  145.6 3.2 collective-permute-start.6
  148.9 4.2 shard_map.146
  154.0 4.4 all-to-all-start.1
  160.3 9.7 %all-to-all-done.1.triple_ref = bf16[4,3,256,128]{3,2,1,0:T(8,128)(2,1)S(1)} async-done(((bf16[4,3,256,128]{3,2,1,0:T(8,128)(2,1)}), bf16[4,3,256,128]{3,2,1,0:T(8,128)(2,1)S(1)}, u32[]{:S(2)}, u32[]{:S(2)}) %all-to-all-start.1) | async-done | bytes 786464 | tf_op jit(solution)/shard_map/all_to_all | solution.py:392
  171.4 9.1 %all_to_all.65.mixed_ref = bf16[4,256,128]{2,1,0:T(8,128)(2,1)S(1)} all-to-all(bf16[4,256,128]{2,1,0:T(8,128)(2,1)S(1)} %shard_map.147), channel_id=1, replica_groups=mesh['section'=2,'seq'=4,'z'=2,'y'=4,'core'=2] {'seq'}, dimensions={0} | all-to-all | bytes 524288 | tf_op jit(solution)/shard_map/all_to_all | solution.py:393
  183.0 3.1 collective-permute-done.1
  186.7 31.3 %all_to_all.66 = bf16[8,512,256]{2,1,0:T(8,128)(2,1)S(1)} all-to-all(bf16[8,512,256]{2,1,0:T(8,128)(2,1)S(1)} %add_convert_fusion.3), channel_id=1, replica_groups=mesh['section'=2,'seq'=4,'z'=2,'y'=4,'core'=2] {'z','y'}, dimensions={0} | all-to-all | bytes 4194304 | tf_op jit(solution)/shard_map/all_to_all | solution.py:53
  219.2 30.0 %all_to_all.67.x_ref = bf16[8,512,256]{2,1,0:T(8,128)(2,1)} all-to-all(bf16[8,512,256]{2,1,0:T(8,128)(2,1)S(1)} %broadcast_in_dim.50), channel_id=1, replica_groups=mesh['section'=2,'seq'=4,'z'=2,'y'=4,'core'=2] {'z','y'}, dimensions={0} | all-to-all | bytes 4194304 | tf_op jit(solution)/shard_map/all_to_all | solution.py:53
  250.4 5.0 convolution_convert_fusion
  255.4 2.9 collective-permute-start.7
  258.3 2.3 shard_map.150
  260.7 2.5 shard_map.151.asked_ref
  263.2 6.8 %collective-permute-done.7.prev_ref = bf16[2,256,512]{2,1,0:T(8,128)(2,1)S(1)} collective-permute-done((bf16[2,256,512]{2,1,0:T(8,128)(2,1)S(1)}, bf16[2,256,512]{2,1,0:T(8,128)(2,1)S(1)}, u32[]{:S(2)}, u32[]{:S(2)}) %collective-permute-start.7) | collective-permute-done | bytes 524320 | tf_op jit(solution)/shard_map/ppermute | solution.py:431
  269.9 2.7 shard_map.154.mixed_ref
  275.2 2.9 collective-permute-done.8
  278.7 30.0 %all_to_all.68 = bf16[8,512,256]{2,1,0:T(8,128)(2,1)S(1)} all-to-all(bf16[8,512,256]{2,1,0:T(8,128)(2,1)S(1)} %add_convert_fusion.2), channel_id=1, replica_groups=mesh['section'=2,'seq'=4,'z'=2,'y'=4,'core'=2] {'z','y'}, dimensions={0} | all-to-all | bytes 4194304 | tf_op jit(solution)/shard_map/all_to_all | solution.py:53
  309.0 2.9 collective-permute-start.9
  311.9 6.6 %collective-permute-done.9 = bf16[512,256]{1,0:T(8,128)(2,1)S(1)} collective-permute-done((bf16[512,256]{1,0:T(8,128)(2,1)S(1)}, bf16[512,256]{1,0:T(8,128)(2,1)S(1)}, u32[]{:S(2)}, u32[]{:S(2)}) %collective-permute-start.9) | collective-permute-done | bytes 262176 | tf_op jit(solution)/shard_map/ppermute | solution.py:49
  318.6 29.4 %all_to_all.69.x_ref = bf16[8,512,256]{2,1,0:T(8,128)(2,1)} all-to-all(bf16[8,512,256]{2,1,0:T(8,128)(2,1)S(1)} %broadcast_in_dim.54), channel_id=1, replica_groups=mesh['section'=2,'seq'=4,'z'=2,'y'=4,'core'=2] {'z','y'}, dimensions={0} | all-to-all | bytes 4194304 | tf_op jit(solution)/shard_map/all_to_all | solution.py:53
  348.0 4.0 shard_map.157
  357.4 3.9 shard_map.158
  361.3 18.3 %all_to_all.70.triple_ref = bf16[4,3,256,128]{3,2,1,0:T(8,128)(2,1)S(1)} all-to-all(bf16[4,3,256,128]{3,2,1,0:T(8,128)(2,1)S(1)} %shard_map.158), channel_id=1, replica_groups=mesh['section'=2,'seq'=4,'z'=2,'y'=4,'core'=2] {'seq'}, dimensions={0} | all-to-all | bytes 1572864 | tf_op jit(solution)/shard_map/all_to_all | solution.py:392
  381.0 9.1 %all_to_all.71.mixed_ref = bf16[4,256,128]{2,1,0:T(8,128)(2,1)S(1)} all-to-all(bf16[4,256,128]{2,1,0:T(8,128)(2,1)S(1)} %shard_map.159), channel_id=1, replica_groups=mesh['section'=2,'seq'=4,'z'=2,'y'=4,'core'=2] {'seq'}, dimensions={0} | all-to-all | bytes 524288 | tf_op jit(solution)/shard_map/all_to_all | solution.py:393
  392.8 2.9 collective-permute-done.11
  396.2 30.0 %all_to_all.72 = bf16[8,512,256]{2,1,0:T(8,128)(2,1)S(1)} all-to-all(bf16[8,512,256]{2,1,0:T(8,128)(2,1)S(1)} %add_convert_fusion.1), channel_id=1, replica_groups=mesh['section'=2,'seq'=4,'z'=2,'y'=4,'core'=2] {'z','y'}, dimensions={0} | all-to-all | bytes 4194304 | tf_op jit(solution)/shard_map/all_to_all | solution.py:53
  426.7 29.5 %all_to_all.73.x_ref = bf16[8,512,256]{2,1,0:T(8,128)(2,1)S(1)} all-to-all(bf16[8,512,256]{2,1,0:T(8,128)(2,1)S(1)} %broadcast_in_dim.55), channel_id=1, replica_groups=mesh['section'=2,'seq'=4,'z'=2,'y'=4,'core'=2] {'z','y'}, dimensions={0} | all-to-all | bytes 4194304 | tf_op jit(solution)/shard_map/all_to_all | solution.py:53
  457.4 3.0 collective-permute-done.12.x_ref
  461.7 2.7 shard_map.164.mixed_ref
  467.1 2.8 collective-permute-done.13
  470.5 30.2 %all_to_all.74 = bf16[8,512,256]{2,1,0:T(8,128)(2,1)S(1)} all-to-all(bf16[8,512,256]{2,1,0:T(8,128)(2,1)S(1)} %add_convert_fusion), channel_id=1, replica_groups=mesh['section'=2,'seq'=4,'z'=2,'y'=4,'core'=2] {'z','y'}, dimensions={0} | all-to-all | bytes 4194304 | tf_op jit(solution)/shard_map/all_to_all | solution.py:53
  503.1 4.5 collective-permute-done.14
  (124 shorter events, 40.0 us)
Async XLA Ops:
  6.5 1.0 copy-start
  6.5 118.3 %all-gather.3.cloned.1.call-start = ((), (), s32[]{:S(2)}) async-start(), calls=%async_computation.13 | async-start | bytes 14483456 | tf_op jit(solution)/shard_map/all_gather | solution.py:304
  10.6 0.9 copy-start.15
  10.6 1.1 copy-start.16
  11.1 1.6 copy-start.12
  14.2 6.0 %copy-start.19 = (s32[2,4,2]{1,2,0:T(2,128)S(1)}, s32[2,4,2]{1,2,0:T(2,128)}, u32[]{:S(2)}) copy-start(s32[2,4,2]{1,2,0:T(2,128)} %param.17) | copy-start | bytes 196
  14.2 6.3 %copy-start.14 = (s32[64,128]{1,0:T(8,128)S(1)}, s32[64,128]{1,0:T(8,128)}, u32[]{:S(2)}) copy-start(s32[64,128]{1,0:T(8,128)} %param.16) | copy-start | bytes 98308
  14.2 45.1 %all-to-all-start = ((bf16[8,512,256]{2,1,0:T(8,128)(2,1)}), bf16[8,512,256]{2,1,0:T(8,128)(2,1)S(1)}, u32[]{:S(2)}, u32[]{:S(2)}) async-start(bf16[8,512,256]{2,1,0:T(8,128)(2,1)} %broadcast_in_dim.28), calls=%async_computation | async-start | bytes 4194304 | tf_op jit(solution)/shard_map/all_to_all | solution.py:53
  31.5 8.0 %collective-permute-start.3 = (bf16[8,64,1024]{2,1,0:T(8,128)(2,1)}, bf16[8,64,1024]{2,1,0:T(8,128)(2,1)}, u32[]{:S(2)}, u32[]{:S(2)}) collective-permute-start(bf16[8,64,1024]{2,1,0:T(8,128)(2,1)} %broadcast_select_fusion), channel_id=1, source_target_pairs={{0,1},{1,0},{2,3},{3,2},{4,5},{5,4},{6,7},{7,6},{8,9},{9,8},{10,11... | collective-permute-start | bytes 3145736 | tf_op jit(solution)/shard_map/ppermute | solution.py:45
  42.3 55.4 %copy-start.18 = (f32[2,1024]{1,0:T(2,128)S(1)}, f32[2,1024]{1,0:T(2,128)}, u32[]{:S(2)}) copy-start(f32[2,1024]{1,0:T(2,128)} %param.19) | copy-start | bytes 24580
  59.3 32.6 %all-to-all-start.5 = ((bf16[8,64,1024]{2,1,0:T(8,128)(2,1)}), bf16[8,64,1024]{2,1,0:T(8,128)(2,1)}, u32[]{:S(2)}, u32[]{:S(2)}) async-start(bf16[8,64,1024]{2,1,0:T(8,128)(2,1)} %select_add_fusion), calls=%async_computation.5 | async-start | bytes 2097152 | tf_op jit(solution)/shard_map/all_to_all | solution.py:53
  69.8 79.1 %collective-permute-start = (bf16[8,512,256]{2,1,0:T(8,128)(2,1)S(1)}, bf16[8,512,256]{2,1,0:T(8,128)(2,1)}, u32[]{:S(2)}, u32[]{:S(2)}) collective-permute-start(bf16[8,512,256]{2,1,0:T(8,128)(2,1)S(1)} %all-to-all-done.x_ref), channel_id=1, source_target_pairs={{0,1},{1,0},{2,3},{3,2},{4,5},{5,4},{6,7},{7,6},{8,9},{9,8},{10,11... | collective-permute-start | bytes 6291464 | tf_op jit(solution)/shard_map/ppermute | solution.py:45
  93.3 10.1 %collective-permute-start.4 = (bf16[64,1024]{1,0:T(8,128)(2,1)S(1)}, bf16[64,1024]{1,0:T(8,128)(2,1)S(1)}, u32[]{:S(2)}, u32[]{:S(2)}) collective-permute-start(bf16[64,1024]{1,0:T(8,128)(2,1)S(1)} %reduce_sum.49), channel_id=1, source_target_pairs={{0,64},{64,0},{1,65},{65,1},{2,66},{66,2},{3,67},{67,3},{4,68},{68... | collective-permute-start | bytes 393224 | tf_op jit(solution)/shard_map/ppermute | solution.py:49
  124.8 8.5 %copy-start.17 = (f32[1,2,4096]{2,1,0:T(2,128)S(1)}, f32[1,2,4096]{2,1,0:T(2,128)}, u32[]{:S(2)}) copy-start(f32[1,2,4096]{2,1,0:T(2,128)} %param.24) | copy-start | bytes 98308
  129.5 10.6 %collective-permute-start.5 = (bf16[128,1024]{1,0:T(8,128)(2,1)S(1)}, bf16[128,1024]{1,0:T(8,128)(2,1)S(1)}, u32[]{:S(2)}, u32[]{:S(2)}) collective-permute-start(bf16[128,1024]{1,0:T(8,128)(2,1)S(1)} %shard_map.152), channel_id=1, source_target_pairs={{0,64},{64,0},{1,65},{65,1},{2,66},{66,2},{3,67},{67,3},{4,68},{68... | collective-permute-start | bytes 786440 | tf_op jit(solution)/shard_map/ppermute | solution.py:49
  140.2 5.5 %copy-start.6 = (bf16[128,1024]{1,0:T(8,128)(2,1)}, bf16[128,1024]{1,0:T(8,128)(2,1)S(1)}, u32[]{:S(2)}) copy-start(bf16[128,1024]{1,0:T(8,128)(2,1)S(1)} %add_convert_fusion.8.x_ref) | copy-start | bytes 786436
  145.6 12.8 %collective-permute-start.6 = (bf16[128,1024]{1,0:T(8,128)(2,1)}, bf16[128,1024]{1,0:T(8,128)(2,1)S(1)}, u32[]{:S(2)}, u32[]{:S(2)}) collective-permute-start(bf16[128,1024]{1,0:T(8,128)(2,1)} %shard_map.153), channel_id=1, source_target_pairs={{0,64},{64,0},{1,65},{65,1},{2,66},{66,2},{3,67},{67,3},{4,68},{68... | collective-permute-start | bytes 786440 | tf_op jit(solution)/shard_map/ppermute | solution.py:49
  153.1 0.9 copy-start.5
  154.0 26.5 %copy-start.2 = (bf16[1,256,4096]{2,1,0:T(8,128)(2,1)S(1)}, bf16[1,256,4096]{2,1,0:T(8,128)(2,1)}, u32[]{:S(2)}) copy-start(bf16[1,256,4096]{2,1,0:T(8,128)(2,1)} %param.26) | copy-start | bytes 6291460
  154.0 16.0 %all-to-all-start.1 = ((bf16[4,3,256,128]{3,2,1,0:T(8,128)(2,1)}), bf16[4,3,256,128]{3,2,1,0:T(8,128)(2,1)S(1)}, u32[]{:S(2)}, u32[]{:S(2)}) async-start(bf16[4,3,256,128]{3,2,1,0:T(8,128)(2,1)} %copy-done.5), calls=%async_computation.1 | async-start | bytes 1572864 | tf_op jit(solution)/shard_map/all_to_all | solution.py:392
  158.5 92.0 %all-gather.5.cloned.1.call-start = ((), (), s32[]{:S(2)}) async-start(), calls=%async_computation.14 | async-start | bytes 4456448 | tf_op jit(solution)/shard_map/all_gather | solution.py:425
  181.7 4.4 collective-permute-start.1
  218.0 1.0 copy-start.13
  219.2 30.0 %copy-start.11 = (bf16[1,1024,2,256]{3,2,1,0:T(2,128)(2,1)S(1)}, bf16[1,1024,2,256]{3,2,1,0:T(2,128)(2,1)}, u32[]{:S(2)}) copy-start(bf16[1,1024,2,256]{3,2,1,0:T(2,128)(2,1)} %param.28) | copy-start | bytes 3145732
  249.2 11.5 %collective-permute-start.2 = (bf16[8,512,256]{2,1,0:T(8,128)(2,1)}, bf16[8,512,256]{2,1,0:T(8,128)(2,1)}, u32[]{:S(2)}, u32[]{:S(2)}) collective-permute-start(bf16[8,512,256]{2,1,0:T(8,128)(2,1)} %all_to_all.67.x_ref), channel_id=1, source_target_pairs={{0,1},{1,0},{2,3},{3,2},{4,5},{5,4},{6,7},{7,6},{8,9},{9,8},{10,11... | collective-permute-start | bytes 6291464 | tf_op jit(solution)/shard_map/ppermute | solution.py:45
  250.4 7.9 %copy-start.4 = (bf16[1,4096,256]{2,1,0:T(8,128)(2,1)S(1)}, bf16[1,4096,256]{2,1,0:T(8,128)(2,1)}, u32[]{:S(2)}) copy-start(bf16[1,4096,256]{2,1,0:T(8,128)(2,1)} %param.27) | copy-start | bytes 6291460
  255.4 14.5 %collective-permute-start.7 = (bf16[2,256,512]{2,1,0:T(8,128)(2,1)S(1)}, bf16[2,256,512]{2,1,0:T(8,128)(2,1)S(1)}, u32[]{:S(2)}, u32[]{:S(2)}) collective-permute-start(bf16[2,256,512]{2,1,0:T(8,128)(2,1)S(1)} %slice_bitcast_fusion), channel_id=1, source_target_pairs={{0,16},{16,32},{32,48},{1,17},{17,33},{33,49},{2,18},{18,34},{34,5... | collective-permute-start | bytes 1572872 | tf_op jit(solution)/shard_map/ppermute | solution.py:431
  263.2 9.5 %copy-start.3 = (bf16[1,256,4096]{2,1,0:T(8,128)(2,1)S(1)}, bf16[1,256,4096]{2,1,0:T(8,128)(2,1)}, u32[]{:S(2)}) copy-start(bf16[1,256,4096]{2,1,0:T(8,128)(2,1)} %param.29) | copy-start | bytes 6291460
  273.9 4.2 collective-permute-start.8
  309.0 9.5 %collective-permute-start.9 = (bf16[512,256]{1,0:T(8,128)(2,1)S(1)}, bf16[512,256]{1,0:T(8,128)(2,1)S(1)}, u32[]{:S(2)}, u32[]{:S(2)}) collective-permute-start(bf16[512,256]{1,0:T(8,128)(2,1)S(1)} %add_convert_fusion.6), channel_id=1, source_target_pairs={{0,64},{64,0},{1,65},{65,1},{2,66},{66,2},{3,67},{67,3},{4,68},{68... | collective-permute-start | bytes 786440 | tf_op jit(solution)/shard_map/ppermute | solution.py:49
  348.0 5.1 collective-permute-start.10
  351.9 1.1 copy-start.9
  353.1 1.4 copy-start.7
  354.4 1.6 copy-start.8
  356.0 1.4 copy-start.10
  391.2 4.5 collective-permute-start.11
  456.2 4.2 collective-permute-start.12
  465.7 4.2 collective-permute-start.13
  470.4 37.8 %copy-start.1 = (bf16[256,1024]{1,0:T(8,128)(2,1)S(1)}, bf16[256,1024]{1,0:T(8,128)(2,1)}, u32[]{:S(2)}) copy-start(bf16[256,1024]{1,0:T(8,128)(2,1)} %param.23) | copy-start | bytes 1572868
  501.0 6.6 %collective-permute-start.14 = (bf16[256,256]{1,0:T(8,128)(2,1)S(1)}, bf16[256,256]{1,0:T(8,128)(2,1)S(1)}, u32[]{:S(2)}, u32[]{:S(2)}) collective-permute-start(bf16[256,256]{1,0:T(8,128)(2,1)S(1)} %slice.41), channel_id=1, source_target_pairs={{0,64},{64,0},{1,65},{65,1},{2,66},{66,2},{3,67},{67,3},{4,68},{68... | collective-permute-start | bytes 393224 | tf_op jit(solution)/shard_map/ppermute | solution.py:49
Sparse Core Ops, SparseCore 0:
  12.8 111.9 all-gather.2
  161.0 42.0 all-gather.4

commit v3 on v2

--- a/solution.py
+++ b/solution.py
@@ -2,6 +2,7 @@
 
 import jax
 import jax.numpy as jnp
+import numpy as np
 from jax import lax
 from jax.experimental import pallas as pl
 from jax.experimental.pallas import tpu as pltpu
@@ -41,6 +42,22 @@
 SCALAR = pl.BlockSpec(memory_space=pltpu.SMEM)
 
 
+PARTS = (352, 160)
+STARTS = (0, 352)
+MASKS = (((4, 1, 3), (1, 3, 4)), ((3, 4, 1), (3, 4, 1)))
+
+
+def block_offsets(masks):
+    return [
+        (masks[0] * (b & 1)) ^ (masks[1] * (b >> 1 & 1)) ^ (masks[2] * (b >> 2 & 1))
+        for b in range(CHIPS)
+    ]
+
+
+OFFSETS = np.array([[block_offsets(m) for m in part] for part in MASKS], np.int32)
+SLOTS = np.argsort(OFFSETS, axis=-1).astype(np.int32)
+
+
 def core_swap(value):
     return lax.ppermute(value, "core", [(0, 1), (1, 0)])
 
@@ -53,80 +70,119 @@
     return lax.all_to_all(value, ("z", "y"), 0, 0, tiled=True)
 
 
+def neighbour(value, part, turn):
+    route = [
+        (2 * chip + core, 2 * (chip ^ MASKS[part][core][turn]) + core)
+        for chip in range(CHIPS)
+        for core in range(2)
+    ]
+    return lax.ppermute(value, MP, route)
+
+
+def places(chip, pick):
+    offsets = lax.dynamic_index_in_dim(jnp.asarray(OFFSETS), pick, 1, keepdims=False)
+    slots = lax.dynamic_index_in_dim(jnp.asarray(SLOTS), pick, 1, keepdims=False)
+    chips = chip ^ offsets
+    blocks = jnp.take_along_axis(slots, jnp.arange(CHIPS)[None] ^ chip, axis=1)
+    return jnp.concatenate(
+        [jnp.reshape(pick, (1,)), chips.reshape(-1), blocks.reshape(-1)]
+    ).astype(jnp.int32)
+
+
 def gather_chips(local):
-    return chips_to_chips(jnp.broadcast_to(local[None], (CHIPS,) + local.shape))
-
-
-def project_kernel(last, units, pick_ref, x_ref, gain_ref, w_ref, *refs):
+    near = []
+    for part, value in enumerate(local):
+        near.append(jnp.stack([value, neighbour(value, part, 0)]))
+    near = [
+        jnp.concatenate([value, neighbour(value, part, 1)]) for part, value in enumerate(near)
+    ]
+    far = [neighbour(value, part, 2) for part, value in enumerate(near)]
+    return near + far
+
+
+def scatter_sum(own, other):
+    wide = [value.astype(f32) for value in own]
+    got = [None] * 4
+    for at in (2, 3, 0, 1):
+        got[at] = core_swap(other[at]).astype(f32)
+    sent = [neighbour((wide[2 + part] + got[2 + part]).astype(bf16), part, 2) for part in range(2)]
+    result = []
+    for part in range(2):
+        low = wide[part] + got[part] + sent[part].astype(f32)
+        second = neighbour(low[2:].astype(bf16), part, 1)
+        low = low[:2] + second.astype(f32)
+        third = neighbour(low[1].astype(bf16), part, 0)
+        result.append(low[0] + third.astype(f32))
+    return result
+
+
+def project_kernel(last, units, place_ref, *refs):
+    x_refs, (gain_ref, w_ref), refs = refs[:4], refs[4:6], refs[6:]
     if last:
-        acc_in, sq_in, out_ref, acc_ref, sq_ref, left_ref = refs
+        acc_in, sq_in, out_ref, sq_ref, left_ref = refs
     else:
         acc_ref, sq_ref, left_ref = refs
     step = pl.program_id(0)
-    parts = w_ref.shape[0]
 
     @pl.when(step == 0)
     def _():
-        if last:
-            acc_ref[...] = acc_in[...]
-            sq_ref[...] = sq_in[...]
-        else:
-            acc_ref[...] = jnp.zeros_like(acc_ref)
-            sq_ref[...] = jnp.zeros_like(sq_ref)
-
-    for at in range(GROUP):
-        wide = x_ref[at].astype(f32)
-        squares = wide * wide
-        sq_ref[...] += squares[:, :128] + squares[:, 128:]
-        left_ref[:, at * WIDTH : (at + 1) * WIDTH] = (wide * gain_ref[at, 0]).astype(bf16)
-    for part in range(parts):
-        right = w_ref[part].reshape(GROUP * WIDTH, WIDTH)
-        acc_ref[part] += jnp.dot(left_ref[...], right, preferred_element_type=f32)
-
-    if last:
-
-        @pl.when(step == CHIPS // GROUP - 1)
-        def _():
-            mean = jnp.sum(sq_ref[...], axis=1, keepdims=True) / D
-            root = jnp.sqrt(mean + epsilon)
-            for part in range(parts):
-                done = (acc_ref[part] / root).astype(bf16)
-                if units:
-                    for unit in range(UNITS):
-                        b, h = divmod(unit, 2)
-                        out_ref[unit, part] = done[
-                            b * ROWS : (b + 1) * ROWS, h * HEAD : (h + 1) * HEAD
-                        ]
-                else:
-                    out_ref[...] = done
-
-
-def project_half(pick, rows, gains, weight, before, units):
+        for part in range(2):
+            rows = slice(STARTS[part], STARTS[part] + PARTS[part])
+            total = sq_in[rows, :] if last else jnp.zeros((PARTS[part], 128), f32)
+            for block in range(CHIPS):
+                chip = place_ref[1 + part * CHIPS + block]
+                wide = x_refs[part + 2 * (block // 4)][block % 4].astype(f32)
+                squares = wide * wide
+                total += squares[:, :128] + squares[:, 128:]
+                cols = pl.ds(pl.multiple_of(chip * WIDTH, WIDTH), WIDTH)
+                left_ref[rows, cols] = (wide * gain_ref[chip, 0]).astype(bf16)
+            sq_ref[rows, :] = total
+
+    right = w_ref[0].reshape(CHIPS * WIDTH, WIDTH)
+    product = jnp.dot(left_ref[...], right, preferred_element_type=f32)
+    if not last:
+        acc_ref[0] = product
+        return
+    mean = jnp.sum(sq_ref[...], axis=1, keepdims=True) / D
+    done = ((acc_in[0] + product) / jnp.sqrt(mean + epsilon)).astype(bf16)
+    if units:
+        for unit in range(UNITS):
+            b, h = divmod(unit, 2)
+            out_ref[unit, 0] = done[b * ROWS : (b + 1) * ROWS, h * HEAD : (h + 1) * HEAD]
+    else:
+        out_ref[...] = done
+
+
+def project_half(place, rows, gains, weight, before, units):
     parts = weight.shape[0]
     count = BATCH * ROWS
     acc = (parts, count, WIDTH)
     sq = (count, 128)
     last = before is not None
-    in_specs = [
-        pl.BlockSpec((GROUP, count, WIDTH), lambda s, pick: (s, 0, 0)),
-        pl.BlockSpec((GROUP, 1, 1, WIDTH), lambda s, pick: (s, pick[0], 0, 0)),
-        pl.BlockSpec((parts, GROUP, 1, WIDTH, WIDTH), lambda s, pick: (0, s, pick[0], 0, 0)),
-    ]
-    scratch = [pltpu.VMEM((count, GROUP * WIDTH), bf16)]
+    acc_spec = pl.BlockSpec((1, count, WIDTH), lambda s, place: (s, 0, 0))
+    in_specs = [whole(value.shape) for value in rows] + [
+        pl.BlockSpec((CHIPS, 1, 1, WIDTH), lambda s, place: (0, place[0], 0, 0)),
+        pl.BlockSpec((1, CHIPS, 1, WIDTH, WIDTH), lambda s, place: (s, 0, place[0], 0, 0)),
+    ]
+    scratch = [pltpu.VMEM((count, CHIPS * WIDTH), bf16)]
     if last:
-        out = (UNITS, parts, ROWS, HEAD) if units else (count, WIDTH)
-        in_specs += [whole(acc), whole(sq)]
-        out_specs = whole(out)
+        in_specs += [acc_spec, whole(sq)]
+        scratch = [pltpu.VMEM(sq, f32)] + scratch
+        if units:
+            out = (UNITS, parts, ROWS, HEAD)
+            out_specs = pl.BlockSpec((UNITS, 1, ROWS, HEAD), lambda s, place: (0, s, 0, 0))
+        else:
+            out = (count, WIDTH)
+            out_specs = whole(out)
         out_shape = jax.ShapeDtypeStruct(out, bf16)
-        scratch = [pltpu.VMEM(acc, f32), pltpu.VMEM(sq, f32)] + scratch
     else:
-        out_specs = [whole(acc), whole(sq)]
+        out_specs = [acc_spec, whole(sq)]
         out_shape = [jax.ShapeDtypeStruct(acc, f32), jax.ShapeDtypeStruct(sq, f32)]
     return pl.pallas_call(
         functools.partial(project_kernel, last, units),
         grid_spec=pltpu.PrefetchScalarGridSpec(
             num_scalar_prefetch=1,
-            grid=(CHIPS // GROUP,),
+            grid=(parts,),
             in_specs=in_specs,
             out_specs=out_specs,
             scratch_shapes=scratch,
@@ -139,19 +195,19 @@
             transcendentals=0,
         ),
     )(
-        pick,
-        rows,
+        place,
+        *rows,
         gains.reshape(CHIPS, 2, 1, WIDTH),
         weight.reshape(parts, CHIPS, 2, WIDTH, WIDTH),
         *(before or ()),
     )
 
 
-def project(core, local, gains, weight, units):
+def project(places_both, local, gains, weight, units):
     same = gather_chips(local)
-    swap = core_swap(same)
-    before = project_half(core, same, gains, weight, None, units)
-    return project_half(1 - core, swap, gains, weight, before, units)
+    swap = [core_swap(value) for value in same]
+    before = project_half(places_both[0], same, gains, weight, None, units)
+    return project_half(places_both[1], swap, gains, weight, before, units)
 
 
 def causal_kernel(triple_ref, out_ref):
@@ -218,50 +274,69 @@
     )(asked, prev, pairs)
 
 
-def terms_kernel(pick_ref, mixed_ref, *refs):
-    *w_refs, out_ref, left_ref = refs
-
-    @pl.when(pl.program_id(0) == 0)
+def terms_kernel(place_ref, mixed_ref, *refs):
+    w_refs, out_refs, left_ref = refs[:GROUP], refs[GROUP : GROUP + 4], refs[-1]
+    step = pl.program_id(0)
+
+    @pl.when(step == 0)
     def _():
         for unit in range(UNITS):
             b, h = divmod(unit, 2)
             left_ref[b * ROWS : (b + 1) * ROWS, h * HEAD : (h + 1) * HEAD] = mixed_ref[unit]
 
     for at, w_ref in enumerate(w_refs):
-        out_ref[at] = jnp.dot(
-            left_ref[...], w_ref[...], preferred_element_type=f32
-        ).astype(bf16)
-
-
-def terms(pick, mixed, weight):
+        product = jnp.dot(left_ref[...], w_ref[...], preferred_element_type=f32).astype(bf16)
+        chip = step * GROUP + at
+        for part in range(2):
+            block = place_ref[1 + (2 + part) * CHIPS + chip]
+            value = product[STARTS[part] : STARTS[part] + PARTS[part], :]
+
+            @pl.when(block < 4)
+            def _():
+                out_refs[part][block] = value
+
+            @pl.when(block >= 4)
+            def _():
+                out_refs[2 + part][block - 4] = value
+
+
+def terms(place, mixed, weight):
     count = BATCH * ROWS
 
     def columns(at):
-        return pl.BlockSpec((WIDTH, WIDTH), lambda s, pick: (0, 2 * (GROUP * s + at) + pick[0]))
-
+        return pl.BlockSpec((WIDTH, WIDTH), lambda s, place: (0, 2 * (GROUP * s + at) + place[0]))
+
+    shapes = [(4, PARTS[at % 2], WIDTH) for at in range(4)]
     return pl.pallas_call(
         terms_kernel,
         grid_spec=pltpu.PrefetchScalarGridSpec(
             num_scalar_prefetch=1,
             grid=(CHIPS // GROUP,),
             in_specs=[whole((UNITS, ROWS, HEAD))] + [columns(at) for at in range(GROUP)],
-            out_specs=pl.BlockSpec((GROUP, count, WIDTH), lambda s, pick: (s, 0, 0)),
+            out_specs=[whole(shape) for shape in shapes],
             scratch_shapes=[pltpu.VMEM((count, WIDTH), bf16)],
         ),
-        out_shape=jax.ShapeDtypeStruct((CHIPS, count, WIDTH), bf16),
+        out_shape=[jax.ShapeDtypeStruct(shape, bf16) for shape in shapes],
         compiler_params=params(),
         cost_estimate=pl.CostEstimate(
             flops=2 * count * WIDTH * D // 2,
             bytes_accessed=D * WIDTH + D * count,
             transcendentals=0,
         ),
-    )(pick, mixed, *([weight] * GROUP))
-
-
-def product_sum(core, mixed, weight):
-    far = core_swap(terms(1 - core, mixed, weight))
-    paired = (terms(core, mixed, weight).astype(f32) + far.astype(f32)).astype(bf16)
-    return jnp.sum(chips_to_chips(paired).astype(f32), axis=0)
+    )(place, mixed, *([weight] * GROUP))
+
+
+def add_product(places_both, states, mixed, weight):
+    other = terms(places_both[1], mixed, weight)
+    own = terms(places_both[0], mixed, weight)
+    return [
+        (state.astype(f32) + total).astype(bf16)
+        for state, total in zip(states, scatter_sum(own, other))
+    ]
+
+
+def by_parts(rows):
+    return [rows[start : start + count] for start, count in zip(STARTS, PARTS)]
 
 
 def look_up(ids, enc_embed, core, section):
@@ -386,15 +461,19 @@
     return (inner.astype(f32) + (fed.astype(f32) + section_swap(fed).astype(f32))).astype(bf16)
 
 
-def decoder_layer(core, states, prev, pairs, weights):
+def after(value, other):
+    return lax.optimization_barrier((value, other))[0]
+
+
+def decoder_layer(places_both, states, make_pairs, weights):
     norms, triple_w, out_w, query_w, back_w = weights
-    triple = project(core, states, norms[0], triple_w, True)
+    triple = project(places_both, states, norms[0], triple_w, True)
     triple = lax.all_to_all(triple, "seq", 0, 0, tiled=True)
     mixed = lax.all_to_all(causal(triple), "seq", 0, 0, tiled=True)
-    middle = (states.astype(f32) + product_sum(core, mixed, out_w)).astype(bf16)
-    asked = project(core, middle, norms[1], query_w[None], False)
-    crossed = cross(asked, prev, pairs)
-    return (middle.astype(f32) + product_sum(core, crossed, back_w)).astype(bf16)
+    middle = add_product(places_both, states, mixed, out_w)
+    asked = project(places_both, middle, norms[1], query_w[None], False)
+    crossed = cross(asked, *make_pairs(mixed))
+    return add_product(places_both, middle, crossed, back_w)
 
 
 def on_device(
@@ -416,19 +495,32 @@
 ):
     section = lax.axis_index("section").astype(jnp.int32)
     core_at = lax.axis_index("core").astype(jnp.int32)
-    core = jnp.reshape(core_at, (1,))
+    chip = lax.axis_index(("z", "y")).astype(jnp.int32)
+    places_both = [places(chip, core_at), places(chip, 1 - core_at)]
     blocks_here = neighbour_table.shape[1]
     pieces = weight_pieces(section, enc_qkv, enc_out, enc_up, enc_down)
     slot_ids = neighbour_ids[neighbour_table.reshape(-1)]
     embedded = look_up(slot_ids, enc_embed, core_at, section)
-    encoded = encode(embedded, enc_norms, pieces, jnp.reshape(section, (1,)))
-    encoded = lax.all_gather(encoded, MP, axis=0, tiled=True)
-    pairs = jnp.dot(
-        encoded, cross_pair[0].reshape(ENC_D, 2 * WIDTH), preferred_element_type=f32
-    ).astype(bf16)
-    pairs = pairs.reshape(BATCH, blocks_here, KEYS, 2 * WIDTH)
     count = lax.axis_size("seq")
-    prev = lax.ppermute(pairs[:, -1], "seq", [(i, i + 1) for i in range(count - 1)])
+
+    def make_pairs(mixed):
+        ready = after(embedded, mixed[0, 0, :1])
+        encoded = encode(ready, enc_norms, pieces, jnp.reshape(section, (1,)))
+        encoded = lax.all_gather(encoded, MP, axis=0, tiled=True)
+        pairs = jnp.dot(
+            encoded, cross_pair[0].reshape(ENC_D, 2 * WIDTH), preferred_element_type=f32
+        ).astype(bf16)
+        pairs = pairs.reshape(BATCH, blocks_here, KEYS, 2 * WIDTH)
+        prev = lax.ppermute(pairs[:, -1], "seq", [(i, i + 1) for i in range(count - 1)])
+        return prev, pairs
+
+    made = []
+
+    def once(mixed):
+        if not made:
+            made.append(make_pairs(mixed))
+        return made[0]
+
     weights = (
         dec_norms[0],
         jnp.transpose(dec_qkv[0], (1, 0, 2)),
@@ -438,8 +530,9 @@
     )
 
     states = hidden_states.reshape(BATCH * ROWS, WIDTH)
-    first = decoder_layer(core, states, prev, pairs, weights)
-    second = decoder_layer(core, section_swap(first), prev, pairs, weights)
+    first = decoder_layer(places_both, by_parts(states), once, weights)
+    handed = section_swap(jnp.concatenate(first))
+    second = jnp.concatenate(decoder_layer(places_both, by_parts(handed), once, weights))
     second = second.reshape(BATCH, ROWS, WIDTH)
     return jnp.where(section == 0, section_swap(second[0]), second[1])[None]
 

time: 525 us -> 560 us (1.067)
  blocking collectives: 247 us -> 52.5 us
  waiting for transfers between devices: 112 us -> 276 us
  starting transfers between devices: 41.1 us -> 90.5 us
  Pallas kernels: 50.9 us -> 76.6 us
  local copies, waits for them, and re-layouts: 32.1 us -> 25.7 us
    all_to_all x7 -> x0, blocking collectives: 210 us -> none  [chips_to_chips(): return lax.all_to_all(value, ('z', 'y'), 0, 0, tiled=True)]
    ppermute x1 -> x49, waiting for transfers between devices: 6.76 us -> 189 us  [the longest x48 185 us: neighbour(): return lax.ppermute(value, MP, route)]
    ppermute x1 -> x49, starting transfers between devices: 2.9 us -> 64.1 us  [the longest x48 61.5 us: neighbour(): return lax.ppermute(value, MP, route)]
    all_to_all x2 -> x1, waiting for transfers between devices: 39.1 us -> 21.7 us  [chips_to_chips(): return lax.all_to_all(value, ('z', 'y'), 0, 0, tiled=True)]
    pallas_call x8, Pallas kernels: 9.7 us -> 27.1 us  [terms(): pl.pallas_call(terms_kernel, grid_spec=pltpu.PrefetchScalarGridSpec(num_s...]
    all_to_all x1 -> x2, blocking collectives: 18.3 us -> 34.4 us  [decoder_layer(): triple = lax.all_to_all(triple, 'seq', 0, 0, tiled=True)]
    all_gather x1, waiting for transfers between devices: 21.4 us -> 36.7 us  [weight_pieces(): return lax.all_gather(local, MP, axis=1, tiled=True)]
    ppermute x9 -> x33, waiting for transfers between devices: 14.8 us -> 0.09 us  [core_swap(): return lax.ppermute(value, 'core', [(0, 1), (1, 0)])]
  transfers between devices with their start and end apart: 20 -> 90, of which waited for: 14 -> 45; matrix products, arithmetic and copies ran while one was open for 7% -> 6% of each run, Pallas kernels for 7% -> 9%
where the time goes in v3:
time: 560 us; the launch traced here: 552 us
  waiting for transfers between devices  276 us (49%)
  starting transfers between devices  90.5 us (16%)
  Pallas kernels  76.6 us (14%)
  blocking collectives  52.5 us (9%)
  local copies, waits for them, and re-layouts  25.7 us (5%)
  between operations  14.9 us (3%)
  other arithmetic  10.4 us (2%)
    ppermute x48, waiting for transfers between devices, neighbour(): return lax.ppermute(value, MP, route)  185 us
    ppermute x48, starting transfers between devices, neighbour(): return lax.ppermute(value, MP, route)  61.5 us
    all_gather x1, waiting for transfers between devices, weight_pieces(): return lax.all_gather(local, MP, axis=1, tiled=True)  36.7 us
    all_to_all x2, blocking collectives, decoder_layer(): triple = lax.all_to_all(triple, 'seq', 0, 0, tiled=True)  34.4 us
    pallas_call x8, Pallas kernels, project_half(): pl.pallas_call(functools.partial(project_kernel, last, units), grid_spec=...  32.1 us
    ppermute x5, waiting for transfers between devices, section_swap(): return lax.ppermute(value, 'section', [(0, 1), (1, 0)])  29 us
    pallas_call x8, Pallas kernels, terms(): pl.pallas_call(terms_kernel, grid_spec=pltpu.PrefetchScalarGridSpec(num_s...  27.1 us
    all_to_all x1, waiting for transfers between devices, chips_to_chips(): return lax.all_to_all(value, ('z', 'y'), 0, 0, tiled=True)  21.7 us
  transfers between devices with their start and end apart: 90, of which 45 were waited for; matrix products, arithmetic and copies ran while one was open for 6% of the time, Pallas kernels for 9%

profile of v3, /device:TPU:0, one launch (start us, length us, event | category | flops | bytes accessed | tf_op | source)
XLA Modules:
  0.0 552.0 jit_solution(8571565145529912174)
XLA Ops:
  12.6 7.1 %gather_fusion.1 = bf16[512,1024]{1,0:T(8,128)(2,1)S(1)} fusion(bf16[4000,1024]{1,0:T(8,128)(2,1)} %param.22, s32[1024]{0:T(1024)S(1)} %pad_clamp_fusion.1), kind=kCustom, calls=%fused_computation.3 | custom fusion | bytes 2099200 | tf_op jit(solution)/shard_map/gather | solution.py:350
  20.9 7.7 %gather_fusion.2 = bf16[512,1024]{1,0:T(8,128)(2,1)S(1)} fusion(bf16[4000,1024]{1,0:T(8,128)(2,1)} %param.22, s32[1024]{0:T(1024)S(1)} %pad_clamp_fusion), kind=kCustom, calls=%fused_computation.4 | custom fusion | bytes 2099200 | tf_op jit(solution)/shard_map/gather | solution.py:350
  29.7 6.0 %all-to-all-start.2 = ((bf16[8,64,1024]{2,1,0:T(8,128)(2,1)}), bf16[8,64,1024]{2,1,0:T(8,128)(2,1)S(1)}, u32[]{:S(2)}, u32[]{:S(2)}) async-start(bf16[8,64,1024]{2,1,0:T(8,128)(2,1)} %select_add_fusion), calls=%async_computation.2 | async-start | bytes 2097152 | tf_op jit(solution)/shard_map/all_to_all | solution.py:70
  37.9 21.7 %all-to-all-done.2 = bf16[8,64,1024]{2,1,0:T(8,128)(2,1)S(1)} async-done(((bf16[8,64,1024]{2,1,0:T(8,128)(2,1)}), bf16[8,64,1024]{2,1,0:T(8,128)(2,1)S(1)}, u32[]{:S(2)}, u32[]{:S(2)}) %all-to-all-start.2) | async-done | bytes 1048608 | tf_op jit(solution)/shard_map/all_to_all | solution.py:70
  59.8 3.7 collective-permute-start.31
  63.5 6.7 %collective-permute-done.31 = bf16[64,1024]{1,0:T(8,128)(2,1)S(1)} collective-permute-done((bf16[64,1024]{1,0:T(8,128)(2,1)S(1)}, bf16[64,1024]{1,0:T(8,128)(2,1)S(1)}, u32[]{:S(2)}, u32[]{:S(2)}) %collective-permute-start.31) | collective-permute-done | bytes 131104 | tf_op jit(solution)/shard_map/ppermute | solution.py:66
  70.2 36.7 %all-gather.3.cloned.1.call-done.q_ref.k_ref.v_ref.o0_ref.o1_ref.w_ref = bf16[13,1024,512]{2,1,0:T(8,128)(2,1)} async-done(((bf16[13,64,512]{2,1,0:T(8,128)(2,1)}), bf16[13,1024,512]{2,1,0:T(8,128)(2,1)}) %all-gather.3.cloned.1.call-update) | async-done | bytes 13631504 | tf_op jit(solution)/shard_map/all_gather | solution.py:379
  107.0 4.6 shard_map.170
  115.1 6.5 %collective-permute-done.32 = bf16[128,1024]{1,0:T(8,128)(2,1)S(1)} collective-permute-done((bf16[128,1024]{1,0:T(8,128)(2,1)S(1)}, bf16[128,1024]{1,0:T(8,128)(2,1)S(1)}, u32[]{:S(2)}, u32[]{:S(2)}) %collective-permute-start.32) | collective-permute-done | bytes 262176 | tf_op jit(solution)/shard_map/ppermute | solution.py:66
  121.8 4.7 shard_map.171
  132.9 4.4 collective-permute-done.33
  139.9 4.9 collective-permute-done.6.refs_2_
  147.9 16.1 %collective-permute-done.8.refs_3_ = bf16[4,160,256]{2,1,0:T(8,128)(2,1)} collective-permute-done((bf16[4,160,256]{2,1,0:T(8,128)(2,1)S(1)}, bf16[4,160,256]{2,1,0:T(8,128)(2,1)}, u32[]{:S(2)}, u32[]{:S(2)}) %collective-permute-start.8) | collective-permute-done | bytes 327712 | tf_op jit(solution)/shard_map/ppermute | solution.py:79
  164.2 5.3 shard_map.163
  169.5 5.3 shard_map.164
  174.8 17.3 %all_to_all.25.triple_ref = bf16[4,3,256,128]{3,2,1,0:T(8,128)(2,1)S(1)} all-to-all(bf16[4,3,256,128]{3,2,1,0:T(8,128)(2,1)S(1)} %shard_map.164), channel_id=1, replica_groups=mesh['section'=2,'seq'=4,'z'=2,'y'=4,'core'=2] {'seq'}, dimensions={0} | all-to-all | bytes 1572864 | tf_op jit(solution)/shard_map/all_to_all | solution.py:471
  193.4 9.1 %all_to_all.26.mixed_ref = bf16[4,256,128]{2,1,0:T(8,128)(2,1)S(1)} all-to-all(bf16[4,256,128]{2,1,0:T(8,128)(2,1)S(1)} %shard_map.165), channel_id=1, replica_groups=mesh['section'=2,'seq'=4,'z'=2,'y'=4,'core'=2] {'seq'}, dimensions={0} | all-to-all | bytes 524288 | tf_op jit(solution)/shard_map/all_to_all | solution.py:472
  212.6 10.0 %collective-permute-done.12 = bf16[4,352,256]{2,1,0:T(8,128)(2,1)S(1)} collective-permute-done((bf16[4,352,256]{2,1,0:T(8,128)(2,1)S(1)}, bf16[4,352,256]{2,1,0:T(8,128)(2,1)S(1)}, u32[]{:S(2)}, u32[]{:S(2)}) %collective-permute-start.12) | collective-permute-done | bytes 720928 | tf_op jit(solution)/shard_map/ppermute | solution.py:79
  223.8 6.8 %collective-permute-done.13 = bf16[2,352,256]{2,1,0:T(8,128)(2,1)S(1)} collective-permute-done((bf16[2,352,256]{2,1,0:T(8,128)(2,1)S(1)}, bf16[2,352,256]{2,1,0:T(8,128)(2,1)S(1)}, u32[]{:S(2)}, u32[]{:S(2)}) %collective-permute-start.13) | collective-permute-done | bytes 360480 | tf_op jit(solution)/shard_map/ppermute | solution.py:79
  231.7 4.5 collective-permute-done.14
  237.2 5.2 collective-permute-done.20
  243.8 4.1 collective-permute-done.21
  256.3 8.2 %collective-permute-done.23 = bf16[160,256]{1,0:T(8,128)(2,1)S(1)} collective-permute-done((bf16[160,256]{1,0:T(8,128)(2,1)S(1)}, bf16[160,256]{1,0:T(8,128)(2,1)S(1)}, u32[]{:S(2)}, u32[]{:S(2)}) %collective-permute-start.23) | collective-permute-done | bytes 81952 | tf_op jit(solution)/shard_map/ppermute | solution.py:79
  270.6 5.0 convolution_convert_fusion
  285.8 3.8 collective-permute-done.34.prev_ref
  304.5 6.8 %collective-permute-done.42 = bf16[4,160,256]{2,1,0:T(8,128)(2,1)S(1)} collective-permute-done((bf16[4,160,256]{2,1,0:T(8,128)(2,1)S(1)}, bf16[4,160,256]{2,1,0:T(8,128)(2,1)S(1)}, u32[]{:S(2)}, u32[]{:S(2)}) %collective-permute-start.42) | collective-permute-done | bytes 327712 | tf_op jit(solution)/shard_map/ppermute | solution.py:79
  322.7 3.7 collective-permute-done.39
  328.0 6.4 %collective-permute-done.45 = bf16[512,256]{1,0:T(8,128)(2,1)S(1)} collective-permute-done((bf16[512,256]{1,0:T(8,128)(2,1)S(1)}, bf16[512,256]{1,0:T(8,128)(2,1)S(1)}, u32[]{:S(2)}, u32[]{:S(2)}) %collective-permute-start.45) | collective-permute-done | bytes 262176 | tf_op jit(solution)/shard_map/ppermute | solution.py:66
  335.8 4.2 collective-permute-done.46
  341.4 6.2 %collective-permute-done.47 = bf16[2,352,256]{2,1,0:T(8,128)(2,1)S(1)} collective-permute-done((bf16[2,352,256]{2,1,0:T(8,128)(2,1)S(1)}, bf16[2,352,256]{2,1,0:T(8,128)(2,1)S(1)}, u32[]{:S(2)}, u32[]{:S(2)}) %collective-permute-start.47) | collective-permute-done | bytes 360480 | tf_op jit(solution)/shard_map/ppermute | solution.py:79
  351.1 10.0 %collective-permute-done.49 = bf16[160,256]{1,0:T(8,128)(2,1)S(1)} collective-permute-done((bf16[160,256]{1,0:T(8,128)(2,1)S(1)}, bf16[160,256]{1,0:T(8,128)(2,1)S(1)}, u32[]{:S(2)}, u32[]{:S(2)}) %collective-permute-start.49) | collective-permute-done | bytes 81952 | tf_op jit(solution)/shard_map/ppermute | solution.py:79
  363.5 3.5 collective-permute-done.50
  367.2 7.0 %collective-permute-done.54.refs_3_ = bf16[4,160,256]{2,1,0:T(8,128)(2,1)S(1)} collective-permute-done((bf16[4,160,256]{2,1,0:T(8,128)(2,1)S(1)}, bf16[4,160,256]{2,1,0:T(8,128)(2,1)S(1)}, u32[]{:S(2)}, u32[]{:S(2)}) %collective-permute-start.54) | collective-permute-done | bytes 327712 | tf_op jit(solution)/shard_map/ppermute | solution.py:79
  374.2 5.2 shard_map.175
  382.0 5.2 shard_map.176
  387.2 17.1 %all_to_all.27.triple_ref = bf16[4,3,256,128]{3,2,1,0:T(8,128)(2,1)S(1)} all-to-all(bf16[4,3,256,128]{3,2,1,0:T(8,128)(2,1)S(1)} %shard_map.176), channel_id=1, replica_groups=mesh['section'=2,'seq'=4,'z'=2,'y'=4,'core'=2] {'seq'}, dimensions={0} | all-to-all | bytes 1572864 | tf_op jit(solution)/shard_map/all_to_all | solution.py:471
  405.7 9.1 %all_to_all.28.mixed_ref = bf16[4,256,128]{2,1,0:T(8,128)(2,1)S(1)} all-to-all(bf16[4,256,128]{2,1,0:T(8,128)(2,1)S(1)} %shard_map.177), channel_id=1, replica_groups=mesh['section'=2,'seq'=4,'z'=2,'y'=4,'core'=2] {'seq'}, dimensions={0} | all-to-all | bytes 524288 | tf_op jit(solution)/shard_map/all_to_all | solution.py:472
  425.2 9.8 %collective-permute-done.58 = bf16[4,352,256]{2,1,0:T(8,128)(2,1)S(1)} collective-permute-done((bf16[4,352,256]{2,1,0:T(8,128)(2,1)S(1)}, bf16[4,352,256]{2,1,0:T(8,128)(2,1)S(1)}, u32[]{:S(2)}, u32[]{:S(2)}) %collective-permute-start.58) | collective-permute-done | bytes 720928 | tf_op jit(solution)/shard_map/ppermute | solution.py:79
  435.9 6.8 %collective-permute-done.59 = bf16[2,352,256]{2,1,0:T(8,128)(2,1)S(1)} collective-permute-done((bf16[2,352,256]{2,1,0:T(8,128)(2,1)S(1)}, bf16[2,352,256]{2,1,0:T(8,128)(2,1)S(1)}, u32[]{:S(2)}, u32[]{:S(2)}) %collective-permute-start.59) | collective-permute-done | bytes 360480 | tf_op jit(solution)/shard_map/ppermute | solution.py:79
  444.4 4.1 collective-permute-done.60
  449.8 4.7 collective-permute-done.66
  456.1 3.9 collective-permute-done.67
  467.2 10.8 %collective-permute-done.68 = bf16[160,256]{1,0:T(8,128)(2,1)S(1)} collective-permute-done((bf16[160,256]{1,0:T(8,128)(2,1)S(1)}, bf16[160,256]{1,0:T(8,128)(2,1)S(1)}, u32[]{:S(2)}, u32[]{:S(2)}) %collective-permute-start.68) | collective-permute-done | bytes 81952 | tf_op jit(solution)/shard_map/ppermute | solution.py:79
  485.1 4.0 collective-permute-done.70
  489.4 7.0 %collective-permute-done.74.refs_3_ = bf16[4,160,256]{2,1,0:T(8,128)(2,1)S(1)} collective-permute-done((bf16[4,160,256]{2,1,0:T(8,128)(2,1)S(1)}, bf16[4,160,256]{2,1,0:T(8,128)(2,1)S(1)}, u32[]{:S(2)}, u32[]{:S(2)}) %collective-permute-start.74) | collective-permute-done | bytes 327712 | tf_op jit(solution)/shard_map/ppermute | solution.py:79
  514.3 8.0 %collective-permute-done.84 = bf16[4,160,256]{2,1,0:T(8,128)(2,1)S(1)} collective-permute-done((bf16[4,160,256]{2,1,0:T(8,128)(2,1)S(1)}, bf16[4,160,256]{2,1,0:T(8,128)(2,1)S(1)}, u32[]{:S(2)}, u32[]{:S(2)}) %collective-permute-start.84) | collective-permute-done | bytes 327712 | tf_op jit(solution)/shard_map/ppermute | solution.py:79
  527.9 4.0 collective-permute-done.79
  539.3 5.0 collective-permute-done.81
  (329 shorter events, 169.2 us)
Async XLA Ops:
  6.5 100.4 %all-gather.3.cloned.1.call-start = ((), (), s32[]{:S(2)}) async-start(), calls=%async_computation.5 | async-start | bytes 14483456 | tf_op jit(solution)/shard_map/all_gather | solution.py:379
  20.9 7.7 %collective-permute-start.30 = (bf16[8,64,1024]{2,1,0:T(8,128)(2,1)}, bf16[8,64,1024]{2,1,0:T(8,128)(2,1)S(1)}, u32[]{:S(2)}, u32[]{:S(2)}) collective-permute-start(bf16[8,64,1024]{2,1,0:T(8,128)(2,1)} %broadcast_select_fusion), channel_id=1, source_target_pairs={{0,1},{1,0},{2,3},{3,2},{4,5},{5,4},{6,7},{7,6},{8,9},{9,8},{10,11... | collective-permute-start | bytes 3145736 | tf_op jit(solution)/shard_map/ppermute | solution.py:62
  29.7 29.9 %all-to-all-start.2 = ((bf16[8,64,1024]{2,1,0:T(8,128)(2,1)}), bf16[8,64,1024]{2,1,0:T(8,128)(2,1)S(1)}, u32[]{:S(2)}, u32[]{:S(2)}) async-start(bf16[8,64,1024]{2,1,0:T(8,128)(2,1)} %select_add_fusion), calls=%async_computation.2 | async-start | bytes 2097152 | tf_op jit(solution)/shard_map/all_to_all | solution.py:70
  35.8 234.8 %all-gather.5.cloned.1.call-start = ((), (), s32[]{:S(2)}) async-start(), calls=%async_computation.6 | async-start | bytes 4456448 | tf_op jit(solution)/shard_map/all_gather | solution.py:509
  35.9 78.7 %collective-permute-start = (bf16[352,256]{1,0:T(8,128)(2,1)S(1)}, bf16[352,256]{1,0:T(8,128)(2,1)S(1)}, u32[]{:S(2)}, u32[]{:S(2)}) collective-permute-start(bf16[352,256]{1,0:T(8,128)(2,1)S(1)} %get-tuple-element.93), channel_id=1, source_target_pairs={{0,8},{1,3},{2,10},{3,1},{4,12},{5,7},{6,14},{7,5},{8,0},{9,11},{1... | collective-permute-start | bytes 540680 | tf_op jit(solution)/shard_map/ppermute | solution.py:79
  59.8 10.4 %collective-permute-start.31 = (bf16[64,1024]{1,0:T(8,128)(2,1)S(1)}, bf16[64,1024]{1,0:T(8,128)(2,1)S(1)}, u32[]{:S(2)}, u32[]{:S(2)}) collective-permute-start(bf16[64,1024]{1,0:T(8,128)(2,1)S(1)} %reduce_sum.12), channel_id=1, source_target_pairs={{0,64},{64,0},{1,65},{65,1},{2,66},{66,2},{3,67},{67,3},{4,68},{68... | collective-permute-start | bytes 393224 | tf_op jit(solution)/shard_map/ppermute | solution.py:66
  111.6 10.1 %collective-permute-start.32 = (bf16[128,1024]{1,0:T(8,128)(2,1)S(1)}, bf16[128,1024]{1,0:T(8,128)(2,1)S(1)}, u32[]{:S(2)}, u32[]{:S(2)}) collective-permute-start(bf16[128,1024]{1,0:T(8,128)(2,1)S(1)} %shard_map.170), channel_id=1, source_target_pairs={{0,64},{64,0},{1,65},{65,1},{2,66},{66,2},{3,67},{67,3},{4,68},{68... | collective-permute-start | bytes 786440 | tf_op jit(solution)/shard_map/ppermute | solution.py:66
  114.6 17.5 %collective-permute-start.1 = (bf16[2,352,256]{2,1,0:T(8,128)(2,1)S(1)}, bf16[2,352,256]{2,1,0:T(8,128)(2,1)S(1)}, u32[]{:S(2)}, u32[]{:S(2)}) collective-permute-start(bf16[2,352,256]{2,1,0:T(8,128)(2,1)S(1)} %pad_maximum_fusion.5), channel_id=1, source_target_pairs={{0,2},{1,7},{2,0},{3,5},{4,6},{5,3},{6,4},{7,1},{8,10},{9,15},{10,... | collective-permute-start | bytes 1081352 | tf_op jit(solution)/shard_map/ppermute | solution.py:79
  126.5 10.8 %collective-permute-start.33 = (bf16[128,1024]{1,0:T(8,128)(2,1)S(1)}, bf16[128,1024]{1,0:T(8,128)(2,1)S(1)}, u32[]{:S(2)}, u32[]{:S(2)}) collective-permute-start(bf16[128,1024]{1,0:T(8,128)(2,1)S(1)} %shard_map.171), channel_id=1, source_target_pairs={{0,64},{64,0},{1,65},{65,1},{2,66},{66,2},{3,67},{67,3},{4,68},{68... | collective-permute-start | bytes 786440 | tf_op jit(solution)/shard_map/ppermute | solution.py:66
  129.4 8.8 %collective-permute-start.3 = (bf16[160,256]{1,0:T(8,128)(2,1)S(1)}, bf16[160,256]{1,0:T(8,128)(2,1)S(1)}, u32[]{:S(2)}, u32[]{:S(2)}) collective-permute-start(bf16[160,256]{1,0:T(8,128)(2,1)S(1)} %get-tuple-element.91), channel_id=1, source_target_pairs={{0,6},{1,7},{2,4},{3,5},{4,2},{5,3},{6,0},{7,1},{8,14},{9,15},{10,... | collective-permute-start | bytes 245768 | tf_op jit(solution)/shard_map/ppermute | solution.py:79
  132.2 12.6 %collective-permute-start.6 = (bf16[4,352,256]{2,1,0:T(8,128)(2,1)S(1)}, bf16[4,352,256]{2,1,0:T(8,128)(2,1)S(1)}, u32[]{:S(2)}, u32[]{:S(2)}) collective-permute-start(bf16[4,352,256]{2,1,0:T(8,128)(2,1)S(1)} %pad_maximum_fusion.1.refs_0_), channel_id=1, source_target_pairs={{0,6},{1,9},{2,4},{3,11},{4,2},{5,13},{6,0},{7,15},{8,14},{9,1},{1... | collective-permute-start | bytes 2162696 | tf_op jit(solution)/shard_map/ppermute | solution.py:79
  139.8 29.7 %collective-permute-start.2 = (bf16[4,352,256]{2,1,0:T(8,128)(2,1)S(1)}, bf16[4,352,256]{2,1,0:T(8,128)(2,1)S(1)}, u32[]{:S(2)}, u32[]{:S(2)}) collective-permute-start(bf16[4,352,256]{2,1,0:T(8,128)(2,1)S(1)} %pad_maximum_fusion.1.refs_0_), channel_id=1, source_target_pairs={{0,1},{1,0},{2,3},{3,2},{4,5},{5,4},{6,7},{7,6},{8,9},{9,8},{10,11... | collective-permute-start | bytes 2162696 | tf_op jit(solution)/shard_map/ppermute | solution.py:62
  144.8 24.7 %collective-permute-start.7 = (bf16[4,352,256]{2,1,0:T(8,128)(2,1)S(1)}, bf16[4,352,256]{2,1,0:T(8,128)(2,1)S(1)}, u32[]{:S(2)}, u32[]{:S(2)}) collective-permute-start(bf16[4,352,256]{2,1,0:T(8,128)(2,1)S(1)} %collective-permute-done.6.refs_2_), channel_id=1, source_target_pairs={{0,1},{1,0},{2,3},{3,2},{4,5},{5,4},{6,7},{7,6},{8,9},{9,8},{10,11... | collective-permute-start | bytes 2162696 | tf_op jit(solution)/shard_map/ppermute | solution.py:62
  146.6 17.4 %collective-permute-start.8 = (bf16[4,160,256]{2,1,0:T(8,128)(2,1)S(1)}, bf16[4,160,256]{2,1,0:T(8,128)(2,1)}, u32[]{:S(2)}, u32[]{:S(2)}) collective-permute-start(bf16[4,160,256]{2,1,0:T(8,128)(2,1)S(1)} %pad_maximum_fusion.9.refs_1_), channel_id=1, source_target_pairs={{0,2},{1,3},{2,0},{3,1},{4,6},{5,7},{6,4},{7,5},{8,10},{9,11},{10,... | collective-permute-start | bytes 983048 | tf_op jit(solution)/shard_map/ppermute | solution.py:79
  147.3 22.2 %collective-permute-start.5 = (bf16[4,160,256]{2,1,0:T(8,128)(2,1)S(1)}, bf16[4,160,256]{2,1,0:T(8,128)(2,1)S(1)}, u32[]{:S(2)}, u32[]{:S(2)}) collective-permute-start(bf16[4,160,256]{2,1,0:T(8,128)(2,1)S(1)} %pad_maximum_fusion.9.refs_1_), channel_id=1, source_target_pairs={{0,1},{1,0},{2,3},{3,2},{4,5},{5,4},{6,7},{7,6},{8,9},{9,8},{10,11... | collective-permute-start | bytes 983048 | tf_op jit(solution)/shard_map/ppermute | solution.py:62
  210.1 12.6 %collective-permute-start.12 = (bf16[4,352,256]{2,1,0:T(8,128)(2,1)S(1)}, bf16[4,352,256]{2,1,0:T(8,128)(2,1)S(1)}, u32[]{:S(2)}, u32[]{:S(2)}) collective-permute-start(bf16[4,352,256]{2,1,0:T(8,128)(2,1)S(1)} %add_convert_fusion.3), channel_id=1, source_target_pairs={{0,6},{1,9},{2,4},{3,11},{4,2},{5,13},{6,0},{7,15},{8,14},{9,1},{1... | collective-permute-start | bytes 2162696 | tf_op jit(solution)/shard_map/ppermute | solution.py:79
  222.9 7.7 %collective-permute-start.13 = (bf16[2,352,256]{2,1,0:T(8,128)(2,1)S(1)}, bf16[2,352,256]{2,1,0:T(8,128)(2,1)S(1)}, u32[]{:S(2)}, u32[]{:S(2)}) collective-permute-start(bf16[2,352,256]{2,1,0:T(8,128)(2,1)S(1)} %slice.352), channel_id=1, source_target_pairs={{0,2},{1,7},{2,0},{3,5},{4,6},{5,3},{6,4},{7,1},{8,10},{9,15},{10,... | collective-permute-start | bytes 1081352 | tf_op jit(solution)/shard_map/ppermute | solution.py:79
  223.2 8.4 %collective-permute-start.19 = (bf16[4,160,256]{2,1,0:T(8,128)(2,1)S(1)}, bf16[4,160,256]{2,1,0:T(8,128)(2,1)S(1)}, u32[]{:S(2)}, u32[]{:S(2)}) collective-permute-start(bf16[4,160,256]{2,1,0:T(8,128)(2,1)S(1)} %get-tuple-element.55), channel_id=1, source_target_pairs={{0,1},{1,0},{2,3},{3,2},{4,5},{5,4},{6,7},{7,6},{8,9},{9,8},{10,11... | collective-permute-start | bytes 983048 | tf_op jit(solution)/shard_map/ppermute | solution.py:62
  223.4 13.8 %collective-permute-start.18 = (bf16[4,160,256]{2,1,0:T(8,128)(2,1)S(1)}, bf16[4,160,256]{2,1,0:T(8,128)(2,1)S(1)}, u32[]{:S(2)}, u32[]{:S(2)}) collective-permute-start(bf16[4,160,256]{2,1,0:T(8,128)(2,1)S(1)} %get-tuple-element.53), channel_id=1, source_target_pairs={{0,1},{1,0},{2,3},{3,2},{4,5},{5,4},{6,7},{7,6},{8,9},{9,8},{10,11... | collective-permute-start | bytes 983048 | tf_op jit(solution)/shard_map/ppermute | solution.py:62
  231.6 10.7 %collective-permute-start.20 = (bf16[4,160,256]{2,1,0:T(8,128)(2,1)S(1)}, bf16[4,160,256]{2,1,0:T(8,128)(2,1)S(1)}, u32[]{:S(2)}, u32[]{:S(2)}) collective-permute-start(bf16[4,160,256]{2,1,0:T(8,128)(2,1)S(1)} %add_convert_fusion.7), channel_id=1, source_target_pairs={{0,2},{1,3},{2,0},{3,1},{4,6},{5,7},{6,4},{7,5},{8,10},{9,11},{10,... | collective-permute-start | bytes 983048 | tf_op jit(solution)/shard_map/ppermute | solution.py:79
  251.0 19.1 %collective-permute-start.26 = (bf16[4,352,256]{2,1,0:T(8,128)(2,1)S(1)}, bf16[4,352,256]{2,1,0:T(8,128)(2,1)}, u32[]{:S(2)}, u32[]{:S(2)}) collective-permute-start(bf16[4,352,256]{2,1,0:T(8,128)(2,1)S(1)} %pad_maximum_fusion.2.refs_0_), channel_id=1, source_target_pairs={{0,6},{1,9},{2,4},{3,11},{4,2},{5,13},{6,0},{7,15},{8,14},{9,1},{1... | collective-permute-start | bytes 2162696 | tf_op jit(solution)/shard_map/ppermute | solution.py:79
  253.8 10.6 %collective-permute-start.23 = (bf16[160,256]{1,0:T(8,128)(2,1)S(1)}, bf16[160,256]{1,0:T(8,128)(2,1)S(1)}, u32[]{:S(2)}, u32[]{:S(2)}) collective-permute-start(bf16[160,256]{1,0:T(8,128)(2,1)S(1)} %fusion.27), channel_id=1, source_target_pairs={{0,6},{1,7},{2,4},{3,5},{4,2},{5,3},{6,0},{7,1},{8,14},{9,15},{10,... | collective-permute-start | bytes 245768 | tf_op jit(solution)/shard_map/ppermute | solution.py:79
  269.9 8.3 %collective-permute-start.28 = (bf16[4,160,256]{2,1,0:T(8,128)(2,1)S(1)}, bf16[4,160,256]{2,1,0:T(8,128)(2,1)}, u32[]{:S(2)}, u32[]{:S(2)}) collective-permute-start(bf16[4,160,256]{2,1,0:T(8,128)(2,1)S(1)} %pad_maximum_fusion.10.refs_1_), channel_id=1, source_target_pairs={{0,2},{1,3},{2,0},{3,1},{4,6},{5,7},{6,4},{7,5},{8,10},{9,11},{10,... | collective-permute-start | bytes 983048 | tf_op jit(solution)/shard_map/ppermute | solution.py:79
  270.0 12.4 %collective-permute-start.17 = (bf16[4,352,256]{2,1,0:T(8,128)(2,1)S(1)}, bf16[4,352,256]{2,1,0:T(8,128)(2,1)}, u32[]{:S(2)}, u32[]{:S(2)}) collective-permute-start(bf16[4,352,256]{2,1,0:T(8,128)(2,1)S(1)} %pad_maximum_fusion.2.refs_0_), channel_id=1, source_target_pairs={{0,1},{1,0},{2,3},{3,2},{4,5},{5,4},{6,7},{7,6},{8,9},{9,8},{10,11... | collective-permute-start | bytes 2162696 | tf_op jit(solution)/shard_map/ppermute | solution.py:62
  270.1 12.3 %collective-permute-start.27 = (bf16[4,352,256]{2,1,0:T(8,128)(2,1)}, bf16[4,352,256]{2,1,0:T(8,128)(2,1)}, u32[]{:S(2)}, u32[]{:S(2)}) collective-permute-start(bf16[4,352,256]{2,1,0:T(8,128)(2,1)} %collective-permute-done.26.refs_2_), channel_id=1, source_target_pairs={{0,1},{1,0},{2,3},{3,2},{4,5},{5,4},{6,7},{7,6},{8,9},{9,8},{10,11... | collective-permute-start | bytes 2162696 | tf_op jit(solution)/shard_map/ppermute | solution.py:62
  275.6 13.9 %collective-permute-start.34 = (bf16[2,256,512]{2,1,0:T(8,128)(2,1)S(1)}, bf16[2,256,512]{2,1,0:T(8,128)(2,1)S(1)}, u32[]{:S(2)}, u32[]{:S(2)}) collective-permute-start(bf16[2,256,512]{2,1,0:T(8,128)(2,1)S(1)} %slice_bitcast_fusion), channel_id=1, source_target_pairs={{0,16},{16,32},{32,48},{1,17},{17,33},{33,49},{2,18},{18,34},{34,5... | collective-permute-start | bytes 1572872 | tf_op jit(solution)/shard_map/ppermute | solution.py:514
  295.8 16.6 %collective-permute-start.35 = (bf16[4,352,256]{2,1,0:T(8,128)(2,1)S(1)}, bf16[4,352,256]{2,1,0:T(8,128)(2,1)S(1)}, u32[]{:S(2)}, u32[]{:S(2)}) collective-permute-start(bf16[4,352,256]{2,1,0:T(8,128)(2,1)S(1)} %get-tuple-element.59), channel_id=1, source_target_pairs={{0,1},{1,0},{2,3},{3,2},{4,5},{5,4},{6,7},{7,6},{8,9},{9,8},{10,11... | collective-permute-start | bytes 2162696 | tf_op jit(solution)/shard_map/ppermute | solution.py:62
  296.3 8.2 %collective-permute-start.40 = (bf16[4,160,256]{2,1,0:T(8,128)(2,1)S(1)}, bf16[4,160,256]{2,1,0:T(8,128)(2,1)S(1)}, u32[]{:S(2)}, u32[]{:S(2)}) collective-permute-start(bf16[4,160,256]{2,1,0:T(8,128)(2,1)S(1)} %get-tuple-element.63), channel_id=1, source_target_pairs={{0,1},{1,0},{2,3},{3,2},{4,5},{5,4},{6,7},{7,6},{8,9},{9,8},{10,11... | collective-permute-start | bytes 983048 | tf_op jit(solution)/shard_map/ppermute | solution.py:62
  300.3 12.6 %collective-permute-start.37 = (bf16[4,352,256]{2,1,0:T(8,128)(2,1)S(1)}, bf16[4,352,256]{2,1,0:T(8,128)(2,1)S(1)}, u32[]{:S(2)}, u32[]{:S(2)}) collective-permute-start(bf16[4,352,256]{2,1,0:T(8,128)(2,1)S(1)} %add_convert_fusion.2), channel_id=1, source_target_pairs={{0,6},{1,9},{2,4},{3,11},{4,2},{5,13},{6,0},{7,15},{8,14},{9,1},{1... | collective-permute-start | bytes 2162696 | tf_op jit(solution)/shard_map/ppermute | solution.py:79
  303.2 8.2 %collective-permute-start.42 = (bf16[4,160,256]{2,1,0:T(8,128)(2,1)S(1)}, bf16[4,160,256]{2,1,0:T(8,128)(2,1)S(1)}, u32[]{:S(2)}, u32[]{:S(2)}) collective-permute-start(bf16[4,160,256]{2,1,0:T(8,128)(2,1)S(1)} %add_convert_fusion.6), channel_id=1, source_target_pairs={{0,2},{1,3},{2,0},{3,1},{4,6},{5,7},{6,4},{7,5},{8,10},{9,11},{10,... | collective-permute-start | bytes 983048 | tf_op jit(solution)/shard_map/ppermute | solution.py:79
  326.5 8.0 %collective-permute-start.45 = (bf16[512,256]{1,0:T(8,128)(2,1)S(1)}, bf16[512,256]{1,0:T(8,128)(2,1)S(1)}, u32[]{:S(2)}, u32[]{:S(2)}) collective-permute-start(bf16[512,256]{1,0:T(8,128)(2,1)S(1)} %pad_maximum_fusion.13), channel_id=1, source_target_pairs={{0,64},{64,0},{1,65},{65,1},{2,66},{66,2},{3,67},{67,3},{4,68},{68... | collective-permute-start | bytes 786440 | tf_op jit(solution)/shard_map/ppermute | solution.py:66
  347.7 15.3 %collective-permute-start.52 = (bf16[4,352,256]{2,1,0:T(8,128)(2,1)S(1)}, bf16[4,352,256]{2,1,0:T(8,128)(2,1)S(1)}, u32[]{:S(2)}, u32[]{:S(2)}) collective-permute-start(bf16[4,352,256]{2,1,0:T(8,128)(2,1)S(1)} %pad_maximum_fusion.3.refs_0_), channel_id=1, source_target_pairs={{0,6},{1,9},{2,4},{3,11},{4,2},{5,13},{6,0},{7,15},{8,14},{9,1},{1... | collective-permute-start | bytes 2162696 | tf_op jit(solution)/shard_map/ppermute | solution.py:79
  350.5 10.7 %collective-permute-start.49 = (bf16[160,256]{1,0:T(8,128)(2,1)S(1)}, bf16[160,256]{1,0:T(8,128)(2,1)S(1)}, u32[]{:S(2)}, u32[]{:S(2)}) collective-permute-start(bf16[160,256]{1,0:T(8,128)(2,1)S(1)} %get-tuple-element.87), channel_id=1, source_target_pairs={{0,6},{1,7},{2,4},{3,5},{4,2},{5,3},{6,0},{7,1},{8,14},{9,15},{10,... | collective-permute-start | bytes 245768 | tf_op jit(solution)/shard_map/ppermute | solution.py:79
  362.9 17.6 %collective-permute-start.48 = (bf16[4,352,256]{2,1,0:T(8,128)(2,1)S(1)}, bf16[4,352,256]{2,1,0:T(8,128)(2,1)S(1)}, u32[]{:S(2)}, u32[]{:S(2)}) collective-permute-start(bf16[4,352,256]{2,1,0:T(8,128)(2,1)S(1)} %pad_maximum_fusion.3.refs_0_), channel_id=1, source_target_pairs={{0,1},{1,0},{2,3},{3,2},{4,5},{5,4},{6,7},{7,6},{8,9},{9,8},{10,11... | collective-permute-start | bytes 2162696 | tf_op jit(solution)/shard_map/ppermute | solution.py:62
  362.9 17.6 %collective-permute-start.53 = (bf16[4,352,256]{2,1,0:T(8,128)(2,1)S(1)}, bf16[4,352,256]{2,1,0:T(8,128)(2,1)S(1)}, u32[]{:S(2)}, u32[]{:S(2)}) collective-permute-start(bf16[4,352,256]{2,1,0:T(8,128)(2,1)S(1)} %collective-permute-done.52.refs_2_), channel_id=1, source_target_pairs={{0,1},{1,0},{2,3},{3,2},{4,5},{5,4},{6,7},{7,6},{8,9},{9,8},{10,11... | collective-permute-start | bytes 2162696 | tf_op jit(solution)/shard_map/ppermute | solution.py:62
  367.2 13.4 %collective-permute-start.51 = (bf16[4,160,256]{2,1,0:T(8,128)(2,1)S(1)}, bf16[4,160,256]{2,1,0:T(8,128)(2,1)S(1)}, u32[]{:S(2)}, u32[]{:S(2)}) collective-permute-start(bf16[4,160,256]{2,1,0:T(8,128)(2,1)S(1)} %pad_maximum_fusion.11.refs_1_), channel_id=1, source_target_pairs={{0,1},{1,0},{2,3},{3,2},{4,5},{5,4},{6,7},{7,6},{8,9},{9,8},{10,11... | collective-permute-start | bytes 983048 | tf_op jit(solution)/shard_map/ppermute | solution.py:62
  422.4 12.6 %collective-permute-start.58 = (bf16[4,352,256]{2,1,0:T(8,128)(2,1)S(1)}, bf16[4,352,256]{2,1,0:T(8,128)(2,1)S(1)}, u32[]{:S(2)}, u32[]{:S(2)}) collective-permute-start(bf16[4,352,256]{2,1,0:T(8,128)(2,1)S(1)} %add_convert_fusion.1), channel_id=1, source_target_pairs={{0,6},{1,9},{2,4},{3,11},{4,2},{5,13},{6,0},{7,15},{8,14},{9,1},{1... | collective-permute-start | bytes 2162696 | tf_op jit(solution)/shard_map/ppermute | solution.py:79
  435.3 8.9 %collective-permute-start.65 = (bf16[4,160,256]{2,1,0:T(8,128)(2,1)S(1)}, bf16[4,160,256]{2,1,0:T(8,128)(2,1)S(1)}, u32[]{:S(2)}, u32[]{:S(2)}) collective-permute-start(bf16[4,160,256]{2,1,0:T(8,128)(2,1)S(1)} %get-tuple-element.75), channel_id=1, source_target_pairs={{0,1},{1,0},{2,3},{3,2},{4,5},{5,4},{6,7},{7,6},{8,9},{9,8},{10,11... | collective-permute-start | bytes 983048 | tf_op jit(solution)/shard_map/ppermute | solution.py:62
  435.8 14.1 %collective-permute-start.64 = (bf16[4,160,256]{2,1,0:T(8,128)(2,1)S(1)}, bf16[4,160,256]{2,1,0:T(8,128)(2,1)S(1)}, u32[]{:S(2)}, u32[]{:S(2)}) collective-permute-start(bf16[4,160,256]{2,1,0:T(8,128)(2,1)S(1)} %get-tuple-element.73), channel_id=1, source_target_pairs={{0,1},{1,0},{2,3},{3,2},{4,5},{5,4},{6,7},{7,6},{8,9},{9,8},{10,11... | collective-permute-start | bytes 983048 | tf_op jit(solution)/shard_map/ppermute | solution.py:62
  444.3 10.2 %collective-permute-start.66 = (bf16[4,160,256]{2,1,0:T(8,128)(2,1)S(1)}, bf16[4,160,256]{2,1,0:T(8,128)(2,1)S(1)}, u32[]{:S(2)}, u32[]{:S(2)}) collective-permute-start(bf16[4,160,256]{2,1,0:T(8,128)(2,1)S(1)} %add_convert_fusion.5), channel_id=1, source_target_pairs={{0,2},{1,3},{2,0},{3,1},{4,6},{5,7},{6,4},{7,5},{8,10},{9,11},{10,... | collective-permute-start | bytes 983048 | tf_op jit(solution)/shard_map/ppermute | solution.py:79
  463.6 21.0 %collective-permute-start.72 = (bf16[4,352,256]{2,1,0:T(8,128)(2,1)S(1)}, bf16[4,352,256]{2,1,0:T(8,128)(2,1)S(1)}, u32[]{:S(2)}, u32[]{:S(2)}) collective-permute-start(bf16[4,352,256]{2,1,0:T(8,128)(2,1)S(1)} %pad_maximum_fusion.4.refs_0_), channel_id=1, source_target_pairs={{0,6},{1,9},{2,4},{3,11},{4,2},{5,13},{6,0},{7,15},{8,14},{9,1},{1... | collective-permute-start | bytes 2162696 | tf_op jit(solution)/shard_map/ppermute | solution.py:79
  466.2 11.8 %collective-permute-start.68 = (bf16[160,256]{1,0:T(8,128)(2,1)S(1)}, bf16[160,256]{1,0:T(8,128)(2,1)S(1)}, u32[]{:S(2)}, u32[]{:S(2)}) collective-permute-start(bf16[160,256]{1,0:T(8,128)(2,1)S(1)} %fusion.32), channel_id=1, source_target_pairs={{0,6},{1,7},{2,4},{3,5},{4,2},{5,3},{6,0},{7,1},{8,14},{9,15},{10,... | collective-permute-start | bytes 245768 | tf_op jit(solution)/shard_map/ppermute | solution.py:79
  484.6 14.0 %collective-permute-start.63 = (bf16[4,352,256]{2,1,0:T(8,128)(2,1)S(1)}, bf16[4,352,256]{2,1,0:T(8,128)(2,1)S(1)}, u32[]{:S(2)}, u32[]{:S(2)}) collective-permute-start(bf16[4,352,256]{2,1,0:T(8,128)(2,1)S(1)} %pad_maximum_fusion.4.refs_0_), channel_id=1, source_target_pairs={{0,1},{1,0},{2,3},{3,2},{4,5},{5,4},{6,7},{7,6},{8,9},{9,8},{10,11... | collective-permute-start | bytes 2162696 | tf_op jit(solution)/shard_map/ppermute | solution.py:62
  484.6 14.0 %collective-permute-start.73 = (bf16[4,352,256]{2,1,0:T(8,128)(2,1)S(1)}, bf16[4,352,256]{2,1,0:T(8,128)(2,1)S(1)}, u32[]{:S(2)}, u32[]{:S(2)}) collective-permute-start(bf16[4,352,256]{2,1,0:T(8,128)(2,1)S(1)} %collective-permute-done.72.refs_2_), channel_id=1, source_target_pairs={{0,1},{1,0},{2,3},{3,2},{4,5},{5,4},{6,7},{7,6},{8,9},{9,8},{10,11... | collective-permute-start | bytes 2162696 | tf_op jit(solution)/shard_map/ppermute | solution.py:62
  489.3 9.3 %collective-permute-start.71 = (bf16[4,160,256]{2,1,0:T(8,128)(2,1)S(1)}, bf16[4,160,256]{2,1,0:T(8,128)(2,1)S(1)}, u32[]{:S(2)}, u32[]{:S(2)}) collective-permute-start(bf16[4,160,256]{2,1,0:T(8,128)(2,1)S(1)} %pad_maximum_fusion.12.refs_1_), channel_id=1, source_target_pairs={{0,1},{1,0},{2,3},{3,2},{4,5},{5,4},{6,7},{7,6},{8,9},{9,8},{10,11... | collective-permute-start | bytes 983048 | tf_op jit(solution)/shard_map/ppermute | solution.py:62
  507.9 15.9 %collective-permute-start.76 = (bf16[4,352,256]{2,1,0:T(8,128)(2,1)S(1)}, bf16[4,352,256]{2,1,0:T(8,128)(2,1)S(1)}, u32[]{:S(2)}, u32[]{:S(2)}) collective-permute-start(bf16[4,352,256]{2,1,0:T(8,128)(2,1)S(1)} %get-tuple-element.79), channel_id=1, source_target_pairs={{0,1},{1,0},{2,3},{3,2},{4,5},{5,4},{6,7},{7,6},{8,9},{9,8},{10,11... | collective-permute-start | bytes 2162696 | tf_op jit(solution)/shard_map/ppermute | solution.py:62
  511.5 12.6 %collective-permute-start.78 = (bf16[4,352,256]{2,1,0:T(8,128)(2,1)S(1)}, bf16[4,352,256]{2,1,0:T(8,128)(2,1)S(1)}, u32[]{:S(2)}, u32[]{:S(2)}) collective-permute-start(bf16[4,352,256]{2,1,0:T(8,128)(2,1)S(1)} %add_convert_fusion), channel_id=1, source_target_pairs={{0,6},{1,9},{2,4},{3,11},{4,2},{5,13},{6,0},{7,15},{8,14},{9,1},{1... | collective-permute-start | bytes 2162696 | tf_op jit(solution)/shard_map/ppermute | solution.py:79
  514.2 8.1 %collective-permute-start.84 = (bf16[4,160,256]{2,1,0:T(8,128)(2,1)S(1)}, bf16[4,160,256]{2,1,0:T(8,128)(2,1)S(1)}, u32[]{:S(2)}, u32[]{:S(2)}) collective-permute-start(bf16[4,160,256]{2,1,0:T(8,128)(2,1)S(1)} %add_convert_fusion.4), channel_id=1, source_target_pairs={{0,2},{1,3},{2,0},{3,1},{4,6},{5,7},{6,4},{7,5},{8,10},{9,11},{10,... | collective-permute-start | bytes 983048 | tf_op jit(solution)/shard_map/ppermute | solution.py:79
  (62 other events, 428.0 us)
Sparse Core Ops, SparseCore 0:
  11.7 95.2 all-gather.2
  138.3 43.7 all-gather.4

commit v4 on v3

--- a/solution.py
+++ b/solution.py
@@ -24,15 +24,14 @@
 GROUP = 4
 MP = ("z", "y", "core")
 KEYS = NEIGH * NB_LEN
-VMEM_LIMIT = 48 * 1024 * 1024
 
 epsilon = 1e-05
 f32 = jnp.float32
 bf16 = jnp.bfloat16
 
 
-def params():
-    return pltpu.CompilerParams(vmem_limit_bytes=VMEM_LIMIT)
+def params(mebibytes=16):
+    return pltpu.CompilerParams(vmem_limit_bytes=mebibytes * 1024 * 1024)
 
 
 def whole(shape):
@@ -89,31 +88,32 @@
     ).astype(jnp.int32)
 
 
+def together(*values):
+    return lax.optimization_barrier(values)
+
+
 def gather_chips(local):
-    near = []
-    for part, value in enumerate(local):
-        near.append(jnp.stack([value, neighbour(value, part, 0)]))
-    near = [
-        jnp.concatenate([value, neighbour(value, part, 1)]) for part, value in enumerate(near)
-    ]
-    far = [neighbour(value, part, 2) for part, value in enumerate(near)]
-    return near + far
+    got = together(*[neighbour(value, part, 0) for part, value in enumerate(local)])
+    near = [jnp.stack([value, other]) for value, other in zip(local, got)]
+    got = together(*[neighbour(value, part, 1) for part, value in enumerate(near)])
+    near = [jnp.concatenate([value, other]) for value, other in zip(near, got)]
+    far = together(*[neighbour(value, part, 2) for part, value in enumerate(near)])
+    return near + list(far)
 
 
 def scatter_sum(own, other):
     wide = [value.astype(f32) for value in own]
-    got = [None] * 4
-    for at in (2, 3, 0, 1):
-        got[at] = core_swap(other[at]).astype(f32)
-    sent = [neighbour((wide[2 + part] + got[2 + part]).astype(bf16), part, 2) for part in range(2)]
-    result = []
-    for part in range(2):
-        low = wide[part] + got[part] + sent[part].astype(f32)
-        second = neighbour(low[2:].astype(bf16), part, 1)
-        low = low[:2] + second.astype(f32)
-        third = neighbour(low[1].astype(bf16), part, 0)
-        result.append(low[0] + third.astype(f32))
-    return result
+    far = together(core_swap(other[2]), core_swap(other[3]))
+    near = [core_swap(other[0]), core_swap(other[1])]
+    sums = [(wide[2 + part] + far[part].astype(f32)).astype(bf16) for part in range(2)]
+    got = together(*[neighbour(sums[part], part, 2) for part in range(2)], *near)
+    low = [
+        wide[part] + got[2 + part].astype(f32) + got[part].astype(f32) for part in range(2)
+    ]
+    got = together(*[neighbour(low[part][2:].astype(bf16), part, 1) for part in range(2)])
+    low = [low[part][:2] + got[part].astype(f32) for part in range(2)]
+    got = together(*[neighbour(low[part][1].astype(bf16), part, 0) for part in range(2)])
+    return [low[part][0] + got[part].astype(f32) for part in range(2)]
 
 
 def project_kernel(last, units, place_ref, *refs):
@@ -352,7 +352,10 @@
         return found.reshape(CHIPS, NB_LEN // 2, ENC_D)
 
     paired = core_swap(rows(1 - core)) + rows(core)
-    half = jnp.sum(chips_to_chips(paired).astype(f32), axis=0).astype(bf16)
+    return jnp.sum(chips_to_chips(paired).astype(f32), axis=0).astype(bf16)
+
+
+def join_halves(half, section):
     far = section_swap(half)
     return jnp.where(
         section == 0, jnp.concatenate([half, far], axis=0), jnp.concatenate([far, half], axis=0)
@@ -456,24 +459,27 @@
         in_specs=[full, gain, pl.BlockSpec((8, ENC_D, width), lambda s: (0, 0, 0))],
         out_specs=full,
         out_shape=out,
-        compiler_params=params(),
+        compiler_params=params(28),
     )(inner, enc_norms[1:], pieces)
     return (inner.astype(f32) + (fed.astype(f32) + section_swap(fed).astype(f32))).astype(bf16)
 
 
-def after(value, other):
-    return lax.optimization_barrier((value, other))[0]
-
-
-def decoder_layer(places_both, states, make_pairs, weights):
+def decoder_layer(places_both, states, looked_up, make_pairs, weights):
     norms, triple_w, out_w, query_w, back_w = weights
     triple = project(places_both, states, norms[0], triple_w, True)
+    looked_up, embedded = looked_up
+    if looked_up is not None:
+        triple, half = together(triple, looked_up)
+        embedded = embedded(half)
     triple = lax.all_to_all(triple, "seq", 0, 0, tiled=True)
     mixed = lax.all_to_all(causal(triple), "seq", 0, 0, tiled=True)
+    if looked_up is not None:
+        mixed, embedded = together(mixed, embedded)
+    prev, pairs = make_pairs(embedded)
     middle = add_product(places_both, states, mixed, out_w)
     asked = project(places_both, middle, norms[1], query_w[None], False)
-    crossed = cross(asked, *make_pairs(mixed))
-    return add_product(places_both, middle, crossed, back_w)
+    crossed = cross(asked, prev, pairs)
+    return add_product(places_both, middle, crossed, back_w), (prev, pairs)
 
 
 def on_device(
@@ -500,26 +506,20 @@
     blocks_here = neighbour_table.shape[1]
     pieces = weight_pieces(section, enc_qkv, enc_out, enc_up, enc_down)
     slot_ids = neighbour_ids[neighbour_table.reshape(-1)]
-    embedded = look_up(slot_ids, enc_embed, core_at, section)
+    half = look_up(slot_ids, enc_embed, core_at, section)
     count = lax.axis_size("seq")
-
-    def make_pairs(mixed):
-        ready = after(embedded, mixed[0, 0, :1])
-        encoded = encode(ready, enc_norms, pieces, jnp.reshape(section, (1,)))
+    pair_w = cross_pair[0].reshape(ENC_D, 2 * WIDTH)
+
+    def pair_rows(rows):
+        return jnp.dot(rows, pair_w, preferred_element_type=f32).astype(bf16)
+
+    def make_pairs(embedded):
+        encoded = encode(embedded, enc_norms, pieces, jnp.reshape(section, (1,)))
         encoded = lax.all_gather(encoded, MP, axis=0, tiled=True)
-        pairs = jnp.dot(
-            encoded, cross_pair[0].reshape(ENC_D, 2 * WIDTH), preferred_element_type=f32
-        ).astype(bf16)
-        pairs = pairs.reshape(BATCH, blocks_here, KEYS, 2 * WIDTH)
-        prev = lax.ppermute(pairs[:, -1], "seq", [(i, i + 1) for i in range(count - 1)])
-        return prev, pairs
-
-    made = []
-
-    def once(mixed):
-        if not made:
-            made.append(make_pairs(mixed))
-        return made[0]
+        edge = encoded.reshape(BATCH, blocks_here, KEYS, ENC_D)[:, -1]
+        edge = pair_rows(edge.reshape(BATCH * KEYS, ENC_D)).reshape(BATCH, KEYS, 2 * WIDTH)
+        prev = lax.ppermute(edge, "seq", [(i, i + 1) for i in range(count - 1)])
+        return prev, pair_rows(encoded).reshape(BATCH, blocks_here, KEYS, 2 * WIDTH)
 
     weights = (
         dec_norms[0],
@@ -530,9 +530,18 @@
     )
 
     states = hidden_states.reshape(BATCH * ROWS, WIDTH)
-    first = decoder_layer(places_both, by_parts(states), once, weights)
+    first, pairs = decoder_layer(
+        places_both,
+        by_parts(states),
+        (half, lambda half: join_halves(half, section)),
+        make_pairs,
+        weights,
+    )
     handed = section_swap(jnp.concatenate(first))
-    second = jnp.concatenate(decoder_layer(places_both, by_parts(handed), once, weights))
+    second, _ = decoder_layer(
+        places_both, by_parts(handed), (None, None), lambda _: pairs, weights
+    )
+    second = jnp.concatenate(second)
     second = second.reshape(BATCH, ROWS, WIDTH)
     return jnp.where(section == 0, section_swap(second[0]), second[1])[None]
 

time: 560 us -> 497 us (0.89)
  waiting for transfers between devices: 276 us -> 224 us
  blocking collectives: 52.5 us -> 25.8 us
  starting transfers between devices: 90.5 us -> 105 us
  local copies, waits for them, and re-layouts: 25.7 us -> 36.6 us
  Pallas kernels: 76.6 us -> 66.1 us
    all_gather x1, waiting for transfers between devices: 36.7 us -> 0.01 us  [weight_pieces(): return lax.all_gather(local, MP, axis=1, tiled=True)]
    all_to_all x1, waiting for transfers between devices: 21.7 us -> 0.01 us  [chips_to_chips(): return lax.all_to_all(value, ('z', 'y'), 0, 0, tiled=True)]
    all_to_all x2 -> x1, blocking collectives: 34.4 us -> 16.8 us  [decoder_layer(): triple = lax.all_to_all(triple, 'seq', 0, 0, tiled=True)]
    all_to_all x0 -> x2, waiting for transfers between devices: none -> 15.6 us  [the longest x1 9.08 us: decoder_layer(): triple = lax.all_to_all(triple, 'seq', 0, 0, tiled=True)]
    ppermute x5, waiting for transfers between devices: 29 us -> 16.9 us  [section_swap(): return lax.ppermute(value, 'section', [(0, 1), (1, 0)])]
    ppermute x33, starting transfers between devices: 7.76 us -> 18.8 us  [core_swap(): return lax.ppermute(value, 'core', [(0, 1), (1, 0)])]
    unnamed x42 -> x58, local copies, waits for them, and re-layouts: 5.62 us -> 15.5 us
    ppermute x48, starting transfers between devices: 61.5 us -> 52.1 us  [neighbour(): return lax.ppermute(value, MP, route)]
  transfers between devices with their start and end apart: 90 -> 92, of which waited for: 45 -> 46; matrix products, arithmetic and copies ran while one was open for 6% -> 6% of each run, Pallas kernels for 9% -> 8%
where the time goes in v4:
time: 497 us; the launch traced here: 488 us
  waiting for transfers between devices  224 us (45%)
  starting transfers between devices  105 us (21%)
  Pallas kernels  66.1 us (13%)
  local copies, waits for them, and re-layouts  36.6 us (7%)
  blocking collectives  25.8 us (5%)
  between operations  15.2 us (3%)
  other arithmetic  12.1 us (2%)
    ppermute x48, waiting for transfers between devices, neighbour(): return lax.ppermute(value, MP, route)  178 us
    ppermute x48, starting transfers between devices, neighbour(): return lax.ppermute(value, MP, route)  52.1 us
    pallas_call x8, Pallas kernels, terms(): pl.pallas_call(terms_kernel, grid_spec=pltpu.PrefetchScalarGridSpec(num_s...  27.1 us
    pallas_call x8, Pallas kernels, project_half(): pl.pallas_call(functools.partial(project_kernel, last, units), grid_spec=...  26.7 us
    ppermute x33, starting transfers between devices, core_swap(): return lax.ppermute(value, 'core', [(0, 1), (1, 0)])  18.8 us
    ppermute x5, waiting for transfers between devices, section_swap(): return lax.ppermute(value, 'section', [(0, 1), (1, 0)])  16.9 us
    all_to_all x1, blocking collectives, decoder_layer(): triple = lax.all_to_all(triple, 'seq', 0, 0, tiled=True)  16.8 us
    ppermute x5, starting transfers between devices, section_swap(): return lax.ppermute(value, 'section', [(0, 1), (1, 0)])  16.6 us
  transfers between devices with their start and end apart: 92, of which 46 were waited for; matrix products, arithmetic and copies ran while one was open for 6% of the time, Pallas kernels for 8%

profile of v4, /device:TPU:0, one launch (start us, length us, event | category | flops | bytes accessed | tf_op | source)
XLA Modules:
  0.0 488.1 jit_solution(13735843207062195299)
XLA Ops:
  17.9 7.1 %gather_fusion.1 = bf16[512,1024]{1,0:T(8,128)(2,1)S(1)} fusion(bf16[4000,1024]{1,0:T(8,128)(2,1)} %param.22, s32[1024]{0:T(1024)S(1)} %pad_clamp_fusion.1), kind=kCustom, calls=%fused_computation.3 | custom fusion | bytes 2099200 | tf_op jit(solution)/shard_map/gather | solution.py:350
  27.1 7.2 %gather_fusion.2 = bf16[512,1024]{1,0:T(8,128)(2,1)S(1)} fusion(bf16[4000,1024]{1,0:T(8,128)(2,1)} %param.22, s32[1024]{0:T(1024)S(1)} %pad_clamp_fusion), kind=kCustom, calls=%fused_computation.4 | custom fusion | bytes 2099200 | tf_op jit(solution)/shard_map/gather | solution.py:350
  36.9 4.5 collective-permute-done.2
  44.7 5.5 %all-to-all-start = ((bf16[8,64,1024]{2,1,0:T(8,128)(2,1)}), bf16[8,64,1024]{2,1,0:T(8,128)(2,1)}, u32[]{:S(2)}, u32[]{:S(2)}) async-start(bf16[8,64,1024]{2,1,0:T(8,128)(2,1)} %select_add_fusion), calls=%async_computation | async-start | bytes 2097152 | tf_op jit(solution)/shard_map/all_to_all | solution.py:69
  50.3 9.3 %collective-permute-done.7.refs_3_ = bf16[4,160,256]{2,1,0:T(8,128)(2,1)} collective-permute-done((bf16[4,160,256]{2,1,0:T(8,128)(2,1)S(1)}, bf16[4,160,256]{2,1,0:T(8,128)(2,1)}, u32[]{:S(2)}, u32[]{:S(2)}) %collective-permute-start.7) | collective-permute-done | bytes 327712 | tf_op jit(solution)/shard_map/ppermute | solution.py:78
  59.6 12.8 %collective-permute-start.8 = (bf16[4,352,256]{2,1,0:T(8,128)(2,1)S(1)}, bf16[4,352,256]{2,1,0:T(8,128)(2,1)}, u32[]{:S(2)}, u32[]{:S(2)}) collective-permute-start(bf16[4,352,256]{2,1,0:T(8,128)(2,1)S(1)} %collective-permute-done.6.refs_2_), channel_id=1, source_target_pairs={{0,1},{1,0},{2,3},{3,2},{4,5},{5,4},{6,7},{7,6},{8,9},{9,8},{10,11... | collective-permute-start | bytes 2162696 | tf_op jit(solution)/shard_map/ppermute | solution.py:61
  78.1 4.6 shard_map.163
  88.8 6.0 %shard_map.164 = bf16[4,3,256,128]{3,2,1,0:T(8,128)(2,1)} custom-call(s32[33]{0:T(128)S(1)} %pad_add_fusion.1.place_ref, bf16[4,352,256]{2,1,0:T(8,128)(2,1)} %collective-permute-done.4.refs_0_, bf16[4,160,256]{2,1,0:T(8,128)(2,1)} %collective-permute-done.5.refs_1_, bf16[4,352,256]{2,1,0:T(8,128)(2,1)} %collective-permute-done.8.refs_2_, ...), custom_call_target="tpu_custom_call" | custom-call | flops 1610612736 | bytes 6815744 | tf_op jit(solution)/shard_map/pallas_call | solution.py:181
  94.8 4.4 all-to-all-start.1
  102.4 9.1 %all-to-all-done.1.triple_ref = bf16[4,3,256,128]{3,2,1,0:T(8,128)(2,1)S(1)} async-done(((bf16[4,3,256,128]{3,2,1,0:T(8,128)(2,1)}), bf16[4,3,256,128]{3,2,1,0:T(8,128)(2,1)S(1)}, u32[]{:S(2)}, u32[]{:S(2)}) %all-to-all-start.1) | async-done | bytes 786464 | tf_op jit(solution)/shard_map/all_to_all | solution.py:474
  117.1 6.5 %all-to-all-done.2.mixed_ref = bf16[4,256,128]{2,1,0:T(8,128)(2,1)S(1)} async-done(((bf16[4,256,128]{2,1,0:T(8,128)(2,1)}), bf16[4,256,128]{2,1,0:T(8,128)(2,1)S(1)}, u32[]{:S(2)}, u32[]{:S(2)}) %all-to-all-start.2) | async-done | bytes 262176 | tf_op jit(solution)/shard_map/all_to_all | solution.py:475
  123.6 4.9 copy-done.4
  130.6 3.6 collective-permute-start.32
  134.2 4.4 collective-permute-done.32
  140.0 3.6 collective-permute-start.33
  143.6 4.4 collective-permute-done.33
  157.2 5.9 %collective-permute-start.15 = (bf16[4,160,256]{2,1,0:T(8,128)(2,1)S(1)}, bf16[4,160,256]{2,1,0:T(8,128)(2,1)S(1)}, u32[]{:S(2)}, u32[]{:S(2)}) collective-permute-start(bf16[4,160,256]{2,1,0:T(8,128)(2,1)S(1)} %add_convert_fusion.7), channel_id=1, source_target_pairs={{0,2},{1,3},{2,0},{3,1},{4,6},{5,7},{6,4},{7,5},{8,10},{9,11},{10,... | collective-permute-start | bytes 983048 | tf_op jit(solution)/shard_map/ppermute | solution.py:78
  163.1 15.3 %collective-permute-done.15 = bf16[4,160,256]{2,1,0:T(8,128)(2,1)S(1)} collective-permute-done((bf16[4,160,256]{2,1,0:T(8,128)(2,1)S(1)}, bf16[4,160,256]{2,1,0:T(8,128)(2,1)S(1)}, u32[]{:S(2)}, u32[]{:S(2)}) %collective-permute-start.15) | collective-permute-done | bytes 327712 | tf_op jit(solution)/shard_map/ppermute | solution.py:78
  178.7 4.7 collective-permute-start.18
  183.9 8.5 %collective-permute-done.19 = bf16[2,160,256]{2,1,0:T(8,128)(2,1)S(1)} collective-permute-done((bf16[2,160,256]{2,1,0:T(8,128)(2,1)S(1)}, bf16[2,160,256]{2,1,0:T(8,128)(2,1)S(1)}, u32[]{:S(2)}, u32[]{:S(2)}) %collective-permute-start.19) | collective-permute-done | bytes 163872 | tf_op jit(solution)/shard_map/ppermute | solution.py:78
  197.8 4.8 collective-permute-done.21
  204.8 6.0 %collective-permute-done.23 = bf16[160,256]{1,0:T(8,128)(2,1)S(1)} collective-permute-done((bf16[160,256]{1,0:T(8,128)(2,1)S(1)}, bf16[160,256]{1,0:T(8,128)(2,1)S(1)}, u32[]{:S(2)}, u32[]{:S(2)}) %collective-permute-start.23) | collective-permute-done | bytes 81952 | tf_op jit(solution)/shard_map/ppermute | solution.py:78
  211.7 6.4 %collective-permute-done.25 = bf16[2,160,256]{2,1,0:T(8,128)(2,1)S(1)} collective-permute-done((bf16[2,160,256]{2,1,0:T(8,128)(2,1)S(1)}, bf16[2,160,256]{2,1,0:T(8,128)(2,1)S(1)}, u32[]{:S(2)}, u32[]{:S(2)}) %collective-permute-start.25) | collective-permute-done | bytes 163872 | tf_op jit(solution)/shard_map/ppermute | solution.py:78
  218.1 3.6 collective-permute-done.24
  222.1 7.0 %collective-permute-done.29.refs_3_ = bf16[4,160,256]{2,1,0:T(8,128)(2,1)S(1)} collective-permute-done((bf16[4,160,256]{2,1,0:T(8,128)(2,1)S(1)}, bf16[4,160,256]{2,1,0:T(8,128)(2,1)S(1)}, u32[]{:S(2)}, u32[]{:S(2)}) %collective-permute-start.29) | collective-permute-done | bytes 327712 | tf_op jit(solution)/shard_map/ppermute | solution.py:78
  229.1 5.3 %collective-permute-done.28.refs_2_ = bf16[4,352,256]{2,1,0:T(8,128)(2,1)S(1)} collective-permute-done((bf16[4,352,256]{2,1,0:T(8,128)(2,1)S(1)}, bf16[4,352,256]{2,1,0:T(8,128)(2,1)S(1)}, u32[]{:S(2)}, u32[]{:S(2)}) %collective-permute-start.28) | collective-permute-done | bytes 720928 | tf_op jit(solution)/shard_map/ppermute | solution.py:78
  242.7 4.1 collective-permute-start.34
  249.2 9.2 %collective-permute-done.34.prev_ref = bf16[2,256,512]{2,1,0:T(8,128)(2,1)S(1)} collective-permute-done((bf16[2,256,512]{2,1,0:T(8,128)(2,1)S(1)}, bf16[2,256,512]{2,1,0:T(8,128)(2,1)S(1)}, u32[]{:S(2)}, u32[]{:S(2)}) %collective-permute-start.34) | collective-permute-done | bytes 524320 | tf_op jit(solution)/shard_map/ppermute | solution.py:521
  271.6 8.7 %collective-permute-done.38 = bf16[4,160,256]{2,1,0:T(8,128)(2,1)S(1)} collective-permute-done((bf16[4,160,256]{2,1,0:T(8,128)(2,1)S(1)}, bf16[4,160,256]{2,1,0:T(8,128)(2,1)S(1)}, u32[]{:S(2)}, u32[]{:S(2)}) %collective-permute-start.38) | collective-permute-done | bytes 327712 | tf_op jit(solution)/shard_map/ppermute | solution.py:78
  282.1 6.6 %collective-permute-done.42 = bf16[2,160,256]{2,1,0:T(8,128)(2,1)S(1)} collective-permute-done((bf16[2,160,256]{2,1,0:T(8,128)(2,1)S(1)}, bf16[2,160,256]{2,1,0:T(8,128)(2,1)S(1)}, u32[]{:S(2)}, u32[]{:S(2)}) %collective-permute-start.42) | collective-permute-done | bytes 163872 | tf_op jit(solution)/shard_map/ppermute | solution.py:78
  290.7 4.6 collective-permute-done.44
  298.7 4.7 collective-permute-done.45
  306.6 4.6 collective-permute-done.47
  312.4 4.4 collective-permute-done.49
  320.5 6.6 %collective-permute-done.53.refs_3_ = bf16[4,160,256]{2,1,0:T(8,128)(2,1)S(1)} collective-permute-done((bf16[4,160,256]{2,1,0:T(8,128)(2,1)S(1)}, bf16[4,160,256]{2,1,0:T(8,128)(2,1)S(1)}, u32[]{:S(2)}, u32[]{:S(2)}) %collective-permute-start.53) | collective-permute-done | bytes 327712 | tf_op jit(solution)/shard_map/ppermute | solution.py:78
  327.2 5.0 %collective-permute-done.52.refs_2_ = bf16[4,352,256]{2,1,0:T(8,128)(2,1)S(1)} collective-permute-done((bf16[4,352,256]{2,1,0:T(8,128)(2,1)S(1)}, bf16[4,352,256]{2,1,0:T(8,128)(2,1)S(1)}, u32[]{:S(2)}, u32[]{:S(2)}) %collective-permute-start.52) | collective-permute-done | bytes 720928 | tf_op jit(solution)/shard_map/ppermute | solution.py:78
  333.0 3.7 shard_map.175
  336.8 3.8 shard_map.176
  340.6 16.8 %all_to_all.25.triple_ref = bf16[4,3,256,128]{3,2,1,0:T(8,128)(2,1)S(1)} all-to-all(bf16[4,3,256,128]{3,2,1,0:T(8,128)(2,1)S(1)} %shard_map.176), channel_id=1, replica_groups=mesh['section'=2,'seq'=4,'z'=2,'y'=4,'core'=2] {'seq'}, dimensions={0} | all-to-all | bytes 1572864 | tf_op jit(solution)/shard_map/all_to_all | solution.py:474
  358.7 9.1 %all_to_all.26.mixed_ref = bf16[4,256,128]{2,1,0:T(8,128)(2,1)S(1)} all-to-all(bf16[4,256,128]{2,1,0:T(8,128)(2,1)S(1)} %shard_map.177), channel_id=1, replica_groups=mesh['section'=2,'seq'=4,'z'=2,'y'=4,'core'=2] {'seq'}, dimensions={0} | all-to-all | bytes 524288 | tf_op jit(solution)/shard_map/all_to_all | solution.py:475
  379.5 8.7 %collective-permute-done.59 = bf16[4,160,256]{2,1,0:T(8,128)(2,1)S(1)} collective-permute-done((bf16[4,160,256]{2,1,0:T(8,128)(2,1)S(1)}, bf16[4,160,256]{2,1,0:T(8,128)(2,1)S(1)}, u32[]{:S(2)}, u32[]{:S(2)}) %collective-permute-start.59) | collective-permute-done | bytes 327712 | tf_op jit(solution)/shard_map/ppermute | solution.py:78
  389.5 5.8 %collective-permute-done.63 = bf16[2,160,256]{2,1,0:T(8,128)(2,1)S(1)} collective-permute-done((bf16[2,160,256]{2,1,0:T(8,128)(2,1)S(1)}, bf16[2,160,256]{2,1,0:T(8,128)(2,1)S(1)}, u32[]{:S(2)}, u32[]{:S(2)}) %collective-permute-start.63) | collective-permute-done | bytes 163872 | tf_op jit(solution)/shard_map/ppermute | solution.py:78
  398.7 3.9 collective-permute-done.65
  411.3 4.1 collective-permute-done.69
  417.6 3.5 collective-permute-start.72
  421.7 6.9 %collective-permute-done.73.refs_3_ = bf16[4,160,256]{2,1,0:T(8,128)(2,1)S(1)} collective-permute-done((bf16[4,160,256]{2,1,0:T(8,128)(2,1)S(1)}, bf16[4,160,256]{2,1,0:T(8,128)(2,1)S(1)}, u32[]{:S(2)}, u32[]{:S(2)}) %collective-permute-start.73) | collective-permute-done | bytes 327712 | tf_op jit(solution)/shard_map/ppermute | solution.py:78
  451.1 8.7 %collective-permute-done.79 = bf16[4,160,256]{2,1,0:T(8,128)(2,1)S(1)} collective-permute-done((bf16[4,160,256]{2,1,0:T(8,128)(2,1)S(1)}, bf16[4,160,256]{2,1,0:T(8,128)(2,1)S(1)}, u32[]{:S(2)}, u32[]{:S(2)}) %collective-permute-start.79) | collective-permute-done | bytes 327712 | tf_op jit(solution)/shard_map/ppermute | solution.py:78
  460.6 6.0 %collective-permute-done.83 = bf16[2,160,256]{2,1,0:T(8,128)(2,1)S(1)} collective-permute-done((bf16[2,160,256]{2,1,0:T(8,128)(2,1)S(1)}, bf16[2,160,256]{2,1,0:T(8,128)(2,1)S(1)}, u32[]{:S(2)}, u32[]{:S(2)}) %collective-permute-start.83) | collective-permute-done | bytes 163872 | tf_op jit(solution)/shard_map/ppermute | solution.py:78
  (349 shorter events, 168.1 us)
Async XLA Ops:
  6.5 117.1 %all-gather.3.cloned.1.call-start = ((), (), s32[]{:S(2)}) async-start(), calls=%async_computation.5 | async-start | bytes 14483456 | tf_op jit(solution)/shard_map/all_gather | solution.py:382
  11.6 14.6 %collective-permute-start = (bf16[352,256]{1,0:T(8,128)(2,1)S(1)}, bf16[352,256]{1,0:T(8,128)(2,1)S(1)}, u32[]{:S(2)}, u32[]{:S(2)}) collective-permute-start(bf16[352,256]{1,0:T(8,128)(2,1)S(1)} %get-tuple-element.229), channel_id=1, source_target_pairs={{0,8},{1,3},{2,10},{3,1},{4,12},{5,7},{6,14},{7,5},{8,0},{9,11},{1... | collective-permute-start | bytes 540680 | tf_op jit(solution)/shard_map/ppermute | solution.py:78
  13.7 12.5 %collective-permute-start.1 = (bf16[160,256]{1,0:T(8,128)(2,1)S(1)}, bf16[160,256]{1,0:T(8,128)(2,1)S(1)}, u32[]{:S(2)}, u32[]{:S(2)}) collective-permute-start(bf16[160,256]{1,0:T(8,128)(2,1)S(1)} %get-tuple-element.227), channel_id=1, source_target_pairs={{0,6},{1,7},{2,4},{3,5},{4,2},{5,3},{6,0},{7,1},{8,14},{9,15},{10,... | collective-permute-start | bytes 245768 | tf_op jit(solution)/shard_map/ppermute | solution.py:78
  26.1 16.2 %collective-permute-start.10 = (bf16[8,64,1024]{2,1,0:T(8,128)(2,1)}, bf16[8,64,1024]{2,1,0:T(8,128)(2,1)}, u32[]{:S(2)}, u32[]{:S(2)}) collective-permute-start(bf16[8,64,1024]{2,1,0:T(8,128)(2,1)} %broadcast_select_fusion), channel_id=1, source_target_pairs={{0,1},{1,0},{2,3},{3,2},{4,5},{5,4},{6,7},{7,6},{8,9},{9,8},{10,11... | collective-permute-start | bytes 3145736 | tf_op jit(solution)/shard_map/ppermute | solution.py:61
  26.2 15.2 %collective-permute-start.2 = (bf16[2,352,256]{2,1,0:T(8,128)(2,1)S(1)}, bf16[2,352,256]{2,1,0:T(8,128)(2,1)S(1)}, u32[]{:S(2)}, u32[]{:S(2)}) collective-permute-start(bf16[2,352,256]{2,1,0:T(8,128)(2,1)S(1)} %pad_maximum_fusion.5), channel_id=1, source_target_pairs={{0,2},{1,7},{2,0},{3,5},{4,6},{5,3},{6,4},{7,1},{8,10},{9,15},{10,... | collective-permute-start | bytes 1081352 | tf_op jit(solution)/shard_map/ppermute | solution.py:78
  26.5 10.4 %collective-permute-start.3 = (bf16[2,160,256]{2,1,0:T(8,128)(2,1)S(1)}, bf16[2,160,256]{2,1,0:T(8,128)(2,1)S(1)}, u32[]{:S(2)}, u32[]{:S(2)}) collective-permute-start(bf16[2,160,256]{2,1,0:T(8,128)(2,1)S(1)} %pad_maximum_fusion.14), channel_id=1, source_target_pairs={{0,8},{1,9},{2,10},{3,11},{4,12},{5,13},{6,14},{7,15},{8,0},{9,1},... | collective-permute-start | bytes 491528 | tf_op jit(solution)/shard_map/ppermute | solution.py:78
  41.5 18.1 %collective-permute-start.6 = (bf16[4,352,256]{2,1,0:T(8,128)(2,1)S(1)}, bf16[4,352,256]{2,1,0:T(8,128)(2,1)S(1)}, u32[]{:S(2)}, u32[]{:S(2)}) collective-permute-start(bf16[4,352,256]{2,1,0:T(8,128)(2,1)S(1)} %pad_maximum_fusion.1.refs_0_), channel_id=1, source_target_pairs={{0,6},{1,9},{2,4},{3,11},{4,2},{5,13},{6,0},{7,15},{8,14},{9,1},{1... | collective-permute-start | bytes 2162696 | tf_op jit(solution)/shard_map/ppermute | solution.py:78
  41.9 17.8 %collective-permute-start.7 = (bf16[4,160,256]{2,1,0:T(8,128)(2,1)S(1)}, bf16[4,160,256]{2,1,0:T(8,128)(2,1)}, u32[]{:S(2)}, u32[]{:S(2)}) collective-permute-start(bf16[4,160,256]{2,1,0:T(8,128)(2,1)S(1)} %pad_maximum_fusion.9.refs_1_), channel_id=1, source_target_pairs={{0,2},{1,3},{2,0},{3,1},{4,6},{5,7},{6,4},{7,5},{8,10},{9,11},{10,... | collective-permute-start | bytes 983048 | tf_op jit(solution)/shard_map/ppermute | solution.py:78
  44.7 38.7 %all-to-all-start = ((bf16[8,64,1024]{2,1,0:T(8,128)(2,1)}), bf16[8,64,1024]{2,1,0:T(8,128)(2,1)}, u32[]{:S(2)}, u32[]{:S(2)}) async-start(bf16[8,64,1024]{2,1,0:T(8,128)(2,1)} %select_add_fusion), calls=%async_computation | async-start | bytes 2097152 | tf_op jit(solution)/shard_map/all_to_all | solution.py:69
  50.2 34.6 %collective-permute-start.4 = (bf16[4,352,256]{2,1,0:T(8,128)(2,1)S(1)}, bf16[4,352,256]{2,1,0:T(8,128)(2,1)}, u32[]{:S(2)}, u32[]{:S(2)}) collective-permute-start(bf16[4,352,256]{2,1,0:T(8,128)(2,1)S(1)} %pad_maximum_fusion.1.refs_0_), channel_id=1, source_target_pairs={{0,1},{1,0},{2,3},{3,2},{4,5},{5,4},{6,7},{7,6},{8,9},{9,8},{10,11... | collective-permute-start | bytes 2162696 | tf_op jit(solution)/shard_map/ppermute | solution.py:61
  59.6 25.3 %collective-permute-start.8 = (bf16[4,352,256]{2,1,0:T(8,128)(2,1)S(1)}, bf16[4,352,256]{2,1,0:T(8,128)(2,1)}, u32[]{:S(2)}, u32[]{:S(2)}) collective-permute-start(bf16[4,352,256]{2,1,0:T(8,128)(2,1)S(1)} %collective-permute-done.6.refs_2_), channel_id=1, source_target_pairs={{0,1},{1,0},{2,3},{3,2},{4,5},{5,4},{6,7},{7,6},{8,9},{9,8},{10,11... | collective-permute-start | bytes 2162696 | tf_op jit(solution)/shard_map/ppermute | solution.py:61
  74.3 10.5 %collective-permute-start.5 = (bf16[4,160,256]{2,1,0:T(8,128)(2,1)S(1)}, bf16[4,160,256]{2,1,0:T(8,128)(2,1)}, u32[]{:S(2)}, u32[]{:S(2)}) collective-permute-start(bf16[4,160,256]{2,1,0:T(8,128)(2,1)S(1)} %pad_maximum_fusion.9.refs_1_), channel_id=1, source_target_pairs={{0,1},{1,0},{2,3},{3,2},{4,5},{5,4},{6,7},{7,6},{8,9},{9,8},{10,11... | collective-permute-start | bytes 983048 | tf_op jit(solution)/shard_map/ppermute | solution.py:61
  74.3 10.6 %collective-permute-start.9 = (bf16[4,160,256]{2,1,0:T(8,128)(2,1)}, bf16[4,160,256]{2,1,0:T(8,128)(2,1)}, u32[]{:S(2)}, u32[]{:S(2)}) collective-permute-start(bf16[4,160,256]{2,1,0:T(8,128)(2,1)} %collective-permute-done.7.refs_3_), channel_id=1, source_target_pairs={{0,1},{1,0},{2,3},{3,2},{4,5},{5,4},{6,7},{7,6},{8,9},{9,8},{10,11... | collective-permute-start | bytes 983048 | tf_op jit(solution)/shard_map/ppermute | solution.py:61
  94.8 16.7 %all-to-all-start.1 = ((bf16[4,3,256,128]{3,2,1,0:T(8,128)(2,1)}), bf16[4,3,256,128]{3,2,1,0:T(8,128)(2,1)S(1)}, u32[]{:S(2)}, u32[]{:S(2)}) async-start(bf16[4,3,256,128]{3,2,1,0:T(8,128)(2,1)} %shard_map.164), calls=%async_computation.1 | async-start | bytes 1572864 | tf_op jit(solution)/shard_map/all_to_all | solution.py:474
  99.2 17.8 %collective-permute-start.11 = (bf16[64,1024]{1,0:T(8,128)(2,1)S(1)}, bf16[64,1024]{1,0:T(8,128)(2,1)S(1)}, u32[]{:S(2)}, u32[]{:S(2)}) collective-permute-start(bf16[64,1024]{1,0:T(8,128)(2,1)S(1)} %reduce_sum.12), channel_id=1, source_target_pairs={{0,64},{64,0},{1,65},{65,1},{2,66},{66,2},{3,67},{67,3},{4,68},{68... | collective-permute-start | bytes 393224 | tf_op jit(solution)/shard_map/ppermute | solution.py:65
  113.5 10.1 %all-to-all-start.2 = ((bf16[4,256,128]{2,1,0:T(8,128)(2,1)}), bf16[4,256,128]{2,1,0:T(8,128)(2,1)S(1)}, u32[]{:S(2)}, u32[]{:S(2)}) async-start(bf16[4,256,128]{2,1,0:T(8,128)(2,1)} %shard_map.165), calls=%async_computation.2 | async-start | bytes 524288 | tf_op jit(solution)/shard_map/all_to_all | solution.py:475
  117.0 123.5 %all-gather.5.cloned.1.call-start = ((), (), s32[]{:S(2)}) async-start(), calls=%async_computation.6 | async-start | bytes 4456448 | tf_op jit(solution)/shard_map/all_gather | solution.py:518
  130.6 8.0 %collective-permute-start.32 = (bf16[128,1024]{1,0:T(8,128)(2,1)S(1)}, bf16[128,1024]{1,0:T(8,128)(2,1)S(1)}, u32[]{:S(2)}, u32[]{:S(2)}) collective-permute-start(bf16[128,1024]{1,0:T(8,128)(2,1)S(1)} %shard_map.170), channel_id=1, source_target_pairs={{0,64},{64,0},{1,65},{65,1},{2,66},{66,2},{3,67},{67,3},{4,68},{68... | collective-permute-start | bytes 786440 | tf_op jit(solution)/shard_map/ppermute | solution.py:65
  140.0 8.0 %collective-permute-start.33 = (bf16[128,1024]{1,0:T(8,128)(2,1)S(1)}, bf16[128,1024]{1,0:T(8,128)(2,1)S(1)}, u32[]{:S(2)}, u32[]{:S(2)}) collective-permute-start(bf16[128,1024]{1,0:T(8,128)(2,1)S(1)} %shard_map.171), channel_id=1, source_target_pairs={{0,64},{64,0},{1,65},{65,1},{2,66},{66,2},{3,67},{67,3},{4,68},{68... | collective-permute-start | bytes 786440 | tf_op jit(solution)/shard_map/ppermute | solution.py:65
  152.8 10.3 %collective-permute-start.16 = (bf16[4,352,256]{2,1,0:T(8,128)(2,1)S(1)}, bf16[4,352,256]{2,1,0:T(8,128)(2,1)S(1)}, u32[]{:S(2)}, u32[]{:S(2)}) collective-permute-start(bf16[4,352,256]{2,1,0:T(8,128)(2,1)S(1)} %get-tuple-element.132), channel_id=1, source_target_pairs={{0,1},{1,0},{2,3},{3,2},{4,5},{5,4},{6,7},{7,6},{8,9},{9,8},{10,11... | collective-permute-start | bytes 2162696 | tf_op jit(solution)/shard_map/ppermute | solution.py:61
  156.5 21.9 %collective-permute-start.14 = (bf16[4,352,256]{2,1,0:T(8,128)(2,1)S(1)}, bf16[4,352,256]{2,1,0:T(8,128)(2,1)S(1)}, u32[]{:S(2)}, u32[]{:S(2)}) collective-permute-start(bf16[4,352,256]{2,1,0:T(8,128)(2,1)S(1)} %add_convert_fusion.3), channel_id=1, source_target_pairs={{0,6},{1,9},{2,4},{3,11},{4,2},{5,13},{6,0},{7,15},{8,14},{9,1},{1... | collective-permute-start | bytes 2162696 | tf_op jit(solution)/shard_map/ppermute | solution.py:78
  157.2 21.2 %collective-permute-start.15 = (bf16[4,160,256]{2,1,0:T(8,128)(2,1)S(1)}, bf16[4,160,256]{2,1,0:T(8,128)(2,1)S(1)}, u32[]{:S(2)}, u32[]{:S(2)}) collective-permute-start(bf16[4,160,256]{2,1,0:T(8,128)(2,1)S(1)} %add_convert_fusion.7), channel_id=1, source_target_pairs={{0,2},{1,3},{2,0},{3,1},{4,6},{5,7},{6,4},{7,5},{8,10},{9,11},{10,... | collective-permute-start | bytes 983048 | tf_op jit(solution)/shard_map/ppermute | solution.py:78
  178.7 16.6 %collective-permute-start.18 = (bf16[2,352,256]{2,1,0:T(8,128)(2,1)S(1)}, bf16[2,352,256]{2,1,0:T(8,128)(2,1)S(1)}, u32[]{:S(2)}, u32[]{:S(2)}) collective-permute-start(bf16[2,352,256]{2,1,0:T(8,128)(2,1)S(1)} %slice.350), channel_id=1, source_target_pairs={{0,2},{1,7},{2,0},{3,5},{4,6},{5,3},{6,4},{7,1},{8,10},{9,15},{10,... | collective-permute-start | bytes 1081352 | tf_op jit(solution)/shard_map/ppermute | solution.py:78
  183.5 8.8 %collective-permute-start.19 = (bf16[2,160,256]{2,1,0:T(8,128)(2,1)S(1)}, bf16[2,160,256]{2,1,0:T(8,128)(2,1)S(1)}, u32[]{:S(2)}, u32[]{:S(2)}) collective-permute-start(bf16[2,160,256]{2,1,0:T(8,128)(2,1)S(1)} %slice.354), channel_id=1, source_target_pairs={{0,8},{1,9},{2,10},{3,11},{4,12},{5,13},{6,14},{7,15},{8,0},{9,1},... | collective-permute-start | bytes 491528 | tf_op jit(solution)/shard_map/ppermute | solution.py:78
  202.7 8.2 %collective-permute-start.22 = (bf16[352,256]{1,0:T(8,128)(2,1)S(1)}, bf16[352,256]{1,0:T(8,128)(2,1)S(1)}, u32[]{:S(2)}, u32[]{:S(2)}) collective-permute-start(bf16[352,256]{1,0:T(8,128)(2,1)S(1)} %fusion.11), channel_id=1, source_target_pairs={{0,8},{1,3},{2,10},{3,1},{4,12},{5,7},{6,14},{7,5},{8,0},{9,11},{1... | collective-permute-start | bytes 540680 | tf_op jit(solution)/shard_map/ppermute | solution.py:78
  210.9 10.8 %collective-permute-start.24 = (bf16[2,352,256]{2,1,0:T(8,128)(2,1)S(1)}, bf16[2,352,256]{2,1,0:T(8,128)(2,1)S(1)}, u32[]{:S(2)}, u32[]{:S(2)}) collective-permute-start(bf16[2,352,256]{2,1,0:T(8,128)(2,1)S(1)} %pad_maximum_fusion.6), channel_id=1, source_target_pairs={{0,2},{1,7},{2,0},{3,5},{4,6},{5,3},{6,4},{7,1},{8,10},{9,15},{10,... | collective-permute-start | bytes 1081352 | tf_op jit(solution)/shard_map/ppermute | solution.py:78
  221.8 12.6 %collective-permute-start.28 = (bf16[4,352,256]{2,1,0:T(8,128)(2,1)S(1)}, bf16[4,352,256]{2,1,0:T(8,128)(2,1)S(1)}, u32[]{:S(2)}, u32[]{:S(2)}) collective-permute-start(bf16[4,352,256]{2,1,0:T(8,128)(2,1)S(1)} %pad_maximum_fusion.2.refs_0_), channel_id=1, source_target_pairs={{0,6},{1,9},{2,4},{3,11},{4,2},{5,13},{6,0},{7,15},{8,14},{9,1},{1... | collective-permute-start | bytes 2162696 | tf_op jit(solution)/shard_map/ppermute | solution.py:78
  222.0 16.3 %collective-permute-start.26 = (bf16[4,352,256]{2,1,0:T(8,128)(2,1)S(1)}, bf16[4,352,256]{2,1,0:T(8,128)(2,1)S(1)}, u32[]{:S(2)}, u32[]{:S(2)}) collective-permute-start(bf16[4,352,256]{2,1,0:T(8,128)(2,1)S(1)} %pad_maximum_fusion.2.refs_0_), channel_id=1, source_target_pairs={{0,1},{1,0},{2,3},{3,2},{4,5},{5,4},{6,7},{7,6},{8,9},{9,8},{10,11... | collective-permute-start | bytes 2162696 | tf_op jit(solution)/shard_map/ppermute | solution.py:61
  242.7 15.8 %collective-permute-start.34 = (bf16[2,256,512]{2,1,0:T(8,128)(2,1)S(1)}, bf16[2,256,512]{2,1,0:T(8,128)(2,1)S(1)}, u32[]{:S(2)}, u32[]{:S(2)}) collective-permute-start(bf16[2,256,512]{2,1,0:T(8,128)(2,1)S(1)} %bitcast.283), channel_id=1, source_target_pairs={{0,16},{16,32},{32,48},{1,17},{17,33},{33,49},{2,18},{18,34},{34,5... | collective-permute-start | bytes 1572872 | tf_op jit(solution)/shard_map/ppermute | solution.py:521
  268.9 12.6 %collective-permute-start.37 = (bf16[4,352,256]{2,1,0:T(8,128)(2,1)S(1)}, bf16[4,352,256]{2,1,0:T(8,128)(2,1)S(1)}, u32[]{:S(2)}, u32[]{:S(2)}) collective-permute-start(bf16[4,352,256]{2,1,0:T(8,128)(2,1)S(1)} %add_convert_fusion.2), channel_id=1, source_target_pairs={{0,6},{1,9},{2,4},{3,11},{4,2},{5,13},{6,0},{7,15},{8,14},{9,1},{1... | collective-permute-start | bytes 2162696 | tf_op jit(solution)/shard_map/ppermute | solution.py:78
  270.0 10.2 %collective-permute-start.38 = (bf16[4,160,256]{2,1,0:T(8,128)(2,1)S(1)}, bf16[4,160,256]{2,1,0:T(8,128)(2,1)S(1)}, u32[]{:S(2)}, u32[]{:S(2)}) collective-permute-start(bf16[4,160,256]{2,1,0:T(8,128)(2,1)S(1)} %add_convert_fusion.6), channel_id=1, source_target_pairs={{0,2},{1,3},{2,0},{3,1},{4,6},{5,7},{6,4},{7,5},{8,10},{9,11},{10,... | collective-permute-start | bytes 983048 | tf_op jit(solution)/shard_map/ppermute | solution.py:78
  281.8 7.5 %collective-permute-start.41 = (bf16[2,352,256]{2,1,0:T(8,128)(2,1)S(1)}, bf16[2,352,256]{2,1,0:T(8,128)(2,1)S(1)}, u32[]{:S(2)}, u32[]{:S(2)}) collective-permute-start(bf16[2,352,256]{2,1,0:T(8,128)(2,1)S(1)} %slice.349), channel_id=1, source_target_pairs={{0,2},{1,7},{2,0},{3,5},{4,6},{5,3},{6,4},{7,1},{8,10},{9,15},{10,... | collective-permute-start | bytes 1081352 | tf_op jit(solution)/shard_map/ppermute | solution.py:78
  295.4 8.0 %collective-permute-start.45 = (bf16[512,256]{1,0:T(8,128)(2,1)S(1)}, bf16[512,256]{1,0:T(8,128)(2,1)S(1)}, u32[]{:S(2)}, u32[]{:S(2)}) collective-permute-start(bf16[512,256]{1,0:T(8,128)(2,1)S(1)} %pad_maximum_fusion.13), channel_id=1, source_target_pairs={{0,64},{64,0},{1,65},{65,1},{2,66},{66,2},{3,67},{67,3},{4,68},{68... | collective-permute-start | bytes 786440 | tf_op jit(solution)/shard_map/ppermute | solution.py:65
  303.4 7.8 %collective-permute-start.46 = (bf16[352,256]{1,0:T(8,128)(2,1)S(1)}, bf16[352,256]{1,0:T(8,128)(2,1)S(1)}, u32[]{:S(2)}, u32[]{:S(2)}) collective-permute-start(bf16[352,256]{1,0:T(8,128)(2,1)S(1)} %get-tuple-element.225), channel_id=1, source_target_pairs={{0,8},{1,3},{2,10},{3,1},{4,12},{5,7},{6,14},{7,5},{8,0},{9,11},{1... | collective-permute-start | bytes 540680 | tf_op jit(solution)/shard_map/ppermute | solution.py:78
  311.3 8.3 %collective-permute-start.48 = (bf16[2,352,256]{2,1,0:T(8,128)(2,1)S(1)}, bf16[2,352,256]{2,1,0:T(8,128)(2,1)S(1)}, u32[]{:S(2)}, u32[]{:S(2)}) collective-permute-start(bf16[2,352,256]{2,1,0:T(8,128)(2,1)S(1)} %pad_maximum_fusion.7), channel_id=1, source_target_pairs={{0,2},{1,7},{2,0},{3,5},{4,6},{5,3},{6,4},{7,1},{8,10},{9,15},{10,... | collective-permute-start | bytes 1081352 | tf_op jit(solution)/shard_map/ppermute | solution.py:78
  319.6 12.6 %collective-permute-start.52 = (bf16[4,352,256]{2,1,0:T(8,128)(2,1)S(1)}, bf16[4,352,256]{2,1,0:T(8,128)(2,1)S(1)}, u32[]{:S(2)}, u32[]{:S(2)}) collective-permute-start(bf16[4,352,256]{2,1,0:T(8,128)(2,1)S(1)} %pad_maximum_fusion.3.refs_0_), channel_id=1, source_target_pairs={{0,6},{1,9},{2,4},{3,11},{4,2},{5,13},{6,0},{7,15},{8,14},{9,1},{1... | collective-permute-start | bytes 2162696 | tf_op jit(solution)/shard_map/ppermute | solution.py:78
  320.5 16.2 %collective-permute-start.50 = (bf16[4,352,256]{2,1,0:T(8,128)(2,1)S(1)}, bf16[4,352,256]{2,1,0:T(8,128)(2,1)S(1)}, u32[]{:S(2)}, u32[]{:S(2)}) collective-permute-start(bf16[4,352,256]{2,1,0:T(8,128)(2,1)S(1)} %pad_maximum_fusion.3.refs_0_), channel_id=1, source_target_pairs={{0,1},{1,0},{2,3},{3,2},{4,5},{5,4},{6,7},{7,6},{8,9},{9,8},{10,11... | collective-permute-start | bytes 2162696 | tf_op jit(solution)/shard_map/ppermute | solution.py:61
  371.8 7.8 %collective-permute-start.60 = (bf16[4,352,256]{2,1,0:T(8,128)(2,1)S(1)}, bf16[4,352,256]{2,1,0:T(8,128)(2,1)S(1)}, u32[]{:S(2)}, u32[]{:S(2)}) collective-permute-start(bf16[4,352,256]{2,1,0:T(8,128)(2,1)S(1)} %get-tuple-element.185), channel_id=1, source_target_pairs={{0,1},{1,0},{2,3},{3,2},{4,5},{5,4},{6,7},{7,6},{8,9},{9,8},{10,11... | collective-permute-start | bytes 2162696 | tf_op jit(solution)/shard_map/ppermute | solution.py:61
  375.5 12.7 %collective-permute-start.58 = (bf16[4,352,256]{2,1,0:T(8,128)(2,1)S(1)}, bf16[4,352,256]{2,1,0:T(8,128)(2,1)S(1)}, u32[]{:S(2)}, u32[]{:S(2)}) collective-permute-start(bf16[4,352,256]{2,1,0:T(8,128)(2,1)S(1)} %add_convert_fusion.1), channel_id=1, source_target_pairs={{0,6},{1,9},{2,4},{3,11},{4,2},{5,13},{6,0},{7,15},{8,14},{9,1},{1... | collective-permute-start | bytes 2162696 | tf_op jit(solution)/shard_map/ppermute | solution.py:78
  378.0 10.2 %collective-permute-start.59 = (bf16[4,160,256]{2,1,0:T(8,128)(2,1)S(1)}, bf16[4,160,256]{2,1,0:T(8,128)(2,1)S(1)}, u32[]{:S(2)}, u32[]{:S(2)}) collective-permute-start(bf16[4,160,256]{2,1,0:T(8,128)(2,1)S(1)} %add_convert_fusion.5), channel_id=1, source_target_pairs={{0,2},{1,3},{2,0},{3,1},{4,6},{5,7},{6,4},{7,5},{8,10},{9,11},{10,... | collective-permute-start | bytes 983048 | tf_op jit(solution)/shard_map/ppermute | solution.py:78
  388.5 7.5 %collective-permute-start.62 = (bf16[2,352,256]{2,1,0:T(8,128)(2,1)S(1)}, bf16[2,352,256]{2,1,0:T(8,128)(2,1)S(1)}, u32[]{:S(2)}, u32[]{:S(2)}) collective-permute-start(bf16[2,352,256]{2,1,0:T(8,128)(2,1)S(1)} %slice.348), channel_id=1, source_target_pairs={{0,2},{1,7},{2,0},{3,5},{4,6},{5,3},{6,4},{7,1},{8,10},{9,15},{10,... | collective-permute-start | bytes 1081352 | tf_op jit(solution)/shard_map/ppermute | solution.py:78
  410.0 7.6 %collective-permute-start.68 = (bf16[2,352,256]{2,1,0:T(8,128)(2,1)S(1)}, bf16[2,352,256]{2,1,0:T(8,128)(2,1)S(1)}, u32[]{:S(2)}, u32[]{:S(2)}) collective-permute-start(bf16[2,352,256]{2,1,0:T(8,128)(2,1)S(1)} %pad_maximum_fusion.8), channel_id=1, source_target_pairs={{0,2},{1,7},{2,0},{3,5},{4,6},{5,3},{6,4},{7,1},{8,10},{9,15},{10,... | collective-permute-start | bytes 1081352 | tf_op jit(solution)/shard_map/ppermute | solution.py:78
  417.6 12.8 %collective-permute-start.72 = (bf16[4,352,256]{2,1,0:T(8,128)(2,1)S(1)}, bf16[4,352,256]{2,1,0:T(8,128)(2,1)S(1)}, u32[]{:S(2)}, u32[]{:S(2)}) collective-permute-start(bf16[4,352,256]{2,1,0:T(8,128)(2,1)S(1)} %pad_maximum_fusion.4.refs_0_), channel_id=1, source_target_pairs={{0,6},{1,9},{2,4},{3,11},{4,2},{5,13},{6,0},{7,15},{8,14},{9,1},{1... | collective-permute-start | bytes 2162696 | tf_op jit(solution)/shard_map/ppermute | solution.py:78
  421.7 11.5 %collective-permute-start.70 = (bf16[4,352,256]{2,1,0:T(8,128)(2,1)S(1)}, bf16[4,352,256]{2,1,0:T(8,128)(2,1)S(1)}, u32[]{:S(2)}, u32[]{:S(2)}) collective-permute-start(bf16[4,352,256]{2,1,0:T(8,128)(2,1)S(1)} %pad_maximum_fusion.4.refs_0_), channel_id=1, source_target_pairs={{0,1},{1,0},{2,3},{3,2},{4,5},{5,4},{6,7},{7,6},{8,9},{9,8},{10,11... | collective-permute-start | bytes 2162696 | tf_op jit(solution)/shard_map/ppermute | solution.py:61
  442.3 8.7 %collective-permute-start.80 = (bf16[4,352,256]{2,1,0:T(8,128)(2,1)S(1)}, bf16[4,352,256]{2,1,0:T(8,128)(2,1)S(1)}, u32[]{:S(2)}, u32[]{:S(2)}) collective-permute-start(bf16[4,352,256]{2,1,0:T(8,128)(2,1)S(1)} %get-tuple-element.211), channel_id=1, source_target_pairs={{0,1},{1,0},{2,3},{3,2},{4,5},{5,4},{6,7},{7,6},{8,9},{9,8},{10,11... | collective-permute-start | bytes 2162696 | tf_op jit(solution)/shard_map/ppermute | solution.py:61
  446.1 13.6 %collective-permute-start.78 = (bf16[4,352,256]{2,1,0:T(8,128)(2,1)S(1)}, bf16[4,352,256]{2,1,0:T(8,128)(2,1)S(1)}, u32[]{:S(2)}, u32[]{:S(2)}) collective-permute-start(bf16[4,352,256]{2,1,0:T(8,128)(2,1)S(1)} %add_convert_fusion), channel_id=1, source_target_pairs={{0,6},{1,9},{2,4},{3,11},{4,2},{5,13},{6,0},{7,15},{8,14},{9,1},{1... | collective-permute-start | bytes 2162696 | tf_op jit(solution)/shard_map/ppermute | solution.py:78
  449.5 10.2 %collective-permute-start.79 = (bf16[4,160,256]{2,1,0:T(8,128)(2,1)S(1)}, bf16[4,160,256]{2,1,0:T(8,128)(2,1)S(1)}, u32[]{:S(2)}, u32[]{:S(2)}) collective-permute-start(bf16[4,160,256]{2,1,0:T(8,128)(2,1)S(1)} %add_convert_fusion.4), channel_id=1, source_target_pairs={{0,2},{1,3},{2,0},{3,1},{4,6},{5,7},{6,4},{7,5},{8,10},{9,11},{10,... | collective-permute-start | bytes 983048 | tf_op jit(solution)/shard_map/ppermute | solution.py:78
  460.0 7.5 %collective-permute-start.82 = (bf16[2,352,256]{2,1,0:T(8,128)(2,1)S(1)}, bf16[2,352,256]{2,1,0:T(8,128)(2,1)S(1)}, u32[]{:S(2)}, u32[]{:S(2)}) collective-permute-start(bf16[2,352,256]{2,1,0:T(8,128)(2,1)S(1)} %slice.347), channel_id=1, source_target_pairs={{0,2},{1,7},{2,0},{3,5},{4,6},{5,3},{6,4},{7,1},{8,10},{9,15},{10,... | collective-permute-start | bytes 1081352 | tf_op jit(solution)/shard_map/ppermute | solution.py:78
  (72 other events, 536.0 us)
Sparse Core Ops, SparseCore 0:
  11.7 104.5 all-gather.2
  148.9 48.0 all-gather.4

commit v5 on v4

--- a/solution.py
+++ b/solution.py
@@ -54,7 +54,6 @@
 
 
 OFFSETS = np.array([[block_offsets(m) for m in part] for part in MASKS], np.int32)
-SLOTS = np.argsort(OFFSETS, axis=-1).astype(np.int32)
 
 
 def core_swap(value):
@@ -80,40 +79,58 @@
 
 def places(chip, pick):
     offsets = lax.dynamic_index_in_dim(jnp.asarray(OFFSETS), pick, 1, keepdims=False)
-    slots = lax.dynamic_index_in_dim(jnp.asarray(SLOTS), pick, 1, keepdims=False)
-    chips = chip ^ offsets
-    blocks = jnp.take_along_axis(slots, jnp.arange(CHIPS)[None] ^ chip, axis=1)
-    return jnp.concatenate(
-        [jnp.reshape(pick, (1,)), chips.reshape(-1), blocks.reshape(-1)]
-    ).astype(jnp.int32)
+    return jnp.concatenate([jnp.reshape(pick, (1,)), (chip ^ offsets).reshape(-1)]).astype(
+        jnp.int32
+    )
 
 
 def together(*values):
     return lax.optimization_barrier(values)
 
 
-def gather_chips(local):
-    got = together(*[neighbour(value, part, 0) for part, value in enumerate(local)])
-    near = [jnp.stack([value, other]) for value, other in zip(local, got)]
-    got = together(*[neighbour(value, part, 1) for part, value in enumerate(near)])
-    near = [jnp.concatenate([value, other]) for value, other in zip(near, got)]
-    far = together(*[neighbour(value, part, 2) for part, value in enumerate(near)])
-    return near + list(far)
-
-
-def scatter_sum(own, other):
-    wide = [value.astype(f32) for value in own]
-    far = together(core_swap(other[2]), core_swap(other[3]))
-    near = [core_swap(other[0]), core_swap(other[1])]
-    sums = [(wide[2 + part] + far[part].astype(f32)).astype(bf16) for part in range(2)]
-    got = together(*[neighbour(sums[part], part, 2) for part in range(2)], *near)
+def gather_chips(local, beside):
+    side = ()
+    near = list(local)
+    for turn in range(2):
+        sent = [neighbour(value, part, turn) for part, value in enumerate(near)]
+        side = beside(turn, side)
+        *got, side = together(*sent, side)
+        if turn == 0:
+            near = [jnp.stack(pair) for pair in zip(near, got)]
+        else:
+            near = [jnp.concatenate(pair) for pair in zip(near, got)]
+    swaps = [core_swap(value) for value in near]
+    far = [neighbour(value, part, 2) for part, value in enumerate(near)]
+    *swaps, side = together(*swaps, side)
+    side = beside(2, side)
+    far = list(together(*far))
+    return near + far, swaps + [core_swap(value) for value in far], side
+
+
+def nothing(turn, side):
+    return side
+
+
+def scatter_sum(places_both, mixed, weight):
+    own, other = places_both
+    other_far = [core_swap(value) for value in terms(other, mixed, weight, 1)]
+    other_near = [core_swap(value) for value in terms(other, mixed, weight, 0)]
+    own_far = terms(own, mixed, weight, 1)
+    own_near = terms(own, mixed, weight, 0)
+    other_far = together(*other_far)
+    sums = [
+        (mine.astype(f32) + got.astype(f32)).astype(bf16)
+        for mine, got in zip(own_far, other_far)
+    ]
+    got = together(*[neighbour(sums[part], part, 2) for part in range(2)], *other_near)
     low = [
-        wide[part] + got[2 + part].astype(f32) + got[part].astype(f32) for part in range(2)
+        own_near[part].astype(f32) + got[2 + part].astype(f32) + got[part].astype(f32)
+        for part in range(2)
     ]
     got = together(*[neighbour(low[part][2:].astype(bf16), part, 1) for part in range(2)])
     low = [low[part][:2] + got[part].astype(f32) for part in range(2)]
-    got = together(*[neighbour(low[part][1].astype(bf16), part, 0) for part in range(2)])
-    return [low[part][0] + got[part].astype(f32) for part in range(2)]
+    got = [neighbour(low[part][1].astype(bf16), part, 0) for part in range(2)]
+    return [low[part][0] for part in range(2)], got
 
 
 def project_kernel(last, units, place_ref, *refs):
@@ -203,11 +220,10 @@
     )
 
 
-def project(places_both, local, gains, weight, units):
-    same = gather_chips(local)
-    swap = [core_swap(value) for value in same]
+def project(places_both, local, gains, weight, units, beside=nothing):
+    same, swap, side = gather_chips(local, beside)
     before = project_half(places_both[0], same, gains, weight, None, units)
-    return project_half(places_both[1], swap, gains, weight, before, units)
+    return project_half(places_both[1], swap, gains, weight, before, units), side
 
 
 def causal_kernel(triple_ref, out_ref):
@@ -275,84 +291,76 @@
 
 
 def terms_kernel(place_ref, mixed_ref, *refs):
-    w_refs, out_refs, left_ref = refs[:GROUP], refs[GROUP : GROUP + 4], refs[-1]
-    step = pl.program_id(0)
-
-    @pl.when(step == 0)
-    def _():
-        for unit in range(UNITS):
-            b, h = divmod(unit, 2)
-            left_ref[b * ROWS : (b + 1) * ROWS, h * HEAD : (h + 1) * HEAD] = mixed_ref[unit]
-
-    for at, w_ref in enumerate(w_refs):
-        product = jnp.dot(left_ref[...], w_ref[...], preferred_element_type=f32).astype(bf16)
-        chip = step * GROUP + at
-        for part in range(2):
-            block = place_ref[1 + (2 + part) * CHIPS + chip]
-            value = product[STARTS[part] : STARTS[part] + PARTS[part], :]
-
-            @pl.when(block < 4)
-            def _():
-                out_refs[part][block] = value
-
-            @pl.when(block >= 4)
-            def _():
-                out_refs[2 + part][block - 4] = value
-
-
-def terms(place, mixed, weight):
+    w_refs, out_refs, left_ref = refs[: 2 * GROUP], refs[2 * GROUP : 2 * GROUP + 2], refs[-1]
+    for unit in range(UNITS):
+        b, h = divmod(unit, 2)
+        left_ref[b * ROWS : (b + 1) * ROWS, h * HEAD : (h + 1) * HEAD] = mixed_ref[unit]
+    for part in range(2):
+        left = left_ref[STARTS[part] : STARTS[part] + PARTS[part], :]
+        for at in range(GROUP):
+            right = w_refs[part * GROUP + at][...]
+            out_refs[part][at] = jnp.dot(left, right, preferred_element_type=f32).astype(bf16)
+
+
+def terms(place, mixed, weight, high):
     count = BATCH * ROWS
 
-    def columns(at):
-        return pl.BlockSpec((WIDTH, WIDTH), lambda s, place: (0, 2 * (GROUP * s + at) + place[0]))
-
-    shapes = [(4, PARTS[at % 2], WIDTH) for at in range(4)]
+    def columns(part, at):
+        index = 1 + part * CHIPS + GROUP * high + at
+        return pl.BlockSpec((WIDTH, WIDTH), lambda s, place: (0, 2 * place[index] + place[0]))
+
+    shapes = [(GROUP, PARTS[part], WIDTH) for part in range(2)]
     return pl.pallas_call(
         terms_kernel,
         grid_spec=pltpu.PrefetchScalarGridSpec(
             num_scalar_prefetch=1,
-            grid=(CHIPS // GROUP,),
-            in_specs=[whole((UNITS, ROWS, HEAD))] + [columns(at) for at in range(GROUP)],
+            grid=(1,),
+            in_specs=[whole((UNITS, ROWS, HEAD))]
+            + [columns(part, at) for part in range(2) for at in range(GROUP)],
             out_specs=[whole(shape) for shape in shapes],
             scratch_shapes=[pltpu.VMEM((count, WIDTH), bf16)],
         ),
         out_shape=[jax.ShapeDtypeStruct(shape, bf16) for shape in shapes],
-        compiler_params=params(),
+        compiler_params=params(8),
         cost_estimate=pl.CostEstimate(
-            flops=2 * count * WIDTH * D // 2,
-            bytes_accessed=D * WIDTH + D * count,
+            flops=2 * count * WIDTH * D // 4,
+            bytes_accessed=D * WIDTH + D * count // 2,
             transcendentals=0,
         ),
-    )(place, mixed, *([weight] * GROUP))
-
-
-def add_product(places_both, states, mixed, weight):
-    other = terms(places_both[1], mixed, weight)
-    own = terms(places_both[0], mixed, weight)
-    return [
-        (state.astype(f32) + total).astype(bf16)
-        for state, total in zip(states, scatter_sum(own, other))
-    ]
+    )(place, mixed, *([weight] * (2 * GROUP)))
+
+
+def add_product(places_both, states, mixed, weight, side=()):
+    low, got = scatter_sum(places_both, mixed, weight)
+    *got, side = together(*got, side)
+    total = [
+        (state.astype(f32) + (mine + far.astype(f32))).astype(bf16)
+        for state, mine, far in zip(states, low, got)
+    ]
+    return total, side
 
 
 def by_parts(rows):
     return [rows[start : start + count] for start, count in zip(STARTS, PARTS)]
 
 
-def look_up(ids, enc_embed, core, section):
+def look_up(ids, enc_embed, places_both, section):
     vocab_here = enc_embed.shape[0]
     mine = lax.dynamic_slice_in_dim(ids, section * (NB_LEN // 2), NB_LEN // 2, axis=1)
-    wanted = mine.reshape(CHIPS, 2, NB_LEN // 2) - lax.axis_index(MP) * vocab_here
-
-    def rows(at):
-        picks = lax.dynamic_index_in_dim(wanted, at, 1, keepdims=False).reshape(-1)
+    wanted = mine - lax.axis_index(MP) * vocab_here
+
+    def rows(place):
+        picks = wanted[2 * place[1 : 1 + CHIPS] + place[0]].reshape(-1)
         inside = (picks >= 0) & (picks < vocab_here)
         found = enc_embed[jnp.clip(picks, 0, vocab_here - 1)]
         found = jnp.where(inside[:, None], found, jnp.zeros((), bf16))
         return found.reshape(CHIPS, NB_LEN // 2, ENC_D)
 
-    paired = core_swap(rows(1 - core)) + rows(core)
-    return jnp.sum(chips_to_chips(paired).astype(f32), axis=0).astype(bf16)
+    far = core_swap(rows(places_both[1]))
+    total = rows(places_both[0]) + far
+    total = total[:4] + neighbour(total[4:], 0, 2)
+    total = total[:2] + neighbour(total[2:], 0, 1)
+    return total[0] + neighbour(total[1], 0, 0)
 
 
 def join_halves(half, section):
@@ -432,11 +440,10 @@
         out_ref[:, at * width : (at + 1) * width] = part.astype(bf16)
 
 
-def encode(embedded, enc_norms, pieces, section):
+def encode_mix(embedded, enc_norms, pieces, section):
     out = jax.ShapeDtypeStruct((NB_LEN, ENC_D), bf16)
     width = ENC_D // 2
     full = whole((NB_LEN, ENC_D))
-    gain = whole((1, ENC_D))
 
     def piece(at):
         return pl.BlockSpec((1, ENC_D, width), lambda s: (at, 0, 0))
@@ -444,42 +451,56 @@
     mixed = pl.pallas_call(
         enc_mix_kernel,
         grid=(1,),
-        in_specs=[SCALAR, full, gain] + [piece(8 + at) for at in range(5)],
+        in_specs=[SCALAR, full, whole((1, ENC_D))] + [piece(8 + at) for at in range(5)],
         out_specs=full,
         out_shape=out,
         scratch_shapes=[pltpu.VMEM((NB_LEN, width), bf16)],
         compiler_params=params(),
     )(section, embedded, enc_norms[:1], *([pieces] * 5))
-    inner = (embedded.astype(f32) + (mixed.astype(f32) + section_swap(mixed).astype(f32))).astype(
-        bf16
-    )
+    return embedded, mixed, section_swap(mixed)
+
+
+def encode_feed(embedded, mixed, far, enc_norms, pieces):
+    width = ENC_D // 2
+    full = whole((NB_LEN, ENC_D))
+    inner = (embedded.astype(f32) + (mixed.astype(f32) + far.astype(f32))).astype(bf16)
     fed = pl.pallas_call(
         enc_feed_kernel,
         grid=(1,),
-        in_specs=[full, gain, pl.BlockSpec((8, ENC_D, width), lambda s: (0, 0, 0))],
+        in_specs=[full, whole((1, ENC_D)), pl.BlockSpec((8, ENC_D, width), lambda s: (0, 0, 0))],
         out_specs=full,
-        out_shape=out,
+        out_shape=jax.ShapeDtypeStruct((NB_LEN, ENC_D), bf16),
         compiler_params=params(28),
     )(inner, enc_norms[1:], pieces)
-    return (inner.astype(f32) + (fed.astype(f32) + section_swap(fed).astype(f32))).astype(bf16)
-
-
-def decoder_layer(places_both, states, looked_up, make_pairs, weights):
+    return inner, fed, section_swap(fed)
+
+
+def encode_end(inner, fed, far):
+    return (inner.astype(f32) + (fed.astype(f32) + far.astype(f32))).astype(bf16)
+
+
+def decoder_layer(places_both, states, weights, encoder=None):
     norms, triple_w, out_w, query_w, back_w = weights
-    triple = project(places_both, states, norms[0], triple_w, True)
-    looked_up, embedded = looked_up
-    if looked_up is not None:
-        triple, half = together(triple, looked_up)
-        embedded = embedded(half)
+    idle = encoder is None
+    first = nothing if idle else encoder.first
+    triple, half = project(places_both, states, norms[0], triple_w, True, first)
     triple = lax.all_to_all(triple, "seq", 0, 0, tiled=True)
+    triple, half = together(triple, half)
+    embedded = half if idle else encoder.join(half)
     mixed = lax.all_to_all(causal(triple), "seq", 0, 0, tiled=True)
-    if looked_up is not None:
-        mixed, embedded = together(mixed, embedded)
-    prev, pairs = make_pairs(embedded)
-    middle = add_product(places_both, states, mixed, out_w)
-    asked = project(places_both, middle, norms[1], query_w[None], False)
-    crossed = cross(asked, prev, pairs)
-    return add_product(places_both, middle, crossed, back_w), (prev, pairs)
+    middle, embedded = add_product(places_both, states, mixed, out_w, embedded)
+
+    def second(turn, side):
+        return side if idle else encoder.second(turn, embedded if turn == 0 else side)
+
+    asked, pairs = project(places_both, middle, norms[1], query_w[None], False, second)
+    pairs = None if idle else pairs
+    return middle, asked, pairs
+
+
+def cross_layer(places_both, middle, asked, pairs, weights):
+    crossed = cross(asked, *pairs)
+    return add_product(places_both, middle, crossed, weights[4])[0]
 
 
 def on_device(
@@ -506,20 +527,37 @@
     blocks_here = neighbour_table.shape[1]
     pieces = weight_pieces(section, enc_qkv, enc_out, enc_up, enc_down)
     slot_ids = neighbour_ids[neighbour_table.reshape(-1)]
-    half = look_up(slot_ids, enc_embed, core_at, section)
     count = lax.axis_size("seq")
     pair_w = cross_pair[0].reshape(ENC_D, 2 * WIDTH)
+    section_ref = jnp.reshape(section, (1,))
 
     def pair_rows(rows):
         return jnp.dot(rows, pair_w, preferred_element_type=f32).astype(bf16)
 
-    def make_pairs(embedded):
-        encoded = encode(embedded, enc_norms, pieces, jnp.reshape(section, (1,)))
-        encoded = lax.all_gather(encoded, MP, axis=0, tiled=True)
-        edge = encoded.reshape(BATCH, blocks_here, KEYS, ENC_D)[:, -1]
-        edge = pair_rows(edge.reshape(BATCH * KEYS, ENC_D)).reshape(BATCH, KEYS, 2 * WIDTH)
-        prev = lax.ppermute(edge, "seq", [(i, i + 1) for i in range(count - 1)])
-        return prev, pair_rows(encoded).reshape(BATCH, blocks_here, KEYS, 2 * WIDTH)
+    class Encoder:
+        @staticmethod
+        def first(turn, side):
+            if turn == 0:
+                return slot_ids
+            if turn == 1:
+                return side
+            return look_up(side, enc_embed, places_both, section)
+
+        @staticmethod
+        def join(half):
+            return join_halves(half, section)
+
+        @staticmethod
+        def second(turn, side):
+            if turn == 0:
+                return encode_mix(side, enc_norms, pieces, section_ref)
+            if turn == 1:
+                return encode_feed(*side, enc_norms, pieces)
+            encoded = lax.all_gather(encode_end(*side), MP, axis=0, tiled=True)
+            edge = encoded.reshape(BATCH, blocks_here, KEYS, ENC_D)[:, -1]
+            edge = pair_rows(edge.reshape(BATCH * KEYS, ENC_D)).reshape(BATCH, KEYS, 2 * WIDTH)
+            prev = lax.ppermute(edge, "seq", [(i, i + 1) for i in range(count - 1)])
+            return prev, pair_rows(encoded).reshape(BATCH, blocks_here, KEYS, 2 * WIDTH)
 
     weights = (
         dec_norms[0],
@@ -530,18 +568,11 @@
     )
 
     states = hidden_states.reshape(BATCH * ROWS, WIDTH)
-    first, pairs = decoder_layer(
-        places_both,
-        by_parts(states),
-        (half, lambda half: join_halves(half, section)),
-        make_pairs,
-        weights,
-    )
+    middle, asked, pairs = decoder_layer(places_both, by_parts(states), weights, Encoder)
+    first = cross_layer(places_both, middle, asked, pairs, weights)
     handed = section_swap(jnp.concatenate(first))
-    second, _ = decoder_layer(
-        places_both, by_parts(handed), (None, None), lambda _: pairs, weights
-    )
-    second = jnp.concatenate(second)
+    middle, asked, _ = decoder_layer(places_both, by_parts(handed), weights)
+    second = jnp.concatenate(cross_layer(places_both, middle, asked, pairs, weights))
     second = second.reshape(BATCH, ROWS, WIDTH)
     return jnp.where(section == 0, section_swap(second[0]), second[1])[None]
 

time: 497 us -> 504 us (1.014)
  Pallas kernels: 66.1 us -> 54.5 us
  starting transfers between devices: 105 us -> 94.6 us
  blocking collectives: 25.8 us -> 35.4 us
  waiting for transfers between devices: 224 us -> 232 us
  other arithmetic: 12.1 us -> 18.1 us
  local copies, waits for them, and re-layouts: 36.6 us -> 42.2 us
    all_gather x1, waiting for transfers between devices: 0.02 us -> 14.3 us  [second(): encoded = lax.all_gather(encode_end(*side), MP, axis=0, tiled=True)]
    ppermute x33, starting transfers between devices: 18.8 us -> 8.32 us  [core_swap(): return lax.ppermute(value, 'core', [(0, 1), (1, 0)])]
    pallas_call x8 -> x16, Pallas kernels: 27.1 us -> 16.8 us  [terms(): pl.pallas_call(terms_kernel, grid_spec=pltpu.PrefetchScalarGridSpec(num_s...]
    all_to_all x1 -> x2, blocking collectives: 9.07 us -> 18.1 us  [decoder_layer(): mixed = lax.all_to_all(causal(triple), 'seq', 0, 0, tiled=True)]
    all_to_all x2 -> x0, starting transfers between devices: 8.93 us -> none  [the longest x1 5.52 us: chips_to_chips(): return lax.all_to_all(value, ('z', 'y'), 0, 0, tiled=True)]
    ppermute x48 -> x51, starting transfers between devices: 52.1 us -> 60.2 us  [neighbour(): return lax.ppermute(value, MP, route)]
    all_to_all x2 -> x0, waiting for transfers between devices: 6.5 us -> none  [the longest x1 6.49 us: decoder_layer(): mixed = lax.all_to_all(causal(triple), 'seq', 0, 0, tiled=True)]
    ppermute x48 -> x51, waiting for transfers between devices: 178 us -> 184 us  [neighbour(): return lax.ppermute(value, MP, route)]
  transfers between devices with their start and end apart: 92 -> 93, of which waited for: 46 -> 49; matrix products, arithmetic and copies ran while one was open for 6% -> 7% of each run, Pallas kernels for 8% -> 8%
where the time goes in v5:
time: 504 us; the launch traced here: 495 us
  waiting for transfers between devices  232 us (46%)
  starting transfers between devices  94.6 us (19%)
  Pallas kernels  54.5 us (11%)
  local copies, waits for them, and re-layouts  42.2 us (8%)
  blocking collectives  35.4 us (7%)
  other arithmetic  18.1 us (4%)
  between operations  15.3 us (3%)
    ppermute x51, waiting for transfers between devices, neighbour(): return lax.ppermute(value, MP, route)  184 us
    ppermute x51, starting transfers between devices, neighbour(): return lax.ppermute(value, MP, route)  60.2 us
    pallas_call x8, Pallas kernels, project_half(): pl.pallas_call(functools.partial(project_kernel, last, units), grid_spec=...  26 us
    all_to_all x2, blocking collectives, decoder_layer(): mixed = lax.all_to_all(causal(triple), 'seq', 0, 0, tiled=True)  18.1 us
    ppermute x5, starting transfers between devices, section_swap(): return lax.ppermute(value, 'section', [(0, 1), (1, 0)])  18.1 us
    unnamed x92, local copies, waits for them, and re-layouts  18.1 us
    all_to_all x1, blocking collectives, decoder_layer(): triple = lax.all_to_all(triple, 'seq', 0, 0, tiled=True)  17.2 us
    pallas_call x16, Pallas kernels, terms(): pl.pallas_call(terms_kernel, grid_spec=pltpu.PrefetchScalarGridSpec(num_s...  16.8 us
  transfers between devices with their start and end apart: 93, of which 49 were waited for; matrix products, arithmetic and copies ran while one was open for 7% of the time, Pallas kernels for 8%

profile of v5, /device:TPU:0, one launch (start us, length us, event | category | flops | bytes accessed | tf_op | source)
XLA Modules:
  0.0 494.7 jit_solution(2185251896736114027)
XLA Ops:
  21.0 7.0 %collective-permute-done.3 = bf16[2,160,256]{2,1,0:T(8,128)(2,1)S(1)} collective-permute-done((bf16[2,160,256]{2,1,0:T(8,128)(2,1)S(1)}, bf16[2,160,256]{2,1,0:T(8,128)(2,1)S(1)}, u32[]{:S(2)}, u32[]{:S(2)}) %collective-permute-start.3) | collective-permute-done | bytes 163872 | tf_op jit(solution)/shard_map/ppermute | solution.py:77
  31.1 5.0 %collective-permute-start.6 = (bf16[4,352,256]{2,1,0:T(8,128)(2,1)S(1)}, bf16[4,352,256]{2,1,0:T(8,128)(2,1)}, u32[]{:S(2)}, u32[]{:S(2)}) collective-permute-start(bf16[4,352,256]{2,1,0:T(8,128)(2,1)S(1)} %pad_maximum_fusion.1.refs_0_), channel_id=1, source_target_pairs={{0,6},{1,9},{2,4},{3,11},{4,2},{5,13},{6,0},{7,15},{8,14},{9,1},{1... | collective-permute-start | bytes 2162696 | tf_op jit(solution)/shard_map/ppermute | solution.py:77
  39.1 7.3 %gather_fusion.4 = bf16[512,1024]{1,0:T(8,128)(2,1)S(1)} fusion(bf16[4000,1024]{1,0:T(8,128)(2,1)} %param.19, s32[1024]{0:T(1024)S(1)} %pad_clamp_fusion), kind=kCustom, calls=%fused_computation.4 | custom fusion | bytes 2099200 | tf_op jit(solution)/shard_map/gather | solution.py:355
  46.7 17.5 %collective-permute-done.7.refs_3_ = bf16[4,160,256]{2,1,0:T(8,128)(2,1)} collective-permute-done((bf16[4,160,256]{2,1,0:T(8,128)(2,1)S(1)}, bf16[4,160,256]{2,1,0:T(8,128)(2,1)}, u32[]{:S(2)}, u32[]{:S(2)}) %collective-permute-start.7) | collective-permute-done | bytes 327712 | tf_op jit(solution)/shard_map/ppermute | solution.py:77
  64.2 8.1 %gather_fusion.2 = bf16[512,1024]{1,0:T(8,128)(2,1)} fusion(bf16[4000,1024]{1,0:T(8,128)(2,1)} %param.19, s32[1024]{0:T(1024)S(1)} %pad_clamp_fusion.2), kind=kCustom, calls=%fused_computation.2 | custom fusion | bytes 2099200 | tf_op jit(solution)/shard_map/gather | solution.py:355
  78.6 8.5 %collective-permute-done.11 = bf16[4,64,1024]{2,1,0:T(8,128)(2,1)} collective-permute-done((bf16[4,64,1024]{2,1,0:T(8,128)(2,1)}, bf16[4,64,1024]{2,1,0:T(8,128)(2,1)}, u32[]{:S(2)}, u32[]{:S(2)}) %collective-permute-start.11) | collective-permute-done | bytes 524320 | tf_op jit(solution)/shard_map/ppermute | solution.py:77
  89.2 12.4 %collective-permute-start.12 = (bf16[2,64,1024]{2,1,0:T(8,128)(2,1)}, bf16[2,64,1024]{2,1,0:T(8,128)(2,1)}, u32[]{:S(2)}, u32[]{:S(2)}) collective-permute-start(bf16[2,64,1024]{2,1,0:T(8,128)(2,1)} %slice.248), channel_id=1, source_target_pairs={{0,2},{1,7},{2,0},{3,5},{4,6},{5,3},{6,4},{7,1},{8,10},{9,15},{10,... | collective-permute-start | bytes 786440 | tf_op jit(solution)/shard_map/ppermute | solution.py:77
  104.4 5.1 %shard_map.154 = (f32[3,512,256]{2,1,0:T(8,128)S(1)}, f32[512,128]{1,0:T(8,128)S(1)}) custom-call(s32[17]{0:T(128)S(1)} %pad_add_fusion.place_ref, bf16[4,352,256]{2,1,0:T(8,128)(2,1)S(1)} %pad_maximum_fusion.1.refs_0_, bf16[4,160,256]{2,1,0:T(8,128)(2,1)S(1)} %pad_maximum_fusion.9.refs_1_, bf16[4,352,256]{2,1,0:T(8,128)(2,1)} %collective-permute-done.6.refs_2_, ...), custom_call_target="tpu_custom_call" | custom-call | flops 1610612736 | bytes 6815744 | tf_op jit(solution)/shard_map/pallas_call | solution.py:198
  109.6 4.8 shard_map.155
  115.3 4.6 all-to-all-start
  121.2 5.0 %collective-permute-done.13 = bf16[64,1024]{1,0:T(8,128)(2,1)S(1)} collective-permute-done((bf16[64,1024]{1,0:T(8,128)(2,1)S(1)}, bf16[64,1024]{1,0:T(8,128)(2,1)S(1)}, u32[]{:S(2)}, u32[]{:S(2)}) %collective-permute-start.13) | collective-permute-done | bytes 131104 | tf_op jit(solution)/shard_map/ppermute | solution.py:77
  126.8 4.7 all-to-all-done.triple_ref
  132.9 9.1 %all_to_all.20.mixed_ref = bf16[4,256,128]{2,1,0:T(8,128)(2,1)S(1)} all-to-all(bf16[4,256,128]{2,1,0:T(8,128)(2,1)S(1)} %shard_map.156), channel_id=1, replica_groups=mesh['section'=2,'seq'=4,'z'=2,'y'=4,'core'=2] {'seq'}, dimensions={0} | all-to-all | bytes 524288 | tf_op jit(solution)/shard_map/all_to_all | solution.py:490
  150.5 9.4 %collective-permute-done.17 = bf16[4,160,256]{2,1,0:T(8,128)(2,1)} collective-permute-done((bf16[4,160,256]{2,1,0:T(8,128)(2,1)}, bf16[4,160,256]{2,1,0:T(8,128)(2,1)}, u32[]{:S(2)}, u32[]{:S(2)}) %collective-permute-start.17) | collective-permute-done | bytes 327712 | tf_op jit(solution)/shard_map/ppermute | solution.py:77
  163.8 5.1 %collective-permute-start.24 = (bf16[64,1024]{1,0:T(8,128)(2,1)S(1)}, bf16[64,1024]{1,0:T(8,128)(2,1)S(1)}, u32[]{:S(2)}, u32[]{:S(2)}) collective-permute-start(bf16[64,1024]{1,0:T(8,128)(2,1)S(1)} %copy-done.31), channel_id=1, source_target_pairs={{0,64},{64,0},{1,65},{65,1},{2,66},{66,2},{3,67},{67,3},{4,68},{68... | collective-permute-start | bytes 393224 | tf_op jit(solution)/shard_map/ppermute | solution.py:64
  172.3 4.1 collective-permute-done.24
  179.3 4.9 copy-done.4
  186.3 4.7 collective-permute-start.27
  193.2 3.6 collective-permute-done.26
  202.5 6.0 %collective-permute-done.29 = bf16[2,160,256]{2,1,0:T(8,128)(2,1)S(1)} collective-permute-done((bf16[2,160,256]{2,1,0:T(8,128)(2,1)S(1)}, bf16[2,160,256]{2,1,0:T(8,128)(2,1)S(1)}, u32[]{:S(2)}, u32[]{:S(2)}) %collective-permute-start.29) | collective-permute-done | bytes 163872 | tf_op jit(solution)/shard_map/ppermute | solution.py:77
  218.0 11.8 %collective-permute-done.34.refs_3_ = bf16[4,160,256]{2,1,0:T(8,128)(2,1)S(1)} collective-permute-done((bf16[4,160,256]{2,1,0:T(8,128)(2,1)S(1)}, bf16[4,160,256]{2,1,0:T(8,128)(2,1)S(1)}, u32[]{:S(2)}, u32[]{:S(2)}) %collective-permute-start.34) | collective-permute-done | bytes 327712 | tf_op jit(solution)/shard_map/ppermute | solution.py:77
  238.0 14.3 %all-gather.5.cloned.1.call-done = bf16[2048,1024]{1,0:T(8,128)(2,1)} async-done(((bf16[128,1024]{1,0:T(8,128)(2,1)}), bf16[2048,1024]{1,0:T(8,128)(2,1)}) %all-gather.5.cloned.1.call-update) | async-done | bytes 4194320 | tf_op jit(solution)/shard_map/all_gather | solution.py:556
  254.5 3.4 collective-permute-start.37
  260.4 9.0 %collective-permute-done.37.prev_ref = bf16[2,256,512]{2,1,0:T(8,128)(2,1)S(1)} collective-permute-done((bf16[2,256,512]{2,1,0:T(8,128)(2,1)S(1)}, bf16[2,256,512]{2,1,0:T(8,128)(2,1)S(1)}, u32[]{:S(2)}, u32[]{:S(2)}) %collective-permute-start.37) | collective-permute-done | bytes 524320 | tf_op jit(solution)/shard_map/ppermute | solution.py:559
  279.2 8.3 %collective-permute-done.41 = bf16[4,160,256]{2,1,0:T(8,128)(2,1)S(1)} collective-permute-done((bf16[4,160,256]{2,1,0:T(8,128)(2,1)S(1)}, bf16[4,160,256]{2,1,0:T(8,128)(2,1)S(1)}, u32[]{:S(2)}, u32[]{:S(2)}) %collective-permute-start.41) | collective-permute-done | bytes 327712 | tf_op jit(solution)/shard_map/ppermute | solution.py:77
  289.7 6.1 %collective-permute-done.45 = bf16[2,160,256]{2,1,0:T(8,128)(2,1)S(1)} collective-permute-done((bf16[2,160,256]{2,1,0:T(8,128)(2,1)S(1)}, bf16[2,160,256]{2,1,0:T(8,128)(2,1)S(1)}, u32[]{:S(2)}, u32[]{:S(2)}) %collective-permute-start.45) | collective-permute-done | bytes 163872 | tf_op jit(solution)/shard_map/ppermute | solution.py:77
  299.1 3.6 collective-permute-done.47
  305.4 5.5 %collective-permute-done.48 = bf16[512,256]{1,0:T(8,128)(2,1)S(1)} collective-permute-done((bf16[512,256]{1,0:T(8,128)(2,1)S(1)}, bf16[512,256]{1,0:T(8,128)(2,1)S(1)}, u32[]{:S(2)}, u32[]{:S(2)}) %collective-permute-start.48) | collective-permute-done | bytes 262176 | tf_op jit(solution)/shard_map/ppermute | solution.py:64
  313.9 5.0 %collective-permute-done.50 = bf16[160,256]{1,0:T(8,128)(2,1)S(1)} collective-permute-done((bf16[160,256]{1,0:T(8,128)(2,1)S(1)}, bf16[160,256]{1,0:T(8,128)(2,1)S(1)}, u32[]{:S(2)}, u32[]{:S(2)}) %collective-permute-start.50) | collective-permute-done | bytes 81952 | tf_op jit(solution)/shard_map/ppermute | solution.py:77
  319.7 4.7 collective-permute-done.52
  324.5 3.3 collective-permute-done.51
  328.6 6.6 %collective-permute-done.56.refs_3_ = bf16[4,160,256]{2,1,0:T(8,128)(2,1)S(1)} collective-permute-done((bf16[4,160,256]{2,1,0:T(8,128)(2,1)S(1)}, bf16[4,160,256]{2,1,0:T(8,128)(2,1)S(1)}, u32[]{:S(2)}, u32[]{:S(2)}) %collective-permute-start.56) | collective-permute-done | bytes 327712 | tf_op jit(solution)/shard_map/ppermute | solution.py:77
  335.2 5.3 %collective-permute-done.55.refs_2_ = bf16[4,352,256]{2,1,0:T(8,128)(2,1)S(1)} collective-permute-done((bf16[4,352,256]{2,1,0:T(8,128)(2,1)S(1)}, bf16[4,352,256]{2,1,0:T(8,128)(2,1)S(1)}, u32[]{:S(2)}, u32[]{:S(2)}) %collective-permute-start.55) | collective-permute-done | bytes 720928 | tf_op jit(solution)/shard_map/ppermute | solution.py:77
  343.1 3.7 shard_map.170
  346.9 3.8 shard_map.171
  350.7 17.2 %all_to_all.21.triple_ref = bf16[4,3,256,128]{3,2,1,0:T(8,128)(2,1)S(1)} all-to-all(bf16[4,3,256,128]{3,2,1,0:T(8,128)(2,1)S(1)} %shard_map.171), channel_id=1, replica_groups=mesh['section'=2,'seq'=4,'z'=2,'y'=4,'core'=2] {'seq'}, dimensions={0} | all-to-all | bytes 1572864 | tf_op jit(solution)/shard_map/all_to_all | solution.py:487
  369.3 9.1 %all_to_all.22.mixed_ref = bf16[4,256,128]{2,1,0:T(8,128)(2,1)S(1)} all-to-all(bf16[4,256,128]{2,1,0:T(8,128)(2,1)S(1)} %shard_map.172), channel_id=1, replica_groups=mesh['section'=2,'seq'=4,'z'=2,'y'=4,'core'=2] {'seq'}, dimensions={0} | all-to-all | bytes 524288 | tf_op jit(solution)/shard_map/all_to_all | solution.py:490
  385.0 8.6 %collective-permute-done.62 = bf16[4,160,256]{2,1,0:T(8,128)(2,1)S(1)} collective-permute-done((bf16[4,160,256]{2,1,0:T(8,128)(2,1)S(1)}, bf16[4,160,256]{2,1,0:T(8,128)(2,1)S(1)}, u32[]{:S(2)}, u32[]{:S(2)}) %collective-permute-start.62) | collective-permute-done | bytes 327712 | tf_op jit(solution)/shard_map/ppermute | solution.py:77
  396.7 5.4 %collective-permute-done.66 = bf16[2,160,256]{2,1,0:T(8,128)(2,1)S(1)} collective-permute-done((bf16[2,160,256]{2,1,0:T(8,128)(2,1)S(1)}, bf16[2,160,256]{2,1,0:T(8,128)(2,1)S(1)}, u32[]{:S(2)}, u32[]{:S(2)}) %collective-permute-start.66) | collective-permute-done | bytes 163872 | tf_op jit(solution)/shard_map/ppermute | solution.py:77
  405.3 4.6 collective-permute-done.68
  412.1 5.4 %collective-permute-done.70 = bf16[160,256]{1,0:T(8,128)(2,1)S(1)} collective-permute-done((bf16[160,256]{1,0:T(8,128)(2,1)S(1)}, bf16[160,256]{1,0:T(8,128)(2,1)S(1)}, u32[]{:S(2)}, u32[]{:S(2)}) %collective-permute-start.70) | collective-permute-done | bytes 81952 | tf_op jit(solution)/shard_map/ppermute | solution.py:77
  418.8 4.2 collective-permute-done.72
  427.4 5.8 %collective-permute-done.76.refs_3_ = bf16[4,160,256]{2,1,0:T(8,128)(2,1)S(1)} collective-permute-done((bf16[4,160,256]{2,1,0:T(8,128)(2,1)S(1)}, bf16[4,160,256]{2,1,0:T(8,128)(2,1)S(1)}, u32[]{:S(2)}, u32[]{:S(2)}) %collective-permute-start.76) | collective-permute-done | bytes 327712 | tf_op jit(solution)/shard_map/ppermute | solution.py:77
  433.2 5.3 %collective-permute-done.75.refs_2_ = bf16[4,352,256]{2,1,0:T(8,128)(2,1)S(1)} collective-permute-done((bf16[4,352,256]{2,1,0:T(8,128)(2,1)S(1)}, bf16[4,352,256]{2,1,0:T(8,128)(2,1)S(1)}, u32[]{:S(2)}, u32[]{:S(2)}) %collective-permute-start.75) | collective-permute-done | bytes 720928 | tf_op jit(solution)/shard_map/ppermute | solution.py:77
  455.1 8.5 %collective-permute-done.82 = bf16[4,160,256]{2,1,0:T(8,128)(2,1)S(1)} collective-permute-done((bf16[4,160,256]{2,1,0:T(8,128)(2,1)S(1)}, bf16[4,160,256]{2,1,0:T(8,128)(2,1)S(1)}, u32[]{:S(2)}, u32[]{:S(2)}) %collective-permute-start.82) | collective-permute-done | bytes 327712 | tf_op jit(solution)/shard_map/ppermute | solution.py:77
  466.9 5.2 %collective-permute-done.86 = bf16[2,160,256]{2,1,0:T(8,128)(2,1)S(1)} collective-permute-done((bf16[2,160,256]{2,1,0:T(8,128)(2,1)S(1)}, bf16[2,160,256]{2,1,0:T(8,128)(2,1)S(1)}, u32[]{:S(2)}, u32[]{:S(2)}) %collective-permute-start.86) | collective-permute-done | bytes 163872 | tf_op jit(solution)/shard_map/ppermute | solution.py:77
  475.4 4.6 collective-permute-done.88
  483.1 3.6 collective-permute-done.89
  (392 shorter events, 160.6 us)
Async XLA Ops:
  6.5 172.8 %all-gather.3.cloned.1.call-start = ((), (), s32[]{:S(2)}) async-start(), calls=%async_computation.4 | async-start | bytes 14483456 | tf_op jit(solution)/shard_map/all_gather | solution.py:390
  11.6 7.8 %collective-permute-start = (bf16[352,256]{1,0:T(8,128)(2,1)S(1)}, bf16[352,256]{1,0:T(8,128)(2,1)S(1)}, u32[]{:S(2)}, u32[]{:S(2)}) collective-permute-start(bf16[352,256]{1,0:T(8,128)(2,1)S(1)} %get-tuple-element.268), channel_id=1, source_target_pairs={{0,8},{1,3},{2,10},{3,1},{4,12},{5,7},{6,14},{7,5},{8,0},{9,11},{1... | collective-permute-start | bytes 540680 | tf_op jit(solution)/shard_map/ppermute | solution.py:77
  19.4 10.8 %collective-permute-start.2 = (bf16[2,352,256]{2,1,0:T(8,128)(2,1)S(1)}, bf16[2,352,256]{2,1,0:T(8,128)(2,1)S(1)}, u32[]{:S(2)}, u32[]{:S(2)}) collective-permute-start(bf16[2,352,256]{2,1,0:T(8,128)(2,1)S(1)} %pad_maximum_fusion.5), channel_id=1, source_target_pairs={{0,2},{1,7},{2,0},{3,5},{4,6},{5,3},{6,4},{7,1},{8,10},{9,15},{10,... | collective-permute-start | bytes 1081352 | tf_op jit(solution)/shard_map/ppermute | solution.py:77
  19.9 8.1 %collective-permute-start.3 = (bf16[2,160,256]{2,1,0:T(8,128)(2,1)S(1)}, bf16[2,160,256]{2,1,0:T(8,128)(2,1)S(1)}, u32[]{:S(2)}, u32[]{:S(2)}) collective-permute-start(bf16[2,160,256]{2,1,0:T(8,128)(2,1)S(1)} %pad_maximum_fusion.14), channel_id=1, source_target_pairs={{0,8},{1,9},{2,10},{3,11},{4,12},{5,13},{6,14},{7,15},{8,0},{9,1},... | collective-permute-start | bytes 491528 | tf_op jit(solution)/shard_map/ppermute | solution.py:77
  31.1 33.1 %collective-permute-start.6 = (bf16[4,352,256]{2,1,0:T(8,128)(2,1)S(1)}, bf16[4,352,256]{2,1,0:T(8,128)(2,1)}, u32[]{:S(2)}, u32[]{:S(2)}) collective-permute-start(bf16[4,352,256]{2,1,0:T(8,128)(2,1)S(1)} %pad_maximum_fusion.1.refs_0_), channel_id=1, source_target_pairs={{0,6},{1,9},{2,4},{3,11},{4,2},{5,13},{6,0},{7,15},{8,14},{9,1},{1... | collective-permute-start | bytes 2162696 | tf_op jit(solution)/shard_map/ppermute | solution.py:77
  46.5 25.8 %collective-permute-start.10 = (bf16[8,64,1024]{2,1,0:T(8,128)(2,1)S(1)}, bf16[8,64,1024]{2,1,0:T(8,128)(2,1)S(1)}, u32[]{:S(2)}, u32[]{:S(2)}) collective-permute-start(bf16[8,64,1024]{2,1,0:T(8,128)(2,1)S(1)} %broadcast_select_fusion), channel_id=1, source_target_pairs={{0,1},{1,0},{2,3},{3,2},{4,5},{5,4},{6,7},{7,6},{8,9},{9,8},{10,11... | collective-permute-start | bytes 3145736 | tf_op jit(solution)/shard_map/ppermute | solution.py:60
  46.6 17.6 %collective-permute-start.7 = (bf16[4,160,256]{2,1,0:T(8,128)(2,1)S(1)}, bf16[4,160,256]{2,1,0:T(8,128)(2,1)}, u32[]{:S(2)}, u32[]{:S(2)}) collective-permute-start(bf16[4,160,256]{2,1,0:T(8,128)(2,1)S(1)} %pad_maximum_fusion.9.refs_1_), channel_id=1, source_target_pairs={{0,2},{1,3},{2,0},{3,1},{4,6},{5,7},{6,4},{7,5},{8,10},{9,11},{10,... | collective-permute-start | bytes 983048 | tf_op jit(solution)/shard_map/ppermute | solution.py:77
  64.2 45.4 %collective-permute-start.8 = (bf16[4,352,256]{2,1,0:T(8,128)(2,1)}, bf16[4,352,256]{2,1,0:T(8,128)(2,1)}, u32[]{:S(2)}, u32[]{:S(2)}) collective-permute-start(bf16[4,352,256]{2,1,0:T(8,128)(2,1)} %collective-permute-done.6.refs_2_), channel_id=1, source_target_pairs={{0,1},{1,0},{2,3},{3,2},{4,5},{5,4},{6,7},{7,6},{8,9},{9,8},{10,11... | collective-permute-start | bytes 2162696 | tf_op jit(solution)/shard_map/ppermute | solution.py:60
  76.4 10.7 %collective-permute-start.11 = (bf16[4,64,1024]{2,1,0:T(8,128)(2,1)}, bf16[4,64,1024]{2,1,0:T(8,128)(2,1)}, u32[]{:S(2)}, u32[]{:S(2)}) collective-permute-start(bf16[4,64,1024]{2,1,0:T(8,128)(2,1)} %slice.246), channel_id=1, source_target_pairs={{0,6},{1,9},{2,4},{3,11},{4,2},{5,13},{6,0},{7,15},{8,14},{9,1},{1... | collective-permute-start | bytes 1572872 | tf_op jit(solution)/shard_map/ppermute | solution.py:77
  78.6 31.0 %collective-permute-start.9 = (bf16[4,160,256]{2,1,0:T(8,128)(2,1)}, bf16[4,160,256]{2,1,0:T(8,128)(2,1)S(1)}, u32[]{:S(2)}, u32[]{:S(2)}) collective-permute-start(bf16[4,160,256]{2,1,0:T(8,128)(2,1)} %collective-permute-done.7.refs_3_), channel_id=1, source_target_pairs={{0,1},{1,0},{2,3},{3,2},{4,5},{5,4},{6,7},{7,6},{8,9},{9,8},{10,11... | collective-permute-start | bytes 983048 | tf_op jit(solution)/shard_map/ppermute | solution.py:60
  89.2 30.7 %collective-permute-start.12 = (bf16[2,64,1024]{2,1,0:T(8,128)(2,1)}, bf16[2,64,1024]{2,1,0:T(8,128)(2,1)}, u32[]{:S(2)}, u32[]{:S(2)}) collective-permute-start(bf16[2,64,1024]{2,1,0:T(8,128)(2,1)} %slice.248), channel_id=1, source_target_pairs={{0,2},{1,7},{2,0},{3,5},{4,6},{5,3},{6,4},{7,1},{8,10},{9,15},{10,... | collective-permute-start | bytes 786440 | tf_op jit(solution)/shard_map/ppermute | solution.py:77
  115.3 16.1 %all-to-all-start = ((bf16[4,3,256,128]{3,2,1,0:T(8,128)(2,1)}), bf16[4,3,256,128]{3,2,1,0:T(8,128)(2,1)S(1)}, u32[]{:S(2)}, u32[]{:S(2)}) async-start(bf16[4,3,256,128]{3,2,1,0:T(8,128)(2,1)} %copy-done.9), calls=%async_computation | async-start | bytes 1572864 | tf_op jit(solution)/shard_map/all_to_all | solution.py:487
  119.9 132.4 %all-gather.5.cloned.1.call-start = ((), (), s32[]{:S(2)}) async-start(), calls=%async_computation.5 | async-start | bytes 4456448 | tf_op jit(solution)/shard_map/all_gather | solution.py:556
  147.5 12.8 %collective-permute-start.16 = (bf16[4,352,256]{2,1,0:T(8,128)(2,1)}, bf16[4,352,256]{2,1,0:T(8,128)(2,1)}, u32[]{:S(2)}, u32[]{:S(2)}) collective-permute-start(bf16[4,352,256]{2,1,0:T(8,128)(2,1)} %add_convert_fusion.3), channel_id=1, source_target_pairs={{0,6},{1,9},{2,4},{3,11},{4,2},{5,13},{6,0},{7,15},{8,14},{9,1},{1... | collective-permute-start | bytes 2162696 | tf_op jit(solution)/shard_map/ppermute | solution.py:77
  149.5 10.4 %collective-permute-start.17 = (bf16[4,160,256]{2,1,0:T(8,128)(2,1)}, bf16[4,160,256]{2,1,0:T(8,128)(2,1)}, u32[]{:S(2)}, u32[]{:S(2)}) collective-permute-start(bf16[4,160,256]{2,1,0:T(8,128)(2,1)} %add_convert_fusion.7), channel_id=1, source_target_pairs={{0,2},{1,3},{2,0},{3,1},{4,6},{5,7},{6,4},{7,5},{8,10},{9,11},{10,... | collective-permute-start | bytes 983048 | tf_op jit(solution)/shard_map/ppermute | solution.py:77
  161.9 8.3 %collective-permute-start.20 = (bf16[2,352,256]{2,1,0:T(8,128)(2,1)S(1)}, bf16[2,352,256]{2,1,0:T(8,128)(2,1)S(1)}, u32[]{:S(2)}, u32[]{:S(2)}) collective-permute-start(bf16[2,352,256]{2,1,0:T(8,128)(2,1)S(1)} %slice.414), channel_id=1, source_target_pairs={{0,2},{1,7},{2,0},{3,5},{4,6},{5,3},{6,4},{7,1},{8,10},{9,15},{10,... | collective-permute-start | bytes 1081352 | tf_op jit(solution)/shard_map/ppermute | solution.py:77
  163.2 7.0 %collective-permute-start.21 = (bf16[2,160,256]{2,1,0:T(8,128)(2,1)S(1)}, bf16[2,160,256]{2,1,0:T(8,128)(2,1)S(1)}, u32[]{:S(2)}, u32[]{:S(2)}) collective-permute-start(bf16[2,160,256]{2,1,0:T(8,128)(2,1)S(1)} %slice.418), channel_id=1, source_target_pairs={{0,8},{1,9},{2,10},{3,11},{4,12},{5,13},{6,14},{7,15},{8,0},{9,1},... | collective-permute-start | bytes 491528 | tf_op jit(solution)/shard_map/ppermute | solution.py:77
  163.8 12.7 %collective-permute-start.24 = (bf16[64,1024]{1,0:T(8,128)(2,1)S(1)}, bf16[64,1024]{1,0:T(8,128)(2,1)S(1)}, u32[]{:S(2)}, u32[]{:S(2)}) collective-permute-start(bf16[64,1024]{1,0:T(8,128)(2,1)S(1)} %copy-done.31), channel_id=1, source_target_pairs={{0,64},{64,0},{1,65},{65,1},{2,66},{66,2},{3,67},{67,3},{4,68},{68... | collective-permute-start | bytes 393224 | tf_op jit(solution)/shard_map/ppermute | solution.py:64
  177.3 19.5 %collective-permute-start.25 = (bf16[352,256]{1,0:T(8,128)(2,1)S(1)}, bf16[352,256]{1,0:T(8,128)(2,1)}, u32[]{:S(2)}, u32[]{:S(2)}) collective-permute-start(bf16[352,256]{1,0:T(8,128)(2,1)S(1)} %fusion.11), channel_id=1, source_target_pairs={{0,8},{1,3},{2,10},{3,1},{4,12},{5,7},{6,14},{7,5},{8,0},{9,11},{1... | collective-permute-start | bytes 540680 | tf_op jit(solution)/shard_map/ppermute | solution.py:77
  186.3 10.5 %collective-permute-start.27 = (bf16[128,1024]{1,0:T(8,128)(2,1)S(1)}, bf16[128,1024]{1,0:T(8,128)(2,1)S(1)}, u32[]{:S(2)}, u32[]{:S(2)}) collective-permute-start(bf16[128,1024]{1,0:T(8,128)(2,1)S(1)} %shard_map.161), channel_id=1, source_target_pairs={{0,64},{64,0},{1,65},{65,1},{2,66},{66,2},{3,67},{67,3},{4,68},{68... | collective-permute-start | bytes 786440 | tf_op jit(solution)/shard_map/ppermute | solution.py:64
  197.8 10.7 %collective-permute-start.28 = (bf16[2,352,256]{2,1,0:T(8,128)(2,1)S(1)}, bf16[2,352,256]{2,1,0:T(8,128)(2,1)S(1)}, u32[]{:S(2)}, u32[]{:S(2)}) collective-permute-start(bf16[2,352,256]{2,1,0:T(8,128)(2,1)S(1)} %pad_maximum_fusion.6), channel_id=1, source_target_pairs={{0,2},{1,7},{2,0},{3,5},{4,6},{5,3},{6,4},{7,1},{8,10},{9,15},{10,... | collective-permute-start | bytes 1081352 | tf_op jit(solution)/shard_map/ppermute | solution.py:77
  199.3 9.2 %collective-permute-start.30 = (bf16[128,1024]{1,0:T(8,128)(2,1)S(1)}, bf16[128,1024]{1,0:T(8,128)(2,1)S(1)}, u32[]{:S(2)}, u32[]{:S(2)}) collective-permute-start(bf16[128,1024]{1,0:T(8,128)(2,1)S(1)} %shard_map.162), channel_id=1, source_target_pairs={{0,64},{64,0},{1,65},{65,1},{2,66},{66,2},{3,67},{67,3},{4,68},{68... | collective-permute-start | bytes 786440 | tf_op jit(solution)/shard_map/ppermute | solution.py:64
  214.8 14.9 %collective-permute-start.33 = (bf16[4,352,256]{2,1,0:T(8,128)(2,1)S(1)}, bf16[4,352,256]{2,1,0:T(8,128)(2,1)S(1)}, u32[]{:S(2)}, u32[]{:S(2)}) collective-permute-start(bf16[4,352,256]{2,1,0:T(8,128)(2,1)S(1)} %pad_maximum_fusion.2.refs_0_), channel_id=1, source_target_pairs={{0,6},{1,9},{2,4},{3,11},{4,2},{5,13},{6,0},{7,15},{8,14},{9,1},{1... | collective-permute-start | bytes 2162696 | tf_op jit(solution)/shard_map/ppermute | solution.py:77
  217.3 12.5 %collective-permute-start.34 = (bf16[4,160,256]{2,1,0:T(8,128)(2,1)S(1)}, bf16[4,160,256]{2,1,0:T(8,128)(2,1)S(1)}, u32[]{:S(2)}, u32[]{:S(2)}) collective-permute-start(bf16[4,160,256]{2,1,0:T(8,128)(2,1)S(1)} %pad_maximum_fusion.10.refs_1_), channel_id=1, source_target_pairs={{0,2},{1,3},{2,0},{3,1},{4,6},{5,7},{6,4},{7,5},{8,10},{9,11},{10,... | collective-permute-start | bytes 983048 | tf_op jit(solution)/shard_map/ppermute | solution.py:77
  254.5 14.8 %collective-permute-start.37 = (bf16[2,256,512]{2,1,0:T(8,128)(2,1)S(1)}, bf16[2,256,512]{2,1,0:T(8,128)(2,1)S(1)}, u32[]{:S(2)}, u32[]{:S(2)}) collective-permute-start(bf16[2,256,512]{2,1,0:T(8,128)(2,1)S(1)} %bitcast.363), channel_id=1, source_target_pairs={{0,16},{16,32},{32,48},{1,17},{17,33},{33,49},{2,18},{18,34},{34,5... | collective-permute-start | bytes 1572872 | tf_op jit(solution)/shard_map/ppermute | solution.py:559
  276.1 12.6 %collective-permute-start.40 = (bf16[4,352,256]{2,1,0:T(8,128)(2,1)S(1)}, bf16[4,352,256]{2,1,0:T(8,128)(2,1)S(1)}, u32[]{:S(2)}, u32[]{:S(2)}) collective-permute-start(bf16[4,352,256]{2,1,0:T(8,128)(2,1)S(1)} %add_convert_fusion.2), channel_id=1, source_target_pairs={{0,6},{1,9},{2,4},{3,11},{4,2},{5,13},{6,0},{7,15},{8,14},{9,1},{1... | collective-permute-start | bytes 2162696 | tf_op jit(solution)/shard_map/ppermute | solution.py:77
  277.3 10.2 %collective-permute-start.41 = (bf16[4,160,256]{2,1,0:T(8,128)(2,1)S(1)}, bf16[4,160,256]{2,1,0:T(8,128)(2,1)S(1)}, u32[]{:S(2)}, u32[]{:S(2)}) collective-permute-start(bf16[4,160,256]{2,1,0:T(8,128)(2,1)S(1)} %add_convert_fusion.6), channel_id=1, source_target_pairs={{0,2},{1,3},{2,0},{3,1},{4,6},{5,7},{6,4},{7,5},{8,10},{9,11},{10,... | collective-permute-start | bytes 983048 | tf_op jit(solution)/shard_map/ppermute | solution.py:77
  289.0 7.5 %collective-permute-start.44 = (bf16[2,352,256]{2,1,0:T(8,128)(2,1)S(1)}, bf16[2,352,256]{2,1,0:T(8,128)(2,1)S(1)}, u32[]{:S(2)}, u32[]{:S(2)}) collective-permute-start(bf16[2,352,256]{2,1,0:T(8,128)(2,1)S(1)} %slice.413), channel_id=1, source_target_pairs={{0,2},{1,7},{2,0},{3,5},{4,6},{5,3},{6,4},{7,1},{8,10},{9,15},{10,... | collective-permute-start | bytes 1081352 | tf_op jit(solution)/shard_map/ppermute | solution.py:77
  289.2 6.7 %collective-permute-start.45 = (bf16[2,160,256]{2,1,0:T(8,128)(2,1)S(1)}, bf16[2,160,256]{2,1,0:T(8,128)(2,1)S(1)}, u32[]{:S(2)}, u32[]{:S(2)}) collective-permute-start(bf16[2,160,256]{2,1,0:T(8,128)(2,1)S(1)} %slice.417), channel_id=1, source_target_pairs={{0,8},{1,9},{2,10},{3,11},{4,12},{5,13},{6,14},{7,15},{8,0},{9,1},... | collective-permute-start | bytes 491528 | tf_op jit(solution)/shard_map/ppermute | solution.py:77
  302.9 8.0 %collective-permute-start.48 = (bf16[512,256]{1,0:T(8,128)(2,1)S(1)}, bf16[512,256]{1,0:T(8,128)(2,1)S(1)}, u32[]{:S(2)}, u32[]{:S(2)}) collective-permute-start(bf16[512,256]{1,0:T(8,128)(2,1)S(1)} %pad_maximum_fusion.13), channel_id=1, source_target_pairs={{0,64},{64,0},{1,65},{65,1},{2,66},{66,2},{3,67},{67,3},{4,68},{68... | collective-permute-start | bytes 786440 | tf_op jit(solution)/shard_map/ppermute | solution.py:64
  310.9 8.0 %collective-permute-start.49 = (bf16[352,256]{1,0:T(8,128)(2,1)S(1)}, bf16[352,256]{1,0:T(8,128)(2,1)S(1)}, u32[]{:S(2)}, u32[]{:S(2)}) collective-permute-start(bf16[352,256]{1,0:T(8,128)(2,1)S(1)} %get-tuple-element.264), channel_id=1, source_target_pairs={{0,8},{1,3},{2,10},{3,1},{4,12},{5,7},{6,14},{7,5},{8,0},{9,11},{1... | collective-permute-start | bytes 540680 | tf_op jit(solution)/shard_map/ppermute | solution.py:77
  318.9 8.9 %collective-permute-start.51 = (bf16[2,352,256]{2,1,0:T(8,128)(2,1)S(1)}, bf16[2,352,256]{2,1,0:T(8,128)(2,1)S(1)}, u32[]{:S(2)}, u32[]{:S(2)}) collective-permute-start(bf16[2,352,256]{2,1,0:T(8,128)(2,1)S(1)} %pad_maximum_fusion.7), channel_id=1, source_target_pairs={{0,2},{1,7},{2,0},{3,5},{4,6},{5,3},{6,4},{7,1},{8,10},{9,15},{10,... | collective-permute-start | bytes 1081352 | tf_op jit(solution)/shard_map/ppermute | solution.py:77
  327.9 12.6 %collective-permute-start.55 = (bf16[4,352,256]{2,1,0:T(8,128)(2,1)S(1)}, bf16[4,352,256]{2,1,0:T(8,128)(2,1)S(1)}, u32[]{:S(2)}, u32[]{:S(2)}) collective-permute-start(bf16[4,352,256]{2,1,0:T(8,128)(2,1)S(1)} %pad_maximum_fusion.3.refs_0_), channel_id=1, source_target_pairs={{0,6},{1,9},{2,4},{3,11},{4,2},{5,13},{6,0},{7,15},{8,14},{9,1},{1... | collective-permute-start | bytes 2162696 | tf_op jit(solution)/shard_map/ppermute | solution.py:77
  328.0 7.2 %collective-permute-start.56 = (bf16[4,160,256]{2,1,0:T(8,128)(2,1)S(1)}, bf16[4,160,256]{2,1,0:T(8,128)(2,1)S(1)}, u32[]{:S(2)}, u32[]{:S(2)}) collective-permute-start(bf16[4,160,256]{2,1,0:T(8,128)(2,1)S(1)} %pad_maximum_fusion.11.refs_1_), channel_id=1, source_target_pairs={{0,2},{1,3},{2,0},{3,1},{4,6},{5,7},{6,4},{7,5},{8,10},{9,11},{10,... | collective-permute-start | bytes 983048 | tf_op jit(solution)/shard_map/ppermute | solution.py:77
  328.6 14.5 %collective-permute-start.53 = (bf16[4,352,256]{2,1,0:T(8,128)(2,1)S(1)}, bf16[4,352,256]{2,1,0:T(8,128)(2,1)S(1)}, u32[]{:S(2)}, u32[]{:S(2)}) collective-permute-start(bf16[4,352,256]{2,1,0:T(8,128)(2,1)S(1)} %pad_maximum_fusion.3.refs_0_), channel_id=1, source_target_pairs={{0,1},{1,0},{2,3},{3,2},{4,5},{5,4},{6,7},{7,6},{8,9},{9,8},{10,11... | collective-permute-start | bytes 2162696 | tf_op jit(solution)/shard_map/ppermute | solution.py:60
  382.4 12.6 %collective-permute-start.61 = (bf16[4,352,256]{2,1,0:T(8,128)(2,1)S(1)}, bf16[4,352,256]{2,1,0:T(8,128)(2,1)S(1)}, u32[]{:S(2)}, u32[]{:S(2)}) collective-permute-start(bf16[4,352,256]{2,1,0:T(8,128)(2,1)S(1)} %add_convert_fusion.1), channel_id=1, source_target_pairs={{0,6},{1,9},{2,4},{3,11},{4,2},{5,13},{6,0},{7,15},{8,14},{9,1},{1... | collective-permute-start | bytes 2162696 | tf_op jit(solution)/shard_map/ppermute | solution.py:77
  383.8 9.7 %collective-permute-start.62 = (bf16[4,160,256]{2,1,0:T(8,128)(2,1)S(1)}, bf16[4,160,256]{2,1,0:T(8,128)(2,1)S(1)}, u32[]{:S(2)}, u32[]{:S(2)}) collective-permute-start(bf16[4,160,256]{2,1,0:T(8,128)(2,1)S(1)} %add_convert_fusion.5), channel_id=1, source_target_pairs={{0,2},{1,3},{2,0},{3,1},{4,6},{5,7},{6,4},{7,5},{8,10},{9,11},{10,... | collective-permute-start | bytes 983048 | tf_op jit(solution)/shard_map/ppermute | solution.py:77
  395.2 7.5 %collective-permute-start.65 = (bf16[2,352,256]{2,1,0:T(8,128)(2,1)S(1)}, bf16[2,352,256]{2,1,0:T(8,128)(2,1)S(1)}, u32[]{:S(2)}, u32[]{:S(2)}) collective-permute-start(bf16[2,352,256]{2,1,0:T(8,128)(2,1)S(1)} %slice.412), channel_id=1, source_target_pairs={{0,2},{1,7},{2,0},{3,5},{4,6},{5,3},{6,4},{7,1},{8,10},{9,15},{10,... | collective-permute-start | bytes 1081352 | tf_op jit(solution)/shard_map/ppermute | solution.py:77
  402.9 7.0 %collective-permute-start.67 = (bf16[352,256]{1,0:T(8,128)(2,1)S(1)}, bf16[352,256]{1,0:T(8,128)(2,1)S(1)}, u32[]{:S(2)}, u32[]{:S(2)}) collective-permute-start(bf16[352,256]{1,0:T(8,128)(2,1)S(1)} %fusion.14), channel_id=1, source_target_pairs={{0,8},{1,3},{2,10},{3,1},{4,12},{5,7},{6,14},{7,5},{8,0},{9,11},{1... | collective-permute-start | bytes 540680 | tf_op jit(solution)/shard_map/ppermute | solution.py:77
  409.9 7.5 %collective-permute-start.69 = (bf16[352,256]{1,0:T(8,128)(2,1)S(1)}, bf16[352,256]{1,0:T(8,128)(2,1)S(1)}, u32[]{:S(2)}, u32[]{:S(2)}) collective-permute-start(bf16[352,256]{1,0:T(8,128)(2,1)S(1)} %fusion.5), channel_id=1, source_target_pairs={{0,8},{1,3},{2,10},{3,1},{4,12},{5,7},{6,14},{7,5},{8,0},{9,11},{1... | collective-permute-start | bytes 540680 | tf_op jit(solution)/shard_map/ppermute | solution.py:77
  417.5 8.3 %collective-permute-start.71 = (bf16[2,352,256]{2,1,0:T(8,128)(2,1)S(1)}, bf16[2,352,256]{2,1,0:T(8,128)(2,1)S(1)}, u32[]{:S(2)}, u32[]{:S(2)}) collective-permute-start(bf16[2,352,256]{2,1,0:T(8,128)(2,1)S(1)} %pad_maximum_fusion.8), channel_id=1, source_target_pairs={{0,2},{1,7},{2,0},{3,5},{4,6},{5,3},{6,4},{7,1},{8,10},{9,15},{10,... | collective-permute-start | bytes 1081352 | tf_op jit(solution)/shard_map/ppermute | solution.py:77
  425.9 12.6 %collective-permute-start.75 = (bf16[4,352,256]{2,1,0:T(8,128)(2,1)S(1)}, bf16[4,352,256]{2,1,0:T(8,128)(2,1)S(1)}, u32[]{:S(2)}, u32[]{:S(2)}) collective-permute-start(bf16[4,352,256]{2,1,0:T(8,128)(2,1)S(1)} %pad_maximum_fusion.4.refs_0_), channel_id=1, source_target_pairs={{0,6},{1,9},{2,4},{3,11},{4,2},{5,13},{6,0},{7,15},{8,14},{9,1},{1... | collective-permute-start | bytes 2162696 | tf_op jit(solution)/shard_map/ppermute | solution.py:77
  426.1 7.2 %collective-permute-start.76 = (bf16[4,160,256]{2,1,0:T(8,128)(2,1)S(1)}, bf16[4,160,256]{2,1,0:T(8,128)(2,1)S(1)}, u32[]{:S(2)}, u32[]{:S(2)}) collective-permute-start(bf16[4,160,256]{2,1,0:T(8,128)(2,1)S(1)} %pad_maximum_fusion.12.refs_1_), channel_id=1, source_target_pairs={{0,2},{1,3},{2,0},{3,1},{4,6},{5,7},{6,4},{7,5},{8,10},{9,11},{10,... | collective-permute-start | bytes 983048 | tf_op jit(solution)/shard_map/ppermute | solution.py:77
  427.1 14.0 %collective-permute-start.73 = (bf16[4,352,256]{2,1,0:T(8,128)(2,1)S(1)}, bf16[4,352,256]{2,1,0:T(8,128)(2,1)S(1)}, u32[]{:S(2)}, u32[]{:S(2)}) collective-permute-start(bf16[4,352,256]{2,1,0:T(8,128)(2,1)S(1)} %pad_maximum_fusion.4.refs_0_), channel_id=1, source_target_pairs={{0,1},{1,0},{2,3},{3,2},{4,5},{5,4},{6,7},{7,6},{8,9},{9,8},{10,11... | collective-permute-start | bytes 2162696 | tf_op jit(solution)/shard_map/ppermute | solution.py:60
  452.3 12.6 %collective-permute-start.81 = (bf16[4,352,256]{2,1,0:T(8,128)(2,1)S(1)}, bf16[4,352,256]{2,1,0:T(8,128)(2,1)S(1)}, u32[]{:S(2)}, u32[]{:S(2)}) collective-permute-start(bf16[4,352,256]{2,1,0:T(8,128)(2,1)S(1)} %add_convert_fusion), channel_id=1, source_target_pairs={{0,6},{1,9},{2,4},{3,11},{4,2},{5,13},{6,0},{7,15},{8,14},{9,1},{1... | collective-permute-start | bytes 2162696 | tf_op jit(solution)/shard_map/ppermute | solution.py:77
  453.9 9.7 %collective-permute-start.82 = (bf16[4,160,256]{2,1,0:T(8,128)(2,1)S(1)}, bf16[4,160,256]{2,1,0:T(8,128)(2,1)S(1)}, u32[]{:S(2)}, u32[]{:S(2)}) collective-permute-start(bf16[4,160,256]{2,1,0:T(8,128)(2,1)S(1)} %add_convert_fusion.4), channel_id=1, source_target_pairs={{0,2},{1,3},{2,0},{3,1},{4,6},{5,7},{6,4},{7,5},{8,10},{9,11},{10,... | collective-permute-start | bytes 983048 | tf_op jit(solution)/shard_map/ppermute | solution.py:77
  465.2 7.5 %collective-permute-start.85 = (bf16[2,352,256]{2,1,0:T(8,128)(2,1)S(1)}, bf16[2,352,256]{2,1,0:T(8,128)(2,1)S(1)}, u32[]{:S(2)}, u32[]{:S(2)}) collective-permute-start(bf16[2,352,256]{2,1,0:T(8,128)(2,1)S(1)} %slice.411), channel_id=1, source_target_pairs={{0,2},{1,7},{2,0},{3,5},{4,6},{5,3},{6,4},{7,1},{8,10},{9,15},{10,... | collective-permute-start | bytes 1081352 | tf_op jit(solution)/shard_map/ppermute | solution.py:77
  472.8 7.3 %collective-permute-start.87 = (bf16[352,256]{1,0:T(8,128)(2,1)S(1)}, bf16[352,256]{1,0:T(8,128)(2,1)S(1)}, u32[]{:S(2)}, u32[]{:S(2)}) collective-permute-start(bf16[352,256]{1,0:T(8,128)(2,1)S(1)} %fusion.15), channel_id=1, source_target_pairs={{0,8},{1,3},{2,10},{3,1},{4,12},{5,7},{6,14},{7,5},{8,0},{9,11},{1... | collective-permute-start | bytes 540680 | tf_op jit(solution)/shard_map/ppermute | solution.py:77
  (90 other events, 615.9 us)
Sparse Core Ops, SparseCore 0:
  11.6 93.6 all-gather.2
  214.9 37.2 all-gather.4

commit v6 on v5

--- a/solution.py
+++ b/solution.py
@@ -43,6 +43,8 @@
 
 PARTS = (352, 160)
 STARTS = (0, 352)
+ENC_PARTS = (80, 48)
+ENC_STARTS = (0, 80)
 MASKS = (((4, 1, 3), (1, 3, 4)), ((3, 4, 1), (3, 4, 1)))
 
 
@@ -103,7 +105,7 @@
     far = [neighbour(value, part, 2) for part, value in enumerate(near)]
     *swaps, side = together(*swaps, side)
     side = beside(2, side)
-    far = list(together(*far))
+    *far, side = together(*far, side)
     return near + far, swaps + [core_swap(value) for value in far], side
 
 
@@ -255,23 +257,26 @@
     )(triple)
 
 
-def crossed_kernel(asked_ref, prev_ref, pairs_ref, out_ref):
+def crossed_kernel(asked_ref, *refs):
+    (prev_refs, pairs_refs), out_ref = (refs[0:2], refs[2:4]), refs[4]
     scaling = HEAD ** (-0.5)
     row = lax.broadcasted_iota(jnp.int32, (BLOCK, 2 * KEYS), 0)
     col = lax.broadcasted_iota(jnp.int32, (BLOCK, 2 * KEYS), 1)
     allowed = (row < BLOCK - 1) == (col < KEYS)
     for unit in range(UNITS):
         b, h = divmod(unit, 2)
-        kcols = slice(h * HEAD, (h + 1) * HEAD)
-        vcols = slice((2 + h) * HEAD, (3 + h) * HEAD)
+
+        def both_blocks(i, cols):
+            before = [ref[b, :, cols] if i == 0 else pair[b, i - 1, :, cols]
+                      for ref, pair in zip(prev_refs, pairs_refs)]
+            return jnp.concatenate(before + [pair[b, i, :, cols] for pair in pairs_refs], axis=0)
+
         for i in range(ROWS // BLOCK):
-            queries = asked_ref[b * ROWS + i * BLOCK : b * ROWS + (i + 1) * BLOCK, kcols]
-            if i == 0:
-                keys = jnp.concatenate([prev_ref[b, :, kcols], pairs_ref[b, 0, :, kcols]], axis=0)
-                values = jnp.concatenate([prev_ref[b, :, vcols], pairs_ref[b, 0, :, vcols]], axis=0)
-            else:
-                keys = pairs_ref[b, i - 1 : i + 1, :, kcols].reshape(2 * KEYS, HEAD)
-                values = pairs_ref[b, i - 1 : i + 1, :, vcols].reshape(2 * KEYS, HEAD)
+            queries = asked_ref[
+                b * ROWS + i * BLOCK : b * ROWS + (i + 1) * BLOCK, h * HEAD : (h + 1) * HEAD
+            ]
+            keys = both_blocks(i, slice(h * HEAD, (h + 1) * HEAD))
+            values = both_blocks(i, slice((2 + h) * HEAD, (3 + h) * HEAD))
             scores = lax.dot_general(
                 queries, keys, (((1,), (1,)), ((), ())), preferred_element_type=f32
             )
@@ -281,13 +286,13 @@
             out_ref[unit, i * BLOCK : (i + 1) * BLOCK, :] = (numer / denom).astype(bf16)
 
 
-def cross(asked, prev, pairs):
+def cross(asked, prevs, pairs):
     out = (UNITS, ROWS, HEAD)
     return pl.pallas_call(
         crossed_kernel,
         out_shape=jax.ShapeDtypeStruct(out, bf16),
         compiler_params=params(),
-    )(asked, prev, pairs)
+    )(asked, *prevs, *pairs)
 
 
 def terms_kernel(place_ref, mixed_ref, *refs):
@@ -356,8 +361,11 @@
         found = jnp.where(inside[:, None], found, jnp.zeros((), bf16))
         return found.reshape(CHIPS, NB_LEN // 2, ENC_D)
 
-    far = core_swap(rows(places_both[1]))
-    total = rows(places_both[0]) + far
+    return rows(places_both[0]), rows(places_both[1])
+
+
+def looked_up(own, other):
+    total = own + core_swap(other)
     total = total[:4] + neighbour(total[4:], 0, 2)
     total = total[:2] + neighbour(total[2:], 0, 1)
     return total[0] + neighbour(total[1], 0, 0)
@@ -370,7 +378,7 @@
     )
 
 
-def weight_pieces(section, enc_qkv, enc_out, enc_up, enc_down):
+def weight_parts(section, enc_qkv, enc_out, enc_up, enc_down):
     width = ENC_D // 2
     triple = lax.dynamic_slice_in_dim(enc_qkv, section * width, width, axis=2)
     up = enc_up.reshape(64, 16, 2, 2, 64)
@@ -378,7 +386,7 @@
     up = jnp.transpose(up, (2, 0, 1, 3)).reshape(2, 64, 2, width)
     down = lax.dynamic_slice_in_dim(enc_down, section * 128, 128, axis=0)
     down = down.reshape(2, 64, 2, width)
-    local = jnp.concatenate(
+    return jnp.concatenate(
         [
             jnp.transpose(up, (0, 2, 1, 3)).reshape(4, 64, width),
             jnp.transpose(down, (0, 2, 1, 3)).reshape(4, 64, width),
@@ -387,7 +395,6 @@
         ],
         axis=0,
     )
-    return lax.all_gather(local, MP, axis=1, tiled=True)
 
 
 def scaled_rows(values, gain):
@@ -479,23 +486,65 @@
     return (inner.astype(f32) + (fed.astype(f32) + far.astype(f32))).astype(bf16)
 
 
+def pairs_kernel(place_ref, *refs):
+    x_refs, (w_ref, out_ref, left_ref) = refs[:4], refs[4:]
+    for part in range(2):
+        for block in range(CHIPS):
+            chip = place_ref[1 + part * CHIPS + block]
+            start = pl.multiple_of(chip * NB_LEN + ENC_STARTS[part], 16)
+            value = x_refs[part + 2 * (block // 4)][block % 4]
+            left_ref[pl.ds(start, ENC_PARTS[part]), :] = value
+    out_ref[...] = jnp.dot(left_ref[...], w_ref[...], preferred_element_type=f32).astype(bf16)
+
+
+def make_pairs(place, rows, weight):
+    out = (CHIPS * NB_LEN, 2 * WIDTH)
+    pairs = pl.pallas_call(
+        pairs_kernel,
+        grid_spec=pltpu.PrefetchScalarGridSpec(
+            num_scalar_prefetch=1,
+            grid=(1,),
+            in_specs=[whole(value.shape) for value in rows] + [whole(weight.shape)],
+            out_specs=whole(out),
+            scratch_shapes=[pltpu.VMEM((CHIPS * NB_LEN, ENC_D), bf16)],
+        ),
+        out_shape=jax.ShapeDtypeStruct(out, bf16),
+        compiler_params=params(20),
+        cost_estimate=pl.CostEstimate(
+            flops=2 * CHIPS * NB_LEN * ENC_D * 2 * WIDTH,
+            bytes_accessed=2 * (CHIPS * NB_LEN + 2 * WIDTH) * ENC_D,
+            transcendentals=0,
+        ),
+    )(place, *rows, weight)
+    pairs = pairs.reshape(BATCH, CHIPS // BATCH, NB_LEN, 2 * WIDTH)
+    count = lax.axis_size("seq")
+    prev = lax.ppermute(pairs[:, -1], "seq", [(i, i + 1) for i in range(count - 1)])
+    return prev, pairs
+
+
 def decoder_layer(places_both, states, weights, encoder=None):
     norms, triple_w, out_w, query_w, back_w = weights
     idle = encoder is None
     first = nothing if idle else encoder.first
-    triple, half = project(places_both, states, norms[0], triple_w, True, first)
-    triple = lax.all_to_all(triple, "seq", 0, 0, tiled=True)
-    triple, half = together(triple, half)
-    embedded = half if idle else encoder.join(half)
+    triple, side = project(places_both, states, norms[0], triple_w, True, first)
+    if idle:
+        triple = lax.all_to_all(triple, "seq", 0, 0, tiled=True)
+        embedded = ()
+    else:
+        found, local = side
+        pieces = encoder.gather(local)
+        triple, found = together(triple, found)
+        triple = lax.all_to_all(triple, "seq", 0, 0, tiled=True)
+        triple, half = together(triple, looked_up(*found))
+        embedded = encoder.join(half)
     mixed = lax.all_to_all(causal(triple), "seq", 0, 0, tiled=True)
     middle, embedded = add_product(places_both, states, mixed, out_w, embedded)
 
     def second(turn, side):
-        return side if idle else encoder.second(turn, embedded if turn == 0 else side)
-
-    asked, pairs = project(places_both, middle, norms[1], query_w[None], False, second)
-    pairs = None if idle else pairs
-    return middle, asked, pairs
+        return side if idle else encoder.second(turn, embedded if turn == 0 else side, pieces)
+
+    asked, encoded = project(places_both, middle, norms[1], query_w[None], False, second)
+    return middle, asked, None if idle else encoder.pairs(encoded)
 
 
 def cross_layer(places_both, middle, asked, pairs, weights):
@@ -524,15 +573,10 @@
     core_at = lax.axis_index("core").astype(jnp.int32)
     chip = lax.axis_index(("z", "y")).astype(jnp.int32)
     places_both = [places(chip, core_at), places(chip, 1 - core_at)]
-    blocks_here = neighbour_table.shape[1]
-    pieces = weight_pieces(section, enc_qkv, enc_out, enc_up, enc_down)
+    local = weight_parts(section, enc_qkv, enc_out, enc_up, enc_down)
     slot_ids = neighbour_ids[neighbour_table.reshape(-1)]
-    count = lax.axis_size("seq")
     pair_w = cross_pair[0].reshape(ENC_D, 2 * WIDTH)
     section_ref = jnp.reshape(section, (1,))
-
-    def pair_rows(rows):
-        return jnp.dot(rows, pair_w, preferred_element_type=f32).astype(bf16)
 
     class Encoder:
         @staticmethod
@@ -541,23 +585,32 @@
                 return slot_ids
             if turn == 1:
                 return side
-            return look_up(side, enc_embed, places_both, section)
+            return look_up(side, enc_embed, places_both, section), local
+
+        @staticmethod
+        def gather(local):
+            return lax.all_gather(local, MP, axis=1, tiled=True)
 
         @staticmethod
         def join(half):
             return join_halves(half, section)
 
         @staticmethod
-        def second(turn, side):
+        def second(turn, side, pieces):
             if turn == 0:
                 return encode_mix(side, enc_norms, pieces, section_ref)
             if turn == 1:
                 return encode_feed(*side, enc_norms, pieces)
-            encoded = lax.all_gather(encode_end(*side), MP, axis=0, tiled=True)
-            edge = encoded.reshape(BATCH, blocks_here, KEYS, ENC_D)[:, -1]
-            edge = pair_rows(edge.reshape(BATCH * KEYS, ENC_D)).reshape(BATCH, KEYS, 2 * WIDTH)
-            prev = lax.ppermute(edge, "seq", [(i, i + 1) for i in range(count - 1)])
-            return prev, pair_rows(encoded).reshape(BATCH, blocks_here, KEYS, 2 * WIDTH)
+            return encode_end(*side)
+
+        @staticmethod
+        def pairs(encoded):
+            parts = [
+                encoded[start : start + count] for start, count in zip(ENC_STARTS, ENC_PARTS)
+            ]
+            both = gather_chips(parts, nothing)[:2]
+            made = [make_pairs(place, rows, pair_w) for place, rows in zip(places_both, both)]
+            return [prev for prev, _ in made], [pairs for _, pairs in made]
 
     weights = (
         dec_norms[0],

time: 504 us -> 487 us (0.966)
  waiting for transfers between devices: 232 us -> 196 us
  starting transfers between devices: 94.6 us -> 114 us
    ppermute x51 -> x57, starting transfers between devices: 60.2 us -> 82.2 us  [neighbour(): return lax.ppermute(value, MP, route)]
    all_gather x2 -> x1, waiting for transfers between devices: 14.3 us -> 0.01 us  [gather(): return lax.all_gather(local, MP, axis=1, tiled=True)]
    ppermute x51 -> x57, waiting for transfers between devices: 184 us -> 171 us  [neighbour(): return lax.ppermute(value, MP, route)]
    ppermute x1 -> x2, waiting for transfers between devices: 8.95 us -> 3.13 us  [make_pairs(): lax.ppermute(pairs[:, -1], 'seq', [(i, i + 1) for i in range(count - 1)])]
    unnamed x92 -> x60, local copies, waits for them, and re-layouts: 18.1 us -> 15.4 us
  transfers between devices with their start and end apart: 93 -> 103, of which waited for: 49 -> 50; matrix products, arithmetic and copies ran while one was open for 7% -> 8% of each run, Pallas kernels for 8% -> 9%
where the time goes in v6:
time: 487 us; the launch traced here: 479 us
  waiting for transfers between devices  196 us (40%)
  starting transfers between devices  114 us (23%)
  Pallas kernels  56.5 us (12%)
  local copies, waits for them, and re-layouts  39.5 us (8%)
  blocking collectives  36.5 us (7%)
  other arithmetic  20.9 us (4%)
  between operations  15.1 us (3%)
    ppermute x57, waiting for transfers between devices, neighbour(): return lax.ppermute(value, MP, route)  171 us
    ppermute x57, starting transfers between devices, neighbour(): return lax.ppermute(value, MP, route)  82.2 us
    pallas_call x8, Pallas kernels, project_half(): pl.pallas_call(functools.partial(project_kernel, last, units), grid_spec=...  24.2 us
    all_to_all x2, blocking collectives, decoder_layer(): mixed = lax.all_to_all(causal(triple), 'seq', 0, 0, tiled=True)  19.7 us
    pallas_call x16, Pallas kernels, terms(): pl.pallas_call(terms_kernel, grid_spec=pltpu.PrefetchScalarGridSpec(num_s...  16.8 us
    all_to_all x1, blocking collectives, decoder_layer(): triple = lax.all_to_all(triple, 'seq', 0, 0, tiled=True)  16.8 us
    gather x2, local copies, waits for them, and re-layouts, rows(): found = enc_embed[jnp.clip(picks, 0, vocab_here - 1)]  15.7 us
    unnamed x60, local copies, waits for them, and re-layouts  15.4 us
  transfers between devices with their start and end apart: 103, of which 50 were waited for; matrix products, arithmetic and copies ran while one was open for 8% of the time, Pallas kernels for 9%

profile of v6, /device:TPU:0, one launch (start us, length us, event | category | flops | bytes accessed | tf_op | source)
XLA Modules:
  0.0 478.8 jit_solution(12334231813900248642)
XLA Ops:
  19.6 3.6 collective-permute-done.3
  33.3 7.8 %gather_fusion.2 = bf16[512,1024]{1,0:T(8,128)(2,1)} fusion(bf16[4000,1024]{1,0:T(8,128)(2,1)} %param.19, s32[1024]{0:T(1024)S(1)} %pad_clamp_fusion.2), kind=kCustom, calls=%fused_computation.2 | custom fusion | bytes 2099200 | tf_op jit(solution)/shard_map/gather | solution.py:360
  43.5 7.8 %gather_fusion.4 = bf16[512,1024]{1,0:T(8,128)(2,1)} fusion(bf16[4000,1024]{1,0:T(8,128)(2,1)} %param.19, s32[1024]{0:T(1024)S(1)} %pad_clamp_fusion), kind=kCustom, calls=%fused_computation.4 | custom fusion | bytes 2099200 | tf_op jit(solution)/shard_map/gather | solution.py:360
  59.6 3.7 shard_map.154
  63.4 3.3 copy-done.7
  66.7 4.4 shard_map.155
  75.2 9.6 %collective-permute-done.11 = bf16[4,64,1024]{2,1,0:T(8,128)(2,1)S(1)} collective-permute-done((bf16[4,64,1024]{2,1,0:T(8,128)(2,1)S(1)}, bf16[4,64,1024]{2,1,0:T(8,128)(2,1)S(1)}, u32[]{:S(2)}, u32[]{:S(2)}) %collective-permute-start.11) | collective-permute-done | bytes 524320 | tf_op jit(solution)/shard_map/ppermute | solution.py:79
  85.7 14.8 %collective-permute-start.12 = (bf16[2,64,1024]{2,1,0:T(8,128)(2,1)S(1)}, bf16[2,64,1024]{2,1,0:T(8,128)(2,1)}, u32[]{:S(2)}, u32[]{:S(2)}) collective-permute-start(bf16[2,64,1024]{2,1,0:T(8,128)(2,1)S(1)} %slice.260), channel_id=1, source_target_pairs={{0,2},{1,7},{2,0},{3,5},{4,6},{5,3},{6,4},{7,1},{8,10},{9,15},{10,... | collective-permute-start | bytes 786440 | tf_op jit(solution)/shard_map/ppermute | solution.py:79
  100.5 4.3 all-to-all-start
  104.8 6.5 %collective-permute-done.12 = bf16[2,64,1024]{2,1,0:T(8,128)(2,1)} collective-permute-done((bf16[2,64,1024]{2,1,0:T(8,128)(2,1)S(1)}, bf16[2,64,1024]{2,1,0:T(8,128)(2,1)}, u32[]{:S(2)}, u32[]{:S(2)}) %collective-permute-start.12) | collective-permute-done | bytes 262176 | tf_op jit(solution)/shard_map/ppermute | solution.py:79
  112.6 7.7 %collective-permute-done.13 = bf16[64,1024]{1,0:T(8,128)(2,1)S(1)} collective-permute-done((bf16[64,1024]{1,0:T(8,128)(2,1)S(1)}, bf16[64,1024]{1,0:T(8,128)(2,1)S(1)}, u32[]{:S(2)}, u32[]{:S(2)}) %collective-permute-start.13) | collective-permute-done | bytes 131104 | tf_op jit(solution)/shard_map/ppermute | solution.py:79
  121.7 10.7 %all_to_all.20.mixed_ref = bf16[4,256,128]{2,1,0:T(8,128)(2,1)S(1)} all-to-all(bf16[4,256,128]{2,1,0:T(8,128)(2,1)S(1)} %shard_map.156), channel_id=1, replica_groups=mesh['section'=2,'seq'=4,'z'=2,'y'=4,'core'=2] {'seq'}, dimensions={0} | all-to-all | bytes 524288 | tf_op jit(solution)/shard_map/all_to_all | solution.py:540
  141.2 9.3 %collective-permute-done.17 = bf16[4,160,256]{2,1,0:T(8,128)(2,1)} collective-permute-done((bf16[4,160,256]{2,1,0:T(8,128)(2,1)}, bf16[4,160,256]{2,1,0:T(8,128)(2,1)}, u32[]{:S(2)}, u32[]{:S(2)}) %collective-permute-start.17) | collective-permute-done | bytes 327712 | tf_op jit(solution)/shard_map/ppermute | solution.py:79
  154.1 4.2 collective-permute-start.24
  169.0 4.9 %copy-done.4 = bf16[13,1024,512]{2,1,0:T(8,128)(2,1)S(1)} copy-done((bf16[13,1024,512]{2,1,0:T(8,128)(2,1)S(1)}, bf16[13,1024,512]{2,1,0:T(8,128)(2,1)}, u32[]{:S(2)}) %copy-start.4) | copy-done | bytes 13631512
  176.0 3.7 collective-permute-start.27
  181.9 3.6 collective-permute-done.26
  191.3 6.0 %collective-permute-done.29 = bf16[2,160,256]{2,1,0:T(8,128)(2,1)S(1)} collective-permute-done((bf16[2,160,256]{2,1,0:T(8,128)(2,1)S(1)}, bf16[2,160,256]{2,1,0:T(8,128)(2,1)S(1)}, u32[]{:S(2)}, u32[]{:S(2)}) %collective-permute-start.29) | collective-permute-done | bytes 163872 | tf_op jit(solution)/shard_map/ppermute | solution.py:79
  202.7 8.4 %collective-permute-done.34.refs_3_ = bf16[4,160,256]{2,1,0:T(8,128)(2,1)S(1)} collective-permute-done((bf16[4,160,256]{2,1,0:T(8,128)(2,1)S(1)}, bf16[4,160,256]{2,1,0:T(8,128)(2,1)S(1)}, u32[]{:S(2)}, u32[]{:S(2)}) %collective-permute-start.34) | collective-permute-done | bytes 327712 | tf_op jit(solution)/shard_map/ppermute | solution.py:79
  215.4 3.6 collective-permute-done.38
  219.4 5.4 %collective-permute-done.40 = bf16[2,48,1024]{2,1,0:T(8,128)(2,1)S(1)} collective-permute-done((bf16[2,48,1024]{2,1,0:T(8,128)(2,1)S(1)}, bf16[2,48,1024]{2,1,0:T(8,128)(2,1)S(1)}, u32[]{:S(2)}, u32[]{:S(2)}) %collective-permute-start.40) | collective-permute-done | bytes 196640 | tf_op jit(solution)/shard_map/ppermute | solution.py:79
  230.5 5.9 %collective-permute-done.42.refs_3_ = bf16[4,48,1024]{2,1,0:T(8,128)(2,1)S(1)} collective-permute-done((bf16[4,48,1024]{2,1,0:T(8,128)(2,1)S(1)}, bf16[4,48,1024]{2,1,0:T(8,128)(2,1)S(1)}, u32[]{:S(2)}, u32[]{:S(2)}) %collective-permute-start.42) | collective-permute-done | bytes 393248 | tf_op jit(solution)/shard_map/ppermute | solution.py:79
  252.8 3.1 collective-permute-done.48.refs_1_
  266.8 8.4 %collective-permute-done.52 = bf16[4,160,256]{2,1,0:T(8,128)(2,1)S(1)} collective-permute-done((bf16[4,160,256]{2,1,0:T(8,128)(2,1)S(1)}, bf16[4,160,256]{2,1,0:T(8,128)(2,1)S(1)}, u32[]{:S(2)}, u32[]{:S(2)}) %collective-permute-start.52) | collective-permute-done | bytes 327712 | tf_op jit(solution)/shard_map/ppermute | solution.py:79
  276.6 5.9 %collective-permute-done.56 = bf16[2,160,256]{2,1,0:T(8,128)(2,1)S(1)} collective-permute-done((bf16[2,160,256]{2,1,0:T(8,128)(2,1)S(1)}, bf16[2,160,256]{2,1,0:T(8,128)(2,1)S(1)}, u32[]{:S(2)}, u32[]{:S(2)}) %collective-permute-start.56) | collective-permute-done | bytes 163872 | tf_op jit(solution)/shard_map/ppermute | solution.py:79
  285.9 3.5 collective-permute-done.58
  291.4 6.3 %collective-permute-done.59 = bf16[512,256]{1,0:T(8,128)(2,1)S(1)} collective-permute-done((bf16[512,256]{1,0:T(8,128)(2,1)S(1)}, bf16[512,256]{1,0:T(8,128)(2,1)S(1)}, u32[]{:S(2)}, u32[]{:S(2)}) %collective-permute-start.59) | collective-permute-done | bytes 262176 | tf_op jit(solution)/shard_map/ppermute | solution.py:66
  301.6 3.5 collective-permute-done.61
  307.0 3.6 collective-permute-done.63
  312.7 3.8 collective-permute-start.66
  317.2 6.9 %collective-permute-done.67.refs_3_ = bf16[4,160,256]{2,1,0:T(8,128)(2,1)S(1)} collective-permute-done((bf16[4,160,256]{2,1,0:T(8,128)(2,1)S(1)}, bf16[4,160,256]{2,1,0:T(8,128)(2,1)S(1)}, u32[]{:S(2)}, u32[]{:S(2)}) %collective-permute-start.67) | collective-permute-done | bytes 327712 | tf_op jit(solution)/shard_map/ppermute | solution.py:79
  328.4 3.7 shard_map.172
  332.2 3.8 shard_map.173
  336.0 16.8 %all_to_all.21.triple_ref = bf16[4,3,256,128]{3,2,1,0:T(8,128)(2,1)S(1)} all-to-all(bf16[4,3,256,128]{3,2,1,0:T(8,128)(2,1)S(1)} %shard_map.173), channel_id=1, replica_groups=mesh['section'=2,'seq'=4,'z'=2,'y'=4,'core'=2] {'seq'}, dimensions={0} | all-to-all | bytes 1572864 | tf_op jit(solution)/shard_map/all_to_all | solution.py:531
  354.2 9.1 %all_to_all.22.mixed_ref = bf16[4,256,128]{2,1,0:T(8,128)(2,1)S(1)} all-to-all(bf16[4,256,128]{2,1,0:T(8,128)(2,1)S(1)} %shard_map.174), channel_id=1, replica_groups=mesh['section'=2,'seq'=4,'z'=2,'y'=4,'core'=2] {'seq'}, dimensions={0} | all-to-all | bytes 524288 | tf_op jit(solution)/shard_map/all_to_all | solution.py:540
  367.2 3.3 collective-permute-start.72
  372.2 8.7 %collective-permute-done.73 = bf16[4,160,256]{2,1,0:T(8,128)(2,1)S(1)} collective-permute-done((bf16[4,160,256]{2,1,0:T(8,128)(2,1)S(1)}, bf16[4,160,256]{2,1,0:T(8,128)(2,1)S(1)}, u32[]{:S(2)}, u32[]{:S(2)}) %collective-permute-start.73) | collective-permute-done | bytes 327712 | tf_op jit(solution)/shard_map/ppermute | solution.py:79
  381.7 6.1 %collective-permute-done.77 = bf16[2,160,256]{2,1,0:T(8,128)(2,1)S(1)} collective-permute-done((bf16[2,160,256]{2,1,0:T(8,128)(2,1)S(1)}, bf16[2,160,256]{2,1,0:T(8,128)(2,1)S(1)}, u32[]{:S(2)}, u32[]{:S(2)}) %collective-permute-start.77) | collective-permute-done | bytes 163872 | tf_op jit(solution)/shard_map/ppermute | solution.py:79
  391.2 3.4 collective-permute-done.79
  399.1 3.4 collective-permute-done.81
  403.5 4.8 collective-permute-done.83
  410.5 3.5 collective-permute-start.86
  414.2 6.9 %collective-permute-done.87.refs_3_ = bf16[4,160,256]{2,1,0:T(8,128)(2,1)S(1)} collective-permute-done((bf16[4,160,256]{2,1,0:T(8,128)(2,1)S(1)}, bf16[4,160,256]{2,1,0:T(8,128)(2,1)S(1)}, u32[]{:S(2)}, u32[]{:S(2)}) %collective-permute-start.87) | collective-permute-done | bytes 327712 | tf_op jit(solution)/shard_map/ppermute | solution.py:79
  437.0 3.3 collective-permute-start.92
  442.0 8.7 %collective-permute-done.93 = bf16[4,160,256]{2,1,0:T(8,128)(2,1)S(1)} collective-permute-done((bf16[4,160,256]{2,1,0:T(8,128)(2,1)S(1)}, bf16[4,160,256]{2,1,0:T(8,128)(2,1)S(1)}, u32[]{:S(2)}, u32[]{:S(2)}) %collective-permute-start.93) | collective-permute-done | bytes 327712 | tf_op jit(solution)/shard_map/ppermute | solution.py:79
  451.5 6.0 %collective-permute-done.97 = bf16[2,160,256]{2,1,0:T(8,128)(2,1)S(1)} collective-permute-done((bf16[2,160,256]{2,1,0:T(8,128)(2,1)S(1)}, bf16[2,160,256]{2,1,0:T(8,128)(2,1)S(1)}, u32[]{:S(2)}, u32[]{:S(2)}) %collective-permute-start.97) | collective-permute-done | bytes 163872 | tf_op jit(solution)/shard_map/ppermute | solution.py:79
  461.0 3.5 collective-permute-done.99
  467.0 4.1 collective-permute-done.100
  (386 shorter events, 180.4 us)
Async XLA Ops:
  6.5 162.5 %all-gather.2.cloned.1.call-start = ((), (), s32[]{:S(2)}) async-start(), calls=%async_computation.4 | async-start | bytes 14483456 | tf_op jit(solution)/shard_map/all_gather | solution.py:592
  7.6 9.7 %collective-permute-start = (bf16[352,256]{1,0:T(8,128)(2,1)S(1)}, bf16[352,256]{1,0:T(8,128)(2,1)S(1)}, u32[]{:S(2)}, u32[]{:S(2)}) collective-permute-start(bf16[352,256]{1,0:T(8,128)(2,1)S(1)} %get-tuple-element.302), channel_id=1, source_target_pairs={{0,8},{1,3},{2,10},{3,1},{4,12},{5,7},{6,14},{7,5},{8,0},{9,11},{1... | collective-permute-start | bytes 540680 | tf_op jit(solution)/shard_map/ppermute | solution.py:79
  17.3 7.6 %collective-permute-start.2 = (bf16[2,352,256]{2,1,0:T(8,128)(2,1)S(1)}, bf16[2,352,256]{2,1,0:T(8,128)(2,1)}, u32[]{:S(2)}, u32[]{:S(2)}) collective-permute-start(bf16[2,352,256]{2,1,0:T(8,128)(2,1)S(1)} %pad_maximum_fusion.7), channel_id=1, source_target_pairs={{0,2},{1,7},{2,0},{3,5},{4,6},{5,3},{6,4},{7,1},{8,10},{9,15},{10,... | collective-permute-start | bytes 1081352 | tf_op jit(solution)/shard_map/ppermute | solution.py:79
  29.8 23.9 %collective-permute-start.6 = (bf16[4,352,256]{2,1,0:T(8,128)(2,1)S(1)}, bf16[4,352,256]{2,1,0:T(8,128)(2,1)S(1)}, u32[]{:S(2)}, u32[]{:S(2)}) collective-permute-start(bf16[4,352,256]{2,1,0:T(8,128)(2,1)S(1)} %pad_maximum_fusion.1.refs_0_), channel_id=1, source_target_pairs={{0,6},{1,9},{2,4},{3,11},{4,2},{5,13},{6,0},{7,15},{8,14},{9,1},{1... | collective-permute-start | bytes 2162696 | tf_op jit(solution)/shard_map/ppermute | solution.py:79
  31.9 21.8 %collective-permute-start.7 = (bf16[4,160,256]{2,1,0:T(8,128)(2,1)S(1)}, bf16[4,160,256]{2,1,0:T(8,128)(2,1)S(1)}, u32[]{:S(2)}, u32[]{:S(2)}) collective-permute-start(bf16[4,160,256]{2,1,0:T(8,128)(2,1)S(1)} %pad_maximum_fusion.11.refs_1_), channel_id=1, source_target_pairs={{0,2},{1,3},{2,0},{3,1},{4,6},{5,7},{6,4},{7,5},{8,10},{9,11},{10,... | collective-permute-start | bytes 983048 | tf_op jit(solution)/shard_map/ppermute | solution.py:79
  54.5 8.9 %collective-permute-start.8 = (bf16[4,352,256]{2,1,0:T(8,128)(2,1)S(1)}, bf16[4,352,256]{2,1,0:T(8,128)(2,1)S(1)}, u32[]{:S(2)}, u32[]{:S(2)}) collective-permute-start(bf16[4,352,256]{2,1,0:T(8,128)(2,1)S(1)} %collective-permute-done.6.refs_2_), channel_id=1, source_target_pairs={{0,1},{1,0},{2,3},{3,2},{4,5},{5,4},{6,7},{7,6},{8,9},{9,8},{10,11... | collective-permute-start | bytes 2162696 | tf_op jit(solution)/shard_map/ppermute | solution.py:62
  54.8 8.6 %collective-permute-start.9 = (bf16[4,160,256]{2,1,0:T(8,128)(2,1)}, bf16[4,160,256]{2,1,0:T(8,128)(2,1)S(1)}, u32[]{:S(2)}, u32[]{:S(2)}) collective-permute-start(bf16[4,160,256]{2,1,0:T(8,128)(2,1)} %copy-done.11), channel_id=1, source_target_pairs={{0,1},{1,0},{2,3},{3,2},{4,5},{5,4},{6,7},{7,6},{8,9},{9,8},{10,11... | collective-permute-start | bytes 983048 | tf_op jit(solution)/shard_map/ppermute | solution.py:62
  74.3 10.5 %collective-permute-start.11 = (bf16[4,64,1024]{2,1,0:T(8,128)(2,1)S(1)}, bf16[4,64,1024]{2,1,0:T(8,128)(2,1)S(1)}, u32[]{:S(2)}, u32[]{:S(2)}) collective-permute-start(bf16[4,64,1024]{2,1,0:T(8,128)(2,1)S(1)} %slice.258), channel_id=1, source_target_pairs={{0,6},{1,9},{2,4},{3,11},{4,2},{5,13},{6,0},{7,15},{8,14},{9,1},{1... | collective-permute-start | bytes 1572872 | tf_op jit(solution)/shard_map/ppermute | solution.py:79
  85.7 25.7 %collective-permute-start.12 = (bf16[2,64,1024]{2,1,0:T(8,128)(2,1)S(1)}, bf16[2,64,1024]{2,1,0:T(8,128)(2,1)}, u32[]{:S(2)}, u32[]{:S(2)}) collective-permute-start(bf16[2,64,1024]{2,1,0:T(8,128)(2,1)S(1)} %slice.260), channel_id=1, source_target_pairs={{0,2},{1,7},{2,0},{3,5},{4,6},{5,3},{6,4},{7,1},{8,10},{9,15},{10,... | collective-permute-start | bytes 786440 | tf_op jit(solution)/shard_map/ppermute | solution.py:79
  100.5 19.8 %all-to-all-start = ((bf16[4,3,256,128]{3,2,1,0:T(8,128)(2,1)}), bf16[4,3,256,128]{3,2,1,0:T(8,128)(2,1)S(1)}, u32[]{:S(2)}, u32[]{:S(2)}) async-start(bf16[4,3,256,128]{3,2,1,0:T(8,128)(2,1)} %shard_map.155), calls=%async_computation | async-start | bytes 1572864 | tf_op jit(solution)/shard_map/all_to_all | solution.py:537
  112.5 7.8 %collective-permute-start.13 = (bf16[64,1024]{1,0:T(8,128)(2,1)S(1)}, bf16[64,1024]{1,0:T(8,128)(2,1)S(1)}, u32[]{:S(2)}, u32[]{:S(2)}) collective-permute-start(bf16[64,1024]{1,0:T(8,128)(2,1)S(1)} %slice_bitcast_fusion.10), channel_id=1, source_target_pairs={{0,8},{1,3},{2,10},{3,1},{4,12},{5,7},{6,14},{7,5},{8,0},{9,11},{1... | collective-permute-start | bytes 393224 | tf_op jit(solution)/shard_map/ppermute | solution.py:79
  137.9 12.8 %collective-permute-start.16 = (bf16[4,352,256]{2,1,0:T(8,128)(2,1)}, bf16[4,352,256]{2,1,0:T(8,128)(2,1)}, u32[]{:S(2)}, u32[]{:S(2)}) collective-permute-start(bf16[4,352,256]{2,1,0:T(8,128)(2,1)} %add_convert_fusion.3), channel_id=1, source_target_pairs={{0,6},{1,9},{2,4},{3,11},{4,2},{5,13},{6,0},{7,15},{8,14},{9,1},{1... | collective-permute-start | bytes 2162696 | tf_op jit(solution)/shard_map/ppermute | solution.py:79
  140.0 10.4 %collective-permute-start.17 = (bf16[4,160,256]{2,1,0:T(8,128)(2,1)}, bf16[4,160,256]{2,1,0:T(8,128)(2,1)}, u32[]{:S(2)}, u32[]{:S(2)}) collective-permute-start(bf16[4,160,256]{2,1,0:T(8,128)(2,1)} %add_convert_fusion.7), channel_id=1, source_target_pairs={{0,2},{1,3},{2,0},{3,1},{4,6},{5,7},{6,4},{7,5},{8,10},{9,11},{10,... | collective-permute-start | bytes 983048 | tf_op jit(solution)/shard_map/ppermute | solution.py:79
  152.3 8.3 %collective-permute-start.20 = (bf16[2,352,256]{2,1,0:T(8,128)(2,1)S(1)}, bf16[2,352,256]{2,1,0:T(8,128)(2,1)S(1)}, u32[]{:S(2)}, u32[]{:S(2)}) collective-permute-start(bf16[2,352,256]{2,1,0:T(8,128)(2,1)S(1)} %slice.431), channel_id=1, source_target_pairs={{0,2},{1,7},{2,0},{3,5},{4,6},{5,3},{6,4},{7,1},{8,10},{9,15},{10,... | collective-permute-start | bytes 1081352 | tf_op jit(solution)/shard_map/ppermute | solution.py:79
  154.1 11.8 %collective-permute-start.24 = (bf16[64,1024]{1,0:T(8,128)(2,1)S(1)}, bf16[64,1024]{1,0:T(8,128)(2,1)S(1)}, u32[]{:S(2)}, u32[]{:S(2)}) collective-permute-start(bf16[64,1024]{1,0:T(8,128)(2,1)S(1)} %fusion.30), channel_id=1, source_target_pairs={{0,64},{64,0},{1,65},{65,1},{2,66},{66,2},{3,67},{67,3},{4,68},{68... | collective-permute-start | bytes 393224 | tf_op jit(solution)/shard_map/ppermute | solution.py:66
  167.2 18.3 %collective-permute-start.25 = (bf16[352,256]{1,0:T(8,128)(2,1)S(1)}, bf16[352,256]{1,0:T(8,128)(2,1)}, u32[]{:S(2)}, u32[]{:S(2)}) collective-permute-start(bf16[352,256]{1,0:T(8,128)(2,1)S(1)} %fusion.11), channel_id=1, source_target_pairs={{0,8},{1,3},{2,10},{3,1},{4,12},{5,7},{6,14},{7,5},{8,0},{9,11},{1... | collective-permute-start | bytes 540680 | tf_op jit(solution)/shard_map/ppermute | solution.py:79
  176.0 9.5 %collective-permute-start.27 = (bf16[128,1024]{1,0:T(8,128)(2,1)S(1)}, bf16[128,1024]{1,0:T(8,128)(2,1)S(1)}, u32[]{:S(2)}, u32[]{:S(2)}) collective-permute-start(bf16[128,1024]{1,0:T(8,128)(2,1)S(1)} %shard_map.161), channel_id=1, source_target_pairs={{0,64},{64,0},{1,65},{65,1},{2,66},{66,2},{3,67},{67,3},{4,68},{68... | collective-permute-start | bytes 786440 | tf_op jit(solution)/shard_map/ppermute | solution.py:66
  186.5 10.9 %collective-permute-start.28 = (bf16[2,352,256]{2,1,0:T(8,128)(2,1)S(1)}, bf16[2,352,256]{2,1,0:T(8,128)(2,1)S(1)}, u32[]{:S(2)}, u32[]{:S(2)}) collective-permute-start(bf16[2,352,256]{2,1,0:T(8,128)(2,1)S(1)} %pad_maximum_fusion.8), channel_id=1, source_target_pairs={{0,2},{1,7},{2,0},{3,5},{4,6},{5,3},{6,4},{7,1},{8,10},{9,15},{10,... | collective-permute-start | bytes 1081352 | tf_op jit(solution)/shard_map/ppermute | solution.py:79
  188.0 9.3 %collective-permute-start.30 = (bf16[128,1024]{1,0:T(8,128)(2,1)S(1)}, bf16[128,1024]{1,0:T(8,128)(2,1)S(1)}, u32[]{:S(2)}, u32[]{:S(2)}) collective-permute-start(bf16[128,1024]{1,0:T(8,128)(2,1)S(1)} %shard_map.162), channel_id=1, source_target_pairs={{0,64},{64,0},{1,65},{65,1},{2,66},{66,2},{3,67},{67,3},{4,68},{68... | collective-permute-start | bytes 786440 | tf_op jit(solution)/shard_map/ppermute | solution.py:66
  198.4 12.7 %collective-permute-start.33 = (bf16[4,352,256]{2,1,0:T(8,128)(2,1)S(1)}, bf16[4,352,256]{2,1,0:T(8,128)(2,1)S(1)}, u32[]{:S(2)}, u32[]{:S(2)}) collective-permute-start(bf16[4,352,256]{2,1,0:T(8,128)(2,1)S(1)} %pad_maximum_fusion.2.refs_0_), channel_id=1, source_target_pairs={{0,6},{1,9},{2,4},{3,11},{4,2},{5,13},{6,0},{7,15},{8,14},{9,1},{1... | collective-permute-start | bytes 2162696 | tf_op jit(solution)/shard_map/ppermute | solution.py:79
  201.0 10.1 %collective-permute-start.34 = (bf16[4,160,256]{2,1,0:T(8,128)(2,1)S(1)}, bf16[4,160,256]{2,1,0:T(8,128)(2,1)S(1)}, u32[]{:S(2)}, u32[]{:S(2)}) collective-permute-start(bf16[4,160,256]{2,1,0:T(8,128)(2,1)S(1)} %pad_maximum_fusion.12.refs_1_), channel_id=1, source_target_pairs={{0,2},{1,3},{2,0},{3,1},{4,6},{5,7},{6,4},{7,5},{8,10},{9,11},{10,... | collective-permute-start | bytes 983048 | tf_op jit(solution)/shard_map/ppermute | solution.py:79
  211.2 7.8 %collective-permute-start.37 = (bf16[80,1024]{1,0:T(8,128)(2,1)S(1)}, bf16[80,1024]{1,0:T(8,128)(2,1)S(1)}, u32[]{:S(2)}, u32[]{:S(2)}) collective-permute-start(bf16[80,1024]{1,0:T(8,128)(2,1)S(1)} %get-tuple-element.298), channel_id=1, source_target_pairs={{0,8},{1,3},{2,10},{3,1},{4,12},{5,7},{6,14},{7,5},{8,0},{9,11},{1... | collective-permute-start | bytes 491528 | tf_op jit(solution)/shard_map/ppermute | solution.py:79
  226.2 11.9 %collective-permute-start.41 = (bf16[4,80,1024]{2,1,0:T(8,128)(2,1)S(1)}, bf16[4,80,1024]{2,1,0:T(8,128)(2,1)S(1)}, u32[]{:S(2)}, u32[]{:S(2)}) collective-permute-start(bf16[4,80,1024]{2,1,0:T(8,128)(2,1)S(1)} %pad_maximum_fusion.5.refs_0_), channel_id=1, source_target_pairs={{0,6},{1,9},{2,4},{3,11},{4,2},{5,13},{6,0},{7,15},{8,14},{9,1},{1... | collective-permute-start | bytes 1966088 | tf_op jit(solution)/shard_map/ppermute | solution.py:79
  228.6 7.9 %collective-permute-start.42 = (bf16[4,48,1024]{2,1,0:T(8,128)(2,1)S(1)}, bf16[4,48,1024]{2,1,0:T(8,128)(2,1)S(1)}, u32[]{:S(2)}, u32[]{:S(2)}) collective-permute-start(bf16[4,48,1024]{2,1,0:T(8,128)(2,1)S(1)} %pad_maximum_fusion.6.refs_1_), channel_id=1, source_target_pairs={{0,2},{1,3},{2,0},{3,1},{4,6},{5,7},{6,4},{7,5},{8,10},{9,11},{10,... | collective-permute-start | bytes 1179656 | tf_op jit(solution)/shard_map/ppermute | solution.py:79
  230.5 10.9 %collective-permute-start.44 = (bf16[4,80,1024]{2,1,0:T(8,128)(2,1)S(1)}, bf16[4,80,1024]{2,1,0:T(8,128)(2,1)S(1)}, u32[]{:S(2)}, u32[]{:S(2)}) collective-permute-start(bf16[4,80,1024]{2,1,0:T(8,128)(2,1)S(1)} %pad_maximum_fusion.5.refs_0_), channel_id=1, source_target_pairs={{0,1},{1,0},{2,3},{3,2},{4,5},{5,4},{6,7},{7,6},{8,9},{9,8},{10,11... | collective-permute-start | bytes 1966088 | tf_op jit(solution)/shard_map/ppermute | solution.py:62
  238.8 11.8 %collective-permute-start.35 = (bf16[4,352,256]{2,1,0:T(8,128)(2,1)S(1)}, bf16[4,352,256]{2,1,0:T(8,128)(2,1)S(1)}, u32[]{:S(2)}, u32[]{:S(2)}) collective-permute-start(bf16[4,352,256]{2,1,0:T(8,128)(2,1)S(1)} %collective-permute-done.33.refs_2_), channel_id=1, source_target_pairs={{0,1},{1,0},{2,3},{3,2},{4,5},{5,4},{6,7},{7,6},{8,9},{9,8},{10,11... | collective-permute-start | bytes 2162696 | tf_op jit(solution)/shard_map/ppermute | solution.py:62
  241.4 9.3 %collective-permute-start.36 = (bf16[4,160,256]{2,1,0:T(8,128)(2,1)S(1)}, bf16[4,160,256]{2,1,0:T(8,128)(2,1)S(1)}, u32[]{:S(2)}, u32[]{:S(2)}) collective-permute-start(bf16[4,160,256]{2,1,0:T(8,128)(2,1)S(1)} %collective-permute-done.34.refs_3_), channel_id=1, source_target_pairs={{0,1},{1,0},{2,3},{3,2},{4,5},{5,4},{6,7},{7,6},{8,9},{9,8},{10,11... | collective-permute-start | bytes 983048 | tf_op jit(solution)/shard_map/ppermute | solution.py:62
  241.5 11.3 %collective-permute-start.43 = (bf16[2,128,512]{2,1,0:T(8,128)(2,1)S(1)}, bf16[2,128,512]{2,1,0:T(8,128)(2,1)S(1)}, u32[]{:S(2)}, u32[]{:S(2)}) collective-permute-start(bf16[2,128,512]{2,1,0:T(8,128)(2,1)S(1)} %slice_bitcast_fusion.5), channel_id=1, source_target_pairs={{0,16},{16,32},{32,48},{1,17},{17,33},{33,49},{2,18},{18,34},{34,5... | collective-permute-start | bytes 786440 | tf_op jit(solution)/shard_map/ppermute | solution.py:521
  246.1 9.8 %collective-permute-start.48 = (bf16[2,128,512]{2,1,0:T(8,128)(2,1)S(1)}, bf16[2,128,512]{2,1,0:T(8,128)(2,1)S(1)}, u32[]{:S(2)}, u32[]{:S(2)}) collective-permute-start(bf16[2,128,512]{2,1,0:T(8,128)(2,1)S(1)} %slice_bitcast_fusion.4), channel_id=1, source_target_pairs={{0,16},{16,32},{32,48},{1,17},{17,33},{33,49},{2,18},{18,34},{34,5... | collective-permute-start | bytes 786440 | tf_op jit(solution)/shard_map/ppermute | solution.py:521
  262.6 12.6 %collective-permute-start.51 = (bf16[4,352,256]{2,1,0:T(8,128)(2,1)S(1)}, bf16[4,352,256]{2,1,0:T(8,128)(2,1)S(1)}, u32[]{:S(2)}, u32[]{:S(2)}) collective-permute-start(bf16[4,352,256]{2,1,0:T(8,128)(2,1)S(1)} %add_convert_fusion.2), channel_id=1, source_target_pairs={{0,6},{1,9},{2,4},{3,11},{4,2},{5,13},{6,0},{7,15},{8,14},{9,1},{1... | collective-permute-start | bytes 2162696 | tf_op jit(solution)/shard_map/ppermute | solution.py:79
  265.1 10.2 %collective-permute-start.52 = (bf16[4,160,256]{2,1,0:T(8,128)(2,1)S(1)}, bf16[4,160,256]{2,1,0:T(8,128)(2,1)S(1)}, u32[]{:S(2)}, u32[]{:S(2)}) collective-permute-start(bf16[4,160,256]{2,1,0:T(8,128)(2,1)S(1)} %add_convert_fusion.6), channel_id=1, source_target_pairs={{0,2},{1,3},{2,0},{3,1},{4,6},{5,7},{6,4},{7,5},{8,10},{9,11},{10,... | collective-permute-start | bytes 983048 | tf_op jit(solution)/shard_map/ppermute | solution.py:79
  275.6 7.5 %collective-permute-start.55 = (bf16[2,352,256]{2,1,0:T(8,128)(2,1)S(1)}, bf16[2,352,256]{2,1,0:T(8,128)(2,1)S(1)}, u32[]{:S(2)}, u32[]{:S(2)}) collective-permute-start(bf16[2,352,256]{2,1,0:T(8,128)(2,1)S(1)} %slice.430), channel_id=1, source_target_pairs={{0,2},{1,7},{2,0},{3,5},{4,6},{5,3},{6,4},{7,1},{8,10},{9,15},{10,... | collective-permute-start | bytes 1081352 | tf_op jit(solution)/shard_map/ppermute | solution.py:79
  289.4 8.2 %collective-permute-start.59 = (bf16[512,256]{1,0:T(8,128)(2,1)S(1)}, bf16[512,256]{1,0:T(8,128)(2,1)S(1)}, u32[]{:S(2)}, u32[]{:S(2)}) collective-permute-start(bf16[512,256]{1,0:T(8,128)(2,1)S(1)} %pad_maximum_fusion.16), channel_id=1, source_target_pairs={{0,64},{64,0},{1,65},{65,1},{2,66},{66,2},{3,67},{67,3},{4,68},{68... | collective-permute-start | bytes 786440 | tf_op jit(solution)/shard_map/ppermute | solution.py:66
  297.7 7.3 %collective-permute-start.60 = (bf16[352,256]{1,0:T(8,128)(2,1)S(1)}, bf16[352,256]{1,0:T(8,128)(2,1)S(1)}, u32[]{:S(2)}, u32[]{:S(2)}) collective-permute-start(bf16[352,256]{1,0:T(8,128)(2,1)S(1)} %get-tuple-element.294), channel_id=1, source_target_pairs={{0,8},{1,3},{2,10},{3,1},{4,12},{5,7},{6,14},{7,5},{8,0},{9,11},{1... | collective-permute-start | bytes 540680 | tf_op jit(solution)/shard_map/ppermute | solution.py:79
  305.1 7.5 %collective-permute-start.62 = (bf16[2,352,256]{2,1,0:T(8,128)(2,1)S(1)}, bf16[2,352,256]{2,1,0:T(8,128)(2,1)S(1)}, u32[]{:S(2)}, u32[]{:S(2)}) collective-permute-start(bf16[2,352,256]{2,1,0:T(8,128)(2,1)S(1)} %pad_maximum_fusion.9), channel_id=1, source_target_pairs={{0,2},{1,7},{2,0},{3,5},{4,6},{5,3},{6,4},{7,1},{8,10},{9,15},{10,... | collective-permute-start | bytes 1081352 | tf_op jit(solution)/shard_map/ppermute | solution.py:79
  312.7 13.1 %collective-permute-start.66 = (bf16[4,352,256]{2,1,0:T(8,128)(2,1)S(1)}, bf16[4,352,256]{2,1,0:T(8,128)(2,1)S(1)}, u32[]{:S(2)}, u32[]{:S(2)}) collective-permute-start(bf16[4,352,256]{2,1,0:T(8,128)(2,1)S(1)} %pad_maximum_fusion.3.refs_0_), channel_id=1, source_target_pairs={{0,6},{1,9},{2,4},{3,11},{4,2},{5,13},{6,0},{7,15},{8,14},{9,1},{1... | collective-permute-start | bytes 2162696 | tf_op jit(solution)/shard_map/ppermute | solution.py:79
  316.5 7.6 %collective-permute-start.67 = (bf16[4,160,256]{2,1,0:T(8,128)(2,1)S(1)}, bf16[4,160,256]{2,1,0:T(8,128)(2,1)S(1)}, u32[]{:S(2)}, u32[]{:S(2)}) collective-permute-start(bf16[4,160,256]{2,1,0:T(8,128)(2,1)S(1)} %pad_maximum_fusion.14.refs_1_), channel_id=1, source_target_pairs={{0,2},{1,3},{2,0},{3,1},{4,6},{5,7},{6,4},{7,5},{8,10},{9,11},{10,... | collective-permute-start | bytes 983048 | tf_op jit(solution)/shard_map/ppermute | solution.py:79
  317.2 11.2 %collective-permute-start.64 = (bf16[4,352,256]{2,1,0:T(8,128)(2,1)S(1)}, bf16[4,352,256]{2,1,0:T(8,128)(2,1)S(1)}, u32[]{:S(2)}, u32[]{:S(2)}) collective-permute-start(bf16[4,352,256]{2,1,0:T(8,128)(2,1)S(1)} %pad_maximum_fusion.3.refs_0_), channel_id=1, source_target_pairs={{0,1},{1,0},{2,3},{3,2},{4,5},{5,4},{6,7},{7,6},{8,9},{9,8},{10,11... | collective-permute-start | bytes 2162696 | tf_op jit(solution)/shard_map/ppermute | solution.py:62
  367.2 13.6 %collective-permute-start.72 = (bf16[4,352,256]{2,1,0:T(8,128)(2,1)S(1)}, bf16[4,352,256]{2,1,0:T(8,128)(2,1)S(1)}, u32[]{:S(2)}, u32[]{:S(2)}) collective-permute-start(bf16[4,352,256]{2,1,0:T(8,128)(2,1)S(1)} %add_convert_fusion.1), channel_id=1, source_target_pairs={{0,6},{1,9},{2,4},{3,11},{4,2},{5,13},{6,0},{7,15},{8,14},{9,1},{1... | collective-permute-start | bytes 2162696 | tf_op jit(solution)/shard_map/ppermute | solution.py:79
  370.6 10.2 %collective-permute-start.73 = (bf16[4,160,256]{2,1,0:T(8,128)(2,1)S(1)}, bf16[4,160,256]{2,1,0:T(8,128)(2,1)S(1)}, u32[]{:S(2)}, u32[]{:S(2)}) collective-permute-start(bf16[4,160,256]{2,1,0:T(8,128)(2,1)S(1)} %add_convert_fusion.5), channel_id=1, source_target_pairs={{0,2},{1,3},{2,0},{3,1},{4,6},{5,7},{6,4},{7,5},{8,10},{9,11},{10,... | collective-permute-start | bytes 983048 | tf_op jit(solution)/shard_map/ppermute | solution.py:79
  381.1 7.5 %collective-permute-start.76 = (bf16[2,352,256]{2,1,0:T(8,128)(2,1)S(1)}, bf16[2,352,256]{2,1,0:T(8,128)(2,1)S(1)}, u32[]{:S(2)}, u32[]{:S(2)}) collective-permute-start(bf16[2,352,256]{2,1,0:T(8,128)(2,1)S(1)} %slice.429), channel_id=1, source_target_pairs={{0,2},{1,7},{2,0},{3,5},{4,6},{5,3},{6,4},{7,1},{8,10},{9,15},{10,... | collective-permute-start | bytes 1081352 | tf_op jit(solution)/shard_map/ppermute | solution.py:79
  394.7 7.9 %collective-permute-start.80 = (bf16[352,256]{1,0:T(8,128)(2,1)S(1)}, bf16[352,256]{1,0:T(8,128)(2,1)S(1)}, u32[]{:S(2)}, u32[]{:S(2)}) collective-permute-start(bf16[352,256]{1,0:T(8,128)(2,1)S(1)} %fusion.5), channel_id=1, source_target_pairs={{0,8},{1,3},{2,10},{3,1},{4,12},{5,7},{6,14},{7,5},{8,0},{9,11},{1... | collective-permute-start | bytes 540680 | tf_op jit(solution)/shard_map/ppermute | solution.py:79
  402.6 7.9 %collective-permute-start.82 = (bf16[2,352,256]{2,1,0:T(8,128)(2,1)S(1)}, bf16[2,352,256]{2,1,0:T(8,128)(2,1)S(1)}, u32[]{:S(2)}, u32[]{:S(2)}) collective-permute-start(bf16[2,352,256]{2,1,0:T(8,128)(2,1)S(1)} %pad_maximum_fusion.10), channel_id=1, source_target_pairs={{0,2},{1,7},{2,0},{3,5},{4,6},{5,3},{6,4},{7,1},{8,10},{9,15},{10,... | collective-permute-start | bytes 1081352 | tf_op jit(solution)/shard_map/ppermute | solution.py:79
  410.5 12.7 %collective-permute-start.86 = (bf16[4,352,256]{2,1,0:T(8,128)(2,1)S(1)}, bf16[4,352,256]{2,1,0:T(8,128)(2,1)S(1)}, u32[]{:S(2)}, u32[]{:S(2)}) collective-permute-start(bf16[4,352,256]{2,1,0:T(8,128)(2,1)S(1)} %pad_maximum_fusion.4.refs_0_), channel_id=1, source_target_pairs={{0,6},{1,9},{2,4},{3,11},{4,2},{5,13},{6,0},{7,15},{8,14},{9,1},{1... | collective-permute-start | bytes 2162696 | tf_op jit(solution)/shard_map/ppermute | solution.py:79
  414.2 11.7 %collective-permute-start.84 = (bf16[4,352,256]{2,1,0:T(8,128)(2,1)S(1)}, bf16[4,352,256]{2,1,0:T(8,128)(2,1)S(1)}, u32[]{:S(2)}, u32[]{:S(2)}) collective-permute-start(bf16[4,352,256]{2,1,0:T(8,128)(2,1)S(1)} %pad_maximum_fusion.4.refs_0_), channel_id=1, source_target_pairs={{0,1},{1,0},{2,3},{3,2},{4,5},{5,4},{6,7},{7,6},{8,9},{9,8},{10,11... | collective-permute-start | bytes 2162696 | tf_op jit(solution)/shard_map/ppermute | solution.py:62
  437.0 13.6 %collective-permute-start.92 = (bf16[4,352,256]{2,1,0:T(8,128)(2,1)S(1)}, bf16[4,352,256]{2,1,0:T(8,128)(2,1)S(1)}, u32[]{:S(2)}, u32[]{:S(2)}) collective-permute-start(bf16[4,352,256]{2,1,0:T(8,128)(2,1)S(1)} %add_convert_fusion), channel_id=1, source_target_pairs={{0,6},{1,9},{2,4},{3,11},{4,2},{5,13},{6,0},{7,15},{8,14},{9,1},{1... | collective-permute-start | bytes 2162696 | tf_op jit(solution)/shard_map/ppermute | solution.py:79
  440.4 10.2 %collective-permute-start.93 = (bf16[4,160,256]{2,1,0:T(8,128)(2,1)S(1)}, bf16[4,160,256]{2,1,0:T(8,128)(2,1)S(1)}, u32[]{:S(2)}, u32[]{:S(2)}) collective-permute-start(bf16[4,160,256]{2,1,0:T(8,128)(2,1)S(1)} %add_convert_fusion.4), channel_id=1, source_target_pairs={{0,2},{1,3},{2,0},{3,1},{4,6},{5,7},{6,4},{7,5},{8,10},{9,11},{10,... | collective-permute-start | bytes 983048 | tf_op jit(solution)/shard_map/ppermute | solution.py:79
  450.9 7.5 %collective-permute-start.96 = (bf16[2,352,256]{2,1,0:T(8,128)(2,1)S(1)}, bf16[2,352,256]{2,1,0:T(8,128)(2,1)S(1)}, u32[]{:S(2)}, u32[]{:S(2)}) collective-permute-start(bf16[2,352,256]{2,1,0:T(8,128)(2,1)S(1)} %slice.428), channel_id=1, source_target_pairs={{0,2},{1,7},{2,0},{3,5},{4,6},{5,3},{6,4},{7,1},{8,10},{9,15},{10,... | collective-permute-start | bytes 1081352 | tf_op jit(solution)/shard_map/ppermute | solution.py:79
  (84 other events, 543.2 us)
Sparse Core Ops, SparseCore 0:
  54.6 86.3 all-gather.1

commit v7 on v6

--- a/solution.py
+++ b/solution.py
@@ -90,27 +90,28 @@
     return lax.optimization_barrier(values)
 
 
-def gather_chips(local, beside):
-    side = ()
-    near = list(local)
-    for turn in range(2):
-        sent = [neighbour(value, part, turn) for part, value in enumerate(near)]
-        side = beside(turn, side)
-        *got, side = together(*sent, side)
-        if turn == 0:
-            near = [jnp.stack(pair) for pair in zip(near, got)]
-        else:
-            near = [jnp.concatenate(pair) for pair in zip(near, got)]
+def first_round(local):
+    return [neighbour(value, part, 0) for part, value in enumerate(local)]
+
+
+def later_rounds(local, got):
+    near = [jnp.stack(pair) for pair in zip(local, got)]
+    got = together(*[neighbour(value, part, 1) for part, value in enumerate(near)])
+    near = [jnp.concatenate(pair) for pair in zip(near, got)]
     swaps = [core_swap(value) for value in near]
     far = [neighbour(value, part, 2) for part, value in enumerate(near)]
-    *swaps, side = together(*swaps, side)
-    side = beside(2, side)
-    *far, side = together(*far, side)
-    return near + far, swaps + [core_swap(value) for value in far], side
-
-
-def nothing(turn, side):
-    return side
+    swaps = list(together(*swaps))
+    far = list(together(*far))
+    return near + far, swaps + [core_swap(value) for value in far]
+
+
+def gather_chips(local):
+    return later_rounds(local, together(*first_round(local)))
+
+
+def spread(local):
+    rows = jnp.concatenate(local)
+    return jnp.broadcast_to(rows[None], (CHIPS,) + rows.shape)
 
 
 def scatter_sum(places_both, mixed, weight):
@@ -136,26 +137,40 @@
 
 
 def project_kernel(last, units, place_ref, *refs):
-    x_refs, (gain_ref, w_ref), refs = refs[:4], refs[4:6], refs[6:]
+    whole_rows = len(refs) == (8 if last else 6)
+    count = 1 if whole_rows else 4
+    x_refs, (gain_ref, w_ref), refs = refs[:count], refs[count : count + 2], refs[count + 2 :]
     if last:
         acc_in, sq_in, out_ref, sq_ref, left_ref = refs
     else:
         acc_ref, sq_ref, left_ref = refs
     step = pl.program_id(0)
 
+    def place_rows(rows, blocks):
+        total = sq_in[rows, :] if last else jnp.zeros((rows.stop - rows.start, 128), f32)
+        for block, chip in blocks:
+            wide = block.astype(f32)
+            squares = wide * wide
+            total += squares[:, :128] + squares[:, 128:]
+            cols = pl.ds(pl.multiple_of(chip * WIDTH, WIDTH), WIDTH)
+            left_ref[rows, cols] = (wide * gain_ref[chip, 0]).astype(bf16)
+        sq_ref[rows, :] = total
+
     @pl.when(step == 0)
     def _():
         for part in range(2):
             rows = slice(STARTS[part], STARTS[part] + PARTS[part])
-            total = sq_in[rows, :] if last else jnp.zeros((PARTS[part], 128), f32)
-            for block in range(CHIPS):
-                chip = place_ref[1 + part * CHIPS + block]
-                wide = x_refs[part + 2 * (block // 4)][block % 4].astype(f32)
-                squares = wide * wide
-                total += squares[:, :128] + squares[:, 128:]
-                cols = pl.ds(pl.multiple_of(chip * WIDTH, WIDTH), WIDTH)
-                left_ref[rows, cols] = (wide * gain_ref[chip, 0]).astype(bf16)
-            sq_ref[rows, :] = total
+            if whole_rows:
+                blocks = [(x_refs[0][chip, rows, :], chip) for chip in range(CHIPS)]
+            else:
+                blocks = [
+                    (
+                        x_refs[part + 2 * (block // 4)][block % 4],
+                        place_ref[1 + part * CHIPS + block],
+                    )
+                    for block in range(CHIPS)
+                ]
+            place_rows(rows, blocks)
 
     right = w_ref[0].reshape(CHIPS * WIDTH, WIDTH)
     product = jnp.dot(left_ref[...], right, preferred_element_type=f32)
@@ -222,10 +237,9 @@
     )
 
 
-def project(places_both, local, gains, weight, units, beside=nothing):
-    same, swap, side = gather_chips(local, beside)
+def project(places_both, same, swap, gains, weight, units):
     before = project_half(places_both[0], same, gains, weight, None, units)
-    return project_half(places_both[1], swap, gains, weight, before, units), side
+    return project_half(places_both[1], swap, gains, weight, before, units)
 
 
 def causal_kernel(triple_ref, out_ref):
@@ -349,26 +363,20 @@
     return [rows[start : start + count] for start, count in zip(STARTS, PARTS)]
 
 
-def look_up(ids, enc_embed, places_both, section):
+def look_up(ids, enc_embed, core, section):
     vocab_here = enc_embed.shape[0]
     mine = lax.dynamic_slice_in_dim(ids, section * (NB_LEN // 2), NB_LEN // 2, axis=1)
-    wanted = mine - lax.axis_index(MP) * vocab_here
-
-    def rows(place):
-        picks = wanted[2 * place[1 : 1 + CHIPS] + place[0]].reshape(-1)
+    wanted = mine.reshape(CHIPS, 2, NB_LEN // 2) - lax.axis_index(MP) * vocab_here
+
+    def rows(at):
+        picks = lax.dynamic_index_in_dim(wanted, at, 1, keepdims=False).reshape(-1)
         inside = (picks >= 0) & (picks < vocab_here)
         found = enc_embed[jnp.clip(picks, 0, vocab_here - 1)]
         found = jnp.where(inside[:, None], found, jnp.zeros((), bf16))
         return found.reshape(CHIPS, NB_LEN // 2, ENC_D)
 
-    return rows(places_both[0]), rows(places_both[1])
-
-
-def looked_up(own, other):
-    total = own + core_swap(other)
-    total = total[:4] + neighbour(total[4:], 0, 2)
-    total = total[:2] + neighbour(total[2:], 0, 1)
-    return total[0] + neighbour(total[1], 0, 0)
+    far = core_swap(rows(1 - core))
+    return rows(core) + far
 
 
 def join_halves(half, section):
@@ -522,33 +530,40 @@
     return prev, pairs
 
 
-def decoder_layer(places_both, states, weights, encoder=None):
+def attention(triple):
+    triple = lax.all_to_all(triple, "seq", 0, 0, tiled=True)
+    return lax.all_to_all(causal(triple), "seq", 0, 0, tiled=True)
+
+
+def first_layer(places_both, states, weights, found, local, join, encoder):
     norms, triple_w, out_w, query_w, back_w = weights
-    idle = encoder is None
-    first = nothing if idle else encoder.first
-    triple, side = project(places_both, states, norms[0], triple_w, True, first)
-    if idle:
-        triple = lax.all_to_all(triple, "seq", 0, 0, tiled=True)
-        embedded = ()
-    else:
-        found, local = side
-        pieces = encoder.gather(local)
-        triple, found = together(triple, found)
-        triple = lax.all_to_all(triple, "seq", 0, 0, tiled=True)
-        triple, half = together(triple, looked_up(*found))
-        embedded = encoder.join(half)
-    mixed = lax.all_to_all(causal(triple), "seq", 0, 0, tiled=True)
-    middle, embedded = add_product(places_both, states, mixed, out_w, embedded)
-
-    def second(turn, side):
-        return side if idle else encoder.second(turn, embedded if turn == 0 else side, pieces)
-
-    asked, encoded = project(places_both, middle, norms[1], query_w[None], False, second)
-    return middle, asked, None if idle else encoder.pairs(encoded)
-
-
-def cross_layer(places_both, middle, asked, pairs, weights):
-    crossed = cross(asked, *pairs)
+    same, local = together(chips_to_chips(spread(states)), local)
+    pieces = lax.all_gather(local, MP, axis=1, tiled=True)
+    same, found = together(same, found)
+    half = jnp.sum(chips_to_chips(found).astype(f32), axis=0).astype(bf16)
+    triple = project(places_both, [same], [core_swap(same)], norms[0], triple_w, True)
+    triple, half = together(triple, half)
+    mixed = attention(triple)
+    middle, embedded = add_product(places_both, states, mixed, out_w, join(half))
+    rows, embedded = together(spread(middle), embedded)
+    same = chips_to_chips(rows)
+    encoded = encoder(embedded, pieces)
+    parts = [encoded[start : start + count] for start, count in zip(ENC_STARTS, ENC_PARTS)]
+    *got, same = together(*first_round(parts), same)
+    asked = project(places_both, [same], [core_swap(same)], norms[1], query_w[None], False)
+    return middle, asked, later_rounds(parts, got)
+
+
+def second_layer(places_both, states, weights):
+    norms, triple_w, out_w, query_w, back_w = weights
+    triple = project(places_both, *gather_chips(states), norms[0], triple_w, True)
+    middle, _ = add_product(places_both, states, attention(triple), out_w)
+    asked = project(places_both, *gather_chips(middle), norms[1], query_w[None], False)
+    return middle, asked
+
+
+def cross_layer(places_both, middle, asked, prevs, pairs, weights):
+    crossed = cross(asked, prevs, pairs)
     return add_product(places_both, middle, crossed, weights[4])[0]
 
 
@@ -575,42 +590,15 @@
     places_both = [places(chip, core_at), places(chip, 1 - core_at)]
     local = weight_parts(section, enc_qkv, enc_out, enc_up, enc_down)
     slot_ids = neighbour_ids[neighbour_table.reshape(-1)]
+    found = look_up(slot_ids, enc_embed, core_at, section)
     pair_w = cross_pair[0].reshape(ENC_D, 2 * WIDTH)
-    section_ref = jnp.reshape(section, (1,))
-
-    class Encoder:
-        @staticmethod
-        def first(turn, side):
-            if turn == 0:
-                return slot_ids
-            if turn == 1:
-                return side
-            return look_up(side, enc_embed, places_both, section), local
-
-        @staticmethod
-        def gather(local):
-            return lax.all_gather(local, MP, axis=1, tiled=True)
-
-        @staticmethod
-        def join(half):
-            return join_halves(half, section)
-
-        @staticmethod
-        def second(turn, side, pieces):
-            if turn == 0:
-                return encode_mix(side, enc_norms, pieces, section_ref)
-            if turn == 1:
-                return encode_feed(*side, enc_norms, pieces)
-            return encode_end(*side)
-
-        @staticmethod
-        def pairs(encoded):
-            parts = [
-                encoded[start : start + count] for start, count in zip(ENC_STARTS, ENC_PARTS)
-            ]
-            both = gather_chips(parts, nothing)[:2]
-            made = [make_pairs(place, rows, pair_w) for place, rows in zip(places_both, both)]
-            return [prev for prev, _ in made], [pairs for _, pairs in made]
+
+    def join(half):
+        return join_halves(half, section)
+
+    def encoder(embedded, pieces):
+        mix = encode_mix(embedded, enc_norms, pieces, jnp.reshape(section, (1,)))
+        return encode_end(*encode_feed(*mix, enc_norms, pieces))
 
     weights = (
         dec_norms[0],
@@ -621,11 +609,15 @@
     )
 
     states = hidden_states.reshape(BATCH * ROWS, WIDTH)
-    middle, asked, pairs = decoder_layer(places_both, by_parts(states), weights, Encoder)
-    first = cross_layer(places_both, middle, asked, pairs, weights)
+    middle, asked, encoded = first_layer(
+        places_both, by_parts(states), weights, found, local, join, encoder
+    )
+    made = [make_pairs(place, rows, pair_w) for place, rows in zip(places_both, encoded)]
+    prevs, pairs = [prev for prev, _ in made], [rows for _, rows in made]
+    first = cross_layer(places_both, middle, asked, prevs, pairs, weights)
     handed = section_swap(jnp.concatenate(first))
-    middle, asked, _ = decoder_layer(places_both, by_parts(handed), weights)
-    second = jnp.concatenate(cross_layer(places_both, middle, asked, pairs, weights))
+    middle, asked = second_layer(places_both, by_parts(handed), weights)
+    second = jnp.concatenate(cross_layer(places_both, middle, asked, prevs, pairs, weights))
     second = second.reshape(BATCH, ROWS, WIDTH)
     return jnp.where(section == 0, section_swap(second[0]), second[1])[None]
 

time: 487 us -> 491 us (level)
  blocking collectives: 36.5 us -> 50.7 us
  starting transfers between devices: 114 us -> 99.9 us
  waiting for transfers between devices: 196 us -> 204 us
  other arithmetic: 20.9 us -> 13.9 us
    ppermute x57 -> x42, waiting for transfers between devices: 171 us -> 124 us  [neighbour(): return lax.ppermute(value, MP, route)]
    all_to_all x1 -> x3, waiting for transfers between devices: 0.01 us -> 34.5 us  [chips_to_chips(): return lax.all_to_all(value, ('z', 'y'), 0, 0, tiled=True)]
    ppermute x5, waiting for transfers between devices: 13.2 us -> 38.2 us  [section_swap(): return lax.ppermute(value, 'section', [(0, 1), (1, 0)])]
    ppermute x57 -> x42, starting transfers between devices: 82.2 us -> 60.5 us  [neighbour(): return lax.ppermute(value, MP, route)]
    all_to_all x3 -> x4, blocking collectives: 36.5 us -> 50.7 us  [the longest x2 32.6 us: attention(): triple = lax.all_to_all(triple, 'seq', 0, 0, tiled=True)]
    all_to_all x1 -> x3, starting transfers between devices: 4.3 us -> 16.8 us  [chips_to_chips(): return lax.all_to_all(value, ('z', 'y'), 0, 0, tiled=True)]
    unnamed x60 -> x46, local copies, waits for them, and re-layouts: 15.4 us -> 14.2 us
  transfers between devices with their start and end apart: 103 -> 84, of which waited for: 50 -> 41; matrix products, arithmetic and copies ran while one was open for 8% -> 8% of each run, Pallas kernels for 9% -> 8%
where the time goes in v7:
time: 491 us; the launch traced here: 483 us
  waiting for transfers between devices  204 us (42%)
  starting transfers between devices  99.9 us (20%)
  Pallas kernels  56.4 us (11%)
  blocking collectives  50.7 us (10%)
  local copies, waits for them, and re-layouts  42.8 us (9%)
  between operations  15.2 us (3%)
  other arithmetic  13.9 us (3%)
    ppermute x42, waiting for transfers between devices, neighbour(): return lax.ppermute(value, MP, route)  124 us
    ppermute x42, starting transfers between devices, neighbour(): return lax.ppermute(value, MP, route)  60.5 us
    ppermute x5, waiting for transfers between devices, section_swap(): return lax.ppermute(value, 'section', [(0, 1), (1, 0)])  38.2 us
    all_to_all x3, waiting for transfers between devices, chips_to_chips(): return lax.all_to_all(value, ('z', 'y'), 0, 0, tiled=True)  34.5 us
    all_to_all x2, blocking collectives, attention(): triple = lax.all_to_all(triple, 'seq', 0, 0, tiled=True)  32.6 us
    pallas_call x8, Pallas kernels, project_half(): pl.pallas_call(functools.partial(project_kernel, last, units), grid_spec=...  25 us
    all_to_all x2, blocking collectives, attention(): return lax.all_to_all(causal(triple), 'seq', 0, 0, tiled=True)  18.1 us
    all_to_all x3, starting transfers between devices, chips_to_chips(): return lax.all_to_all(value, ('z', 'y'), 0, 0, tiled=True)  16.8 us
  transfers between devices with their start and end apart: 84, of which 41 were waited for; matrix products, arithmetic and copies ran while one was open for 8% of the time, Pallas kernels for 8%

profile of v7, /device:TPU:0, one launch (start us, length us, event | category | flops | bytes accessed | tf_op | source)
XLA Modules:
  0.0 483.0 jit_solution(3418633425851800762)
XLA Ops:
  9.0 5.9 %all-to-all-start = ((bf16[8,512,256]{2,1,0:T(8,128)(2,1)}), bf16[8,512,256]{2,1,0:T(8,128)(2,1)S(1)}, u32[]{:S(2)}, u32[]{:S(2)}) async-start(bf16[8,512,256]{2,1,0:T(8,128)(2,1)} %broadcast_in_dim.38), calls=%async_computation | async-start | bytes 4194304 | tf_op jit(solution)/shard_map/all_to_all | solution.py:70
  15.2 3.4 reshape.199
  23.0 18.8 %all-to-all-done.refs_0_ = bf16[8,512,256]{2,1,0:T(8,128)(2,1)S(1)} async-done(((bf16[8,512,256]{2,1,0:T(8,128)(2,1)}), bf16[8,512,256]{2,1,0:T(8,128)(2,1)S(1)}, u32[]{:S(2)}, u32[]{:S(2)}) %all-to-all-start) | async-done | bytes 2097184 | tf_op jit(solution)/shard_map/all_to_all | solution.py:70
  43.0 7.8 %gather_fusion.2 = bf16[512,1024]{1,0:T(8,128)(2,1)} fusion(bf16[4000,1024]{1,0:T(8,128)(2,1)} %param.19, s32[1024]{0:T(1024)S(1)} %pad_clamp_fusion), kind=kCustom, calls=%fused_computation.2 | custom fusion | bytes 2099200 | tf_op jit(solution)/shard_map/gather | solution.py:374
  53.1 8.1 %gather_fusion.1 = bf16[512,1024]{1,0:T(8,128)(2,1)} fusion(bf16[4000,1024]{1,0:T(8,128)(2,1)} %param.19, s32[1024]{0:T(1024)S(1)} %pad_clamp_fusion.1), kind=kCustom, calls=%fused_computation.1 | custom fusion | bytes 2099200 | tf_op jit(solution)/shard_map/gather | solution.py:374
  64.7 6.0 %all-to-all-start.1 = ((bf16[8,64,1024]{2,1,0:T(8,128)(2,1)}), bf16[8,64,1024]{2,1,0:T(8,128)(2,1)}, u32[]{:S(2)}, u32[]{:S(2)}) async-start(bf16[8,64,1024]{2,1,0:T(8,128)(2,1)} %select_add_fusion), calls=%async_computation.1 | async-start | bytes 2097152 | tf_op jit(solution)/shard_map/all_to_all | solution.py:70
  73.7 3.6 shard_map.154
  78.5 15.7 %all-to-all-done.1 = bf16[8,64,1024]{2,1,0:T(8,128)(2,1)} async-done(((bf16[8,64,1024]{2,1,0:T(8,128)(2,1)}), bf16[8,64,1024]{2,1,0:T(8,128)(2,1)}, u32[]{:S(2)}, u32[]{:S(2)}) %all-to-all-start.1) | async-done | bytes 1048608 | tf_op jit(solution)/shard_map/all_to_all | solution.py:70
  99.9 5.2 %shard_map.155 = bf16[4,3,256,128]{3,2,1,0:T(8,128)(2,1)S(1)} custom-call(s32[17]{0:T(128)S(1)} %pad_add_fusion.1.place_ref, bf16[8,512,256]{2,1,0:T(8,128)(2,1)} %collective-permute-done.1.refs_0_, f32[8,2,1,256]{3,2,1,0:T(1,128)S(1)} %bitcast.313, bf16[3,8,2,256,256]{4,3,2,1,0:T(8,128)(2,1)S(1)} %bitcast.291, f32[3,512,256]{2,1,0:T(8,128)S(1)} %copy-done.10, ...), custom_call_target="tpu_custom_call" | custom-call | flops 1610612736 | bytes 6815744 | tf_op jit(solution)/shard_map/pallas_call | solution.py:215
  105.2 15.9 %all_to_all.35.triple_ref = bf16[4,3,256,128]{3,2,1,0:T(8,128)(2,1)S(1)} all-to-all(bf16[4,3,256,128]{3,2,1,0:T(8,128)(2,1)S(1)} %shard_map.155), channel_id=1, replica_groups=mesh['section'=2,'seq'=4,'z'=2,'y'=4,'core'=2] {'seq'}, dimensions={0} | all-to-all | bytes 1572864 | tf_op jit(solution)/shard_map/all_to_all | solution.py:534
  122.5 9.1 %all_to_all.36.mixed_ref = bf16[4,256,128]{2,1,0:T(8,128)(2,1)S(1)} all-to-all(bf16[4,256,128]{2,1,0:T(8,128)(2,1)S(1)} %shard_map.156), channel_id=1, replica_groups=mesh['section'=2,'seq'=4,'z'=2,'y'=4,'core'=2] {'seq'}, dimensions={0} | all-to-all | bytes 524288 | tf_op jit(solution)/shard_map/all_to_all | solution.py:535
  135.6 4.8 %collective-permute-start.4 = (bf16[4,352,256]{2,1,0:T(8,128)(2,1)S(1)}, bf16[4,352,256]{2,1,0:T(8,128)(2,1)S(1)}, u32[]{:S(2)}, u32[]{:S(2)}) collective-permute-start(bf16[4,352,256]{2,1,0:T(8,128)(2,1)S(1)} %add_convert_fusion.3), channel_id=1, source_target_pairs={{0,6},{1,9},{2,4},{3,11},{4,2},{5,13},{6,0},{7,15},{8,14},{9,1},{1... | collective-permute-start | bytes 2162696 | tf_op jit(solution)/shard_map/ppermute | solution.py:79
  142.7 8.0 %collective-permute-done.5 = bf16[4,160,256]{2,1,0:T(8,128)(2,1)S(1)} collective-permute-done((bf16[4,160,256]{2,1,0:T(8,128)(2,1)S(1)}, bf16[4,160,256]{2,1,0:T(8,128)(2,1)S(1)}, u32[]{:S(2)}, u32[]{:S(2)}) %collective-permute-start.5) | collective-permute-done | bytes 327712 | tf_op jit(solution)/shard_map/ppermute | solution.py:79
  154.1 3.5 collective-permute-start.12
  164.8 3.4 collective-permute-done.11
  169.8 4.9 %all-to-all-start.4 = ((bf16[8,512,256]{2,1,0:T(8,128)(2,1)}), bf16[8,512,256]{2,1,0:T(8,128)(2,1)}, u32[]{:S(2)}, u32[]{:S(2)}) async-start(bf16[8,512,256]{2,1,0:T(8,128)(2,1)} %broadcast_in_dim.42), calls=%async_computation.4 | async-start | bytes 4194304 | tf_op jit(solution)/shard_map/all_to_all | solution.py:70
  174.8 4.9 %copy-done.4 = bf16[13,1024,512]{2,1,0:T(8,128)(2,1)S(1)} copy-done((bf16[13,1024,512]{2,1,0:T(8,128)(2,1)S(1)}, bf16[13,1024,512]{2,1,0:T(8,128)(2,1)}, u32[]{:S(2)}) %copy-start.4) | copy-done | bytes 13631512
  181.8 3.8 collective-permute-start.13
  185.6 19.9 %collective-permute-done.13 = bf16[128,1024]{1,0:T(8,128)(2,1)S(1)} collective-permute-done((bf16[128,1024]{1,0:T(8,128)(2,1)S(1)}, bf16[128,1024]{1,0:T(8,128)(2,1)S(1)}, u32[]{:S(2)}, u32[]{:S(2)}) %collective-permute-start.13) | collective-permute-done | bytes 262176 | tf_op jit(solution)/shard_map/ppermute | solution.py:66
  207.0 7.9 %collective-permute-done.14 = bf16[128,1024]{1,0:T(8,128)(2,1)S(1)} collective-permute-done((bf16[128,1024]{1,0:T(8,128)(2,1)S(1)}, bf16[128,1024]{1,0:T(8,128)(2,1)S(1)}, u32[]{:S(2)}, u32[]{:S(2)}) %collective-permute-start.14) | collective-permute-done | bytes 262176 | tf_op jit(solution)/shard_map/ppermute | solution.py:66
  218.8 3.3 collective-permute-done.16
  224.3 5.5 %collective-permute-done.19 = bf16[2,48,1024]{2,1,0:T(8,128)(2,1)S(1)} collective-permute-done((bf16[2,48,1024]{2,1,0:T(8,128)(2,1)S(1)}, bf16[2,48,1024]{2,1,0:T(8,128)(2,1)S(1)}, u32[]{:S(2)}, u32[]{:S(2)}) %collective-permute-start.19) | collective-permute-done | bytes 196640 | tf_op jit(solution)/shard_map/ppermute | solution.py:79
  234.3 5.6 %collective-permute-done.21.refs_3_ = bf16[4,48,1024]{2,1,0:T(8,128)(2,1)S(1)} collective-permute-done((bf16[4,48,1024]{2,1,0:T(8,128)(2,1)S(1)}, bf16[4,48,1024]{2,1,0:T(8,128)(2,1)S(1)}, u32[]{:S(2)}, u32[]{:S(2)}) %collective-permute-start.21) | collective-permute-done | bytes 393248 | tf_op jit(solution)/shard_map/ppermute | solution.py:79
  268.9 8.7 %collective-permute-done.31 = bf16[4,160,256]{2,1,0:T(8,128)(2,1)S(1)} collective-permute-done((bf16[4,160,256]{2,1,0:T(8,128)(2,1)S(1)}, bf16[4,160,256]{2,1,0:T(8,128)(2,1)S(1)}, u32[]{:S(2)}, u32[]{:S(2)}) %collective-permute-start.31) | collective-permute-done | bytes 327712 | tf_op jit(solution)/shard_map/ppermute | solution.py:79
  279.4 5.4 %collective-permute-done.35 = bf16[2,160,256]{2,1,0:T(8,128)(2,1)S(1)} collective-permute-done((bf16[2,160,256]{2,1,0:T(8,128)(2,1)S(1)}, bf16[2,160,256]{2,1,0:T(8,128)(2,1)S(1)}, u32[]{:S(2)}, u32[]{:S(2)}) %collective-permute-start.35) | collective-permute-done | bytes 163872 | tf_op jit(solution)/shard_map/ppermute | solution.py:79
  288.8 3.5 collective-permute-done.37
  294.0 6.4 %collective-permute-done.38 = bf16[512,256]{1,0:T(8,128)(2,1)S(1)} collective-permute-done((bf16[512,256]{1,0:T(8,128)(2,1)S(1)}, bf16[512,256]{1,0:T(8,128)(2,1)S(1)}, u32[]{:S(2)}, u32[]{:S(2)}) %collective-permute-start.38) | collective-permute-done | bytes 262176 | tf_op jit(solution)/shard_map/ppermute | solution.py:66
  303.9 3.5 collective-permute-done.40
  308.7 4.2 collective-permute-done.42
  315.2 4.5 collective-permute-start.45
  319.9 7.0 %collective-permute-done.46.refs_3_ = bf16[4,160,256]{2,1,0:T(8,128)(2,1)S(1)} collective-permute-done((bf16[4,160,256]{2,1,0:T(8,128)(2,1)S(1)}, bf16[4,160,256]{2,1,0:T(8,128)(2,1)S(1)}, u32[]{:S(2)}, u32[]{:S(2)}) %collective-permute-start.46) | collective-permute-done | bytes 327712 | tf_op jit(solution)/shard_map/ppermute | solution.py:79
  331.6 3.7 shard_map.172
  335.4 3.8 shard_map.173
  339.1 16.7 %all_to_all.37.triple_ref = bf16[4,3,256,128]{3,2,1,0:T(8,128)(2,1)S(1)} all-to-all(bf16[4,3,256,128]{3,2,1,0:T(8,128)(2,1)S(1)} %shard_map.173), channel_id=1, replica_groups=mesh['section'=2,'seq'=4,'z'=2,'y'=4,'core'=2] {'seq'}, dimensions={0} | all-to-all | bytes 1572864 | tf_op jit(solution)/shard_map/all_to_all | solution.py:534
  357.2 9.1 %all_to_all.38.mixed_ref = bf16[4,256,128]{2,1,0:T(8,128)(2,1)S(1)} all-to-all(bf16[4,256,128]{2,1,0:T(8,128)(2,1)S(1)} %shard_map.174), channel_id=1, replica_groups=mesh['section'=2,'seq'=4,'z'=2,'y'=4,'core'=2] {'seq'}, dimensions={0} | all-to-all | bytes 524288 | tf_op jit(solution)/shard_map/all_to_all | solution.py:535
  370.3 3.3 collective-permute-start.51
  375.2 8.7 %collective-permute-done.52 = bf16[4,160,256]{2,1,0:T(8,128)(2,1)S(1)} collective-permute-done((bf16[4,160,256]{2,1,0:T(8,128)(2,1)S(1)}, bf16[4,160,256]{2,1,0:T(8,128)(2,1)S(1)}, u32[]{:S(2)}, u32[]{:S(2)}) %collective-permute-start.52) | collective-permute-done | bytes 327712 | tf_op jit(solution)/shard_map/ppermute | solution.py:79
  385.3 5.5 %collective-permute-done.56 = bf16[2,160,256]{2,1,0:T(8,128)(2,1)S(1)} collective-permute-done((bf16[2,160,256]{2,1,0:T(8,128)(2,1)S(1)}, bf16[2,160,256]{2,1,0:T(8,128)(2,1)S(1)}, u32[]{:S(2)}, u32[]{:S(2)}) %collective-permute-start.56) | collective-permute-done | bytes 163872 | tf_op jit(solution)/shard_map/ppermute | solution.py:79
  394.7 3.4 collective-permute-done.58
  402.1 3.4 collective-permute-done.60
  406.5 4.7 collective-permute-done.62
  413.6 4.1 collective-permute-start.65
  417.9 7.0 %collective-permute-done.66.refs_3_ = bf16[4,160,256]{2,1,0:T(8,128)(2,1)S(1)} collective-permute-done((bf16[4,160,256]{2,1,0:T(8,128)(2,1)S(1)}, bf16[4,160,256]{2,1,0:T(8,128)(2,1)S(1)}, u32[]{:S(2)}, u32[]{:S(2)}) %collective-permute-start.66) | collective-permute-done | bytes 327712 | tf_op jit(solution)/shard_map/ppermute | solution.py:79
  441.0 3.3 collective-permute-start.71
  445.9 8.7 %collective-permute-done.72 = bf16[4,160,256]{2,1,0:T(8,128)(2,1)S(1)} collective-permute-done((bf16[4,160,256]{2,1,0:T(8,128)(2,1)S(1)}, bf16[4,160,256]{2,1,0:T(8,128)(2,1)S(1)}, u32[]{:S(2)}, u32[]{:S(2)}) %collective-permute-start.72) | collective-permute-done | bytes 327712 | tf_op jit(solution)/shard_map/ppermute | solution.py:79
  455.5 6.0 %collective-permute-done.76 = bf16[2,160,256]{2,1,0:T(8,128)(2,1)S(1)} collective-permute-done((bf16[2,160,256]{2,1,0:T(8,128)(2,1)S(1)}, bf16[2,160,256]{2,1,0:T(8,128)(2,1)S(1)}, u32[]{:S(2)}, u32[]{:S(2)}) %collective-permute-start.76) | collective-permute-done | bytes 163872 | tf_op jit(solution)/shard_map/ppermute | solution.py:79
  464.9 3.5 collective-permute-done.78
  470.9 4.1 collective-permute-done.79
  (317 shorter events, 150.7 us)
Async XLA Ops:
  9.0 32.8 %all-to-all-start = ((bf16[8,512,256]{2,1,0:T(8,128)(2,1)}), bf16[8,512,256]{2,1,0:T(8,128)(2,1)S(1)}, u32[]{:S(2)}, u32[]{:S(2)}) async-start(bf16[8,512,256]{2,1,0:T(8,128)(2,1)} %broadcast_in_dim.38), calls=%async_computation | async-start | bytes 4194304 | tf_op jit(solution)/shard_map/all_to_all | solution.py:70
  14.9 159.8 %all-gather.2.cloned.1.call-start = ((), (), s32[]{:S(2)}) async-start(), calls=%async_computation.7 | async-start | bytes 14483456 | tf_op jit(solution)/shard_map/all_gather | solution.py:541
  53.1 8.2 %collective-permute-start = (bf16[8,64,1024]{2,1,0:T(8,128)(2,1)}, bf16[8,64,1024]{2,1,0:T(8,128)(2,1)}, u32[]{:S(2)}, u32[]{:S(2)}) collective-permute-start(bf16[8,64,1024]{2,1,0:T(8,128)(2,1)} %broadcast_select_fusion), channel_id=1, source_target_pairs={{0,1},{1,0},{2,3},{3,2},{4,5},{5,4},{6,7},{7,6},{8,9},{9,8},{10,11... | collective-permute-start | bytes 3145736 | tf_op jit(solution)/shard_map/ppermute | solution.py:62
  64.1 31.5 %collective-permute-start.1 = (bf16[8,512,256]{2,1,0:T(8,128)(2,1)S(1)}, bf16[8,512,256]{2,1,0:T(8,128)(2,1)}, u32[]{:S(2)}, u32[]{:S(2)}) collective-permute-start(bf16[8,512,256]{2,1,0:T(8,128)(2,1)S(1)} %all-to-all-done.refs_0_), channel_id=1, source_target_pairs={{0,1},{1,0},{2,3},{3,2},{4,5},{5,4},{6,7},{7,6},{8,9},{9,8},{10,11... | collective-permute-start | bytes 6291464 | tf_op jit(solution)/shard_map/ppermute | solution.py:62
  64.7 29.5 %all-to-all-start.1 = ((bf16[8,64,1024]{2,1,0:T(8,128)(2,1)}), bf16[8,64,1024]{2,1,0:T(8,128)(2,1)}, u32[]{:S(2)}, u32[]{:S(2)}) async-start(bf16[8,64,1024]{2,1,0:T(8,128)(2,1)} %select_add_fusion), calls=%async_computation.1 | async-start | bytes 2097152 | tf_op jit(solution)/shard_map/all_to_all | solution.py:70
  134.2 8.5 %collective-permute-start.6 = (bf16[4,352,256]{2,1,0:T(8,128)(2,1)S(1)}, bf16[4,352,256]{2,1,0:T(8,128)(2,1)S(1)}, u32[]{:S(2)}, u32[]{:S(2)}) collective-permute-start(bf16[4,352,256]{2,1,0:T(8,128)(2,1)S(1)} %get-tuple-element.132), channel_id=1, source_target_pairs={{0,1},{1,0},{2,3},{3,2},{4,5},{5,4},{6,7},{7,6},{8,9},{9,8},{10,11... | collective-permute-start | bytes 2162696 | tf_op jit(solution)/shard_map/ppermute | solution.py:62
  135.6 15.1 %collective-permute-start.4 = (bf16[4,352,256]{2,1,0:T(8,128)(2,1)S(1)}, bf16[4,352,256]{2,1,0:T(8,128)(2,1)S(1)}, u32[]{:S(2)}, u32[]{:S(2)}) collective-permute-start(bf16[4,352,256]{2,1,0:T(8,128)(2,1)S(1)} %add_convert_fusion.3), channel_id=1, source_target_pairs={{0,6},{1,9},{2,4},{3,11},{4,2},{5,13},{6,0},{7,15},{8,14},{9,1},{1... | collective-permute-start | bytes 2162696 | tf_op jit(solution)/shard_map/ppermute | solution.py:79
  140.5 10.2 %collective-permute-start.5 = (bf16[4,160,256]{2,1,0:T(8,128)(2,1)S(1)}, bf16[4,160,256]{2,1,0:T(8,128)(2,1)S(1)}, u32[]{:S(2)}, u32[]{:S(2)}) collective-permute-start(bf16[4,160,256]{2,1,0:T(8,128)(2,1)S(1)} %add_convert_fusion.7), channel_id=1, source_target_pairs={{0,2},{1,3},{2,0},{3,1},{4,6},{5,7},{6,4},{7,5},{8,10},{9,11},{10,... | collective-permute-start | bytes 983048 | tf_op jit(solution)/shard_map/ppermute | solution.py:79
  151.8 8.1 %collective-permute-start.8 = (bf16[2,352,256]{2,1,0:T(8,128)(2,1)}, bf16[2,352,256]{2,1,0:T(8,128)(2,1)}, u32[]{:S(2)}, u32[]{:S(2)}) collective-permute-start(bf16[2,352,256]{2,1,0:T(8,128)(2,1)} %slice.364), channel_id=1, source_target_pairs={{0,2},{1,7},{2,0},{3,5},{4,6},{5,3},{6,4},{7,1},{8,10},{9,15},{10,... | collective-permute-start | bytes 1081352 | tf_op jit(solution)/shard_map/ppermute | solution.py:79
  153.3 6.5 %collective-permute-start.9 = (bf16[2,160,256]{2,1,0:T(8,128)(2,1)S(1)}, bf16[2,160,256]{2,1,0:T(8,128)(2,1)S(1)}, u32[]{:S(2)}, u32[]{:S(2)}) collective-permute-start(bf16[2,160,256]{2,1,0:T(8,128)(2,1)S(1)} %slice.368), channel_id=1, source_target_pairs={{0,8},{1,9},{2,10},{3,11},{4,12},{5,13},{6,14},{7,15},{8,0},{9,1},... | collective-permute-start | bytes 491528 | tf_op jit(solution)/shard_map/ppermute | solution.py:79
  154.1 10.7 %collective-permute-start.12 = (bf16[64,1024]{1,0:T(8,128)(2,1)S(1)}, bf16[64,1024]{1,0:T(8,128)(2,1)S(1)}, u32[]{:S(2)}, u32[]{:S(2)}) collective-permute-start(bf16[64,1024]{1,0:T(8,128)(2,1)S(1)} %reduce_sum.12), channel_id=1, source_target_pairs={{0,64},{64,0},{1,65},{65,1},{2,66},{66,2},{3,67},{67,3},{4,68},{68... | collective-permute-start | bytes 393224 | tf_op jit(solution)/shard_map/ppermute | solution.py:66
  161.2 7.1 %collective-permute-start.10 = (bf16[352,256]{1,0:T(8,128)(2,1)S(1)}, bf16[352,256]{1,0:T(8,128)(2,1)S(1)}, u32[]{:S(2)}, u32[]{:S(2)}) collective-permute-start(bf16[352,256]{1,0:T(8,128)(2,1)S(1)} %fusion.12), channel_id=1, source_target_pairs={{0,8},{1,3},{2,10},{3,1},{4,12},{5,7},{6,14},{7,5},{8,0},{9,11},{1... | collective-permute-start | bytes 540680 | tf_op jit(solution)/shard_map/ppermute | solution.py:79
  169.8 49.0 %all-to-all-start.4 = ((bf16[8,512,256]{2,1,0:T(8,128)(2,1)}), bf16[8,512,256]{2,1,0:T(8,128)(2,1)}, u32[]{:S(2)}, u32[]{:S(2)}) async-start(bf16[8,512,256]{2,1,0:T(8,128)(2,1)} %broadcast_in_dim.42), calls=%async_computation.4 | async-start | bytes 4194304 | tf_op jit(solution)/shard_map/all_to_all | solution.py:70
  181.8 23.7 %collective-permute-start.13 = (bf16[128,1024]{1,0:T(8,128)(2,1)S(1)}, bf16[128,1024]{1,0:T(8,128)(2,1)S(1)}, u32[]{:S(2)}, u32[]{:S(2)}) collective-permute-start(bf16[128,1024]{1,0:T(8,128)(2,1)S(1)} %shard_map.161), channel_id=1, source_target_pairs={{0,64},{64,0},{1,65},{65,1},{2,66},{66,2},{3,67},{67,3},{4,68},{68... | collective-permute-start | bytes 786440 | tf_op jit(solution)/shard_map/ppermute | solution.py:66
  206.9 8.0 %collective-permute-start.14 = (bf16[128,1024]{1,0:T(8,128)(2,1)S(1)}, bf16[128,1024]{1,0:T(8,128)(2,1)S(1)}, u32[]{:S(2)}, u32[]{:S(2)}) collective-permute-start(bf16[128,1024]{1,0:T(8,128)(2,1)S(1)} %shard_map.162), channel_id=1, source_target_pairs={{0,64},{64,0},{1,65},{65,1},{2,66},{66,2},{3,67},{67,3},{4,68},{68... | collective-permute-start | bytes 786440 | tf_op jit(solution)/shard_map/ppermute | solution.py:66
  215.0 7.1 %collective-permute-start.15 = (bf16[80,1024]{1,0:T(8,128)(2,1)S(1)}, bf16[80,1024]{1,0:T(8,128)(2,1)S(1)}, u32[]{:S(2)}, u32[]{:S(2)}) collective-permute-start(bf16[80,1024]{1,0:T(8,128)(2,1)S(1)} %get-tuple-element.240), channel_id=1, source_target_pairs={{0,8},{1,3},{2,10},{3,1},{4,12},{5,7},{6,14},{7,5},{8,0},{9,11},{1... | collective-permute-start | bytes 491528 | tf_op jit(solution)/shard_map/ppermute | solution.py:79
  222.2 7.6 %collective-permute-start.18 = (bf16[2,80,1024]{2,1,0:T(8,128)(2,1)S(1)}, bf16[2,80,1024]{2,1,0:T(8,128)(2,1)S(1)}, u32[]{:S(2)}, u32[]{:S(2)}) collective-permute-start(bf16[2,80,1024]{2,1,0:T(8,128)(2,1)S(1)} %pad_maximum_fusion.7), channel_id=1, source_target_pairs={{0,2},{1,7},{2,0},{3,5},{4,6},{5,3},{6,4},{7,1},{8,10},{9,15},{10,... | collective-permute-start | bytes 983048 | tf_op jit(solution)/shard_map/ppermute | solution.py:79
  224.3 30.0 %collective-permute-start.17 = (bf16[8,512,256]{2,1,0:T(8,128)(2,1)}, bf16[8,512,256]{2,1,0:T(8,128)(2,1)S(1)}, u32[]{:S(2)}, u32[]{:S(2)}) collective-permute-start(bf16[8,512,256]{2,1,0:T(8,128)(2,1)} %all-to-all-done.4.refs_0_), channel_id=1, source_target_pairs={{0,1},{1,0},{2,3},{3,2},{4,5},{5,4},{6,7},{7,6},{8,9},{9,8},{10,11... | collective-permute-start | bytes 6291464 | tf_op jit(solution)/shard_map/ppermute | solution.py:62
  229.9 11.9 %collective-permute-start.20 = (bf16[4,80,1024]{2,1,0:T(8,128)(2,1)S(1)}, bf16[4,80,1024]{2,1,0:T(8,128)(2,1)S(1)}, u32[]{:S(2)}, u32[]{:S(2)}) collective-permute-start(bf16[4,80,1024]{2,1,0:T(8,128)(2,1)S(1)} %pad_maximum_fusion.3.refs_0_), channel_id=1, source_target_pairs={{0,6},{1,9},{2,4},{3,11},{4,2},{5,13},{6,0},{7,15},{8,14},{9,1},{1... | collective-permute-start | bytes 1966088 | tf_op jit(solution)/shard_map/ppermute | solution.py:79
  232.0 7.9 %collective-permute-start.21 = (bf16[4,48,1024]{2,1,0:T(8,128)(2,1)S(1)}, bf16[4,48,1024]{2,1,0:T(8,128)(2,1)S(1)}, u32[]{:S(2)}, u32[]{:S(2)}) collective-permute-start(bf16[4,48,1024]{2,1,0:T(8,128)(2,1)S(1)} %pad_maximum_fusion.4.refs_1_), channel_id=1, source_target_pairs={{0,2},{1,3},{2,0},{3,1},{4,6},{5,7},{6,4},{7,5},{8,10},{9,11},{10,... | collective-permute-start | bytes 1179656 | tf_op jit(solution)/shard_map/ppermute | solution.py:79
  233.8 8.7 %collective-permute-start.23 = (bf16[4,80,1024]{2,1,0:T(8,128)(2,1)S(1)}, bf16[4,80,1024]{2,1,0:T(8,128)(2,1)S(1)}, u32[]{:S(2)}, u32[]{:S(2)}) collective-permute-start(bf16[4,80,1024]{2,1,0:T(8,128)(2,1)S(1)} %pad_maximum_fusion.3.refs_0_), channel_id=1, source_target_pairs={{0,1},{1,0},{2,3},{3,2},{4,5},{5,4},{6,7},{7,6},{8,9},{9,8},{10,11... | collective-permute-start | bytes 1966088 | tf_op jit(solution)/shard_map/ppermute | solution.py:62
  233.8 8.7 %collective-permute-start.24 = (bf16[4,48,1024]{2,1,0:T(8,128)(2,1)S(1)}, bf16[4,48,1024]{2,1,0:T(8,128)(2,1)S(1)}, u32[]{:S(2)}, u32[]{:S(2)}) collective-permute-start(bf16[4,48,1024]{2,1,0:T(8,128)(2,1)S(1)} %pad_maximum_fusion.4.refs_1_), channel_id=1, source_target_pairs={{0,1},{1,0},{2,3},{3,2},{4,5},{5,4},{6,7},{7,6},{8,9},{9,8},{10,11... | collective-permute-start | bytes 1179656 | tf_op jit(solution)/shard_map/ppermute | solution.py:62
  244.5 11.3 %collective-permute-start.22 = (bf16[2,128,512]{2,1,0:T(8,128)(2,1)S(1)}, bf16[2,128,512]{2,1,0:T(8,128)(2,1)S(1)}, u32[]{:S(2)}, u32[]{:S(2)}) collective-permute-start(bf16[2,128,512]{2,1,0:T(8,128)(2,1)S(1)} %slice_bitcast_fusion.5), channel_id=1, source_target_pairs={{0,16},{16,32},{32,48},{1,17},{17,33},{33,49},{2,18},{18,34},{34,5... | collective-permute-start | bytes 786440 | tf_op jit(solution)/shard_map/ppermute | solution.py:529
  248.9 9.4 %collective-permute-start.27 = (bf16[2,128,512]{2,1,0:T(8,128)(2,1)S(1)}, bf16[2,128,512]{2,1,0:T(8,128)(2,1)S(1)}, u32[]{:S(2)}, u32[]{:S(2)}) collective-permute-start(bf16[2,128,512]{2,1,0:T(8,128)(2,1)S(1)} %slice_bitcast_fusion.4), channel_id=1, source_target_pairs={{0,16},{16,32},{32,48},{1,17},{17,33},{33,49},{2,18},{18,34},{34,5... | collective-permute-start | bytes 786440 | tf_op jit(solution)/shard_map/ppermute | solution.py:529
  265.0 12.6 %collective-permute-start.30 = (bf16[4,352,256]{2,1,0:T(8,128)(2,1)S(1)}, bf16[4,352,256]{2,1,0:T(8,128)(2,1)S(1)}, u32[]{:S(2)}, u32[]{:S(2)}) collective-permute-start(bf16[4,352,256]{2,1,0:T(8,128)(2,1)S(1)} %add_convert_fusion.2), channel_id=1, source_target_pairs={{0,6},{1,9},{2,4},{3,11},{4,2},{5,13},{6,0},{7,15},{8,14},{9,1},{1... | collective-permute-start | bytes 2162696 | tf_op jit(solution)/shard_map/ppermute | solution.py:79
  267.4 10.2 %collective-permute-start.31 = (bf16[4,160,256]{2,1,0:T(8,128)(2,1)S(1)}, bf16[4,160,256]{2,1,0:T(8,128)(2,1)S(1)}, u32[]{:S(2)}, u32[]{:S(2)}) collective-permute-start(bf16[4,160,256]{2,1,0:T(8,128)(2,1)S(1)} %add_convert_fusion.6), channel_id=1, source_target_pairs={{0,2},{1,3},{2,0},{3,1},{4,6},{5,7},{6,4},{7,5},{8,10},{9,11},{10,... | collective-permute-start | bytes 983048 | tf_op jit(solution)/shard_map/ppermute | solution.py:79
  277.9 7.5 %collective-permute-start.34 = (bf16[2,352,256]{2,1,0:T(8,128)(2,1)S(1)}, bf16[2,352,256]{2,1,0:T(8,128)(2,1)S(1)}, u32[]{:S(2)}, u32[]{:S(2)}) collective-permute-start(bf16[2,352,256]{2,1,0:T(8,128)(2,1)S(1)} %slice.363), channel_id=1, source_target_pairs={{0,2},{1,7},{2,0},{3,5},{4,6},{5,3},{6,4},{7,1},{8,10},{9,15},{10,... | collective-permute-start | bytes 1081352 | tf_op jit(solution)/shard_map/ppermute | solution.py:79
  285.5 6.8 %collective-permute-start.36 = (bf16[352,256]{1,0:T(8,128)(2,1)S(1)}, bf16[352,256]{1,0:T(8,128)(2,1)S(1)}, u32[]{:S(2)}, u32[]{:S(2)}) collective-permute-start(bf16[352,256]{1,0:T(8,128)(2,1)S(1)} %fusion.13), channel_id=1, source_target_pairs={{0,8},{1,3},{2,10},{3,1},{4,12},{5,7},{6,14},{7,5},{8,0},{9,11},{1... | collective-permute-start | bytes 540680 | tf_op jit(solution)/shard_map/ppermute | solution.py:79
  292.4 8.0 %collective-permute-start.38 = (bf16[512,256]{1,0:T(8,128)(2,1)S(1)}, bf16[512,256]{1,0:T(8,128)(2,1)S(1)}, u32[]{:S(2)}, u32[]{:S(2)}) collective-permute-start(bf16[512,256]{1,0:T(8,128)(2,1)S(1)} %pad_maximum_fusion.11), channel_id=1, source_target_pairs={{0,64},{64,0},{1,65},{65,1},{2,66},{66,2},{3,67},{67,3},{4,68},{68... | collective-permute-start | bytes 786440 | tf_op jit(solution)/shard_map/ppermute | solution.py:66
  300.4 7.0 %collective-permute-start.39 = (bf16[352,256]{1,0:T(8,128)(2,1)S(1)}, bf16[352,256]{1,0:T(8,128)(2,1)S(1)}, u32[]{:S(2)}, u32[]{:S(2)}) collective-permute-start(bf16[352,256]{1,0:T(8,128)(2,1)S(1)} %get-tuple-element.236), channel_id=1, source_target_pairs={{0,8},{1,3},{2,10},{3,1},{4,12},{5,7},{6,14},{7,5},{8,0},{9,11},{1... | collective-permute-start | bytes 540680 | tf_op jit(solution)/shard_map/ppermute | solution.py:79
  307.4 7.7 %collective-permute-start.41 = (bf16[2,352,256]{2,1,0:T(8,128)(2,1)S(1)}, bf16[2,352,256]{2,1,0:T(8,128)(2,1)S(1)}, u32[]{:S(2)}, u32[]{:S(2)}) collective-permute-start(bf16[2,352,256]{2,1,0:T(8,128)(2,1)S(1)} %pad_maximum_fusion.5), channel_id=1, source_target_pairs={{0,2},{1,7},{2,0},{3,5},{4,6},{5,3},{6,4},{7,1},{8,10},{9,15},{10,... | collective-permute-start | bytes 1081352 | tf_op jit(solution)/shard_map/ppermute | solution.py:79
  315.2 13.7 %collective-permute-start.45 = (bf16[4,352,256]{2,1,0:T(8,128)(2,1)S(1)}, bf16[4,352,256]{2,1,0:T(8,128)(2,1)S(1)}, u32[]{:S(2)}, u32[]{:S(2)}) collective-permute-start(bf16[4,352,256]{2,1,0:T(8,128)(2,1)S(1)} %pad_maximum_fusion.1.refs_0_), channel_id=1, source_target_pairs={{0,6},{1,9},{2,4},{3,11},{4,2},{5,13},{6,0},{7,15},{8,14},{9,1},{1... | collective-permute-start | bytes 2162696 | tf_op jit(solution)/shard_map/ppermute | solution.py:79
  319.7 7.2 %collective-permute-start.46 = (bf16[4,160,256]{2,1,0:T(8,128)(2,1)S(1)}, bf16[4,160,256]{2,1,0:T(8,128)(2,1)S(1)}, u32[]{:S(2)}, u32[]{:S(2)}) collective-permute-start(bf16[4,160,256]{2,1,0:T(8,128)(2,1)S(1)} %pad_maximum_fusion.8.refs_1_), channel_id=1, source_target_pairs={{0,2},{1,3},{2,0},{3,1},{4,6},{5,7},{6,4},{7,5},{8,10},{9,11},{10,... | collective-permute-start | bytes 983048 | tf_op jit(solution)/shard_map/ppermute | solution.py:79
  319.8 11.8 %collective-permute-start.43 = (bf16[4,352,256]{2,1,0:T(8,128)(2,1)S(1)}, bf16[4,352,256]{2,1,0:T(8,128)(2,1)S(1)}, u32[]{:S(2)}, u32[]{:S(2)}) collective-permute-start(bf16[4,352,256]{2,1,0:T(8,128)(2,1)S(1)} %pad_maximum_fusion.1.refs_0_), channel_id=1, source_target_pairs={{0,1},{1,0},{2,3},{3,2},{4,5},{5,4},{6,7},{7,6},{8,9},{9,8},{10,11... | collective-permute-start | bytes 2162696 | tf_op jit(solution)/shard_map/ppermute | solution.py:62
  328.9 6.4 %collective-permute-start.47 = (bf16[4,352,256]{2,1,0:T(8,128)(2,1)S(1)}, bf16[4,352,256]{2,1,0:T(8,128)(2,1)S(1)}, u32[]{:S(2)}, u32[]{:S(2)}) collective-permute-start(bf16[4,352,256]{2,1,0:T(8,128)(2,1)S(1)} %collective-permute-done.45.refs_2_), channel_id=1, source_target_pairs={{0,1},{1,0},{2,3},{3,2},{4,5},{5,4},{6,7},{7,6},{8,9},{9,8},{10,11... | collective-permute-start | bytes 2162696 | tf_op jit(solution)/shard_map/ppermute | solution.py:62
  370.3 13.6 %collective-permute-start.51 = (bf16[4,352,256]{2,1,0:T(8,128)(2,1)S(1)}, bf16[4,352,256]{2,1,0:T(8,128)(2,1)S(1)}, u32[]{:S(2)}, u32[]{:S(2)}) collective-permute-start(bf16[4,352,256]{2,1,0:T(8,128)(2,1)S(1)} %add_convert_fusion.1), channel_id=1, source_target_pairs={{0,6},{1,9},{2,4},{3,11},{4,2},{5,13},{6,0},{7,15},{8,14},{9,1},{1... | collective-permute-start | bytes 2162696 | tf_op jit(solution)/shard_map/ppermute | solution.py:79
  373.7 10.2 %collective-permute-start.52 = (bf16[4,160,256]{2,1,0:T(8,128)(2,1)S(1)}, bf16[4,160,256]{2,1,0:T(8,128)(2,1)S(1)}, u32[]{:S(2)}, u32[]{:S(2)}) collective-permute-start(bf16[4,160,256]{2,1,0:T(8,128)(2,1)S(1)} %add_convert_fusion.5), channel_id=1, source_target_pairs={{0,2},{1,3},{2,0},{3,1},{4,6},{5,7},{6,4},{7,5},{8,10},{9,11},{10,... | collective-permute-start | bytes 983048 | tf_op jit(solution)/shard_map/ppermute | solution.py:79
  384.1 7.5 %collective-permute-start.55 = (bf16[2,352,256]{2,1,0:T(8,128)(2,1)S(1)}, bf16[2,352,256]{2,1,0:T(8,128)(2,1)S(1)}, u32[]{:S(2)}, u32[]{:S(2)}) collective-permute-start(bf16[2,352,256]{2,1,0:T(8,128)(2,1)S(1)} %slice.362), channel_id=1, source_target_pairs={{0,2},{1,7},{2,0},{3,5},{4,6},{5,3},{6,4},{7,1},{8,10},{9,15},{10,... | collective-permute-start | bytes 1081352 | tf_op jit(solution)/shard_map/ppermute | solution.py:79
  398.3 7.3 %collective-permute-start.59 = (bf16[352,256]{1,0:T(8,128)(2,1)S(1)}, bf16[352,256]{1,0:T(8,128)(2,1)S(1)}, u32[]{:S(2)}, u32[]{:S(2)}) collective-permute-start(bf16[352,256]{1,0:T(8,128)(2,1)S(1)} %fusion.5), channel_id=1, source_target_pairs={{0,8},{1,3},{2,10},{3,1},{4,12},{5,7},{6,14},{7,5},{8,0},{9,11},{1... | collective-permute-start | bytes 540680 | tf_op jit(solution)/shard_map/ppermute | solution.py:79
  405.6 7.9 %collective-permute-start.61 = (bf16[2,352,256]{2,1,0:T(8,128)(2,1)S(1)}, bf16[2,352,256]{2,1,0:T(8,128)(2,1)S(1)}, u32[]{:S(2)}, u32[]{:S(2)}) collective-permute-start(bf16[2,352,256]{2,1,0:T(8,128)(2,1)S(1)} %pad_maximum_fusion.6), channel_id=1, source_target_pairs={{0,2},{1,7},{2,0},{3,5},{4,6},{5,3},{6,4},{7,1},{8,10},{9,15},{10,... | collective-permute-start | bytes 1081352 | tf_op jit(solution)/shard_map/ppermute | solution.py:79
  413.6 13.4 %collective-permute-start.65 = (bf16[4,352,256]{2,1,0:T(8,128)(2,1)S(1)}, bf16[4,352,256]{2,1,0:T(8,128)(2,1)S(1)}, u32[]{:S(2)}, u32[]{:S(2)}) collective-permute-start(bf16[4,352,256]{2,1,0:T(8,128)(2,1)S(1)} %pad_maximum_fusion.2.refs_0_), channel_id=1, source_target_pairs={{0,6},{1,9},{2,4},{3,11},{4,2},{5,13},{6,0},{7,15},{8,14},{9,1},{1... | collective-permute-start | bytes 2162696 | tf_op jit(solution)/shard_map/ppermute | solution.py:79
  417.7 7.2 %collective-permute-start.66 = (bf16[4,160,256]{2,1,0:T(8,128)(2,1)S(1)}, bf16[4,160,256]{2,1,0:T(8,128)(2,1)S(1)}, u32[]{:S(2)}, u32[]{:S(2)}) collective-permute-start(bf16[4,160,256]{2,1,0:T(8,128)(2,1)S(1)} %pad_maximum_fusion.9.refs_1_), channel_id=1, source_target_pairs={{0,2},{1,3},{2,0},{3,1},{4,6},{5,7},{6,4},{7,5},{8,10},{9,11},{10,... | collective-permute-start | bytes 983048 | tf_op jit(solution)/shard_map/ppermute | solution.py:79
  417.8 12.0 %collective-permute-start.63 = (bf16[4,352,256]{2,1,0:T(8,128)(2,1)S(1)}, bf16[4,352,256]{2,1,0:T(8,128)(2,1)S(1)}, u32[]{:S(2)}, u32[]{:S(2)}) collective-permute-start(bf16[4,352,256]{2,1,0:T(8,128)(2,1)S(1)} %pad_maximum_fusion.2.refs_0_), channel_id=1, source_target_pairs={{0,1},{1,0},{2,3},{3,2},{4,5},{5,4},{6,7},{7,6},{8,9},{9,8},{10,11... | collective-permute-start | bytes 2162696 | tf_op jit(solution)/shard_map/ppermute | solution.py:62
  439.5 6.4 %collective-permute-start.73 = (bf16[4,352,256]{2,1,0:T(8,128)(2,1)S(1)}, bf16[4,352,256]{2,1,0:T(8,128)(2,1)S(1)}, u32[]{:S(2)}, u32[]{:S(2)}) collective-permute-start(bf16[4,352,256]{2,1,0:T(8,128)(2,1)S(1)} %get-tuple-element.222), channel_id=1, source_target_pairs={{0,1},{1,0},{2,3},{3,2},{4,5},{5,4},{6,7},{7,6},{8,9},{9,8},{10,11... | collective-permute-start | bytes 2162696 | tf_op jit(solution)/shard_map/ppermute | solution.py:62
  441.0 13.6 %collective-permute-start.71 = (bf16[4,352,256]{2,1,0:T(8,128)(2,1)S(1)}, bf16[4,352,256]{2,1,0:T(8,128)(2,1)S(1)}, u32[]{:S(2)}, u32[]{:S(2)}) collective-permute-start(bf16[4,352,256]{2,1,0:T(8,128)(2,1)S(1)} %add_convert_fusion), channel_id=1, source_target_pairs={{0,6},{1,9},{2,4},{3,11},{4,2},{5,13},{6,0},{7,15},{8,14},{9,1},{1... | collective-permute-start | bytes 2162696 | tf_op jit(solution)/shard_map/ppermute | solution.py:79
  444.4 10.2 %collective-permute-start.72 = (bf16[4,160,256]{2,1,0:T(8,128)(2,1)S(1)}, bf16[4,160,256]{2,1,0:T(8,128)(2,1)S(1)}, u32[]{:S(2)}, u32[]{:S(2)}) collective-permute-start(bf16[4,160,256]{2,1,0:T(8,128)(2,1)S(1)} %add_convert_fusion.4), channel_id=1, source_target_pairs={{0,2},{1,3},{2,0},{3,1},{4,6},{5,7},{6,4},{7,5},{8,10},{9,11},{10,... | collective-permute-start | bytes 983048 | tf_op jit(solution)/shard_map/ppermute | solution.py:79
  454.9 7.5 %collective-permute-start.75 = (bf16[2,352,256]{2,1,0:T(8,128)(2,1)S(1)}, bf16[2,352,256]{2,1,0:T(8,128)(2,1)S(1)}, u32[]{:S(2)}, u32[]{:S(2)}) collective-permute-start(bf16[2,352,256]{2,1,0:T(8,128)(2,1)S(1)} %slice.361), channel_id=1, source_target_pairs={{0,2},{1,7},{2,0},{3,5},{4,6},{5,3},{6,4},{7,1},{8,10},{9,15},{10,... | collective-permute-start | bytes 1081352 | tf_op jit(solution)/shard_map/ppermute | solution.py:79
  468.5 6.6 %collective-permute-start.79 = (bf16[256,256]{1,0:T(8,128)(2,1)S(1)}, bf16[256,256]{1,0:T(8,128)(2,1)S(1)}, u32[]{:S(2)}, u32[]{:S(2)}) collective-permute-start(bf16[256,256]{1,0:T(8,128)(2,1)S(1)} %slice.253), channel_id=1, source_target_pairs={{0,64},{64,0},{1,65},{65,1},{2,66},{66,2},{3,67},{67,3},{4,68},{68... | collective-permute-start | bytes 393224 | tf_op jit(solution)/shard_map/ppermute | solution.py:66
  (58 other events, 460.4 us)
Sparse Core Ops, SparseCore 0:
  42.0 90.4 all-gather.1

commit v8 on v7

--- a/solution.py
+++ b/solution.py
@@ -45,6 +45,7 @@
 STARTS = (0, 352)
 ENC_PARTS = (80, 48)
 ENC_STARTS = (0, 80)
+PIECE = 512
 MASKS = (((4, 1, 3), (1, 3, 4)), ((3, 4, 1), (3, 4, 1)))
 
 
@@ -107,11 +108,6 @@
 
 def gather_chips(local):
     return later_rounds(local, together(*first_round(local)))
-
-
-def spread(local):
-    rows = jnp.concatenate(local)
-    return jnp.broadcast_to(rows[None], (CHIPS,) + rows.shape)
 
 
 def scatter_sum(places_both, mixed, weight):
@@ -363,46 +359,31 @@
     return [rows[start : start + count] for start, count in zip(STARTS, PARTS)]
 
 
-def look_up(ids, enc_embed, core, section):
-    vocab_here = enc_embed.shape[0]
-    mine = lax.dynamic_slice_in_dim(ids, section * (NB_LEN // 2), NB_LEN // 2, axis=1)
-    wanted = mine.reshape(CHIPS, 2, NB_LEN // 2) - lax.axis_index(MP) * vocab_here
-
-    def rows(at):
-        picks = lax.dynamic_index_in_dim(wanted, at, 1, keepdims=False).reshape(-1)
-        inside = (picks >= 0) & (picks < vocab_here)
-        found = enc_embed[jnp.clip(picks, 0, vocab_here - 1)]
-        found = jnp.where(inside[:, None], found, jnp.zeros((), bf16))
-        return found.reshape(CHIPS, NB_LEN // 2, ENC_D)
-
-    far = core_swap(rows(1 - core))
-    return rows(core) + far
-
-
-def join_halves(half, section):
-    far = section_swap(half)
-    return jnp.where(
-        section == 0, jnp.concatenate([half, far], axis=0), jnp.concatenate([far, half], axis=0)
-    )
-
-
-def weight_parts(section, enc_qkv, enc_out, enc_up, enc_down):
-    width = ENC_D // 2
-    triple = lax.dynamic_slice_in_dim(enc_qkv, section * width, width, axis=2)
+def looked_up(own, other):
+    total = own + core_swap(other)
+    total = total[:4] + neighbour(total[4:], 0, 2)
+    total = total[:2] + neighbour(total[2:], 0, 1)
+    return total[0] + neighbour(total[1], 0, 0)
+
+
+def weight_parts(enc_qkv, enc_out, enc_up, enc_down):
     up = enc_up.reshape(64, 16, 2, 2, 64)
-    up = lax.dynamic_index_in_dim(up, section, 2, keepdims=False)
-    up = jnp.transpose(up, (2, 0, 1, 3)).reshape(2, 64, 2, width)
-    down = lax.dynamic_slice_in_dim(enc_down, section * 128, 128, axis=0)
-    down = down.reshape(2, 64, 2, width)
-    return jnp.concatenate(
-        [
-            jnp.transpose(up, (0, 2, 1, 3)).reshape(4, 64, width),
-            jnp.transpose(down, (0, 2, 1, 3)).reshape(4, 64, width),
-            jnp.transpose(triple, (1, 0, 2)),
-            jnp.transpose(enc_out.reshape(64, 2, width), (1, 0, 2)),
-        ],
-        axis=0,
-    )
+    up = jnp.transpose(up, (2, 3, 0, 1, 4)).reshape(2, 2, 64, 2, PIECE)
+    up = jnp.transpose(up, (0, 1, 3, 2, 4)).reshape(2, 4, 64, PIECE)
+    down = enc_down.reshape(2, 2, 64, 2, PIECE)
+    down = jnp.transpose(down, (0, 1, 3, 2, 4)).reshape(2, 4, 64, PIECE)
+    triple = jnp.transpose(enc_qkv.reshape(64, 3, 2, PIECE), (2, 1, 0, 3)).reshape(6, 64, PIECE)
+    out = jnp.transpose(enc_out.reshape(64, 2, PIECE), (1, 0, 2))
+    feed = jnp.concatenate([up, down], axis=1).reshape(16, 64, PIECE)
+    return [feed, jnp.concatenate([triple, out], axis=0)]
+
+
+def assemble(place_refs, refs, part, piece, w_ref):
+    for place_ref, (near, far) in zip(place_refs, (refs[:2], refs[2:])):
+        for block in range(CHIPS):
+            chip = place_ref[1 + part * CHIPS + block]
+            start = pl.multiple_of((2 * chip + place_ref[0]) * 64, 64)
+            w_ref[pl.ds(start, 64), :] = (near if block < 4 else far)[block % 4, piece]
 
 
 def scaled_rows(values, gain):
@@ -411,87 +392,118 @@
     return (wide * gain).astype(bf16), root
 
 
-def enc_mix_kernel(section_ref, x_ref, gain_ref, q_ref, k_ref, v_ref, o0_ref, o1_ref, out_ref, mix_ref):
+def enc_mix_kernel(own_ref, other_ref, x_ref, gain_ref, *refs):
+    blocks, (out_ref, w_ref, mix_ref) = refs[:4], refs[4:]
+    places_both = (own_ref, other_ref)
+    for piece in range(8):
+        assemble(places_both, blocks, 1, piece, w_ref.at[piece])
     scaled, root = scaled_rows(x_ref[...], gain_ref[...])
-    triple = [
-        (jnp.dot(scaled, ref[0], preferred_element_type=f32) / root).astype(bf16)
-        for ref in (q_ref, k_ref, v_ref)
+    for half in range(2):
+        triple = []
+        for part in range(3):
+            product = jnp.dot(scaled, w_ref[3 * half + part], preferred_element_type=f32)
+            triple.append((product / root).astype(bf16))
+        for head in range(ENC_HEADS // 2):
+            cols = slice(head * ENC_HEAD, (head + 1) * ENC_HEAD)
+            scores = lax.dot_general(
+                triple[0][:, cols],
+                triple[1][:, cols],
+                (((1,), (1,)), ((), ())),
+                preferred_element_type=f32,
+            )
+            weights = jnp.exp(scores * ENC_HEAD ** (-0.5))
+            denom = jnp.sum(weights, axis=1, keepdims=True)
+            numer = jnp.dot(weights.astype(bf16), triple[2][:, cols], preferred_element_type=f32)
+            start = half * PIECE + head * ENC_HEAD
+            mix_ref[:, start : start + ENC_HEAD] = (numer / denom).astype(bf16)
+    mixed = mix_ref[...]
+    for at in range(2):
+        cols = slice(at * PIECE, (at + 1) * PIECE)
+        product = jnp.dot(mixed, w_ref[6 + at], preferred_element_type=f32)
+        out_ref[:, cols] = (x_ref[:, cols].astype(f32) + product).astype(bf16)
+
+
+def enc_feed_kernel(own_ref, other_ref, x_ref, gain_ref, *refs):
+    blocks, (out_ref, w_ref, acc_ref) = refs[:4], refs[4:]
+    places_both = (own_ref, other_ref)
+    for piece in range(8):
+        assemble(places_both, blocks, 0, piece, w_ref.at[piece])
+    scaled, root = scaled_rows(x_ref[...], gain_ref[...])
+
+    @pl.when(pl.program_id(0) == 0)
+    def _():
+        acc_ref[...] = x_ref[...].astype(f32)
+
+    for row in range(2):
+        hidden = []
+        for piece in range(2):
+            product = jnp.dot(scaled, w_ref[2 * row + piece], preferred_element_type=f32)
+            hidden.append(jax.nn.gelu(product / root, approximate=True).astype(bf16))
+        hidden = jnp.concatenate(hidden, axis=1)
+        for at in range(2):
+            cols = slice(at * PIECE, (at + 1) * PIECE)
+            right = w_ref[4 + 2 * row + at]
+            acc_ref[:, cols] += jnp.dot(hidden, right, preferred_element_type=f32)
+
+    @pl.when(pl.program_id(0) == 1)
+    def _():
+        out_ref[...] = acc_ref[...].astype(bf16)
+
+
+def encode(places_both, embedded, enc_norms, feed, mix):
+    out = jax.ShapeDtypeStruct((NB_LEN, ENC_D), bf16)
+    full = whole((NB_LEN, ENC_D))
+    gain = whole((1, ENC_D))
+
+    def call(kernel, steps, pieces, scratch, x, gains, rows):
+        block = (4, rows[0].shape[1] // steps, 64, PIECE)
+        return pl.pallas_call(
+            kernel,
+            grid_spec=pltpu.PrefetchScalarGridSpec(
+                num_scalar_prefetch=2,
+                grid=(steps,),
+                in_specs=[full, gain]
+                + [pl.BlockSpec(block, lambda s, *_: (0, s, 0, 0)) for _ in rows],
+                out_specs=full,
+                scratch_shapes=[pltpu.VMEM((pieces, ENC_D, PIECE), bf16), scratch],
+            ),
+            out_shape=out,
+            compiler_params=params(40),
+        )(*places_both, x, gains, *rows)
+
+    inner = call(
+        enc_mix_kernel, 1, 8, pltpu.VMEM((NB_LEN, ENC_D), bf16), embedded, enc_norms[:1], mix
+    )
+    return call(
+        enc_feed_kernel, 2, 8, pltpu.VMEM((NB_LEN, ENC_D), f32), inner, enc_norms[1:], feed
+    )
+
+
+def encode_neighbour(places_both, ids, enc_embed, enc_norms, local):
+    vocab_here = enc_embed.shape[0]
+    wanted = ids - lax.axis_index(MP) * vocab_here
+
+    def rows(place, wanted):
+        picks = wanted[2 * place[1 : 1 + CHIPS] + place[0]].reshape(-1)
+        inside = (picks >= 0) & (picks < vocab_here)
+        found = enc_embed[jnp.clip(picks, 0, vocab_here - 1)]
+        found = jnp.where(inside[:, None], found, jnp.zeros((), bf16))
+        return found.reshape(CHIPS, NB_LEN, ENC_D)
+
+    other = rows(places_both[1], wanted)
+    *got, other, wanted = together(*first_round(local), other, wanted)
+    near = [jnp.stack(pair) for pair in zip(local, got)]
+    own = rows(places_both[0], wanted)
+    *got, own = together(*[neighbour(value, part, 1) for part, value in enumerate(near)], own)
+    near = [jnp.concatenate(pair) for pair in zip(near, got)]
+    far = [neighbour(value, part, 2) for part, value in enumerate(near)]
+    swaps = [core_swap(value) for value in near]
+    *far, embedded = together(*far, looked_up(own, other))
+    far_swaps = [core_swap(value) for value in far]
+    feed, mix = [
+        [near[part], far[part], swaps[part], far_swaps[part]] for part in range(2)
     ]
-    for head in range(ENC_HEADS // 2):
-        cols = slice(head * ENC_HEAD, (head + 1) * ENC_HEAD)
-        scores = lax.dot_general(
-            triple[0][:, cols],
-            triple[1][:, cols],
-            (((1,), (1,)), ((), ())),
-            preferred_element_type=f32,
-        )
-        weights = jnp.exp(scores * ENC_HEAD ** (-0.5))
-        denom = jnp.sum(weights, axis=1, keepdims=True)
-        numer = jnp.dot(weights.astype(bf16), triple[2][:, cols], preferred_element_type=f32)
-        mix_ref[:, cols] = (numer / denom).astype(bf16)
-    mixed = mix_ref[...]
-    width = ENC_D // 2
-    rows = pl.ds(pl.multiple_of(section_ref[0] * width, width), width)
-    for at, ref in enumerate((o0_ref, o1_ref)):
-        part = jnp.dot(mixed, ref[0, rows, :], preferred_element_type=f32)
-        out_ref[:, at * width : (at + 1) * width] = part.astype(bf16)
-
-
-def enc_feed_kernel(x_ref, gain_ref, w_ref, out_ref):
-    scaled, root = scaled_rows(x_ref[...], gain_ref[...])
-    width = ENC_D // 2
-    hidden = [
-        jax.nn.gelu(
-            jnp.dot(scaled, w_ref[piece], preferred_element_type=f32) / root, approximate=True
-        ).astype(bf16)
-        for piece in range(4)
-    ]
-    for at in range(2):
-        part = jnp.zeros((NB_LEN, width), f32)
-        for piece in range(4):
-            rows = slice((piece % 2) * width, (piece % 2 + 1) * width)
-            down = w_ref[4 + 2 * (piece // 2) + at, rows, :]
-            part += jnp.dot(hidden[piece], down, preferred_element_type=f32)
-        out_ref[:, at * width : (at + 1) * width] = part.astype(bf16)
-
-
-def encode_mix(embedded, enc_norms, pieces, section):
-    out = jax.ShapeDtypeStruct((NB_LEN, ENC_D), bf16)
-    width = ENC_D // 2
-    full = whole((NB_LEN, ENC_D))
-
-    def piece(at):
-        return pl.BlockSpec((1, ENC_D, width), lambda s: (at, 0, 0))
-
-    mixed = pl.pallas_call(
-        enc_mix_kernel,
-        grid=(1,),
-        in_specs=[SCALAR, full, whole((1, ENC_D))] + [piece(8 + at) for at in range(5)],
-        out_specs=full,
-        out_shape=out,
-        scratch_shapes=[pltpu.VMEM((NB_LEN, width), bf16)],
-        compiler_params=params(),
-    )(section, embedded, enc_norms[:1], *([pieces] * 5))
-    return embedded, mixed, section_swap(mixed)
-
-
-def encode_feed(embedded, mixed, far, enc_norms, pieces):
-    width = ENC_D // 2
-    full = whole((NB_LEN, ENC_D))
-    inner = (embedded.astype(f32) + (mixed.astype(f32) + far.astype(f32))).astype(bf16)
-    fed = pl.pallas_call(
-        enc_feed_kernel,
-        grid=(1,),
-        in_specs=[full, whole((1, ENC_D)), pl.BlockSpec((8, ENC_D, width), lambda s: (0, 0, 0))],
-        out_specs=full,
-        out_shape=jax.ShapeDtypeStruct((NB_LEN, ENC_D), bf16),
-        compiler_params=params(28),
-    )(inner, enc_norms[1:], pieces)
-    return inner, fed, section_swap(fed)
-
-
-def encode_end(inner, fed, far):
-    return (inner.astype(f32) + (fed.astype(f32) + far.astype(f32))).astype(bf16)
+    return encode(places_both, embedded, enc_norms, feed, mix)
 
 
 def pairs_kernel(place_ref, *refs):
@@ -535,26 +547,7 @@
     return lax.all_to_all(causal(triple), "seq", 0, 0, tiled=True)
 
 
-def first_layer(places_both, states, weights, found, local, join, encoder):
-    norms, triple_w, out_w, query_w, back_w = weights
-    same, local = together(chips_to_chips(spread(states)), local)
-    pieces = lax.all_gather(local, MP, axis=1, tiled=True)
-    same, found = together(same, found)
-    half = jnp.sum(chips_to_chips(found).astype(f32), axis=0).astype(bf16)
-    triple = project(places_both, [same], [core_swap(same)], norms[0], triple_w, True)
-    triple, half = together(triple, half)
-    mixed = attention(triple)
-    middle, embedded = add_product(places_both, states, mixed, out_w, join(half))
-    rows, embedded = together(spread(middle), embedded)
-    same = chips_to_chips(rows)
-    encoded = encoder(embedded, pieces)
-    parts = [encoded[start : start + count] for start, count in zip(ENC_STARTS, ENC_PARTS)]
-    *got, same = together(*first_round(parts), same)
-    asked = project(places_both, [same], [core_swap(same)], norms[1], query_w[None], False)
-    return middle, asked, later_rounds(parts, got)
-
-
-def second_layer(places_both, states, weights):
+def to_queries(places_both, states, weights):
     norms, triple_w, out_w, query_w, back_w = weights
     triple = project(places_both, *gather_chips(states), norms[0], triple_w, True)
     middle, _ = add_product(places_both, states, attention(triple), out_w)
@@ -588,18 +581,8 @@
     core_at = lax.axis_index("core").astype(jnp.int32)
     chip = lax.axis_index(("z", "y")).astype(jnp.int32)
     places_both = [places(chip, core_at), places(chip, 1 - core_at)]
-    local = weight_parts(section, enc_qkv, enc_out, enc_up, enc_down)
     slot_ids = neighbour_ids[neighbour_table.reshape(-1)]
-    found = look_up(slot_ids, enc_embed, core_at, section)
     pair_w = cross_pair[0].reshape(ENC_D, 2 * WIDTH)
-
-    def join(half):
-        return join_halves(half, section)
-
-    def encoder(embedded, pieces):
-        mix = encode_mix(embedded, enc_norms, pieces, jnp.reshape(section, (1,)))
-        return encode_end(*encode_feed(*mix, enc_norms, pieces))
-
     weights = (
         dec_norms[0],
         jnp.transpose(dec_qkv[0], (1, 0, 2)),
@@ -609,14 +592,27 @@
     )
 
     states = hidden_states.reshape(BATCH * ROWS, WIDTH)
-    middle, asked, encoded = first_layer(
-        places_both, by_parts(states), weights, found, local, join, encoder
+
+    def decode():
+        middle, asked = to_queries(places_both, by_parts(states), weights)
+        return jnp.concatenate(middle), asked, jnp.zeros((NB_LEN, ENC_D), bf16)
+
+    def encode_all():
+        local = weight_parts(enc_qkv, enc_out, enc_up, enc_down)
+        blank = jnp.zeros(states.shape, bf16)
+        return blank, blank, encode_neighbour(places_both, slot_ids, enc_embed, enc_norms, local)
+
+    middle, asked, encoded = lax.cond(section == 0, decode, encode_all)
+    middle = by_parts(middle)
+    encoded = jnp.where(section == 0, section_swap(encoded), encoded)
+    encoded = gather_chips(
+        [encoded[start : start + count] for start, count in zip(ENC_STARTS, ENC_PARTS)]
     )
     made = [make_pairs(place, rows, pair_w) for place, rows in zip(places_both, encoded)]
     prevs, pairs = [prev for prev, _ in made], [rows for _, rows in made]
     first = cross_layer(places_both, middle, asked, prevs, pairs, weights)
     handed = section_swap(jnp.concatenate(first))
-    middle, asked = second_layer(places_both, by_parts(handed), weights)
+    middle, asked = to_queries(places_both, by_parts(handed), weights)
     second = jnp.concatenate(cross_layer(places_both, middle, asked, prevs, pairs, weights))
     second = second.reshape(BATCH, ROWS, WIDTH)
     return jnp.where(section == 0, section_swap(second[0]), second[1])[None]

time: 491 us -> 457 us (0.931)
  local copies, waits for them, and re-layouts: 42.8 us -> 3.74 us
  starting transfers between devices: 99.9 us -> 134 us
  waiting for transfers between devices: 204 us -> 188 us
  between operations: 15.2 us -> 1.04 us
  loops' own time: 0 us -> 9.33 us
  other arithmetic: 13.9 us -> 5.65 us
    ppermute x42 -> x54, waiting for transfers between devices: 124 us -> 163 us  [neighbour(): return lax.ppermute(value, MP, route)]
    all_to_all x3 -> x0, waiting for transfers between devices: 34.5 us -> none  [chips_to_chips(): return lax.all_to_all(value, ('z', 'y'), 0, 0, tiled=True)]
    ppermute x5 -> x3, starting transfers between devices: 11.4 us -> 45.8 us  [section_swap(): return lax.ppermute(value, 'section', [(0, 1), (1, 0)])]
    ppermute x5 -> x3, waiting for transfers between devices: 38.2 us -> 14.2 us  [section_swap(): return lax.ppermute(value, 'section', [(0, 1), (1, 0)])]
    all_to_all x3 -> x0, starting transfers between devices: 16.8 us -> none  [chips_to_chips(): return lax.all_to_all(value, ('z', 'y'), 0, 0, tiled=True)]
    gather x3 -> x0, local copies, waits for them, and re-layouts: 16.5 us -> none  [the longest x2 16 us: rows(): found = enc_embed[jnp.clip(picks, 0, vocab_here - 1)]]
    ppermute x42 -> x54, starting transfers between devices: 60.5 us -> 73.8 us  [neighbour(): return lax.ppermute(value, MP, route)]
    unnamed x46 -> x16, local copies, waits for them, and re-layouts: 14.2 us -> 1.05 us
  transfers between devices with their start and end apart: 84 -> 95, of which waited for: 41 -> 52; matrix products, arithmetic and copies ran while one was open for 8% -> 1% of each run, Pallas kernels for 8% -> 7%
where the time goes in v8:
time: 457 us; the launch traced here: 448 us
  waiting for transfers between devices  188 us (41%)
  starting transfers between devices  134 us (29%)
  Pallas kernels  53.4 us (12%)
  blocking collectives  52.5 us (11%)
  loops' own time  9.33 us (2%)
  other arithmetic  5.65 us (1%)
    ppermute x54, waiting for transfers between devices, neighbour(): return lax.ppermute(value, MP, route)  163 us
    ppermute x54, starting transfers between devices, neighbour(): return lax.ppermute(value, MP, route)  73.8 us
    ppermute x3, starting transfers between devices, section_swap(): return lax.ppermute(value, 'section', [(0, 1), (1, 0)])  45.8 us
    all_to_all x2, blocking collectives, attention(): triple = lax.all_to_all(triple, 'seq', 0, 0, tiled=True)  34.4 us
    pallas_call x8, Pallas kernels, project_half(): pl.pallas_call(functools.partial(project_kernel, last, units), grid_spec=...  25.3 us
    all_to_all x2, blocking collectives, attention(): return lax.all_to_all(causal(triple), 'seq', 0, 0, tiled=True)  18.1 us
    pallas_call x16, Pallas kernels, terms(): pl.pallas_call(terms_kernel, grid_spec=pltpu.PrefetchScalarGridSpec(num_s...  16.1 us
    ppermute x3, waiting for transfers between devices, section_swap(): return lax.ppermute(value, 'section', [(0, 1), (1, 0)])  14.2 us
  transfers between devices with their start and end apart: 95, of which 52 were waited for; matrix products, arithmetic and copies ran while one was open for 1% of the time, Pallas kernels for 7%

profile of v8, /device:TPU:0, one launch (start us, length us, event | category | flops | bytes accessed | tf_op | source)
XLA Modules:
  0.0 448.1 jit_solution(5489292217809082825)
XLA Ops:
  1.8 142.4 %conditional.1 = (bf16[512,256]{1,0:T(8,128)(2,1)S(1)}, bf16[512,256]{1,0:T(8,128)(2,1)S(1)}, bf16[128,1024]{1,0:T(8,128)(2,1)S(1)}) conditional(s32[]{:T(128)} %convert_element_type.283, (bf16[64,4096]{1,0:T(8,128)(2,1)}, bf16[256,1024]{1,0:T(8,128)(2,1)}, bf16[64,3,1024]{2,0,1:T(8,128)(2,1)}, bf16[64,1024]{1,0:T(8,128)(2,1)}, s32[64,128]{1,0:T(8,128)}, ...), branch_computations={%region_0.1_spmd, %region_1.2_spmd} | conditional | flops 5377753088 | bytes 199018080 | solution.py:605
  14.5 3.1 collective-permute-start.1
  21.4 5.7 %collective-permute-done.3 = bf16[2,160,256]{2,1,0:T(8,128)(2,1)S(1)} collective-permute-done((bf16[2,160,256]{2,1,0:T(8,128)(2,1)S(1)}, bf16[2,160,256]{2,1,0:T(8,128)(2,1)S(1)}, u32[]{:S(2)}, u32[]{:S(2)}) %collective-permute-start.3) | collective-permute-done | bytes 163872 | tf_op jit(solution)/shard_map/cond/branch_1_fun/ppermute | solution.py:80
  27.9 3.1 collective-permute-start.6
  31.7 6.7 %collective-permute-done.7.refs_3_ = bf16[4,160,256]{2,1,0:T(8,128)(2,1)S(1)} collective-permute-done((bf16[4,160,256]{2,1,0:T(8,128)(2,1)S(1)}, bf16[4,160,256]{2,1,0:T(8,128)(2,1)S(1)}, u32[]{:S(2)}, u32[]{:S(2)}) %collective-permute-start.7) | collective-permute-done | bytes 327712 | tf_op jit(solution)/shard_map/cond/branch_1_fun/ppermute | solution.py:80
  41.0 5.3 %branch_1_fun.9 = (f32[3,512,256]{2,1,0:T(8,128)S(1)}, f32[512,128]{1,0:T(8,128)S(1)}) custom-call(s32[17]{0:T(128)S(1)} %get-tuple-element.71.place_ref, bf16[4,352,256]{2,1,0:T(8,128)(2,1)S(1)} %pad_maximum_fusion.refs_0_, bf16[4,160,256]{2,1,0:T(8,128)(2,1)S(1)} %pad_maximum_fusion.4.refs_1_, bf16[4,352,256]{2,1,0:T(8,128)(2,1)S(1)} %collective-permute-done.6.refs_2_, ...), custom_call_target="tpu_custom_call" | custom-call | flops 1610612736 | bytes 6815744 | tf_op jit(solution)/shard_map/cond/branch_1_fun/pallas_call | solution.py:211
  46.3 3.8 branch_1_fun.10
  50.1 16.7 %all_to_all.18.triple_ref = bf16[4,3,256,128]{3,2,1,0:T(8,128)(2,1)S(1)} all-to-all(bf16[4,3,256,128]{3,2,1,0:T(8,128)(2,1)S(1)} %branch_1_fun.10), channel_id=1, replica_groups=mesh['section'=2,'seq'=4,'z'=2,'y'=4,'core'=2] {'seq'}, dimensions={0} | all-to-all | bytes 1572864 | tf_op jit(solution)/shard_map/cond/branch_1_fun/all_to_all | solution.py:546
  68.2 9.1 %all_to_all.19.mixed_ref = bf16[4,256,128]{2,1,0:T(8,128)(2,1)S(1)} all-to-all(bf16[4,256,128]{2,1,0:T(8,128)(2,1)S(1)} %branch_1_fun.11), channel_id=1, replica_groups=mesh['section'=2,'seq'=4,'z'=2,'y'=4,'core'=2] {'seq'}, dimensions={0} | all-to-all | bytes 524288 | tf_op jit(solution)/shard_map/cond/branch_1_fun/all_to_all | solution.py:547
  86.0 8.7 %collective-permute-done.13 = bf16[4,160,256]{2,1,0:T(8,128)(2,1)S(1)} collective-permute-done((bf16[4,160,256]{2,1,0:T(8,128)(2,1)S(1)}, bf16[4,160,256]{2,1,0:T(8,128)(2,1)S(1)}, u32[]{:S(2)}, u32[]{:S(2)}) %collective-permute-start.13) | collective-permute-done | bytes 327712 | tf_op jit(solution)/shard_map/cond/branch_1_fun/ppermute | solution.py:80
  95.9 5.9 %collective-permute-done.17 = bf16[2,160,256]{2,1,0:T(8,128)(2,1)S(1)} collective-permute-done((bf16[2,160,256]{2,1,0:T(8,128)(2,1)S(1)}, bf16[2,160,256]{2,1,0:T(8,128)(2,1)S(1)}, u32[]{:S(2)}, u32[]{:S(2)}) %collective-permute-start.17) | collective-permute-done | bytes 163872 | tf_op jit(solution)/shard_map/cond/branch_1_fun/ppermute | solution.py:80
  105.2 3.4 collective-permute-done.19
  113.0 3.4 collective-permute-done.21
  116.9 5.0 %collective-permute-done.23 = bf16[2,160,256]{2,1,0:T(8,128)(2,1)S(1)} collective-permute-done((bf16[2,160,256]{2,1,0:T(8,128)(2,1)S(1)}, bf16[2,160,256]{2,1,0:T(8,128)(2,1)S(1)}, u32[]{:S(2)}, u32[]{:S(2)}) %collective-permute-start.23) | collective-permute-done | bytes 163872 | tf_op jit(solution)/shard_map/cond/branch_1_fun/ppermute | solution.py:80
  124.2 3.5 collective-permute-start.26
  127.9 7.0 %collective-permute-done.27.refs_3_ = bf16[4,160,256]{2,1,0:T(8,128)(2,1)S(1)} collective-permute-done((bf16[4,160,256]{2,1,0:T(8,128)(2,1)S(1)}, bf16[4,160,256]{2,1,0:T(8,128)(2,1)S(1)}, u32[]{:S(2)}, u32[]{:S(2)}) %collective-permute-start.27) | collective-permute-done | bytes 327712 | tf_op jit(solution)/shard_map/cond/branch_1_fun/ppermute | solution.py:80
  144.2 37.7 %collective-permute-start.44 = (bf16[128,1024]{1,0:T(8,128)(2,1)S(1)}, bf16[128,1024]{1,0:T(8,128)(2,1)S(1)}, u32[]{:S(2)}, u32[]{:S(2)}) collective-permute-start(bf16[128,1024]{1,0:T(8,128)(2,1)S(1)} %get-tuple-element.202), channel_id=1, source_target_pairs={{0,64},{64,0},{1,65},{65,1},{2,66},{66,2},{3,67},{67,3},{4,68},{68... | collective-permute-start | bytes 786440 | tf_op jit(solution)/shard_map/ppermute | solution.py:67
  181.9 6.6 %collective-permute-done.44 = bf16[128,1024]{1,0:T(8,128)(2,1)S(1)} collective-permute-done((bf16[128,1024]{1,0:T(8,128)(2,1)S(1)}, bf16[128,1024]{1,0:T(8,128)(2,1)S(1)}, u32[]{:S(2)}, u32[]{:S(2)}) %collective-permute-start.44) | collective-permute-done | bytes 262176 | tf_op jit(solution)/shard_map/ppermute | solution.py:67
  190.7 3.9 collective-permute-done.46
  196.9 4.9 %collective-permute-done.48 = bf16[2,48,1024]{2,1,0:T(8,128)(2,1)S(1)} collective-permute-done((bf16[2,48,1024]{2,1,0:T(8,128)(2,1)S(1)}, bf16[2,48,1024]{2,1,0:T(8,128)(2,1)S(1)}, u32[]{:S(2)}, u32[]{:S(2)}) %collective-permute-start.48) | collective-permute-done | bytes 196640 | tf_op jit(solution)/shard_map/ppermute | solution.py:80
  205.1 7.3 %collective-permute-done.50.refs_3_ = bf16[4,48,1024]{2,1,0:T(8,128)(2,1)S(1)} collective-permute-done((bf16[4,48,1024]{2,1,0:T(8,128)(2,1)S(1)}, bf16[4,48,1024]{2,1,0:T(8,128)(2,1)S(1)}, u32[]{:S(2)}, u32[]{:S(2)}) %collective-permute-start.50) | collective-permute-done | bytes 393248 | tf_op jit(solution)/shard_map/ppermute | solution.py:80
  216.5 3.4 collective-permute-start.51
  221.9 3.5 collective-permute-start.56
  225.9 5.3 %collective-permute-done.56.refs_1_ = bf16[2,128,512]{2,1,0:T(8,128)(2,1)S(1)} collective-permute-done((bf16[2,128,512]{2,1,0:T(8,128)(2,1)S(1)}, bf16[2,128,512]{2,1,0:T(8,128)(2,1)S(1)}, u32[]{:S(2)}, u32[]{:S(2)}) %collective-permute-start.56) | collective-permute-done | bytes 262176 | tf_op jit(solution)/shard_map/ppermute | solution.py:541
  241.8 8.4 %collective-permute-done.60 = bf16[4,160,256]{2,1,0:T(8,128)(2,1)S(1)} collective-permute-done((bf16[4,160,256]{2,1,0:T(8,128)(2,1)S(1)}, bf16[4,160,256]{2,1,0:T(8,128)(2,1)S(1)}, u32[]{:S(2)}, u32[]{:S(2)}) %collective-permute-start.60) | collective-permute-done | bytes 327712 | tf_op jit(solution)/shard_map/ppermute | solution.py:80
  253.2 4.8 %collective-permute-done.64 = bf16[2,160,256]{2,1,0:T(8,128)(2,1)S(1)} collective-permute-done((bf16[2,160,256]{2,1,0:T(8,128)(2,1)S(1)}, bf16[2,160,256]{2,1,0:T(8,128)(2,1)S(1)}, u32[]{:S(2)}, u32[]{:S(2)}) %collective-permute-start.64) | collective-permute-done | bytes 163872 | tf_op jit(solution)/shard_map/ppermute | solution.py:80
  263.0 3.8 collective-permute-done.66
  266.9 3.3 collective-permute-start.67
  270.2 4.6 %collective-permute-done.67 = bf16[512,256]{1,0:T(8,128)(2,1)S(1)} collective-permute-done((bf16[512,256]{1,0:T(8,128)(2,1)S(1)}, bf16[512,256]{1,0:T(8,128)(2,1)S(1)}, u32[]{:S(2)}, u32[]{:S(2)}) %collective-permute-start.67) | collective-permute-done | bytes 262176 | tf_op jit(solution)/shard_map/ppermute | solution.py:67
  277.0 4.4 collective-permute-done.69
  283.0 4.8 %collective-permute-done.71 = bf16[2,160,256]{2,1,0:T(8,128)(2,1)S(1)} collective-permute-done((bf16[2,160,256]{2,1,0:T(8,128)(2,1)S(1)}, bf16[2,160,256]{2,1,0:T(8,128)(2,1)S(1)}, u32[]{:S(2)}, u32[]{:S(2)}) %collective-permute-start.71) | collective-permute-done | bytes 163872 | tf_op jit(solution)/shard_map/ppermute | solution.py:80
  293.0 5.4 %collective-permute-done.75.refs_3_ = bf16[4,160,256]{2,1,0:T(8,128)(2,1)S(1)} collective-permute-done((bf16[4,160,256]{2,1,0:T(8,128)(2,1)S(1)}, bf16[4,160,256]{2,1,0:T(8,128)(2,1)S(1)}, u32[]{:S(2)}, u32[]{:S(2)}) %collective-permute-start.75) | collective-permute-done | bytes 327712 | tf_op jit(solution)/shard_map/ppermute | solution.py:80
  298.4 3.2 collective-permute-done.74.refs_2_
  302.2 3.7 shard_map.169
  305.9 3.8 shard_map.170
  309.8 17.7 %all_to_all.20.triple_ref = bf16[4,3,256,128]{3,2,1,0:T(8,128)(2,1)S(1)} all-to-all(bf16[4,3,256,128]{3,2,1,0:T(8,128)(2,1)S(1)} %shard_map.170), channel_id=1, replica_groups=mesh['section'=2,'seq'=4,'z'=2,'y'=4,'core'=2] {'seq'}, dimensions={0} | all-to-all | bytes 1572864 | tf_op jit(solution)/shard_map/all_to_all | solution.py:546
  328.9 9.1 %all_to_all.21.mixed_ref = bf16[4,256,128]{2,1,0:T(8,128)(2,1)S(1)} all-to-all(bf16[4,256,128]{2,1,0:T(8,128)(2,1)S(1)} %shard_map.171), channel_id=1, replica_groups=mesh['section'=2,'seq'=4,'z'=2,'y'=4,'core'=2] {'seq'}, dimensions={0} | all-to-all | bytes 524288 | tf_op jit(solution)/shard_map/all_to_all | solution.py:547
  345.7 8.8 %collective-permute-done.81 = bf16[4,160,256]{2,1,0:T(8,128)(2,1)S(1)} collective-permute-done((bf16[4,160,256]{2,1,0:T(8,128)(2,1)S(1)}, bf16[4,160,256]{2,1,0:T(8,128)(2,1)S(1)}, u32[]{:S(2)}, u32[]{:S(2)}) %collective-permute-start.81) | collective-permute-done | bytes 327712 | tf_op jit(solution)/shard_map/ppermute | solution.py:80
  357.4 4.3 collective-permute-done.85
  366.6 3.6 collective-permute-done.87
  372.7 3.7 collective-permute-done.89
  378.5 3.5 collective-permute-done.91
  387.5 5.9 %collective-permute-done.95.refs_3_ = bf16[4,160,256]{2,1,0:T(8,128)(2,1)S(1)} collective-permute-done((bf16[4,160,256]{2,1,0:T(8,128)(2,1)S(1)}, bf16[4,160,256]{2,1,0:T(8,128)(2,1)S(1)}, u32[]{:S(2)}, u32[]{:S(2)}) %collective-permute-start.95) | collective-permute-done | bytes 327712 | tf_op jit(solution)/shard_map/ppermute | solution.py:80
  393.4 3.2 collective-permute-done.94.refs_2_
  414.5 8.7 %collective-permute-done.101 = bf16[4,160,256]{2,1,0:T(8,128)(2,1)S(1)} collective-permute-done((bf16[4,160,256]{2,1,0:T(8,128)(2,1)S(1)}, bf16[4,160,256]{2,1,0:T(8,128)(2,1)S(1)}, u32[]{:S(2)}, u32[]{:S(2)}) %collective-permute-start.101) | collective-permute-done | bytes 327712 | tf_op jit(solution)/shard_map/ppermute | solution.py:80
  426.4 4.3 collective-permute-done.105
  435.9 3.5 collective-permute-done.107
  439.4 4.8 %collective-permute-start.108 = (bf16[256,256]{1,0:T(8,128)(2,1)S(1)}, bf16[256,256]{1,0:T(8,128)(2,1)S(1)}, u32[]{:S(2)}, u32[]{:S(2)}) collective-permute-start(bf16[256,256]{1,0:T(8,128)(2,1)S(1)} %slice.288), channel_id=1, source_target_pairs={{0,64},{64,0},{1,65},{65,1},{2,66},{66,2},{3,67},{67,3},{4,68},{68... | collective-permute-start | bytes 393224 | tf_op jit(solution)/shard_map/ppermute | solution.py:67
  (296 shorter events, 143.3 us)
Async XLA Ops:
  11.5 8.7 %collective-permute-start = (bf16[352,256]{1,0:T(8,128)(2,1)S(1)}, bf16[352,256]{1,0:T(8,128)(2,1)S(1)}, u32[]{:S(2)}, u32[]{:S(2)}) collective-permute-start(bf16[352,256]{1,0:T(8,128)(2,1)S(1)} %get-tuple-element.333), channel_id=1, source_target_pairs={{0,8},{1,3},{2,10},{3,1},{4,12},{5,7},{6,14},{7,5},{8,0},{9,11},{1... | collective-permute-start | bytes 540680 | tf_op jit(solution)/shard_map/cond/branch_1_fun/ppermute | solution.py:80
  20.3 7.5 %collective-permute-start.2 = (bf16[2,352,256]{2,1,0:T(8,128)(2,1)S(1)}, bf16[2,352,256]{2,1,0:T(8,128)(2,1)S(1)}, u32[]{:S(2)}, u32[]{:S(2)}) collective-permute-start(bf16[2,352,256]{2,1,0:T(8,128)(2,1)S(1)} %pad_maximum_fusion.2), channel_id=1, source_target_pairs={{0,2},{1,7},{2,0},{3,5},{4,6},{5,3},{6,4},{7,1},{8,10},{9,15},{10,... | collective-permute-start | bytes 1081352 | tf_op jit(solution)/shard_map/cond/branch_1_fun/ppermute | solution.py:80
  27.9 12.6 %collective-permute-start.6 = (bf16[4,352,256]{2,1,0:T(8,128)(2,1)S(1)}, bf16[4,352,256]{2,1,0:T(8,128)(2,1)S(1)}, u32[]{:S(2)}, u32[]{:S(2)}) collective-permute-start(bf16[4,352,256]{2,1,0:T(8,128)(2,1)S(1)} %pad_maximum_fusion.refs_0_), channel_id=1, source_target_pairs={{0,6},{1,9},{2,4},{3,11},{4,2},{5,13},{6,0},{7,15},{8,14},{9,1},{1... | collective-permute-start | bytes 2162696 | tf_op jit(solution)/shard_map/cond/branch_1_fun/ppermute | solution.py:80
  31.0 7.3 %collective-permute-start.7 = (bf16[4,160,256]{2,1,0:T(8,128)(2,1)S(1)}, bf16[4,160,256]{2,1,0:T(8,128)(2,1)S(1)}, u32[]{:S(2)}, u32[]{:S(2)}) collective-permute-start(bf16[4,160,256]{2,1,0:T(8,128)(2,1)S(1)} %pad_maximum_fusion.4.refs_1_), channel_id=1, source_target_pairs={{0,2},{1,3},{2,0},{3,1},{4,6},{5,7},{6,4},{7,5},{8,10},{9,11},{10,... | collective-permute-start | bytes 983048 | tf_op jit(solution)/shard_map/cond/branch_1_fun/ppermute | solution.py:80
  31.1 9.9 %collective-permute-start.5 = (bf16[4,160,256]{2,1,0:T(8,128)(2,1)S(1)}, bf16[4,160,256]{2,1,0:T(8,128)(2,1)S(1)}, u32[]{:S(2)}, u32[]{:S(2)}) collective-permute-start(bf16[4,160,256]{2,1,0:T(8,128)(2,1)S(1)} %pad_maximum_fusion.4.refs_1_), channel_id=1, source_target_pairs={{0,1},{1,0},{2,3},{3,2},{4,5},{5,4},{6,7},{7,6},{8,9},{9,8},{10,11... | collective-permute-start | bytes 983048 | tf_op jit(solution)/shard_map/cond/branch_1_fun/ppermute | solution.py:63
  31.2 9.8 %collective-permute-start.4 = (bf16[4,352,256]{2,1,0:T(8,128)(2,1)S(1)}, bf16[4,352,256]{2,1,0:T(8,128)(2,1)S(1)}, u32[]{:S(2)}, u32[]{:S(2)}) collective-permute-start(bf16[4,352,256]{2,1,0:T(8,128)(2,1)S(1)} %pad_maximum_fusion.refs_0_), channel_id=1, source_target_pairs={{0,1},{1,0},{2,3},{3,2},{4,5},{5,4},{6,7},{7,6},{8,9},{9,8},{10,11... | collective-permute-start | bytes 2162696 | tf_op jit(solution)/shard_map/cond/branch_1_fun/ppermute | solution.py:63
  81.3 13.4 %collective-permute-start.12 = (bf16[4,352,256]{2,1,0:T(8,128)(2,1)S(1)}, bf16[4,352,256]{2,1,0:T(8,128)(2,1)S(1)}, u32[]{:S(2)}, u32[]{:S(2)}) collective-permute-start(bf16[4,352,256]{2,1,0:T(8,128)(2,1)S(1)} %add_convert_fusion), channel_id=1, source_target_pairs={{0,6},{1,9},{2,4},{3,11},{4,2},{5,13},{6,0},{7,15},{8,14},{9,1},{1... | collective-permute-start | bytes 2162696 | tf_op jit(solution)/shard_map/cond/branch_1_fun/ppermute | solution.py:80
  84.5 10.2 %collective-permute-start.13 = (bf16[4,160,256]{2,1,0:T(8,128)(2,1)S(1)}, bf16[4,160,256]{2,1,0:T(8,128)(2,1)S(1)}, u32[]{:S(2)}, u32[]{:S(2)}) collective-permute-start(bf16[4,160,256]{2,1,0:T(8,128)(2,1)S(1)} %add_convert_fusion.1), channel_id=1, source_target_pairs={{0,2},{1,3},{2,0},{3,1},{4,6},{5,7},{6,4},{7,5},{8,10},{9,11},{10,... | collective-permute-start | bytes 983048 | tf_op jit(solution)/shard_map/cond/branch_1_fun/ppermute | solution.py:80
  95.0 7.5 %collective-permute-start.16 = (bf16[2,352,256]{2,1,0:T(8,128)(2,1)S(1)}, bf16[2,352,256]{2,1,0:T(8,128)(2,1)S(1)}, u32[]{:S(2)}, u32[]{:S(2)}) collective-permute-start(bf16[2,352,256]{2,1,0:T(8,128)(2,1)S(1)} %slice.408), channel_id=1, source_target_pairs={{0,2},{1,7},{2,0},{3,5},{4,6},{5,3},{6,4},{7,1},{8,10},{9,15},{10,... | collective-permute-start | bytes 1081352 | tf_op jit(solution)/shard_map/cond/branch_1_fun/ppermute | solution.py:80
  108.7 7.7 %collective-permute-start.20 = (bf16[352,256]{1,0:T(8,128)(2,1)S(1)}, bf16[352,256]{1,0:T(8,128)(2,1)S(1)}, u32[]{:S(2)}, u32[]{:S(2)}) collective-permute-start(bf16[352,256]{1,0:T(8,128)(2,1)S(1)} %fusion.2), channel_id=1, source_target_pairs={{0,8},{1,3},{2,10},{3,1},{4,12},{5,7},{6,14},{7,5},{8,0},{9,11},{1... | collective-permute-start | bytes 540680 | tf_op jit(solution)/shard_map/cond/branch_1_fun/ppermute | solution.py:80
  116.4 7.7 %collective-permute-start.22 = (bf16[2,352,256]{2,1,0:T(8,128)(2,1)S(1)}, bf16[2,352,256]{2,1,0:T(8,128)(2,1)S(1)}, u32[]{:S(2)}, u32[]{:S(2)}) collective-permute-start(bf16[2,352,256]{2,1,0:T(8,128)(2,1)S(1)} %pad_maximum_fusion.3), channel_id=1, source_target_pairs={{0,2},{1,7},{2,0},{3,5},{4,6},{5,3},{6,4},{7,1},{8,10},{9,15},{10,... | collective-permute-start | bytes 1081352 | tf_op jit(solution)/shard_map/cond/branch_1_fun/ppermute | solution.py:80
  124.2 12.8 %collective-permute-start.26 = (bf16[4,352,256]{2,1,0:T(8,128)(2,1)S(1)}, bf16[4,352,256]{2,1,0:T(8,128)(2,1)S(1)}, u32[]{:S(2)}, u32[]{:S(2)}) collective-permute-start(bf16[4,352,256]{2,1,0:T(8,128)(2,1)S(1)} %pad_maximum_fusion.1.refs_0_), channel_id=1, source_target_pairs={{0,6},{1,9},{2,4},{3,11},{4,2},{5,13},{6,0},{7,15},{8,14},{9,1},{1... | collective-permute-start | bytes 2162696 | tf_op jit(solution)/shard_map/cond/branch_1_fun/ppermute | solution.py:80
  127.7 7.2 %collective-permute-start.27 = (bf16[4,160,256]{2,1,0:T(8,128)(2,1)S(1)}, bf16[4,160,256]{2,1,0:T(8,128)(2,1)S(1)}, u32[]{:S(2)}, u32[]{:S(2)}) collective-permute-start(bf16[4,160,256]{2,1,0:T(8,128)(2,1)S(1)} %pad_maximum_fusion.5.refs_1_), channel_id=1, source_target_pairs={{0,2},{1,3},{2,0},{3,1},{4,6},{5,7},{6,4},{7,5},{8,10},{9,11},{10,... | collective-permute-start | bytes 983048 | tf_op jit(solution)/shard_map/cond/branch_1_fun/ppermute | solution.py:80
  127.8 11.8 %collective-permute-start.24 = (bf16[4,352,256]{2,1,0:T(8,128)(2,1)S(1)}, bf16[4,352,256]{2,1,0:T(8,128)(2,1)S(1)}, u32[]{:S(2)}, u32[]{:S(2)}) collective-permute-start(bf16[4,352,256]{2,1,0:T(8,128)(2,1)S(1)} %pad_maximum_fusion.1.refs_0_), channel_id=1, source_target_pairs={{0,1},{1,0},{2,3},{3,2},{4,5},{5,4},{6,7},{7,6},{8,9},{9,8},{10,11... | collective-permute-start | bytes 2162696 | tf_op jit(solution)/shard_map/cond/branch_1_fun/ppermute | solution.py:63
  144.2 44.3 %collective-permute-start.44 = (bf16[128,1024]{1,0:T(8,128)(2,1)S(1)}, bf16[128,1024]{1,0:T(8,128)(2,1)S(1)}, u32[]{:S(2)}, u32[]{:S(2)}) collective-permute-start(bf16[128,1024]{1,0:T(8,128)(2,1)S(1)} %get-tuple-element.202), channel_id=1, source_target_pairs={{0,64},{64,0},{1,65},{65,1},{2,66},{66,2},{3,67},{67,3},{4,68},{68... | collective-permute-start | bytes 786440 | tf_op jit(solution)/shard_map/ppermute | solution.py:67
  194.7 7.2 %collective-permute-start.47 = (bf16[2,80,1024]{2,1,0:T(8,128)(2,1)S(1)}, bf16[2,80,1024]{2,1,0:T(8,128)(2,1)S(1)}, u32[]{:S(2)}, u32[]{:S(2)}) collective-permute-start(bf16[2,80,1024]{2,1,0:T(8,128)(2,1)S(1)} %pad_maximum_fusion.21), channel_id=1, source_target_pairs={{0,2},{1,7},{2,0},{3,5},{4,6},{5,3},{6,4},{7,1},{8,10},{9,15},{10,... | collective-permute-start | bytes 983048 | tf_op jit(solution)/shard_map/ppermute | solution.py:80
  194.8 7.0 %collective-permute-start.48 = (bf16[2,48,1024]{2,1,0:T(8,128)(2,1)S(1)}, bf16[2,48,1024]{2,1,0:T(8,128)(2,1)S(1)}, u32[]{:S(2)}, u32[]{:S(2)}) collective-permute-start(bf16[2,48,1024]{2,1,0:T(8,128)(2,1)S(1)} %pad_maximum_fusion.25), channel_id=1, source_target_pairs={{0,8},{1,9},{2,10},{3,11},{4,12},{5,13},{6,14},{7,15},{8,0},{9,1},... | collective-permute-start | bytes 589832 | tf_op jit(solution)/shard_map/ppermute | solution.py:80
  201.9 11.9 %collective-permute-start.49 = (bf16[4,80,1024]{2,1,0:T(8,128)(2,1)S(1)}, bf16[4,80,1024]{2,1,0:T(8,128)(2,1)S(1)}, u32[]{:S(2)}, u32[]{:S(2)}) collective-permute-start(bf16[4,80,1024]{2,1,0:T(8,128)(2,1)S(1)} %pad_maximum_fusion.17.refs_0_), channel_id=1, source_target_pairs={{0,6},{1,9},{2,4},{3,11},{4,2},{5,13},{6,0},{7,15},{8,14},{9,1},{1... | collective-permute-start | bytes 1966088 | tf_op jit(solution)/shard_map/ppermute | solution.py:80
  203.9 8.4 %collective-permute-start.50 = (bf16[4,48,1024]{2,1,0:T(8,128)(2,1)S(1)}, bf16[4,48,1024]{2,1,0:T(8,128)(2,1)S(1)}, u32[]{:S(2)}, u32[]{:S(2)}) collective-permute-start(bf16[4,48,1024]{2,1,0:T(8,128)(2,1)S(1)} %pad_maximum_fusion.18.refs_1_), channel_id=1, source_target_pairs={{0,2},{1,3},{2,0},{3,1},{4,6},{5,7},{6,4},{7,5},{8,10},{9,11},{10,... | collective-permute-start | bytes 1179656 | tf_op jit(solution)/shard_map/ppermute | solution.py:80
  204.5 10.0 %collective-permute-start.52 = (bf16[4,80,1024]{2,1,0:T(8,128)(2,1)S(1)}, bf16[4,80,1024]{2,1,0:T(8,128)(2,1)S(1)}, u32[]{:S(2)}, u32[]{:S(2)}) collective-permute-start(bf16[4,80,1024]{2,1,0:T(8,128)(2,1)S(1)} %pad_maximum_fusion.17.refs_0_), channel_id=1, source_target_pairs={{0,1},{1,0},{2,3},{3,2},{4,5},{5,4},{6,7},{7,6},{8,9},{9,8},{10,11... | collective-permute-start | bytes 1966088 | tf_op jit(solution)/shard_map/ppermute | solution.py:63
  204.5 10.0 %collective-permute-start.53 = (bf16[4,48,1024]{2,1,0:T(8,128)(2,1)S(1)}, bf16[4,48,1024]{2,1,0:T(8,128)(2,1)S(1)}, u32[]{:S(2)}, u32[]{:S(2)}) collective-permute-start(bf16[4,48,1024]{2,1,0:T(8,128)(2,1)S(1)} %pad_maximum_fusion.18.refs_1_), channel_id=1, source_target_pairs={{0,1},{1,0},{2,3},{3,2},{4,5},{5,4},{6,7},{7,6},{8,9},{9,8},{10,11... | collective-permute-start | bytes 1179656 | tf_op jit(solution)/shard_map/ppermute | solution.py:63
  216.5 9.4 %collective-permute-start.51 = (bf16[2,128,512]{2,1,0:T(8,128)(2,1)S(1)}, bf16[2,128,512]{2,1,0:T(8,128)(2,1)S(1)}, u32[]{:S(2)}, u32[]{:S(2)}) collective-permute-start(bf16[2,128,512]{2,1,0:T(8,128)(2,1)S(1)} %slice_bitcast_fusion.10), channel_id=1, source_target_pairs={{0,16},{16,32},{32,48},{1,17},{17,33},{33,49},{2,18},{18,34},{34,5... | collective-permute-start | bytes 786440 | tf_op jit(solution)/shard_map/ppermute | solution.py:541
  221.9 9.3 %collective-permute-start.56 = (bf16[2,128,512]{2,1,0:T(8,128)(2,1)S(1)}, bf16[2,128,512]{2,1,0:T(8,128)(2,1)S(1)}, u32[]{:S(2)}, u32[]{:S(2)}) collective-permute-start(bf16[2,128,512]{2,1,0:T(8,128)(2,1)S(1)} %slice_bitcast_fusion.9), channel_id=1, source_target_pairs={{0,16},{16,32},{32,48},{1,17},{17,33},{33,49},{2,18},{18,34},{34,5... | collective-permute-start | bytes 786440 | tf_op jit(solution)/shard_map/ppermute | solution.py:541
  238.0 12.6 %collective-permute-start.59 = (bf16[4,352,256]{2,1,0:T(8,128)(2,1)S(1)}, bf16[4,352,256]{2,1,0:T(8,128)(2,1)S(1)}, u32[]{:S(2)}, u32[]{:S(2)}) collective-permute-start(bf16[4,352,256]{2,1,0:T(8,128)(2,1)S(1)} %add_convert_fusion.4), channel_id=1, source_target_pairs={{0,6},{1,9},{2,4},{3,11},{4,2},{5,13},{6,0},{7,15},{8,14},{9,1},{1... | collective-permute-start | bytes 2162696 | tf_op jit(solution)/shard_map/ppermute | solution.py:80
  240.3 9.9 %collective-permute-start.60 = (bf16[4,160,256]{2,1,0:T(8,128)(2,1)S(1)}, bf16[4,160,256]{2,1,0:T(8,128)(2,1)S(1)}, u32[]{:S(2)}, u32[]{:S(2)}) collective-permute-start(bf16[4,160,256]{2,1,0:T(8,128)(2,1)S(1)} %add_convert_fusion.7), channel_id=1, source_target_pairs={{0,2},{1,3},{2,0},{3,1},{4,6},{5,7},{6,4},{7,5},{8,10},{9,11},{10,... | collective-permute-start | bytes 983048 | tf_op jit(solution)/shard_map/ppermute | solution.py:80
  250.9 7.5 %collective-permute-start.63 = (bf16[2,352,256]{2,1,0:T(8,128)(2,1)S(1)}, bf16[2,352,256]{2,1,0:T(8,128)(2,1)S(1)}, u32[]{:S(2)}, u32[]{:S(2)}) collective-permute-start(bf16[2,352,256]{2,1,0:T(8,128)(2,1)S(1)} %slice.412), channel_id=1, source_target_pairs={{0,2},{1,7},{2,0},{3,5},{4,6},{5,3},{6,4},{7,1},{8,10},{9,15},{10,... | collective-permute-start | bytes 1081352 | tf_op jit(solution)/shard_map/ppermute | solution.py:80
  251.1 6.9 %collective-permute-start.64 = (bf16[2,160,256]{2,1,0:T(8,128)(2,1)S(1)}, bf16[2,160,256]{2,1,0:T(8,128)(2,1)S(1)}, u32[]{:S(2)}, u32[]{:S(2)}) collective-permute-start(bf16[2,160,256]{2,1,0:T(8,128)(2,1)S(1)} %slice.415), channel_id=1, source_target_pairs={{0,8},{1,9},{2,10},{3,11},{4,12},{5,13},{6,14},{7,15},{8,0},{9,1},... | collective-permute-start | bytes 491528 | tf_op jit(solution)/shard_map/ppermute | solution.py:80
  258.5 8.3 %collective-permute-start.65 = (bf16[352,256]{1,0:T(8,128)(2,1)S(1)}, bf16[352,256]{1,0:T(8,128)(2,1)S(1)}, u32[]{:S(2)}, u32[]{:S(2)}) collective-permute-start(bf16[352,256]{1,0:T(8,128)(2,1)S(1)} %fusion.20), channel_id=1, source_target_pairs={{0,8},{1,3},{2,10},{3,1},{4,12},{5,7},{6,14},{7,5},{8,0},{9,11},{1... | collective-permute-start | bytes 540680 | tf_op jit(solution)/shard_map/ppermute | solution.py:80
  266.9 8.0 %collective-permute-start.67 = (bf16[512,256]{1,0:T(8,128)(2,1)S(1)}, bf16[512,256]{1,0:T(8,128)(2,1)S(1)}, u32[]{:S(2)}, u32[]{:S(2)}) collective-permute-start(bf16[512,256]{1,0:T(8,128)(2,1)S(1)} %pad_maximum_fusion.24), channel_id=1, source_target_pairs={{0,64},{64,0},{1,65},{65,1},{2,66},{66,2},{3,67},{67,3},{4,68},{68... | collective-permute-start | bytes 786440 | tf_op jit(solution)/shard_map/ppermute | solution.py:67
  281.4 7.5 %collective-permute-start.70 = (bf16[2,352,256]{2,1,0:T(8,128)(2,1)S(1)}, bf16[2,352,256]{2,1,0:T(8,128)(2,1)S(1)}, u32[]{:S(2)}, u32[]{:S(2)}) collective-permute-start(bf16[2,352,256]{2,1,0:T(8,128)(2,1)S(1)} %pad_maximum_fusion.19), channel_id=1, source_target_pairs={{0,2},{1,7},{2,0},{3,5},{4,6},{5,3},{6,4},{7,1},{8,10},{9,15},{10,... | collective-permute-start | bytes 1081352 | tf_op jit(solution)/shard_map/ppermute | solution.py:80
  289.0 12.6 %collective-permute-start.74 = (bf16[4,352,256]{2,1,0:T(8,128)(2,1)S(1)}, bf16[4,352,256]{2,1,0:T(8,128)(2,1)S(1)}, u32[]{:S(2)}, u32[]{:S(2)}) collective-permute-start(bf16[4,352,256]{2,1,0:T(8,128)(2,1)S(1)} %pad_maximum_fusion.15.refs_0_), channel_id=1, source_target_pairs={{0,6},{1,9},{2,4},{3,11},{4,2},{5,13},{6,0},{7,15},{8,14},{9,1},{1... | collective-permute-start | bytes 2162696 | tf_op jit(solution)/shard_map/ppermute | solution.py:80
  291.2 7.2 %collective-permute-start.75 = (bf16[4,160,256]{2,1,0:T(8,128)(2,1)S(1)}, bf16[4,160,256]{2,1,0:T(8,128)(2,1)S(1)}, u32[]{:S(2)}, u32[]{:S(2)}) collective-permute-start(bf16[4,160,256]{2,1,0:T(8,128)(2,1)S(1)} %pad_maximum_fusion.22.refs_1_), channel_id=1, source_target_pairs={{0,2},{1,3},{2,0},{3,1},{4,6},{5,7},{6,4},{7,5},{8,10},{9,11},{10,... | collective-permute-start | bytes 983048 | tf_op jit(solution)/shard_map/ppermute | solution.py:80
  292.5 9.7 %collective-permute-start.73 = (bf16[4,160,256]{2,1,0:T(8,128)(2,1)S(1)}, bf16[4,160,256]{2,1,0:T(8,128)(2,1)S(1)}, u32[]{:S(2)}, u32[]{:S(2)}) collective-permute-start(bf16[4,160,256]{2,1,0:T(8,128)(2,1)S(1)} %pad_maximum_fusion.22.refs_1_), channel_id=1, source_target_pairs={{0,1},{1,0},{2,3},{3,2},{4,5},{5,4},{6,7},{7,6},{8,9},{9,8},{10,11... | collective-permute-start | bytes 983048 | tf_op jit(solution)/shard_map/ppermute | solution.py:63
  292.5 9.7 %collective-permute-start.72 = (bf16[4,352,256]{2,1,0:T(8,128)(2,1)S(1)}, bf16[4,352,256]{2,1,0:T(8,128)(2,1)S(1)}, u32[]{:S(2)}, u32[]{:S(2)}) collective-permute-start(bf16[4,352,256]{2,1,0:T(8,128)(2,1)S(1)} %pad_maximum_fusion.15.refs_0_), channel_id=1, source_target_pairs={{0,1},{1,0},{2,3},{3,2},{4,5},{5,4},{6,7},{7,6},{8,9},{9,8},{10,11... | collective-permute-start | bytes 2162696 | tf_op jit(solution)/shard_map/ppermute | solution.py:63
  341.9 12.6 %collective-permute-start.80 = (bf16[4,352,256]{2,1,0:T(8,128)(2,1)S(1)}, bf16[4,352,256]{2,1,0:T(8,128)(2,1)S(1)}, u32[]{:S(2)}, u32[]{:S(2)}) collective-permute-start(bf16[4,352,256]{2,1,0:T(8,128)(2,1)S(1)} %add_convert_fusion.3), channel_id=1, source_target_pairs={{0,6},{1,9},{2,4},{3,11},{4,2},{5,13},{6,0},{7,15},{8,14},{9,1},{1... | collective-permute-start | bytes 2162696 | tf_op jit(solution)/shard_map/ppermute | solution.py:80
  344.2 10.4 %collective-permute-start.81 = (bf16[4,160,256]{2,1,0:T(8,128)(2,1)S(1)}, bf16[4,160,256]{2,1,0:T(8,128)(2,1)S(1)}, u32[]{:S(2)}, u32[]{:S(2)}) collective-permute-start(bf16[4,160,256]{2,1,0:T(8,128)(2,1)S(1)} %add_convert_fusion.6), channel_id=1, source_target_pairs={{0,2},{1,3},{2,0},{3,1},{4,6},{5,7},{6,4},{7,5},{8,10},{9,11},{10,... | collective-permute-start | bytes 983048 | tf_op jit(solution)/shard_map/ppermute | solution.py:80
  354.8 7.5 %collective-permute-start.84 = (bf16[2,352,256]{2,1,0:T(8,128)(2,1)S(1)}, bf16[2,352,256]{2,1,0:T(8,128)(2,1)S(1)}, u32[]{:S(2)}, u32[]{:S(2)}) collective-permute-start(bf16[2,352,256]{2,1,0:T(8,128)(2,1)S(1)} %slice.411), channel_id=1, source_target_pairs={{0,2},{1,7},{2,0},{3,5},{4,6},{5,3},{6,4},{7,1},{8,10},{9,15},{10,... | collective-permute-start | bytes 1081352 | tf_op jit(solution)/shard_map/ppermute | solution.py:80
  362.5 7.8 %collective-permute-start.86 = (bf16[352,256]{1,0:T(8,128)(2,1)S(1)}, bf16[352,256]{1,0:T(8,128)(2,1)S(1)}, u32[]{:S(2)}, u32[]{:S(2)}) collective-permute-start(bf16[352,256]{1,0:T(8,128)(2,1)S(1)} %fusion.21), channel_id=1, source_target_pairs={{0,8},{1,3},{2,10},{3,1},{4,12},{5,7},{6,14},{7,5},{8,0},{9,11},{1... | collective-permute-start | bytes 540680 | tf_op jit(solution)/shard_map/ppermute | solution.py:80
  376.4 7.5 %collective-permute-start.90 = (bf16[2,352,256]{2,1,0:T(8,128)(2,1)S(1)}, bf16[2,352,256]{2,1,0:T(8,128)(2,1)S(1)}, u32[]{:S(2)}, u32[]{:S(2)}) collective-permute-start(bf16[2,352,256]{2,1,0:T(8,128)(2,1)S(1)} %pad_maximum_fusion.20), channel_id=1, source_target_pairs={{0,2},{1,7},{2,0},{3,5},{4,6},{5,3},{6,4},{7,1},{8,10},{9,15},{10,... | collective-permute-start | bytes 1081352 | tf_op jit(solution)/shard_map/ppermute | solution.py:80
  384.0 12.6 %collective-permute-start.94 = (bf16[4,352,256]{2,1,0:T(8,128)(2,1)S(1)}, bf16[4,352,256]{2,1,0:T(8,128)(2,1)S(1)}, u32[]{:S(2)}, u32[]{:S(2)}) collective-permute-start(bf16[4,352,256]{2,1,0:T(8,128)(2,1)S(1)} %pad_maximum_fusion.16.refs_0_), channel_id=1, source_target_pairs={{0,6},{1,9},{2,4},{3,11},{4,2},{5,13},{6,0},{7,15},{8,14},{9,1},{1... | collective-permute-start | bytes 2162696 | tf_op jit(solution)/shard_map/ppermute | solution.py:80
  386.2 7.2 %collective-permute-start.95 = (bf16[4,160,256]{2,1,0:T(8,128)(2,1)S(1)}, bf16[4,160,256]{2,1,0:T(8,128)(2,1)S(1)}, u32[]{:S(2)}, u32[]{:S(2)}) collective-permute-start(bf16[4,160,256]{2,1,0:T(8,128)(2,1)S(1)} %pad_maximum_fusion.23.refs_1_), channel_id=1, source_target_pairs={{0,2},{1,3},{2,0},{3,1},{4,6},{5,7},{6,4},{7,5},{8,10},{9,11},{10,... | collective-permute-start | bytes 983048 | tf_op jit(solution)/shard_map/ppermute | solution.py:80
  387.5 11.7 %collective-permute-start.92 = (bf16[4,352,256]{2,1,0:T(8,128)(2,1)S(1)}, bf16[4,352,256]{2,1,0:T(8,128)(2,1)S(1)}, u32[]{:S(2)}, u32[]{:S(2)}) collective-permute-start(bf16[4,352,256]{2,1,0:T(8,128)(2,1)S(1)} %pad_maximum_fusion.16.refs_0_), channel_id=1, source_target_pairs={{0,1},{1,0},{2,3},{3,2},{4,5},{5,4},{6,7},{7,6},{8,9},{9,8},{10,11... | collective-permute-start | bytes 2162696 | tf_op jit(solution)/shard_map/ppermute | solution.py:63
  410.4 12.8 %collective-permute-start.100 = (bf16[4,352,256]{2,1,0:T(8,128)(2,1)S(1)}, bf16[4,352,256]{2,1,0:T(8,128)(2,1)S(1)}, u32[]{:S(2)}, u32[]{:S(2)}) collective-permute-start(bf16[4,352,256]{2,1,0:T(8,128)(2,1)S(1)} %add_convert_fusion.2), channel_id=1, source_target_pairs={{0,6},{1,9},{2,4},{3,11},{4,2},{5,13},{6,0},{7,15},{8,14},{9,1},{1... | collective-permute-start | bytes 2162696 | tf_op jit(solution)/shard_map/ppermute | solution.py:80
  413.1 10.1 %collective-permute-start.101 = (bf16[4,160,256]{2,1,0:T(8,128)(2,1)S(1)}, bf16[4,160,256]{2,1,0:T(8,128)(2,1)S(1)}, u32[]{:S(2)}, u32[]{:S(2)}) collective-permute-start(bf16[4,160,256]{2,1,0:T(8,128)(2,1)S(1)} %add_convert_fusion.5), channel_id=1, source_target_pairs={{0,2},{1,3},{2,0},{3,1},{4,6},{5,7},{6,4},{7,5},{8,10},{9,11},{10,... | collective-permute-start | bytes 983048 | tf_op jit(solution)/shard_map/ppermute | solution.py:80
  423.5 7.5 %collective-permute-start.104 = (bf16[2,352,256]{2,1,0:T(8,128)(2,1)S(1)}, bf16[2,352,256]{2,1,0:T(8,128)(2,1)S(1)}, u32[]{:S(2)}, u32[]{:S(2)}) collective-permute-start(bf16[2,352,256]{2,1,0:T(8,128)(2,1)S(1)} %slice.410), channel_id=1, source_target_pairs={{0,2},{1,7},{2,0},{3,5},{4,6},{5,3},{6,4},{7,1},{8,10},{9,15},{10,... | collective-permute-start | bytes 1081352 | tf_op jit(solution)/shard_map/ppermute | solution.py:80
  423.9 6.9 %collective-permute-start.105 = (bf16[2,160,256]{2,1,0:T(8,128)(2,1)S(1)}, bf16[2,160,256]{2,1,0:T(8,128)(2,1)S(1)}, u32[]{:S(2)}, u32[]{:S(2)}) collective-permute-start(bf16[2,160,256]{2,1,0:T(8,128)(2,1)S(1)} %slice.413), channel_id=1, source_target_pairs={{0,8},{1,9},{2,10},{3,11},{4,12},{5,13},{6,14},{7,15},{8,0},{9,1},... | collective-permute-start | bytes 491528 | tf_op jit(solution)/shard_map/ppermute | solution.py:80
  431.1 8.2 %collective-permute-start.106 = (bf16[352,256]{1,0:T(8,128)(2,1)S(1)}, bf16[352,256]{1,0:T(8,128)(2,1)S(1)}, u32[]{:S(2)}, u32[]{:S(2)}) collective-permute-start(bf16[352,256]{1,0:T(8,128)(2,1)S(1)} %fusion.22), channel_id=1, source_target_pairs={{0,8},{1,3},{2,10},{3,1},{4,12},{5,7},{6,14},{7,5},{8,0},{9,11},{1... | collective-permute-start | bytes 540680 | tf_op jit(solution)/shard_map/ppermute | solution.py:80
  439.4 7.7 %collective-permute-start.108 = (bf16[256,256]{1,0:T(8,128)(2,1)S(1)}, bf16[256,256]{1,0:T(8,128)(2,1)S(1)}, u32[]{:S(2)}, u32[]{:S(2)}) collective-permute-start(bf16[256,256]{1,0:T(8,128)(2,1)S(1)} %slice.288), channel_id=1, source_target_pairs={{0,64},{64,0},{1,65},{65,1},{2,66},{66,2},{3,67},{67,3},{4,68},{68... | collective-permute-start | bytes 393224 | tf_op jit(solution)/shard_map/ppermute | solution.py:67
  (60 other events, 591.2 us)

commit v9 on v8

--- a/solution.py
+++ b/solution.py
@@ -267,8 +267,8 @@
     )(triple)
 
 
-def crossed_kernel(asked_ref, *refs):
-    (prev_refs, pairs_refs), out_ref = (refs[0:2], refs[2:4]), refs[4]
+def crossed_kernel(asked_ref, prev_ref, *refs):
+    pairs_refs, out_ref = refs[:2], refs[2]
     scaling = HEAD ** (-0.5)
     row = lax.broadcasted_iota(jnp.int32, (BLOCK, 2 * KEYS), 0)
     col = lax.broadcasted_iota(jnp.int32, (BLOCK, 2 * KEYS), 1)
@@ -277,8 +277,10 @@
         b, h = divmod(unit, 2)
 
         def both_blocks(i, cols):
-            before = [ref[b, :, cols] if i == 0 else pair[b, i - 1, :, cols]
-                      for ref, pair in zip(prev_refs, pairs_refs)]
+            before = [
+                prev_ref[pick, b, :, cols] if i == 0 else pair[b, i - 1, :, cols]
+                for pick, pair in enumerate(pairs_refs)
+            ]
             return jnp.concatenate(before + [pair[b, i, :, cols] for pair in pairs_refs], axis=0)
 
         for i in range(ROWS // BLOCK):
@@ -302,7 +304,7 @@
         crossed_kernel,
         out_shape=jax.ShapeDtypeStruct(out, bf16),
         compiler_params=params(),
-    )(asked, *prevs, *pairs)
+    )(asked, prevs, *pairs)
 
 
 def terms_kernel(place_ref, mixed_ref, *refs):
@@ -357,13 +359,6 @@
 
 def by_parts(rows):
     return [rows[start : start + count] for start, count in zip(STARTS, PARTS)]
-
-
-def looked_up(own, other):
-    total = own + core_swap(other)
-    total = total[:4] + neighbour(total[4:], 0, 2)
-    total = total[:2] + neighbour(total[2:], 0, 1)
-    return total[0] + neighbour(total[1], 0, 0)
 
 
 def weight_parts(enc_qkv, enc_out, enc_up, enc_down):
@@ -493,13 +488,17 @@
     other = rows(places_both[1], wanted)
     *got, other, wanted = together(*first_round(local), other, wanted)
     near = [jnp.stack(pair) for pair in zip(local, got)]
-    own = rows(places_both[0], wanted)
-    *got, own = together(*[neighbour(value, part, 1) for part, value in enumerate(near)], own)
+    sent = [neighbour(value, part, 1) for part, value in enumerate(near)]
+    total = rows(places_both[0], wanted) + core_swap(other)
+    summed = neighbour(total[4:], 0, 2)
+    *got, summed = together(*sent, summed)
     near = [jnp.concatenate(pair) for pair in zip(near, got)]
-    far = [neighbour(value, part, 2) for part, value in enumerate(near)]
     swaps = [core_swap(value) for value in near]
-    *far, embedded = together(*far, looked_up(own, other))
+    far = together(*[neighbour(value, part, 2) for part, value in enumerate(near)])
     far_swaps = [core_swap(value) for value in far]
+    total = total[:4] + summed
+    total = total[:2] + neighbour(total[2:], 0, 1)
+    embedded = total[0] + neighbour(total[1], 0, 0)
     feed, mix = [
         [near[part], far[part], swaps[part], far_swaps[part]] for part in range(2)
     ]
@@ -536,10 +535,7 @@
             transcendentals=0,
         ),
     )(place, *rows, weight)
-    pairs = pairs.reshape(BATCH, CHIPS // BATCH, NB_LEN, 2 * WIDTH)
-    count = lax.axis_size("seq")
-    prev = lax.ppermute(pairs[:, -1], "seq", [(i, i + 1) for i in range(count - 1)])
-    return prev, pairs
+    return pairs.reshape(BATCH, CHIPS // BATCH, NB_LEN, 2 * WIDTH)
 
 
 def attention(triple):
@@ -608,8 +604,10 @@
     encoded = gather_chips(
         [encoded[start : start + count] for start, count in zip(ENC_STARTS, ENC_PARTS)]
     )
-    made = [make_pairs(place, rows, pair_w) for place, rows in zip(places_both, encoded)]
-    prevs, pairs = [prev for prev, _ in made], [rows for _, rows in made]
+    pairs = [make_pairs(place, rows, pair_w) for place, rows in zip(places_both, encoded)]
+    edges = jnp.stack([rows[:, -1] for rows in pairs])
+    count = lax.axis_size("seq")
+    prevs = lax.ppermute(edges, "seq", [(i, i + 1) for i in range(count - 1)])
     first = cross_layer(places_both, middle, asked, prevs, pairs, weights)
     handed = section_swap(jnp.concatenate(first))
     middle, asked = to_queries(places_both, by_parts(handed), weights)

time: 457 us -> 446 us (0.976)
  starting transfers between devices: 134 us -> 120 us
    ppermute x3, starting transfers between devices: 45.8 us -> 30.8 us  [section_swap(): return lax.ppermute(value, 'section', [(0, 1), (1, 0)])]
    ppermute x2 -> x1, waiting for transfers between devices: 5.81 us -> 11.4 us  [on_device(): prevs = lax.ppermute(edges, 'seq', [(i, i + 1) for i in range(count - 1)])]
  transfers between devices with their start and end apart: 95 -> 94, of which waited for: 52 -> 49; matrix products, arithmetic and copies ran while one was open for 1% -> 1% of each run, Pallas kernels for 7% -> 6%
where the time goes in v9:
time: 446 us; the launch traced here: 438 us
  waiting for transfers between devices  191 us (43%)
  starting transfers between devices  120 us (27%)
  Pallas kernels  53.4 us (12%)
  blocking collectives  52.5 us (12%)
  loops' own time  9.58 us (2%)
  other arithmetic  5.71 us (1%)
    ppermute x54, waiting for transfers between devices, neighbour(): return lax.ppermute(value, MP, route)  161 us
    ppermute x54, starting transfers between devices, neighbour(): return lax.ppermute(value, MP, route)  78.3 us
    all_to_all x2, blocking collectives, attention(): triple = lax.all_to_all(triple, 'seq', 0, 0, tiled=True)  34.4 us
    ppermute x3, starting transfers between devices, section_swap(): return lax.ppermute(value, 'section', [(0, 1), (1, 0)])  30.8 us
    pallas_call x8, Pallas kernels, project_half(): pl.pallas_call(functools.partial(project_kernel, last, units), grid_spec=...  25.3 us
    all_to_all x2, blocking collectives, attention(): return lax.all_to_all(causal(triple), 'seq', 0, 0, tiled=True)  18.1 us
    pallas_call x16, Pallas kernels, terms(): pl.pallas_call(terms_kernel, grid_spec=pltpu.PrefetchScalarGridSpec(num_s...  16.1 us
    ppermute x3, waiting for transfers between devices, section_swap(): return lax.ppermute(value, 'section', [(0, 1), (1, 0)])  13.8 us
  transfers between devices with their start and end apart: 94, of which 49 were waited for; matrix products, arithmetic and copies ran while one was open for 1% of the time, Pallas kernels for 6%

profile of v9, /device:TPU:0, one launch (start us, length us, event | category | flops | bytes accessed | tf_op | source)
XLA Modules:
  0.0 437.7 jit_solution(14177807076249973827)
XLA Ops:
  1.8 142.6 %conditional.1 = (bf16[512,256]{1,0:T(8,128)(2,1)S(1)}, bf16[512,256]{1,0:T(8,128)(2,1)S(1)}, bf16[128,1024]{1,0:T(8,128)(2,1)S(1)}) conditional(s32[]{:T(128)} %convert_element_type.283, (bf16[64,4096]{1,0:T(8,128)(2,1)}, bf16[256,1024]{1,0:T(8,128)(2,1)}, bf16[64,3,1024]{2,0,1:T(8,128)(2,1)}, bf16[64,1024]{1,0:T(8,128)(2,1)}, s32[64,128]{1,0:T(8,128)}, ...), branch_computations={%region_0.1_spmd, %region_1.2_spmd} | conditional | flops 5377753088 | bytes 194823744 | solution.py:601
  14.6 3.1 collective-permute-start.1
  21.5 5.7 %collective-permute-done.3 = bf16[2,160,256]{2,1,0:T(8,128)(2,1)S(1)} collective-permute-done((bf16[2,160,256]{2,1,0:T(8,128)(2,1)S(1)}, bf16[2,160,256]{2,1,0:T(8,128)(2,1)S(1)}, u32[]{:S(2)}, u32[]{:S(2)}) %collective-permute-start.3) | collective-permute-done | bytes 163872 | tf_op jit(solution)/shard_map/cond/branch_1_fun/ppermute | solution.py:80
  27.9 3.1 collective-permute-start.6
  31.7 6.7 %collective-permute-done.7.refs_3_ = bf16[4,160,256]{2,1,0:T(8,128)(2,1)S(1)} collective-permute-done((bf16[4,160,256]{2,1,0:T(8,128)(2,1)S(1)}, bf16[4,160,256]{2,1,0:T(8,128)(2,1)S(1)}, u32[]{:S(2)}, u32[]{:S(2)}) %collective-permute-start.7) | collective-permute-done | bytes 327712 | tf_op jit(solution)/shard_map/cond/branch_1_fun/ppermute | solution.py:80
  41.1 5.3 %branch_1_fun.9 = (f32[3,512,256]{2,1,0:T(8,128)S(1)}, f32[512,128]{1,0:T(8,128)S(1)}) custom-call(s32[17]{0:T(128)S(1)} %get-tuple-element.70.place_ref, bf16[4,352,256]{2,1,0:T(8,128)(2,1)S(1)} %pad_maximum_fusion.refs_0_, bf16[4,160,256]{2,1,0:T(8,128)(2,1)S(1)} %pad_maximum_fusion.4.refs_1_, bf16[4,352,256]{2,1,0:T(8,128)(2,1)S(1)} %collective-permute-done.6.refs_2_, ...), custom_call_target="tpu_custom_call" | custom-call | flops 1610612736 | bytes 6815744 | tf_op jit(solution)/shard_map/cond/branch_1_fun/pallas_call | solution.py:211
  46.4 3.8 branch_1_fun.10
  50.2 16.7 %all_to_all.18.triple_ref = bf16[4,3,256,128]{3,2,1,0:T(8,128)(2,1)S(1)} all-to-all(bf16[4,3,256,128]{3,2,1,0:T(8,128)(2,1)S(1)} %branch_1_fun.10), channel_id=1, replica_groups=mesh['section'=2,'seq'=4,'z'=2,'y'=4,'core'=2] {'seq'}, dimensions={0} | all-to-all | bytes 1572864 | tf_op jit(solution)/shard_map/cond/branch_1_fun/all_to_all | solution.py:542
  68.3 9.1 %all_to_all.19.mixed_ref = bf16[4,256,128]{2,1,0:T(8,128)(2,1)S(1)} all-to-all(bf16[4,256,128]{2,1,0:T(8,128)(2,1)S(1)} %branch_1_fun.11), channel_id=1, replica_groups=mesh['section'=2,'seq'=4,'z'=2,'y'=4,'core'=2] {'seq'}, dimensions={0} | all-to-all | bytes 524288 | tf_op jit(solution)/shard_map/cond/branch_1_fun/all_to_all | solution.py:543
  86.1 8.7 %collective-permute-done.13 = bf16[4,160,256]{2,1,0:T(8,128)(2,1)S(1)} collective-permute-done((bf16[4,160,256]{2,1,0:T(8,128)(2,1)S(1)}, bf16[4,160,256]{2,1,0:T(8,128)(2,1)S(1)}, u32[]{:S(2)}, u32[]{:S(2)}) %collective-permute-start.13) | collective-permute-done | bytes 327712 | tf_op jit(solution)/shard_map/cond/branch_1_fun/ppermute | solution.py:80
  96.0 5.9 %collective-permute-done.17 = bf16[2,160,256]{2,1,0:T(8,128)(2,1)S(1)} collective-permute-done((bf16[2,160,256]{2,1,0:T(8,128)(2,1)S(1)}, bf16[2,160,256]{2,1,0:T(8,128)(2,1)S(1)}, u32[]{:S(2)}, u32[]{:S(2)}) %collective-permute-start.17) | collective-permute-done | bytes 163872 | tf_op jit(solution)/shard_map/cond/branch_1_fun/ppermute | solution.py:80
  105.3 3.4 collective-permute-done.19
  113.0 3.4 collective-permute-done.21
  117.0 5.0 %collective-permute-done.23 = bf16[2,160,256]{2,1,0:T(8,128)(2,1)S(1)} collective-permute-done((bf16[2,160,256]{2,1,0:T(8,128)(2,1)S(1)}, bf16[2,160,256]{2,1,0:T(8,128)(2,1)S(1)}, u32[]{:S(2)}, u32[]{:S(2)}) %collective-permute-start.23) | collective-permute-done | bytes 163872 | tf_op jit(solution)/shard_map/cond/branch_1_fun/ppermute | solution.py:80
  124.2 3.4 collective-permute-start.26
  127.8 7.0 %collective-permute-done.27.refs_3_ = bf16[4,160,256]{2,1,0:T(8,128)(2,1)S(1)} collective-permute-done((bf16[4,160,256]{2,1,0:T(8,128)(2,1)S(1)}, bf16[4,160,256]{2,1,0:T(8,128)(2,1)S(1)}, u32[]{:S(2)}, u32[]{:S(2)}) %collective-permute-start.27) | collective-permute-done | bytes 327712 | tf_op jit(solution)/shard_map/cond/branch_1_fun/ppermute | solution.py:80
  144.4 23.8 %collective-permute-start.44 = (bf16[128,1024]{1,0:T(8,128)(2,1)S(1)}, bf16[128,1024]{1,0:T(8,128)(2,1)S(1)}, u32[]{:S(2)}, u32[]{:S(2)}) collective-permute-start(bf16[128,1024]{1,0:T(8,128)(2,1)S(1)} %get-tuple-element.201), channel_id=1, source_target_pairs={{0,64},{64,0},{1,65},{65,1},{2,66},{66,2},{3,67},{67,3},{4,68},{68... | collective-permute-start | bytes 786440 | tf_op jit(solution)/shard_map/ppermute | solution.py:67
  168.2 6.2 %collective-permute-done.44 = bf16[128,1024]{1,0:T(8,128)(2,1)S(1)} collective-permute-done((bf16[128,1024]{1,0:T(8,128)(2,1)S(1)}, bf16[128,1024]{1,0:T(8,128)(2,1)S(1)}, u32[]{:S(2)}, u32[]{:S(2)}) %collective-permute-start.44) | collective-permute-done | bytes 262176 | tf_op jit(solution)/shard_map/ppermute | solution.py:67
  176.8 3.9 collective-permute-done.46
  182.8 4.4 %collective-permute-done.48 = bf16[2,48,1024]{2,1,0:T(8,128)(2,1)S(1)} collective-permute-done((bf16[2,48,1024]{2,1,0:T(8,128)(2,1)S(1)}, bf16[2,48,1024]{2,1,0:T(8,128)(2,1)S(1)}, u32[]{:S(2)}, u32[]{:S(2)}) %collective-permute-start.48) | collective-permute-done | bytes 196640 | tf_op jit(solution)/shard_map/ppermute | solution.py:80
  191.7 6.3 %collective-permute-done.50.refs_3_ = bf16[4,48,1024]{2,1,0:T(8,128)(2,1)S(1)} collective-permute-done((bf16[4,48,1024]{2,1,0:T(8,128)(2,1)S(1)}, bf16[4,48,1024]{2,1,0:T(8,128)(2,1)S(1)}, u32[]{:S(2)}, u32[]{:S(2)}) %collective-permute-start.50) | collective-permute-done | bytes 393248 | tf_op jit(solution)/shard_map/ppermute | solution.py:80
  204.7 3.6 collective-permute-start.55
  208.2 11.4 %collective-permute-done.55.prev_ref = bf16[2,2,128,512]{3,2,1,0:T(8,128)(2,1)S(1)} collective-permute-done((bf16[2,2,128,512]{3,2,1,0:T(8,128)(2,1)S(1)}, bf16[2,2,128,512]{3,2,1,0:T(8,128)(2,1)S(1)}, u32[]{:S(2)}, u32[]{:S(2)}) %collective-permute-start.55) | collective-permute-done | bytes 524320 | tf_op jit(solution)/shard_map/ppermute | solution.py:610
  230.3 8.3 %collective-permute-done.59 = bf16[4,160,256]{2,1,0:T(8,128)(2,1)S(1)} collective-permute-done((bf16[4,160,256]{2,1,0:T(8,128)(2,1)S(1)}, bf16[4,160,256]{2,1,0:T(8,128)(2,1)S(1)}, u32[]{:S(2)}, u32[]{:S(2)}) %collective-permute-start.59) | collective-permute-done | bytes 327712 | tf_op jit(solution)/shard_map/ppermute | solution.py:80
  241.5 4.6 %collective-permute-done.63 = bf16[2,160,256]{2,1,0:T(8,128)(2,1)S(1)} collective-permute-done((bf16[2,160,256]{2,1,0:T(8,128)(2,1)S(1)}, bf16[2,160,256]{2,1,0:T(8,128)(2,1)S(1)}, u32[]{:S(2)}, u32[]{:S(2)}) %collective-permute-start.63) | collective-permute-done | bytes 163872 | tf_op jit(solution)/shard_map/ppermute | solution.py:80
  250.7 3.9 collective-permute-done.65
  254.8 3.3 collective-permute-start.66
  258.1 4.6 %collective-permute-done.66 = bf16[512,256]{1,0:T(8,128)(2,1)S(1)} collective-permute-done((bf16[512,256]{1,0:T(8,128)(2,1)S(1)}, bf16[512,256]{1,0:T(8,128)(2,1)S(1)}, u32[]{:S(2)}, u32[]{:S(2)}) %collective-permute-start.66) | collective-permute-done | bytes 262176 | tf_op jit(solution)/shard_map/ppermute | solution.py:67
  265.1 3.7 collective-permute-done.68
  270.8 4.4 collective-permute-done.70
  281.0 5.7 %collective-permute-done.74.refs_3_ = bf16[4,160,256]{2,1,0:T(8,128)(2,1)S(1)} collective-permute-done((bf16[4,160,256]{2,1,0:T(8,128)(2,1)S(1)}, bf16[4,160,256]{2,1,0:T(8,128)(2,1)S(1)}, u32[]{:S(2)}, u32[]{:S(2)}) %collective-permute-start.74) | collective-permute-done | bytes 327712 | tf_op jit(solution)/shard_map/ppermute | solution.py:80
  289.7 3.7 shard_map.169
  293.4 3.8 shard_map.170
  297.3 17.7 %all_to_all.20.triple_ref = bf16[4,3,256,128]{3,2,1,0:T(8,128)(2,1)S(1)} all-to-all(bf16[4,3,256,128]{3,2,1,0:T(8,128)(2,1)S(1)} %shard_map.170), channel_id=1, replica_groups=mesh['section'=2,'seq'=4,'z'=2,'y'=4,'core'=2] {'seq'}, dimensions={0} | all-to-all | bytes 1572864 | tf_op jit(solution)/shard_map/all_to_all | solution.py:542
  316.3 9.1 %all_to_all.21.mixed_ref = bf16[4,256,128]{2,1,0:T(8,128)(2,1)S(1)} all-to-all(bf16[4,256,128]{2,1,0:T(8,128)(2,1)S(1)} %shard_map.171), channel_id=1, replica_groups=mesh['section'=2,'seq'=4,'z'=2,'y'=4,'core'=2] {'seq'}, dimensions={0} | all-to-all | bytes 524288 | tf_op jit(solution)/shard_map/all_to_all | solution.py:543
  329.4 3.1 collective-permute-start.79
  334.1 8.7 %collective-permute-done.80 = bf16[4,160,256]{2,1,0:T(8,128)(2,1)S(1)} collective-permute-done((bf16[4,160,256]{2,1,0:T(8,128)(2,1)S(1)}, bf16[4,160,256]{2,1,0:T(8,128)(2,1)S(1)}, u32[]{:S(2)}, u32[]{:S(2)}) %collective-permute-start.80) | collective-permute-done | bytes 327712 | tf_op jit(solution)/shard_map/ppermute | solution.py:80
  346.8 4.4 collective-permute-done.84
  356.3 3.5 collective-permute-done.86
  362.2 4.0 collective-permute-done.88
  368.0 3.8 collective-permute-done.90
  377.2 6.0 %collective-permute-done.94.refs_3_ = bf16[4,160,256]{2,1,0:T(8,128)(2,1)S(1)} collective-permute-done((bf16[4,160,256]{2,1,0:T(8,128)(2,1)S(1)}, bf16[4,160,256]{2,1,0:T(8,128)(2,1)S(1)}, u32[]{:S(2)}, u32[]{:S(2)}) %collective-permute-start.94) | collective-permute-done | bytes 327712 | tf_op jit(solution)/shard_map/ppermute | solution.py:80
  383.2 3.3 collective-permute-done.93.refs_2_
  404.0 8.9 %collective-permute-done.100 = bf16[4,160,256]{2,1,0:T(8,128)(2,1)S(1)} collective-permute-done((bf16[4,160,256]{2,1,0:T(8,128)(2,1)S(1)}, bf16[4,160,256]{2,1,0:T(8,128)(2,1)S(1)}, u32[]{:S(2)}, u32[]{:S(2)}) %collective-permute-start.100) | collective-permute-done | bytes 327712 | tf_op jit(solution)/shard_map/ppermute | solution.py:80
  413.7 3.2 collective-permute-start.104
  416.9 4.3 collective-permute-done.104
  426.1 3.7 collective-permute-done.106
  429.9 3.7 collective-permute-start.107
  (295 shorter events, 143.8 us)
Async XLA Ops:
  11.6 8.7 %collective-permute-start = (bf16[352,256]{1,0:T(8,128)(2,1)S(1)}, bf16[352,256]{1,0:T(8,128)(2,1)S(1)}, u32[]{:S(2)}, u32[]{:S(2)}) collective-permute-start(bf16[352,256]{1,0:T(8,128)(2,1)S(1)} %get-tuple-element.332), channel_id=1, source_target_pairs={{0,8},{1,3},{2,10},{3,1},{4,12},{5,7},{6,14},{7,5},{8,0},{9,11},{1... | collective-permute-start | bytes 540680 | tf_op jit(solution)/shard_map/cond/branch_1_fun/ppermute | solution.py:80
  20.3 7.5 %collective-permute-start.2 = (bf16[2,352,256]{2,1,0:T(8,128)(2,1)S(1)}, bf16[2,352,256]{2,1,0:T(8,128)(2,1)S(1)}, u32[]{:S(2)}, u32[]{:S(2)}) collective-permute-start(bf16[2,352,256]{2,1,0:T(8,128)(2,1)S(1)} %pad_maximum_fusion.2), channel_id=1, source_target_pairs={{0,2},{1,7},{2,0},{3,5},{4,6},{5,3},{6,4},{7,1},{8,10},{9,15},{10,... | collective-permute-start | bytes 1081352 | tf_op jit(solution)/shard_map/cond/branch_1_fun/ppermute | solution.py:80
  27.9 12.6 %collective-permute-start.6 = (bf16[4,352,256]{2,1,0:T(8,128)(2,1)S(1)}, bf16[4,352,256]{2,1,0:T(8,128)(2,1)S(1)}, u32[]{:S(2)}, u32[]{:S(2)}) collective-permute-start(bf16[4,352,256]{2,1,0:T(8,128)(2,1)S(1)} %pad_maximum_fusion.refs_0_), channel_id=1, source_target_pairs={{0,6},{1,9},{2,4},{3,11},{4,2},{5,13},{6,0},{7,15},{8,14},{9,1},{1... | collective-permute-start | bytes 2162696 | tf_op jit(solution)/shard_map/cond/branch_1_fun/ppermute | solution.py:80
  31.0 7.3 %collective-permute-start.7 = (bf16[4,160,256]{2,1,0:T(8,128)(2,1)S(1)}, bf16[4,160,256]{2,1,0:T(8,128)(2,1)S(1)}, u32[]{:S(2)}, u32[]{:S(2)}) collective-permute-start(bf16[4,160,256]{2,1,0:T(8,128)(2,1)S(1)} %pad_maximum_fusion.4.refs_1_), channel_id=1, source_target_pairs={{0,2},{1,3},{2,0},{3,1},{4,6},{5,7},{6,4},{7,5},{8,10},{9,11},{10,... | collective-permute-start | bytes 983048 | tf_op jit(solution)/shard_map/cond/branch_1_fun/ppermute | solution.py:80
  31.1 9.9 %collective-permute-start.4 = (bf16[4,352,256]{2,1,0:T(8,128)(2,1)S(1)}, bf16[4,352,256]{2,1,0:T(8,128)(2,1)S(1)}, u32[]{:S(2)}, u32[]{:S(2)}) collective-permute-start(bf16[4,352,256]{2,1,0:T(8,128)(2,1)S(1)} %pad_maximum_fusion.refs_0_), channel_id=1, source_target_pairs={{0,1},{1,0},{2,3},{3,2},{4,5},{5,4},{6,7},{7,6},{8,9},{9,8},{10,11... | collective-permute-start | bytes 2162696 | tf_op jit(solution)/shard_map/cond/branch_1_fun/ppermute | solution.py:63
  31.2 9.8 %collective-permute-start.5 = (bf16[4,160,256]{2,1,0:T(8,128)(2,1)S(1)}, bf16[4,160,256]{2,1,0:T(8,128)(2,1)S(1)}, u32[]{:S(2)}, u32[]{:S(2)}) collective-permute-start(bf16[4,160,256]{2,1,0:T(8,128)(2,1)S(1)} %pad_maximum_fusion.4.refs_1_), channel_id=1, source_target_pairs={{0,1},{1,0},{2,3},{3,2},{4,5},{5,4},{6,7},{7,6},{8,9},{9,8},{10,11... | collective-permute-start | bytes 983048 | tf_op jit(solution)/shard_map/cond/branch_1_fun/ppermute | solution.py:63
  81.4 13.4 %collective-permute-start.12 = (bf16[4,352,256]{2,1,0:T(8,128)(2,1)S(1)}, bf16[4,352,256]{2,1,0:T(8,128)(2,1)S(1)}, u32[]{:S(2)}, u32[]{:S(2)}) collective-permute-start(bf16[4,352,256]{2,1,0:T(8,128)(2,1)S(1)} %add_convert_fusion), channel_id=1, source_target_pairs={{0,6},{1,9},{2,4},{3,11},{4,2},{5,13},{6,0},{7,15},{8,14},{9,1},{1... | collective-permute-start | bytes 2162696 | tf_op jit(solution)/shard_map/cond/branch_1_fun/ppermute | solution.py:80
  84.5 10.2 %collective-permute-start.13 = (bf16[4,160,256]{2,1,0:T(8,128)(2,1)S(1)}, bf16[4,160,256]{2,1,0:T(8,128)(2,1)S(1)}, u32[]{:S(2)}, u32[]{:S(2)}) collective-permute-start(bf16[4,160,256]{2,1,0:T(8,128)(2,1)S(1)} %add_convert_fusion.1), channel_id=1, source_target_pairs={{0,2},{1,3},{2,0},{3,1},{4,6},{5,7},{6,4},{7,5},{8,10},{9,11},{10,... | collective-permute-start | bytes 983048 | tf_op jit(solution)/shard_map/cond/branch_1_fun/ppermute | solution.py:80
  95.0 7.5 %collective-permute-start.16 = (bf16[2,352,256]{2,1,0:T(8,128)(2,1)S(1)}, bf16[2,352,256]{2,1,0:T(8,128)(2,1)S(1)}, u32[]{:S(2)}, u32[]{:S(2)}) collective-permute-start(bf16[2,352,256]{2,1,0:T(8,128)(2,1)S(1)} %slice.408), channel_id=1, source_target_pairs={{0,2},{1,7},{2,0},{3,5},{4,6},{5,3},{6,4},{7,1},{8,10},{9,15},{10,... | collective-permute-start | bytes 1081352 | tf_op jit(solution)/shard_map/cond/branch_1_fun/ppermute | solution.py:80
  108.8 7.7 %collective-permute-start.20 = (bf16[352,256]{1,0:T(8,128)(2,1)S(1)}, bf16[352,256]{1,0:T(8,128)(2,1)S(1)}, u32[]{:S(2)}, u32[]{:S(2)}) collective-permute-start(bf16[352,256]{1,0:T(8,128)(2,1)S(1)} %fusion.2), channel_id=1, source_target_pairs={{0,8},{1,3},{2,10},{3,1},{4,12},{5,7},{6,14},{7,5},{8,0},{9,11},{1... | collective-permute-start | bytes 540680 | tf_op jit(solution)/shard_map/cond/branch_1_fun/ppermute | solution.py:80
  116.5 7.6 %collective-permute-start.22 = (bf16[2,352,256]{2,1,0:T(8,128)(2,1)S(1)}, bf16[2,352,256]{2,1,0:T(8,128)(2,1)S(1)}, u32[]{:S(2)}, u32[]{:S(2)}) collective-permute-start(bf16[2,352,256]{2,1,0:T(8,128)(2,1)S(1)} %pad_maximum_fusion.3), channel_id=1, source_target_pairs={{0,2},{1,7},{2,0},{3,5},{4,6},{5,3},{6,4},{7,1},{8,10},{9,15},{10,... | collective-permute-start | bytes 1081352 | tf_op jit(solution)/shard_map/cond/branch_1_fun/ppermute | solution.py:80
  124.2 12.7 %collective-permute-start.26 = (bf16[4,352,256]{2,1,0:T(8,128)(2,1)S(1)}, bf16[4,352,256]{2,1,0:T(8,128)(2,1)S(1)}, u32[]{:S(2)}, u32[]{:S(2)}) collective-permute-start(bf16[4,352,256]{2,1,0:T(8,128)(2,1)S(1)} %pad_maximum_fusion.1.refs_0_), channel_id=1, source_target_pairs={{0,6},{1,9},{2,4},{3,11},{4,2},{5,13},{6,0},{7,15},{8,14},{9,1},{1... | collective-permute-start | bytes 2162696 | tf_op jit(solution)/shard_map/cond/branch_1_fun/ppermute | solution.py:80
  127.7 7.2 %collective-permute-start.27 = (bf16[4,160,256]{2,1,0:T(8,128)(2,1)S(1)}, bf16[4,160,256]{2,1,0:T(8,128)(2,1)S(1)}, u32[]{:S(2)}, u32[]{:S(2)}) collective-permute-start(bf16[4,160,256]{2,1,0:T(8,128)(2,1)S(1)} %pad_maximum_fusion.5.refs_1_), channel_id=1, source_target_pairs={{0,2},{1,3},{2,0},{3,1},{4,6},{5,7},{6,4},{7,5},{8,10},{9,11},{10,... | collective-permute-start | bytes 983048 | tf_op jit(solution)/shard_map/cond/branch_1_fun/ppermute | solution.py:80
  127.8 11.8 %collective-permute-start.24 = (bf16[4,352,256]{2,1,0:T(8,128)(2,1)S(1)}, bf16[4,352,256]{2,1,0:T(8,128)(2,1)S(1)}, u32[]{:S(2)}, u32[]{:S(2)}) collective-permute-start(bf16[4,352,256]{2,1,0:T(8,128)(2,1)S(1)} %pad_maximum_fusion.1.refs_0_), channel_id=1, source_target_pairs={{0,1},{1,0},{2,3},{3,2},{4,5},{5,4},{6,7},{7,6},{8,9},{9,8},{10,11... | collective-permute-start | bytes 2162696 | tf_op jit(solution)/shard_map/cond/branch_1_fun/ppermute | solution.py:63
  144.4 30.0 %collective-permute-start.44 = (bf16[128,1024]{1,0:T(8,128)(2,1)S(1)}, bf16[128,1024]{1,0:T(8,128)(2,1)S(1)}, u32[]{:S(2)}, u32[]{:S(2)}) collective-permute-start(bf16[128,1024]{1,0:T(8,128)(2,1)S(1)} %get-tuple-element.201), channel_id=1, source_target_pairs={{0,64},{64,0},{1,65},{65,1},{2,66},{66,2},{3,67},{67,3},{4,68},{68... | collective-permute-start | bytes 786440 | tf_op jit(solution)/shard_map/ppermute | solution.py:67
  180.8 7.2 %collective-permute-start.47 = (bf16[2,80,1024]{2,1,0:T(8,128)(2,1)S(1)}, bf16[2,80,1024]{2,1,0:T(8,128)(2,1)S(1)}, u32[]{:S(2)}, u32[]{:S(2)}) collective-permute-start(bf16[2,80,1024]{2,1,0:T(8,128)(2,1)S(1)} %pad_maximum_fusion.22), channel_id=1, source_target_pairs={{0,2},{1,7},{2,0},{3,5},{4,6},{5,3},{6,4},{7,1},{8,10},{9,15},{10,... | collective-permute-start | bytes 983048 | tf_op jit(solution)/shard_map/ppermute | solution.py:80
  188.0 11.9 %collective-permute-start.49 = (bf16[4,80,1024]{2,1,0:T(8,128)(2,1)S(1)}, bf16[4,80,1024]{2,1,0:T(8,128)(2,1)S(1)}, u32[]{:S(2)}, u32[]{:S(2)}) collective-permute-start(bf16[4,80,1024]{2,1,0:T(8,128)(2,1)S(1)} %pad_maximum_fusion.17.refs_0_), channel_id=1, source_target_pairs={{0,6},{1,9},{2,4},{3,11},{4,2},{5,13},{6,0},{7,15},{8,14},{9,1},{1... | collective-permute-start | bytes 1966088 | tf_op jit(solution)/shard_map/ppermute | solution.py:80
  190.1 7.9 %collective-permute-start.50 = (bf16[4,48,1024]{2,1,0:T(8,128)(2,1)S(1)}, bf16[4,48,1024]{2,1,0:T(8,128)(2,1)S(1)}, u32[]{:S(2)}, u32[]{:S(2)}) collective-permute-start(bf16[4,48,1024]{2,1,0:T(8,128)(2,1)S(1)} %pad_maximum_fusion.19.refs_1_), channel_id=1, source_target_pairs={{0,2},{1,3},{2,0},{3,1},{4,6},{5,7},{6,4},{7,5},{8,10},{9,11},{10,... | collective-permute-start | bytes 1179656 | tf_op jit(solution)/shard_map/ppermute | solution.py:80
  191.2 9.5 %collective-permute-start.51 = (bf16[4,80,1024]{2,1,0:T(8,128)(2,1)S(1)}, bf16[4,80,1024]{2,1,0:T(8,128)(2,1)S(1)}, u32[]{:S(2)}, u32[]{:S(2)}) collective-permute-start(bf16[4,80,1024]{2,1,0:T(8,128)(2,1)S(1)} %pad_maximum_fusion.17.refs_0_), channel_id=1, source_target_pairs={{0,1},{1,0},{2,3},{3,2},{4,5},{5,4},{6,7},{7,6},{8,9},{9,8},{10,11... | collective-permute-start | bytes 1966088 | tf_op jit(solution)/shard_map/ppermute | solution.py:63
  191.2 9.5 %collective-permute-start.52 = (bf16[4,48,1024]{2,1,0:T(8,128)(2,1)S(1)}, bf16[4,48,1024]{2,1,0:T(8,128)(2,1)S(1)}, u32[]{:S(2)}, u32[]{:S(2)}) collective-permute-start(bf16[4,48,1024]{2,1,0:T(8,128)(2,1)S(1)} %pad_maximum_fusion.19.refs_1_), channel_id=1, source_target_pairs={{0,1},{1,0},{2,3},{3,2},{4,5},{5,4},{6,7},{7,6},{8,9},{9,8},{10,11... | collective-permute-start | bytes 1179656 | tf_op jit(solution)/shard_map/ppermute | solution.py:63
  204.7 14.9 %collective-permute-start.55 = (bf16[2,2,128,512]{3,2,1,0:T(8,128)(2,1)S(1)}, bf16[2,2,128,512]{3,2,1,0:T(8,128)(2,1)S(1)}, u32[]{:S(2)}, u32[]{:S(2)}) collective-permute-start(bf16[2,2,128,512]{3,2,1,0:T(8,128)(2,1)S(1)} %pad_maximum_fusion.18), channel_id=1, source_target_pairs={{0,16},{16,32},{32,48},{1,17},{17,33},{33,49},{2,18},{18,34},{34,5... | collective-permute-start | bytes 1572872 | tf_op jit(solution)/shard_map/ppermute | solution.py:610
  226.4 12.6 %collective-permute-start.58 = (bf16[4,352,256]{2,1,0:T(8,128)(2,1)S(1)}, bf16[4,352,256]{2,1,0:T(8,128)(2,1)S(1)}, u32[]{:S(2)}, u32[]{:S(2)}) collective-permute-start(bf16[4,352,256]{2,1,0:T(8,128)(2,1)S(1)} %add_convert_fusion.4), channel_id=1, source_target_pairs={{0,6},{1,9},{2,4},{3,11},{4,2},{5,13},{6,0},{7,15},{8,14},{9,1},{1... | collective-permute-start | bytes 2162696 | tf_op jit(solution)/shard_map/ppermute | solution.py:80
  228.4 10.2 %collective-permute-start.59 = (bf16[4,160,256]{2,1,0:T(8,128)(2,1)S(1)}, bf16[4,160,256]{2,1,0:T(8,128)(2,1)S(1)}, u32[]{:S(2)}, u32[]{:S(2)}) collective-permute-start(bf16[4,160,256]{2,1,0:T(8,128)(2,1)S(1)} %add_convert_fusion.7), channel_id=1, source_target_pairs={{0,2},{1,3},{2,0},{3,1},{4,6},{5,7},{6,4},{7,5},{8,10},{9,11},{10,... | collective-permute-start | bytes 983048 | tf_op jit(solution)/shard_map/ppermute | solution.py:80
  239.2 7.5 %collective-permute-start.62 = (bf16[2,352,256]{2,1,0:T(8,128)(2,1)S(1)}, bf16[2,352,256]{2,1,0:T(8,128)(2,1)S(1)}, u32[]{:S(2)}, u32[]{:S(2)}) collective-permute-start(bf16[2,352,256]{2,1,0:T(8,128)(2,1)S(1)} %slice.412), channel_id=1, source_target_pairs={{0,2},{1,7},{2,0},{3,5},{4,6},{5,3},{6,4},{7,1},{8,10},{9,15},{10,... | collective-permute-start | bytes 1081352 | tf_op jit(solution)/shard_map/ppermute | solution.py:80
  239.5 6.6 %collective-permute-start.63 = (bf16[2,160,256]{2,1,0:T(8,128)(2,1)S(1)}, bf16[2,160,256]{2,1,0:T(8,128)(2,1)S(1)}, u32[]{:S(2)}, u32[]{:S(2)}) collective-permute-start(bf16[2,160,256]{2,1,0:T(8,128)(2,1)S(1)} %slice.415), channel_id=1, source_target_pairs={{0,8},{1,9},{2,10},{3,11},{4,12},{5,13},{6,14},{7,15},{8,0},{9,1},... | collective-permute-start | bytes 491528 | tf_op jit(solution)/shard_map/ppermute | solution.py:80
  246.9 7.7 %collective-permute-start.64 = (bf16[352,256]{1,0:T(8,128)(2,1)S(1)}, bf16[352,256]{1,0:T(8,128)(2,1)S(1)}, u32[]{:S(2)}, u32[]{:S(2)}) collective-permute-start(bf16[352,256]{1,0:T(8,128)(2,1)S(1)} %fusion.20), channel_id=1, source_target_pairs={{0,8},{1,3},{2,10},{3,1},{4,12},{5,7},{6,14},{7,5},{8,0},{9,11},{1... | collective-permute-start | bytes 540680 | tf_op jit(solution)/shard_map/ppermute | solution.py:80
  254.8 8.0 %collective-permute-start.66 = (bf16[512,256]{1,0:T(8,128)(2,1)S(1)}, bf16[512,256]{1,0:T(8,128)(2,1)S(1)}, u32[]{:S(2)}, u32[]{:S(2)}) collective-permute-start(bf16[512,256]{1,0:T(8,128)(2,1)S(1)} %pad_maximum_fusion.25), channel_id=1, source_target_pairs={{0,64},{64,0},{1,65},{65,1},{2,66},{66,2},{3,67},{67,3},{4,68},{68... | collective-permute-start | bytes 786440 | tf_op jit(solution)/shard_map/ppermute | solution.py:67
  268.9 7.5 %collective-permute-start.69 = (bf16[2,352,256]{2,1,0:T(8,128)(2,1)S(1)}, bf16[2,352,256]{2,1,0:T(8,128)(2,1)S(1)}, u32[]{:S(2)}, u32[]{:S(2)}) collective-permute-start(bf16[2,352,256]{2,1,0:T(8,128)(2,1)S(1)} %pad_maximum_fusion.20), channel_id=1, source_target_pairs={{0,2},{1,7},{2,0},{3,5},{4,6},{5,3},{6,4},{7,1},{8,10},{9,15},{10,... | collective-permute-start | bytes 1081352 | tf_op jit(solution)/shard_map/ppermute | solution.py:80
  276.5 12.6 %collective-permute-start.73 = (bf16[4,352,256]{2,1,0:T(8,128)(2,1)S(1)}, bf16[4,352,256]{2,1,0:T(8,128)(2,1)S(1)}, u32[]{:S(2)}, u32[]{:S(2)}) collective-permute-start(bf16[4,352,256]{2,1,0:T(8,128)(2,1)S(1)} %pad_maximum_fusion.15.refs_0_), channel_id=1, source_target_pairs={{0,6},{1,9},{2,4},{3,11},{4,2},{5,13},{6,0},{7,15},{8,14},{9,1},{1... | collective-permute-start | bytes 2162696 | tf_op jit(solution)/shard_map/ppermute | solution.py:80
  279.5 7.2 %collective-permute-start.74 = (bf16[4,160,256]{2,1,0:T(8,128)(2,1)S(1)}, bf16[4,160,256]{2,1,0:T(8,128)(2,1)S(1)}, u32[]{:S(2)}, u32[]{:S(2)}) collective-permute-start(bf16[4,160,256]{2,1,0:T(8,128)(2,1)S(1)} %pad_maximum_fusion.23.refs_1_), channel_id=1, source_target_pairs={{0,2},{1,3},{2,0},{3,1},{4,6},{5,7},{6,4},{7,5},{8,10},{9,11},{10,... | collective-permute-start | bytes 983048 | tf_op jit(solution)/shard_map/ppermute | solution.py:80
  280.4 9.2 %collective-permute-start.71 = (bf16[4,352,256]{2,1,0:T(8,128)(2,1)S(1)}, bf16[4,352,256]{2,1,0:T(8,128)(2,1)S(1)}, u32[]{:S(2)}, u32[]{:S(2)}) collective-permute-start(bf16[4,352,256]{2,1,0:T(8,128)(2,1)S(1)} %pad_maximum_fusion.15.refs_0_), channel_id=1, source_target_pairs={{0,1},{1,0},{2,3},{3,2},{4,5},{5,4},{6,7},{7,6},{8,9},{9,8},{10,11... | collective-permute-start | bytes 2162696 | tf_op jit(solution)/shard_map/ppermute | solution.py:63
  280.5 9.2 %collective-permute-start.72 = (bf16[4,160,256]{2,1,0:T(8,128)(2,1)S(1)}, bf16[4,160,256]{2,1,0:T(8,128)(2,1)S(1)}, u32[]{:S(2)}, u32[]{:S(2)}) collective-permute-start(bf16[4,160,256]{2,1,0:T(8,128)(2,1)S(1)} %pad_maximum_fusion.23.refs_1_), channel_id=1, source_target_pairs={{0,1},{1,0},{2,3},{3,2},{4,5},{5,4},{6,7},{7,6},{8,9},{9,8},{10,11... | collective-permute-start | bytes 983048 | tf_op jit(solution)/shard_map/ppermute | solution.py:63
  329.4 13.4 %collective-permute-start.79 = (bf16[4,352,256]{2,1,0:T(8,128)(2,1)S(1)}, bf16[4,352,256]{2,1,0:T(8,128)(2,1)S(1)}, u32[]{:S(2)}, u32[]{:S(2)}) collective-permute-start(bf16[4,352,256]{2,1,0:T(8,128)(2,1)S(1)} %add_convert_fusion.3), channel_id=1, source_target_pairs={{0,6},{1,9},{2,4},{3,11},{4,2},{5,13},{6,0},{7,15},{8,14},{9,1},{1... | collective-permute-start | bytes 2162696 | tf_op jit(solution)/shard_map/ppermute | solution.py:80
  332.6 10.2 %collective-permute-start.80 = (bf16[4,160,256]{2,1,0:T(8,128)(2,1)S(1)}, bf16[4,160,256]{2,1,0:T(8,128)(2,1)S(1)}, u32[]{:S(2)}, u32[]{:S(2)}) collective-permute-start(bf16[4,160,256]{2,1,0:T(8,128)(2,1)S(1)} %add_convert_fusion.6), channel_id=1, source_target_pairs={{0,2},{1,3},{2,0},{3,1},{4,6},{5,7},{6,4},{7,5},{8,10},{9,11},{10,... | collective-permute-start | bytes 983048 | tf_op jit(solution)/shard_map/ppermute | solution.py:80
  343.1 8.1 %collective-permute-start.83 = (bf16[2,352,256]{2,1,0:T(8,128)(2,1)S(1)}, bf16[2,352,256]{2,1,0:T(8,128)(2,1)S(1)}, u32[]{:S(2)}, u32[]{:S(2)}) collective-permute-start(bf16[2,352,256]{2,1,0:T(8,128)(2,1)S(1)} %slice.411), channel_id=1, source_target_pairs={{0,2},{1,7},{2,0},{3,5},{4,6},{5,3},{6,4},{7,1},{8,10},{9,15},{10,... | collective-permute-start | bytes 1081352 | tf_op jit(solution)/shard_map/ppermute | solution.py:80
  343.8 7.4 %collective-permute-start.84 = (bf16[2,160,256]{2,1,0:T(8,128)(2,1)S(1)}, bf16[2,160,256]{2,1,0:T(8,128)(2,1)S(1)}, u32[]{:S(2)}, u32[]{:S(2)}) collective-permute-start(bf16[2,160,256]{2,1,0:T(8,128)(2,1)S(1)} %slice.414), channel_id=1, source_target_pairs={{0,8},{1,9},{2,10},{3,11},{4,12},{5,13},{6,14},{7,15},{8,0},{9,1},... | collective-permute-start | bytes 491528 | tf_op jit(solution)/shard_map/ppermute | solution.py:80
  351.3 8.4 %collective-permute-start.85 = (bf16[352,256]{1,0:T(8,128)(2,1)S(1)}, bf16[352,256]{1,0:T(8,128)(2,1)S(1)}, u32[]{:S(2)}, u32[]{:S(2)}) collective-permute-start(bf16[352,256]{1,0:T(8,128)(2,1)S(1)} %fusion.21), channel_id=1, source_target_pairs={{0,8},{1,3},{2,10},{3,1},{4,12},{5,7},{6,14},{7,5},{8,0},{9,11},{1... | collective-permute-start | bytes 540680 | tf_op jit(solution)/shard_map/ppermute | solution.py:80
  359.8 6.4 %collective-permute-start.87 = (bf16[352,256]{1,0:T(8,128)(2,1)S(1)}, bf16[352,256]{1,0:T(8,128)(2,1)S(1)}, u32[]{:S(2)}, u32[]{:S(2)}) collective-permute-start(bf16[352,256]{1,0:T(8,128)(2,1)S(1)} %fusion.16), channel_id=1, source_target_pairs={{0,8},{1,3},{2,10},{3,1},{4,12},{5,7},{6,14},{7,5},{8,0},{9,11},{1... | collective-permute-start | bytes 540680 | tf_op jit(solution)/shard_map/ppermute | solution.py:80
  366.3 7.5 %collective-permute-start.89 = (bf16[2,352,256]{2,1,0:T(8,128)(2,1)S(1)}, bf16[2,352,256]{2,1,0:T(8,128)(2,1)S(1)}, u32[]{:S(2)}, u32[]{:S(2)}) collective-permute-start(bf16[2,352,256]{2,1,0:T(8,128)(2,1)S(1)} %pad_maximum_fusion.21), channel_id=1, source_target_pairs={{0,2},{1,7},{2,0},{3,5},{4,6},{5,3},{6,4},{7,1},{8,10},{9,15},{10,... | collective-permute-start | bytes 1081352 | tf_op jit(solution)/shard_map/ppermute | solution.py:80
  373.9 12.6 %collective-permute-start.93 = (bf16[4,352,256]{2,1,0:T(8,128)(2,1)S(1)}, bf16[4,352,256]{2,1,0:T(8,128)(2,1)S(1)}, u32[]{:S(2)}, u32[]{:S(2)}) collective-permute-start(bf16[4,352,256]{2,1,0:T(8,128)(2,1)S(1)} %pad_maximum_fusion.16.refs_0_), channel_id=1, source_target_pairs={{0,6},{1,9},{2,4},{3,11},{4,2},{5,13},{6,0},{7,15},{8,14},{9,1},{1... | collective-permute-start | bytes 2162696 | tf_op jit(solution)/shard_map/ppermute | solution.py:80
  376.0 7.2 %collective-permute-start.94 = (bf16[4,160,256]{2,1,0:T(8,128)(2,1)S(1)}, bf16[4,160,256]{2,1,0:T(8,128)(2,1)S(1)}, u32[]{:S(2)}, u32[]{:S(2)}) collective-permute-start(bf16[4,160,256]{2,1,0:T(8,128)(2,1)S(1)} %pad_maximum_fusion.24.refs_1_), channel_id=1, source_target_pairs={{0,2},{1,3},{2,0},{3,1},{4,6},{5,7},{6,4},{7,5},{8,10},{9,11},{10,... | collective-permute-start | bytes 983048 | tf_op jit(solution)/shard_map/ppermute | solution.py:80
  377.2 11.9 %collective-permute-start.91 = (bf16[4,352,256]{2,1,0:T(8,128)(2,1)S(1)}, bf16[4,352,256]{2,1,0:T(8,128)(2,1)S(1)}, u32[]{:S(2)}, u32[]{:S(2)}) collective-permute-start(bf16[4,352,256]{2,1,0:T(8,128)(2,1)S(1)} %pad_maximum_fusion.16.refs_0_), channel_id=1, source_target_pairs={{0,1},{1,0},{2,3},{3,2},{4,5},{5,4},{6,7},{7,6},{8,9},{9,8},{10,11... | collective-permute-start | bytes 2162696 | tf_op jit(solution)/shard_map/ppermute | solution.py:63
  400.3 12.7 %collective-permute-start.99 = (bf16[4,352,256]{2,1,0:T(8,128)(2,1)S(1)}, bf16[4,352,256]{2,1,0:T(8,128)(2,1)S(1)}, u32[]{:S(2)}, u32[]{:S(2)}) collective-permute-start(bf16[4,352,256]{2,1,0:T(8,128)(2,1)S(1)} %add_convert_fusion.2), channel_id=1, source_target_pairs={{0,6},{1,9},{2,4},{3,11},{4,2},{5,13},{6,0},{7,15},{8,14},{9,1},{1... | collective-permute-start | bytes 2162696 | tf_op jit(solution)/shard_map/ppermute | solution.py:80
  402.5 10.4 %collective-permute-start.100 = (bf16[4,160,256]{2,1,0:T(8,128)(2,1)S(1)}, bf16[4,160,256]{2,1,0:T(8,128)(2,1)S(1)}, u32[]{:S(2)}, u32[]{:S(2)}) collective-permute-start(bf16[4,160,256]{2,1,0:T(8,128)(2,1)S(1)} %add_convert_fusion.5), channel_id=1, source_target_pairs={{0,2},{1,3},{2,0},{3,1},{4,6},{5,7},{6,4},{7,5},{8,10},{9,11},{10,... | collective-permute-start | bytes 983048 | tf_op jit(solution)/shard_map/ppermute | solution.py:80
  413.2 8.0 %collective-permute-start.103 = (bf16[2,352,256]{2,1,0:T(8,128)(2,1)S(1)}, bf16[2,352,256]{2,1,0:T(8,128)(2,1)S(1)}, u32[]{:S(2)}, u32[]{:S(2)}) collective-permute-start(bf16[2,352,256]{2,1,0:T(8,128)(2,1)S(1)} %slice.410), channel_id=1, source_target_pairs={{0,2},{1,7},{2,0},{3,5},{4,6},{5,3},{6,4},{7,1},{8,10},{9,15},{10,... | collective-permute-start | bytes 1081352 | tf_op jit(solution)/shard_map/ppermute | solution.py:80
  413.7 7.5 %collective-permute-start.104 = (bf16[2,160,256]{2,1,0:T(8,128)(2,1)S(1)}, bf16[2,160,256]{2,1,0:T(8,128)(2,1)S(1)}, u32[]{:S(2)}, u32[]{:S(2)}) collective-permute-start(bf16[2,160,256]{2,1,0:T(8,128)(2,1)S(1)} %slice.413), channel_id=1, source_target_pairs={{0,8},{1,9},{2,10},{3,11},{4,12},{5,13},{6,14},{7,15},{8,0},{9,1},... | collective-permute-start | bytes 491528 | tf_op jit(solution)/shard_map/ppermute | solution.py:80
  421.3 8.5 %collective-permute-start.105 = (bf16[352,256]{1,0:T(8,128)(2,1)S(1)}, bf16[352,256]{1,0:T(8,128)(2,1)S(1)}, u32[]{:S(2)}, u32[]{:S(2)}) collective-permute-start(bf16[352,256]{1,0:T(8,128)(2,1)S(1)} %fusion.22), channel_id=1, source_target_pairs={{0,8},{1,3},{2,10},{3,1},{4,12},{5,7},{6,14},{7,5},{8,0},{9,11},{1... | collective-permute-start | bytes 540680 | tf_op jit(solution)/shard_map/ppermute | solution.py:80
  429.9 6.6 %collective-permute-start.107 = (bf16[256,256]{1,0:T(8,128)(2,1)S(1)}, bf16[256,256]{1,0:T(8,128)(2,1)S(1)}, u32[]{:S(2)}, u32[]{:S(2)}) collective-permute-start(bf16[256,256]{1,0:T(8,128)(2,1)S(1)} %slice.288), channel_id=1, source_target_pairs={{0,64},{64,0},{1,65},{65,1},{2,66},{66,2},{3,67},{67,3},{4,68},{68... | collective-permute-start | bytes 393224 | tf_op jit(solution)/shard_map/ppermute | solution.py:67
  (59 other events, 575.7 us)

commit v10 on v9

--- a/solution.py
+++ b/solution.py
@@ -374,11 +374,11 @@
 
 
 def assemble(place_refs, refs, part, piece, w_ref):
-    for place_ref, (near, far) in zip(place_refs, (refs[:2], refs[2:])):
-        for block in range(CHIPS):
-            chip = place_ref[1 + part * CHIPS + block]
+    for place_ref, blocks in zip(place_refs, (refs[:CHIPS], refs[CHIPS:])):
+        for at, block in enumerate(blocks):
+            chip = place_ref[1 + part * CHIPS + at]
             start = pl.multiple_of((2 * chip + place_ref[0]) * 64, 64)
-            w_ref[pl.ds(start, 64), :] = (near if block < 4 else far)[block % 4, piece]
+            w_ref[pl.ds(start, 64), :] = block[piece]
 
 
 def scaled_rows(values, gain):
@@ -388,7 +388,7 @@
 
 
 def enc_mix_kernel(own_ref, other_ref, x_ref, gain_ref, *refs):
-    blocks, (out_ref, w_ref, mix_ref) = refs[:4], refs[4:]
+    blocks, (out_ref, w_ref, mix_ref) = refs[: 2 * CHIPS], refs[2 * CHIPS :]
     places_both = (own_ref, other_ref)
     for piece in range(8):
         assemble(places_both, blocks, 1, piece, w_ref.at[piece])
@@ -419,7 +419,7 @@
 
 
 def enc_feed_kernel(own_ref, other_ref, x_ref, gain_ref, *refs):
-    blocks, (out_ref, w_ref, acc_ref) = refs[:4], refs[4:]
+    blocks, (out_ref, w_ref, acc_ref) = refs[: 2 * CHIPS], refs[2 * CHIPS :]
     places_both = (own_ref, other_ref)
     for piece in range(8):
         assemble(places_both, blocks, 0, piece, w_ref.at[piece])
@@ -451,14 +451,14 @@
     gain = whole((1, ENC_D))
 
     def call(kernel, steps, pieces, scratch, x, gains, rows):
-        block = (4, rows[0].shape[1] // steps, 64, PIECE)
+        block = (rows[0].shape[0] // steps, 64, PIECE)
         return pl.pallas_call(
             kernel,
             grid_spec=pltpu.PrefetchScalarGridSpec(
                 num_scalar_prefetch=2,
                 grid=(steps,),
                 in_specs=[full, gain]
-                + [pl.BlockSpec(block, lambda s, *_: (0, s, 0, 0)) for _ in rows],
+                + [pl.BlockSpec(block, lambda s, *_: (s, 0, 0)) for _ in rows],
                 out_specs=full,
                 scratch_shapes=[pltpu.VMEM((pieces, ENC_D, PIECE), bf16), scratch],
             ),
@@ -485,23 +485,25 @@
         found = jnp.where(inside[:, None], found, jnp.zeros((), bf16))
         return found.reshape(CHIPS, NB_LEN, ENC_D)
 
-    other = rows(places_both[1], wanted)
-    *got, other, wanted = together(*first_round(local), other, wanted)
-    near = [jnp.stack(pair) for pair in zip(local, got)]
-    sent = [neighbour(value, part, 1) for part, value in enumerate(near)]
-    total = rows(places_both[0], wanted) + core_swap(other)
+    sent = [[neighbour(value, part, turn) for part, value in enumerate(local)] for turn in range(3)]
+    sent[1][0], sent[1][1], *first, wanted = together(*sent[1], *sent[0], wanted)
+    passed = [
+        [neighbour(value, part, turn) for part, value in enumerate(first)] for turn in (1, 2)
+    ]
+    other = core_swap(rows(places_both[1], wanted))
+    total = rows(places_both[0], wanted) + other
     summed = neighbour(total[4:], 0, 2)
-    *got, summed = together(*sent, summed)
-    near = [jnp.concatenate(pair) for pair in zip(near, got)]
-    swaps = [core_swap(value) for value in near]
-    far = together(*[neighbour(value, part, 2) for part, value in enumerate(near)])
-    far_swaps = [core_swap(value) for value in far]
+    blocks = []
+    for part in range(2):
+        second, third = sent[1][part], passed[0][part]
+        blocks.append(
+            [local[part], first[part], second, third, sent[2][part], passed[1][part]]
+            + [neighbour(second, part, 2), neighbour(third, part, 2)]
+        )
     total = total[:4] + summed
     total = total[:2] + neighbour(total[2:], 0, 1)
     embedded = total[0] + neighbour(total[1], 0, 0)
-    feed, mix = [
-        [near[part], far[part], swaps[part], far_swaps[part]] for part in range(2)
-    ]
+    feed, mix = [part + [core_swap(value) for value in part] for part in blocks]
     return encode(places_both, embedded, enc_norms, feed, mix)
 
 

time: 446 us -> 467 us (1.047)
  starting transfers between devices: 120 us -> 135 us
  waiting for transfers between devices: 191 us -> 198 us
    ppermute x3, starting transfers between devices: 30.8 us -> 52.6 us  [section_swap(): return lax.ppermute(value, 'section', [(0, 1), (1, 0)])]
    ppermute x54, starting transfers between devices: 78.3 us -> 68.5 us  [neighbour(): return lax.ppermute(value, MP, route)]
    ppermute x54, waiting for transfers between devices: 161 us -> 167 us  [neighbour(): return lax.ppermute(value, MP, route)]
where the time goes in v10:
time: 467 us; the launch traced here: 459 us
  waiting for transfers between devices  198 us (42%)
  starting transfers between devices  135 us (29%)
  Pallas kernels  53.3 us (11%)
  blocking collectives  52.5 us (11%)
  loops' own time  9.56 us (2%)
  other arithmetic  5.63 us (1%)
    ppermute x54, waiting for transfers between devices, neighbour(): return lax.ppermute(value, MP, route)  167 us
    ppermute x54, starting transfers between devices, neighbour(): return lax.ppermute(value, MP, route)  68.5 us
    ppermute x3, starting transfers between devices, section_swap(): return lax.ppermute(value, 'section', [(0, 1), (1, 0)])  52.6 us
    all_to_all x2, blocking collectives, attention(): triple = lax.all_to_all(triple, 'seq', 0, 0, tiled=True)  34.4 us
    pallas_call x8, Pallas kernels, project_half(): pl.pallas_call(functools.partial(project_kernel, last, units), grid_spec=...  25.2 us
    all_to_all x2, blocking collectives, attention(): return lax.all_to_all(causal(triple), 'seq', 0, 0, tiled=True)  18.1 us
    pallas_call x16, Pallas kernels, terms(): pl.pallas_call(terms_kernel, grid_spec=pltpu.PrefetchScalarGridSpec(num_s...  16.1 us
    ppermute x3, waiting for transfers between devices, section_swap(): return lax.ppermute(value, 'section', [(0, 1), (1, 0)])  14.6 us
  transfers between devices with their start and end apart: 94, of which 49 were waited for; matrix products, arithmetic and copies ran while one was open for 1% of the time, Pallas kernels for 6%

profile of v10, /device:TPU:0, one launch (start us, length us, event | category | flops | bytes accessed | tf_op | source)
XLA Modules:
  0.0 458.7 jit_solution(6918184617614871885)
XLA Ops:
  1.8 142.6 %conditional.1 = (bf16[512,256]{1,0:T(8,128)(2,1)S(1)}, bf16[512,256]{1,0:T(8,128)(2,1)S(1)}, bf16[128,1024]{1,0:T(8,128)(2,1)S(1)}) conditional(s32[]{:T(128)} %convert_element_type.283, (bf16[64,4096]{1,0:T(8,128)(2,1)}, bf16[256,1024]{1,0:T(8,128)(2,1)}, bf16[64,3,1024]{2,0,1:T(8,128)(2,1)}, bf16[64,1024]{1,0:T(8,128)(2,1)}, s32[64,128]{1,0:T(8,128)}, ...), branch_computations={%region_0.1_spmd, %region_1.2_spmd} | conditional | flops 5377753088 | bytes 167038432 | solution.py:603
  14.5 3.1 collective-permute-start.1
  21.4 5.7 %collective-permute-done.3 = bf16[2,160,256]{2,1,0:T(8,128)(2,1)S(1)} collective-permute-done((bf16[2,160,256]{2,1,0:T(8,128)(2,1)S(1)}, bf16[2,160,256]{2,1,0:T(8,128)(2,1)S(1)}, u32[]{:S(2)}, u32[]{:S(2)}) %collective-permute-start.3) | collective-permute-done | bytes 163872 | tf_op jit(solution)/shard_map/cond/branch_1_fun/ppermute | solution.py:80
  27.9 3.1 collective-permute-start.6
  31.7 6.7 %collective-permute-done.7.refs_3_ = bf16[4,160,256]{2,1,0:T(8,128)(2,1)S(1)} collective-permute-done((bf16[4,160,256]{2,1,0:T(8,128)(2,1)S(1)}, bf16[4,160,256]{2,1,0:T(8,128)(2,1)S(1)}, u32[]{:S(2)}, u32[]{:S(2)}) %collective-permute-start.7) | collective-permute-done | bytes 327712 | tf_op jit(solution)/shard_map/cond/branch_1_fun/ppermute | solution.py:80
  41.0 5.3 %branch_1_fun.9 = (f32[3,512,256]{2,1,0:T(8,128)S(1)}, f32[512,128]{1,0:T(8,128)S(1)}) custom-call(s32[17]{0:T(128)S(1)} %get-tuple-element.66.place_ref, bf16[4,352,256]{2,1,0:T(8,128)(2,1)S(1)} %pad_maximum_fusion.refs_0_, bf16[4,160,256]{2,1,0:T(8,128)(2,1)S(1)} %pad_maximum_fusion.4.refs_1_, bf16[4,352,256]{2,1,0:T(8,128)(2,1)S(1)} %collective-permute-done.6.refs_2_, ...), custom_call_target="tpu_custom_call" | custom-call | flops 1610612736 | bytes 6815744 | tf_op jit(solution)/shard_map/cond/branch_1_fun/pallas_call | solution.py:211
  46.4 3.8 branch_1_fun.10
  50.2 16.7 %all_to_all.18.triple_ref = bf16[4,3,256,128]{3,2,1,0:T(8,128)(2,1)S(1)} all-to-all(bf16[4,3,256,128]{3,2,1,0:T(8,128)(2,1)S(1)} %branch_1_fun.10), channel_id=1, replica_groups=mesh['section'=2,'seq'=4,'z'=2,'y'=4,'core'=2] {'seq'}, dimensions={0} | all-to-all | bytes 1572864 | tf_op jit(solution)/shard_map/cond/branch_1_fun/all_to_all | solution.py:544
  68.2 9.1 %all_to_all.19.mixed_ref = bf16[4,256,128]{2,1,0:T(8,128)(2,1)S(1)} all-to-all(bf16[4,256,128]{2,1,0:T(8,128)(2,1)S(1)} %branch_1_fun.11), channel_id=1, replica_groups=mesh['section'=2,'seq'=4,'z'=2,'y'=4,'core'=2] {'seq'}, dimensions={0} | all-to-all | bytes 524288 | tf_op jit(solution)/shard_map/cond/branch_1_fun/all_to_all | solution.py:545
  81.3 3.1 collective-permute-start.12
  86.1 8.7 %collective-permute-done.13 = bf16[4,160,256]{2,1,0:T(8,128)(2,1)S(1)} collective-permute-done((bf16[4,160,256]{2,1,0:T(8,128)(2,1)S(1)}, bf16[4,160,256]{2,1,0:T(8,128)(2,1)S(1)}, u32[]{:S(2)}, u32[]{:S(2)}) %collective-permute-start.13) | collective-permute-done | bytes 327712 | tf_op jit(solution)/shard_map/cond/branch_1_fun/ppermute | solution.py:80
  96.0 5.9 %collective-permute-done.17 = bf16[2,160,256]{2,1,0:T(8,128)(2,1)S(1)} collective-permute-done((bf16[2,160,256]{2,1,0:T(8,128)(2,1)S(1)}, bf16[2,160,256]{2,1,0:T(8,128)(2,1)S(1)}, u32[]{:S(2)}, u32[]{:S(2)}) %collective-permute-start.17) | collective-permute-done | bytes 163872 | tf_op jit(solution)/shard_map/cond/branch_1_fun/ppermute | solution.py:80
  105.3 3.4 collective-permute-done.19
  113.0 3.4 collective-permute-done.21
  117.0 5.0 %collective-permute-done.23 = bf16[2,160,256]{2,1,0:T(8,128)(2,1)S(1)} collective-permute-done((bf16[2,160,256]{2,1,0:T(8,128)(2,1)S(1)}, bf16[2,160,256]{2,1,0:T(8,128)(2,1)S(1)}, u32[]{:S(2)}, u32[]{:S(2)}) %collective-permute-start.23) | collective-permute-done | bytes 163872 | tf_op jit(solution)/shard_map/cond/branch_1_fun/ppermute | solution.py:80
  124.2 3.5 collective-permute-start.26
  127.9 7.0 %collective-permute-done.27.refs_3_ = bf16[4,160,256]{2,1,0:T(8,128)(2,1)S(1)} collective-permute-done((bf16[4,160,256]{2,1,0:T(8,128)(2,1)S(1)}, bf16[4,160,256]{2,1,0:T(8,128)(2,1)S(1)}, u32[]{:S(2)}, u32[]{:S(2)}) %collective-permute-start.27) | collective-permute-done | bytes 327712 | tf_op jit(solution)/shard_map/cond/branch_1_fun/ppermute | solution.py:80
  144.4 46.2 %collective-permute-start.64 = (bf16[128,1024]{1,0:T(8,128)(2,1)S(1)}, bf16[128,1024]{1,0:T(8,128)(2,1)S(1)}, u32[]{:S(2)}, u32[]{:S(2)}) collective-permute-start(bf16[128,1024]{1,0:T(8,128)(2,1)S(1)} %get-tuple-element.197), channel_id=1, source_target_pairs={{0,64},{64,0},{1,65},{65,1},{2,66},{66,2},{3,67},{67,3},{4,68},{68... | collective-permute-start | bytes 786440 | tf_op jit(solution)/shard_map/ppermute | solution.py:67
  190.6 6.5 %collective-permute-done.64 = bf16[128,1024]{1,0:T(8,128)(2,1)S(1)} collective-permute-done((bf16[128,1024]{1,0:T(8,128)(2,1)S(1)}, bf16[128,1024]{1,0:T(8,128)(2,1)S(1)}, u32[]{:S(2)}, u32[]{:S(2)}) %collective-permute-start.64) | collective-permute-done | bytes 262176 | tf_op jit(solution)/shard_map/ppermute | solution.py:67
  198.9 4.3 collective-permute-done.66
  205.4 4.4 collective-permute-done.68
  213.3 6.7 %collective-permute-done.70.refs_3_ = bf16[4,48,1024]{2,1,0:T(8,128)(2,1)S(1)} collective-permute-done((bf16[4,48,1024]{2,1,0:T(8,128)(2,1)S(1)}, bf16[4,48,1024]{2,1,0:T(8,128)(2,1)S(1)}, u32[]{:S(2)}, u32[]{:S(2)}) %collective-permute-start.70) | collective-permute-done | bytes 393248 | tf_op jit(solution)/shard_map/ppermute | solution.py:80
  227.0 3.4 collective-permute-start.75
  230.4 11.4 %collective-permute-done.75.prev_ref = bf16[2,2,128,512]{3,2,1,0:T(8,128)(2,1)S(1)} collective-permute-done((bf16[2,2,128,512]{3,2,1,0:T(8,128)(2,1)S(1)}, bf16[2,2,128,512]{3,2,1,0:T(8,128)(2,1)S(1)}, u32[]{:S(2)}, u32[]{:S(2)}) %collective-permute-start.75) | collective-permute-done | bytes 524320 | tf_op jit(solution)/shard_map/ppermute | solution.py:612
  253.1 7.4 %collective-permute-done.79 = bf16[4,160,256]{2,1,0:T(8,128)(2,1)S(1)} collective-permute-done((bf16[4,160,256]{2,1,0:T(8,128)(2,1)S(1)}, bf16[4,160,256]{2,1,0:T(8,128)(2,1)S(1)}, u32[]{:S(2)}, u32[]{:S(2)}) %collective-permute-start.79) | collective-permute-done | bytes 327712 | tf_op jit(solution)/shard_map/ppermute | solution.py:80
  263.7 4.8 %collective-permute-done.83 = bf16[2,160,256]{2,1,0:T(8,128)(2,1)S(1)} collective-permute-done((bf16[2,160,256]{2,1,0:T(8,128)(2,1)S(1)}, bf16[2,160,256]{2,1,0:T(8,128)(2,1)S(1)}, u32[]{:S(2)}, u32[]{:S(2)}) %collective-permute-start.83) | collective-permute-done | bytes 163872 | tf_op jit(solution)/shard_map/ppermute | solution.py:80
  273.0 4.1 collective-permute-done.85
  277.2 3.3 collective-permute-start.86
  280.5 4.6 %collective-permute-done.86 = bf16[512,256]{1,0:T(8,128)(2,1)S(1)} collective-permute-done((bf16[512,256]{1,0:T(8,128)(2,1)S(1)}, bf16[512,256]{1,0:T(8,128)(2,1)S(1)}, u32[]{:S(2)}, u32[]{:S(2)}) %collective-permute-start.86) | collective-permute-done | bytes 262176 | tf_op jit(solution)/shard_map/ppermute | solution.py:67
  287.0 4.9 %collective-permute-done.88 = bf16[160,256]{1,0:T(8,128)(2,1)S(1)} collective-permute-done((bf16[160,256]{1,0:T(8,128)(2,1)S(1)}, bf16[160,256]{1,0:T(8,128)(2,1)S(1)}, u32[]{:S(2)}, u32[]{:S(2)}) %collective-permute-start.88) | collective-permute-done | bytes 81952 | tf_op jit(solution)/shard_map/ppermute | solution.py:80
  293.7 3.7 collective-permute-done.90
  303.0 5.4 %collective-permute-done.94.refs_3_ = bf16[4,160,256]{2,1,0:T(8,128)(2,1)S(1)} collective-permute-done((bf16[4,160,256]{2,1,0:T(8,128)(2,1)S(1)}, bf16[4,160,256]{2,1,0:T(8,128)(2,1)S(1)}, u32[]{:S(2)}, u32[]{:S(2)}) %collective-permute-start.94) | collective-permute-done | bytes 327712 | tf_op jit(solution)/shard_map/ppermute | solution.py:80
  308.4 3.7 collective-permute-done.93.refs_2_
  312.7 3.7 shard_map.169
  316.5 3.8 shard_map.170
  320.3 17.7 %all_to_all.20.triple_ref = bf16[4,3,256,128]{3,2,1,0:T(8,128)(2,1)S(1)} all-to-all(bf16[4,3,256,128]{3,2,1,0:T(8,128)(2,1)S(1)} %shard_map.170), channel_id=1, replica_groups=mesh['section'=2,'seq'=4,'z'=2,'y'=4,'core'=2] {'seq'}, dimensions={0} | all-to-all | bytes 1572864 | tf_op jit(solution)/shard_map/all_to_all | solution.py:544
  339.4 9.1 %all_to_all.21.mixed_ref = bf16[4,256,128]{2,1,0:T(8,128)(2,1)S(1)} all-to-all(bf16[4,256,128]{2,1,0:T(8,128)(2,1)S(1)} %shard_map.171), channel_id=1, replica_groups=mesh['section'=2,'seq'=4,'z'=2,'y'=4,'core'=2] {'seq'}, dimensions={0} | all-to-all | bytes 524288 | tf_op jit(solution)/shard_map/all_to_all | solution.py:545
  357.2 8.6 %collective-permute-done.100 = bf16[4,160,256]{2,1,0:T(8,128)(2,1)S(1)} collective-permute-done((bf16[4,160,256]{2,1,0:T(8,128)(2,1)S(1)}, bf16[4,160,256]{2,1,0:T(8,128)(2,1)S(1)}, u32[]{:S(2)}, u32[]{:S(2)}) %collective-permute-start.100) | collective-permute-done | bytes 327712 | tf_op jit(solution)/shard_map/ppermute | solution.py:80
  368.7 5.0 %collective-permute-done.104 = bf16[2,160,256]{2,1,0:T(8,128)(2,1)S(1)} collective-permute-done((bf16[2,160,256]{2,1,0:T(8,128)(2,1)S(1)}, bf16[2,160,256]{2,1,0:T(8,128)(2,1)S(1)}, u32[]{:S(2)}, u32[]{:S(2)}) %collective-permute-start.104) | collective-permute-done | bytes 163872 | tf_op jit(solution)/shard_map/ppermute | solution.py:80
  377.5 4.4 collective-permute-done.106
  383.4 4.4 collective-permute-done.108
  390.1 3.3 collective-permute-done.110
  398.1 6.1 %collective-permute-done.114.refs_3_ = bf16[4,160,256]{2,1,0:T(8,128)(2,1)S(1)} collective-permute-done((bf16[4,160,256]{2,1,0:T(8,128)(2,1)S(1)}, bf16[4,160,256]{2,1,0:T(8,128)(2,1)S(1)}, u32[]{:S(2)}, u32[]{:S(2)}) %collective-permute-start.114) | collective-permute-done | bytes 327712 | tf_op jit(solution)/shard_map/ppermute | solution.py:80
  404.3 3.8 collective-permute-done.113.refs_2_
  426.0 8.5 %collective-permute-done.120 = bf16[4,160,256]{2,1,0:T(8,128)(2,1)S(1)} collective-permute-done((bf16[4,160,256]{2,1,0:T(8,128)(2,1)S(1)}, bf16[4,160,256]{2,1,0:T(8,128)(2,1)S(1)}, u32[]{:S(2)}, u32[]{:S(2)}) %collective-permute-start.120) | collective-permute-done | bytes 327712 | tf_op jit(solution)/shard_map/ppermute | solution.py:80
  437.8 4.8 %collective-permute-done.124 = bf16[2,160,256]{2,1,0:T(8,128)(2,1)S(1)} collective-permute-done((bf16[2,160,256]{2,1,0:T(8,128)(2,1)S(1)}, bf16[2,160,256]{2,1,0:T(8,128)(2,1)S(1)}, u32[]{:S(2)}, u32[]{:S(2)}) %collective-permute-start.124) | collective-permute-done | bytes 163872 | tf_op jit(solution)/shard_map/ppermute | solution.py:80
  446.4 4.6 collective-permute-done.126
  454.1 3.5 collective-permute-done.127
  (295 shorter events, 138.4 us)
Async XLA Ops:
  11.5 8.7 %collective-permute-start = (bf16[352,256]{1,0:T(8,128)(2,1)S(1)}, bf16[352,256]{1,0:T(8,128)(2,1)S(1)}, u32[]{:S(2)}, u32[]{:S(2)}) collective-permute-start(bf16[352,256]{1,0:T(8,128)(2,1)S(1)} %get-tuple-element.328), channel_id=1, source_target_pairs={{0,8},{1,3},{2,10},{3,1},{4,12},{5,7},{6,14},{7,5},{8,0},{9,11},{1... | collective-permute-start | bytes 540680 | tf_op jit(solution)/shard_map/cond/branch_1_fun/ppermute | solution.py:80
  20.3 7.5 %collective-permute-start.2 = (bf16[2,352,256]{2,1,0:T(8,128)(2,1)S(1)}, bf16[2,352,256]{2,1,0:T(8,128)(2,1)S(1)}, u32[]{:S(2)}, u32[]{:S(2)}) collective-permute-start(bf16[2,352,256]{2,1,0:T(8,128)(2,1)S(1)} %pad_maximum_fusion.2), channel_id=1, source_target_pairs={{0,2},{1,7},{2,0},{3,5},{4,6},{5,3},{6,4},{7,1},{8,10},{9,15},{10,... | collective-permute-start | bytes 1081352 | tf_op jit(solution)/shard_map/cond/branch_1_fun/ppermute | solution.py:80
  27.9 12.6 %collective-permute-start.6 = (bf16[4,352,256]{2,1,0:T(8,128)(2,1)S(1)}, bf16[4,352,256]{2,1,0:T(8,128)(2,1)S(1)}, u32[]{:S(2)}, u32[]{:S(2)}) collective-permute-start(bf16[4,352,256]{2,1,0:T(8,128)(2,1)S(1)} %pad_maximum_fusion.refs_0_), channel_id=1, source_target_pairs={{0,6},{1,9},{2,4},{3,11},{4,2},{5,13},{6,0},{7,15},{8,14},{9,1},{1... | collective-permute-start | bytes 2162696 | tf_op jit(solution)/shard_map/cond/branch_1_fun/ppermute | solution.py:80
  31.0 7.3 %collective-permute-start.7 = (bf16[4,160,256]{2,1,0:T(8,128)(2,1)S(1)}, bf16[4,160,256]{2,1,0:T(8,128)(2,1)S(1)}, u32[]{:S(2)}, u32[]{:S(2)}) collective-permute-start(bf16[4,160,256]{2,1,0:T(8,128)(2,1)S(1)} %pad_maximum_fusion.4.refs_1_), channel_id=1, source_target_pairs={{0,2},{1,3},{2,0},{3,1},{4,6},{5,7},{6,4},{7,5},{8,10},{9,11},{10,... | collective-permute-start | bytes 983048 | tf_op jit(solution)/shard_map/cond/branch_1_fun/ppermute | solution.py:80
  31.1 9.9 %collective-permute-start.5 = (bf16[4,160,256]{2,1,0:T(8,128)(2,1)S(1)}, bf16[4,160,256]{2,1,0:T(8,128)(2,1)S(1)}, u32[]{:S(2)}, u32[]{:S(2)}) collective-permute-start(bf16[4,160,256]{2,1,0:T(8,128)(2,1)S(1)} %pad_maximum_fusion.4.refs_1_), channel_id=1, source_target_pairs={{0,1},{1,0},{2,3},{3,2},{4,5},{5,4},{6,7},{7,6},{8,9},{9,8},{10,11... | collective-permute-start | bytes 983048 | tf_op jit(solution)/shard_map/cond/branch_1_fun/ppermute | solution.py:63
  31.2 9.8 %collective-permute-start.4 = (bf16[4,352,256]{2,1,0:T(8,128)(2,1)S(1)}, bf16[4,352,256]{2,1,0:T(8,128)(2,1)S(1)}, u32[]{:S(2)}, u32[]{:S(2)}) collective-permute-start(bf16[4,352,256]{2,1,0:T(8,128)(2,1)S(1)} %pad_maximum_fusion.refs_0_), channel_id=1, source_target_pairs={{0,1},{1,0},{2,3},{3,2},{4,5},{5,4},{6,7},{7,6},{8,9},{9,8},{10,11... | collective-permute-start | bytes 2162696 | tf_op jit(solution)/shard_map/cond/branch_1_fun/ppermute | solution.py:63
  81.3 13.4 %collective-permute-start.12 = (bf16[4,352,256]{2,1,0:T(8,128)(2,1)S(1)}, bf16[4,352,256]{2,1,0:T(8,128)(2,1)S(1)}, u32[]{:S(2)}, u32[]{:S(2)}) collective-permute-start(bf16[4,352,256]{2,1,0:T(8,128)(2,1)S(1)} %add_convert_fusion), channel_id=1, source_target_pairs={{0,6},{1,9},{2,4},{3,11},{4,2},{5,13},{6,0},{7,15},{8,14},{9,1},{1... | collective-permute-start | bytes 2162696 | tf_op jit(solution)/shard_map/cond/branch_1_fun/ppermute | solution.py:80
  84.5 10.2 %collective-permute-start.13 = (bf16[4,160,256]{2,1,0:T(8,128)(2,1)S(1)}, bf16[4,160,256]{2,1,0:T(8,128)(2,1)S(1)}, u32[]{:S(2)}, u32[]{:S(2)}) collective-permute-start(bf16[4,160,256]{2,1,0:T(8,128)(2,1)S(1)} %add_convert_fusion.1), channel_id=1, source_target_pairs={{0,2},{1,3},{2,0},{3,1},{4,6},{5,7},{6,4},{7,5},{8,10},{9,11},{10,... | collective-permute-start | bytes 983048 | tf_op jit(solution)/shard_map/cond/branch_1_fun/ppermute | solution.py:80
  95.0 7.5 %collective-permute-start.16 = (bf16[2,352,256]{2,1,0:T(8,128)(2,1)S(1)}, bf16[2,352,256]{2,1,0:T(8,128)(2,1)S(1)}, u32[]{:S(2)}, u32[]{:S(2)}) collective-permute-start(bf16[2,352,256]{2,1,0:T(8,128)(2,1)S(1)} %slice.408), channel_id=1, source_target_pairs={{0,2},{1,7},{2,0},{3,5},{4,6},{5,3},{6,4},{7,1},{8,10},{9,15},{10,... | collective-permute-start | bytes 1081352 | tf_op jit(solution)/shard_map/cond/branch_1_fun/ppermute | solution.py:80
  108.8 7.7 %collective-permute-start.20 = (bf16[352,256]{1,0:T(8,128)(2,1)S(1)}, bf16[352,256]{1,0:T(8,128)(2,1)S(1)}, u32[]{:S(2)}, u32[]{:S(2)}) collective-permute-start(bf16[352,256]{1,0:T(8,128)(2,1)S(1)} %fusion.2), channel_id=1, source_target_pairs={{0,8},{1,3},{2,10},{3,1},{4,12},{5,7},{6,14},{7,5},{8,0},{9,11},{1... | collective-permute-start | bytes 540680 | tf_op jit(solution)/shard_map/cond/branch_1_fun/ppermute | solution.py:80
  116.5 7.6 %collective-permute-start.22 = (bf16[2,352,256]{2,1,0:T(8,128)(2,1)S(1)}, bf16[2,352,256]{2,1,0:T(8,128)(2,1)S(1)}, u32[]{:S(2)}, u32[]{:S(2)}) collective-permute-start(bf16[2,352,256]{2,1,0:T(8,128)(2,1)S(1)} %pad_maximum_fusion.3), channel_id=1, source_target_pairs={{0,2},{1,7},{2,0},{3,5},{4,6},{5,3},{6,4},{7,1},{8,10},{9,15},{10,... | collective-permute-start | bytes 1081352 | tf_op jit(solution)/shard_map/cond/branch_1_fun/ppermute | solution.py:80
  124.2 12.8 %collective-permute-start.26 = (bf16[4,352,256]{2,1,0:T(8,128)(2,1)S(1)}, bf16[4,352,256]{2,1,0:T(8,128)(2,1)S(1)}, u32[]{:S(2)}, u32[]{:S(2)}) collective-permute-start(bf16[4,352,256]{2,1,0:T(8,128)(2,1)S(1)} %pad_maximum_fusion.1.refs_0_), channel_id=1, source_target_pairs={{0,6},{1,9},{2,4},{3,11},{4,2},{5,13},{6,0},{7,15},{8,14},{9,1},{1... | collective-permute-start | bytes 2162696 | tf_op jit(solution)/shard_map/cond/branch_1_fun/ppermute | solution.py:80
  127.7 7.2 %collective-permute-start.27 = (bf16[4,160,256]{2,1,0:T(8,128)(2,1)S(1)}, bf16[4,160,256]{2,1,0:T(8,128)(2,1)S(1)}, u32[]{:S(2)}, u32[]{:S(2)}) collective-permute-start(bf16[4,160,256]{2,1,0:T(8,128)(2,1)S(1)} %pad_maximum_fusion.5.refs_1_), channel_id=1, source_target_pairs={{0,2},{1,3},{2,0},{3,1},{4,6},{5,7},{6,4},{7,5},{8,10},{9,11},{10,... | collective-permute-start | bytes 983048 | tf_op jit(solution)/shard_map/cond/branch_1_fun/ppermute | solution.py:80
  127.8 11.8 %collective-permute-start.24 = (bf16[4,352,256]{2,1,0:T(8,128)(2,1)S(1)}, bf16[4,352,256]{2,1,0:T(8,128)(2,1)S(1)}, u32[]{:S(2)}, u32[]{:S(2)}) collective-permute-start(bf16[4,352,256]{2,1,0:T(8,128)(2,1)S(1)} %pad_maximum_fusion.1.refs_0_), channel_id=1, source_target_pairs={{0,1},{1,0},{2,3},{3,2},{4,5},{5,4},{6,7},{7,6},{8,9},{9,8},{10,11... | collective-permute-start | bytes 2162696 | tf_op jit(solution)/shard_map/cond/branch_1_fun/ppermute | solution.py:63
  144.4 52.6 %collective-permute-start.64 = (bf16[128,1024]{1,0:T(8,128)(2,1)S(1)}, bf16[128,1024]{1,0:T(8,128)(2,1)S(1)}, u32[]{:S(2)}, u32[]{:S(2)}) collective-permute-start(bf16[128,1024]{1,0:T(8,128)(2,1)S(1)} %get-tuple-element.197), channel_id=1, source_target_pairs={{0,64},{64,0},{1,65},{65,1},{2,66},{66,2},{3,67},{67,3},{4,68},{68... | collective-permute-start | bytes 786440 | tf_op jit(solution)/shard_map/ppermute | solution.py:67
  203.2 7.2 %collective-permute-start.67 = (bf16[2,80,1024]{2,1,0:T(8,128)(2,1)S(1)}, bf16[2,80,1024]{2,1,0:T(8,128)(2,1)S(1)}, u32[]{:S(2)}, u32[]{:S(2)}) collective-permute-start(bf16[2,80,1024]{2,1,0:T(8,128)(2,1)S(1)} %pad_maximum_fusion.18), channel_id=1, source_target_pairs={{0,2},{1,7},{2,0},{3,5},{4,6},{5,3},{6,4},{7,1},{8,10},{9,15},{10,... | collective-permute-start | bytes 983048 | tf_op jit(solution)/shard_map/ppermute | solution.py:80
  210.4 11.9 %collective-permute-start.69 = (bf16[4,80,1024]{2,1,0:T(8,128)(2,1)S(1)}, bf16[4,80,1024]{2,1,0:T(8,128)(2,1)S(1)}, u32[]{:S(2)}, u32[]{:S(2)}) collective-permute-start(bf16[4,80,1024]{2,1,0:T(8,128)(2,1)S(1)} %pad_maximum_fusion.13.refs_0_), channel_id=1, source_target_pairs={{0,6},{1,9},{2,4},{3,11},{4,2},{5,13},{6,0},{7,15},{8,14},{9,1},{1... | collective-permute-start | bytes 1966088 | tf_op jit(solution)/shard_map/ppermute | solution.py:80
  212.1 8.0 %collective-permute-start.70 = (bf16[4,48,1024]{2,1,0:T(8,128)(2,1)S(1)}, bf16[4,48,1024]{2,1,0:T(8,128)(2,1)S(1)}, u32[]{:S(2)}, u32[]{:S(2)}) collective-permute-start(bf16[4,48,1024]{2,1,0:T(8,128)(2,1)S(1)} %pad_maximum_fusion.15.refs_1_), channel_id=1, source_target_pairs={{0,2},{1,3},{2,0},{3,1},{4,6},{5,7},{6,4},{7,5},{8,10},{9,11},{10,... | collective-permute-start | bytes 1179656 | tf_op jit(solution)/shard_map/ppermute | solution.py:80
  212.8 10.2 %collective-permute-start.71 = (bf16[4,80,1024]{2,1,0:T(8,128)(2,1)S(1)}, bf16[4,80,1024]{2,1,0:T(8,128)(2,1)S(1)}, u32[]{:S(2)}, u32[]{:S(2)}) collective-permute-start(bf16[4,80,1024]{2,1,0:T(8,128)(2,1)S(1)} %pad_maximum_fusion.13.refs_0_), channel_id=1, source_target_pairs={{0,1},{1,0},{2,3},{3,2},{4,5},{5,4},{6,7},{7,6},{8,9},{9,8},{10,11... | collective-permute-start | bytes 1966088 | tf_op jit(solution)/shard_map/ppermute | solution.py:63
  212.8 10.2 %collective-permute-start.72 = (bf16[4,48,1024]{2,1,0:T(8,128)(2,1)S(1)}, bf16[4,48,1024]{2,1,0:T(8,128)(2,1)S(1)}, u32[]{:S(2)}, u32[]{:S(2)}) collective-permute-start(bf16[4,48,1024]{2,1,0:T(8,128)(2,1)S(1)} %pad_maximum_fusion.15.refs_1_), channel_id=1, source_target_pairs={{0,1},{1,0},{2,3},{3,2},{4,5},{5,4},{6,7},{7,6},{8,9},{9,8},{10,11... | collective-permute-start | bytes 1179656 | tf_op jit(solution)/shard_map/ppermute | solution.py:63
  227.0 14.8 %collective-permute-start.75 = (bf16[2,2,128,512]{3,2,1,0:T(8,128)(2,1)S(1)}, bf16[2,2,128,512]{3,2,1,0:T(8,128)(2,1)S(1)}, u32[]{:S(2)}, u32[]{:S(2)}) collective-permute-start(bf16[2,2,128,512]{3,2,1,0:T(8,128)(2,1)S(1)} %pad_maximum_fusion.14), channel_id=1, source_target_pairs={{0,16},{16,32},{32,48},{1,17},{17,33},{33,49},{2,18},{18,34},{34,5... | collective-permute-start | bytes 1572872 | tf_op jit(solution)/shard_map/ppermute | solution.py:612
  248.5 12.6 %collective-permute-start.78 = (bf16[4,352,256]{2,1,0:T(8,128)(2,1)S(1)}, bf16[4,352,256]{2,1,0:T(8,128)(2,1)S(1)}, u32[]{:S(2)}, u32[]{:S(2)}) collective-permute-start(bf16[4,352,256]{2,1,0:T(8,128)(2,1)S(1)} %add_convert_fusion.4), channel_id=1, source_target_pairs={{0,6},{1,9},{2,4},{3,11},{4,2},{5,13},{6,0},{7,15},{8,14},{9,1},{1... | collective-permute-start | bytes 2162696 | tf_op jit(solution)/shard_map/ppermute | solution.py:80
  250.8 9.7 %collective-permute-start.79 = (bf16[4,160,256]{2,1,0:T(8,128)(2,1)S(1)}, bf16[4,160,256]{2,1,0:T(8,128)(2,1)S(1)}, u32[]{:S(2)}, u32[]{:S(2)}) collective-permute-start(bf16[4,160,256]{2,1,0:T(8,128)(2,1)S(1)} %add_convert_fusion.7), channel_id=1, source_target_pairs={{0,2},{1,3},{2,0},{3,1},{4,6},{5,7},{6,4},{7,5},{8,10},{9,11},{10,... | collective-permute-start | bytes 983048 | tf_op jit(solution)/shard_map/ppermute | solution.py:80
  261.4 7.5 %collective-permute-start.82 = (bf16[2,352,256]{2,1,0:T(8,128)(2,1)S(1)}, bf16[2,352,256]{2,1,0:T(8,128)(2,1)S(1)}, u32[]{:S(2)}, u32[]{:S(2)}) collective-permute-start(bf16[2,352,256]{2,1,0:T(8,128)(2,1)S(1)} %slice.412), channel_id=1, source_target_pairs={{0,2},{1,7},{2,0},{3,5},{4,6},{5,3},{6,4},{7,1},{8,10},{9,15},{10,... | collective-permute-start | bytes 1081352 | tf_op jit(solution)/shard_map/ppermute | solution.py:80
  269.0 8.1 %collective-permute-start.84 = (bf16[352,256]{1,0:T(8,128)(2,1)S(1)}, bf16[352,256]{1,0:T(8,128)(2,1)S(1)}, u32[]{:S(2)}, u32[]{:S(2)}) collective-permute-start(bf16[352,256]{1,0:T(8,128)(2,1)S(1)} %fusion.19), channel_id=1, source_target_pairs={{0,8},{1,3},{2,10},{3,1},{4,12},{5,7},{6,14},{7,5},{8,0},{9,11},{1... | collective-permute-start | bytes 540680 | tf_op jit(solution)/shard_map/ppermute | solution.py:80
  277.2 8.0 %collective-permute-start.86 = (bf16[512,256]{1,0:T(8,128)(2,1)S(1)}, bf16[512,256]{1,0:T(8,128)(2,1)S(1)}, u32[]{:S(2)}, u32[]{:S(2)}) collective-permute-start(bf16[512,256]{1,0:T(8,128)(2,1)S(1)} %pad_maximum_fusion.21), channel_id=1, source_target_pairs={{0,64},{64,0},{1,65},{65,1},{2,66},{66,2},{3,67},{67,3},{4,68},{68... | collective-permute-start | bytes 786440 | tf_op jit(solution)/shard_map/ppermute | solution.py:67
  285.2 6.7 %collective-permute-start.87 = (bf16[352,256]{1,0:T(8,128)(2,1)S(1)}, bf16[352,256]{1,0:T(8,128)(2,1)S(1)}, u32[]{:S(2)}, u32[]{:S(2)}) collective-permute-start(bf16[352,256]{1,0:T(8,128)(2,1)S(1)} %get-tuple-element.338), channel_id=1, source_target_pairs={{0,8},{1,3},{2,10},{3,1},{4,12},{5,7},{6,14},{7,5},{8,0},{9,11},{1... | collective-permute-start | bytes 540680 | tf_op jit(solution)/shard_map/ppermute | solution.py:80
  285.3 6.6 %collective-permute-start.88 = (bf16[160,256]{1,0:T(8,128)(2,1)S(1)}, bf16[160,256]{1,0:T(8,128)(2,1)S(1)}, u32[]{:S(2)}, u32[]{:S(2)}) collective-permute-start(bf16[160,256]{1,0:T(8,128)(2,1)S(1)} %get-tuple-element.336), channel_id=1, source_target_pairs={{0,6},{1,7},{2,4},{3,5},{4,2},{5,3},{6,0},{7,1},{8,14},{9,15},{10,... | collective-permute-start | bytes 245768 | tf_op jit(solution)/shard_map/ppermute | solution.py:80
  291.9 7.6 %collective-permute-start.89 = (bf16[2,352,256]{2,1,0:T(8,128)(2,1)S(1)}, bf16[2,352,256]{2,1,0:T(8,128)(2,1)S(1)}, u32[]{:S(2)}, u32[]{:S(2)}) collective-permute-start(bf16[2,352,256]{2,1,0:T(8,128)(2,1)S(1)} %pad_maximum_fusion.16), channel_id=1, source_target_pairs={{0,2},{1,7},{2,0},{3,5},{4,6},{5,3},{6,4},{7,1},{8,10},{9,15},{10,... | collective-permute-start | bytes 1081352 | tf_op jit(solution)/shard_map/ppermute | solution.py:80
  299.5 12.6 %collective-permute-start.93 = (bf16[4,352,256]{2,1,0:T(8,128)(2,1)S(1)}, bf16[4,352,256]{2,1,0:T(8,128)(2,1)S(1)}, u32[]{:S(2)}, u32[]{:S(2)}) collective-permute-start(bf16[4,352,256]{2,1,0:T(8,128)(2,1)S(1)} %pad_maximum_fusion.11.refs_0_), channel_id=1, source_target_pairs={{0,6},{1,9},{2,4},{3,11},{4,2},{5,13},{6,0},{7,15},{8,14},{9,1},{1... | collective-permute-start | bytes 2162696 | tf_op jit(solution)/shard_map/ppermute | solution.py:80
  301.2 7.2 %collective-permute-start.94 = (bf16[4,160,256]{2,1,0:T(8,128)(2,1)S(1)}, bf16[4,160,256]{2,1,0:T(8,128)(2,1)S(1)}, u32[]{:S(2)}, u32[]{:S(2)}) collective-permute-start(bf16[4,160,256]{2,1,0:T(8,128)(2,1)S(1)} %pad_maximum_fusion.19.refs_1_), channel_id=1, source_target_pairs={{0,2},{1,3},{2,0},{3,1},{4,6},{5,7},{6,4},{7,5},{8,10},{9,11},{10,... | collective-permute-start | bytes 983048 | tf_op jit(solution)/shard_map/ppermute | solution.py:80
  302.5 10.2 %collective-permute-start.92 = (bf16[4,160,256]{2,1,0:T(8,128)(2,1)S(1)}, bf16[4,160,256]{2,1,0:T(8,128)(2,1)S(1)}, u32[]{:S(2)}, u32[]{:S(2)}) collective-permute-start(bf16[4,160,256]{2,1,0:T(8,128)(2,1)S(1)} %pad_maximum_fusion.19.refs_1_), channel_id=1, source_target_pairs={{0,1},{1,0},{2,3},{3,2},{4,5},{5,4},{6,7},{7,6},{8,9},{9,8},{10,11... | collective-permute-start | bytes 983048 | tf_op jit(solution)/shard_map/ppermute | solution.py:63
  302.5 10.2 %collective-permute-start.91 = (bf16[4,352,256]{2,1,0:T(8,128)(2,1)S(1)}, bf16[4,352,256]{2,1,0:T(8,128)(2,1)S(1)}, u32[]{:S(2)}, u32[]{:S(2)}) collective-permute-start(bf16[4,352,256]{2,1,0:T(8,128)(2,1)S(1)} %pad_maximum_fusion.11.refs_0_), channel_id=1, source_target_pairs={{0,1},{1,0},{2,3},{3,2},{4,5},{5,4},{6,7},{7,6},{8,9},{9,8},{10,11... | collective-permute-start | bytes 2162696 | tf_op jit(solution)/shard_map/ppermute | solution.py:63
  352.4 13.3 %collective-permute-start.99 = (bf16[4,352,256]{2,1,0:T(8,128)(2,1)S(1)}, bf16[4,352,256]{2,1,0:T(8,128)(2,1)S(1)}, u32[]{:S(2)}, u32[]{:S(2)}) collective-permute-start(bf16[4,352,256]{2,1,0:T(8,128)(2,1)S(1)} %add_convert_fusion.3), channel_id=1, source_target_pairs={{0,6},{1,9},{2,4},{3,11},{4,2},{5,13},{6,0},{7,15},{8,14},{9,1},{1... | collective-permute-start | bytes 2162696 | tf_op jit(solution)/shard_map/ppermute | solution.py:80
  355.8 9.9 %collective-permute-start.100 = (bf16[4,160,256]{2,1,0:T(8,128)(2,1)S(1)}, bf16[4,160,256]{2,1,0:T(8,128)(2,1)S(1)}, u32[]{:S(2)}, u32[]{:S(2)}) collective-permute-start(bf16[4,160,256]{2,1,0:T(8,128)(2,1)S(1)} %add_convert_fusion.6), channel_id=1, source_target_pairs={{0,2},{1,3},{2,0},{3,1},{4,6},{5,7},{6,4},{7,5},{8,10},{9,11},{10,... | collective-permute-start | bytes 983048 | tf_op jit(solution)/shard_map/ppermute | solution.py:80
  366.0 7.7 %collective-permute-start.103 = (bf16[2,352,256]{2,1,0:T(8,128)(2,1)S(1)}, bf16[2,352,256]{2,1,0:T(8,128)(2,1)S(1)}, u32[]{:S(2)}, u32[]{:S(2)}) collective-permute-start(bf16[2,352,256]{2,1,0:T(8,128)(2,1)S(1)} %slice.411), channel_id=1, source_target_pairs={{0,2},{1,7},{2,0},{3,5},{4,6},{5,3},{6,4},{7,1},{8,10},{9,15},{10,... | collective-permute-start | bytes 1081352 | tf_op jit(solution)/shard_map/ppermute | solution.py:80
  366.5 7.2 %collective-permute-start.104 = (bf16[2,160,256]{2,1,0:T(8,128)(2,1)S(1)}, bf16[2,160,256]{2,1,0:T(8,128)(2,1)S(1)}, u32[]{:S(2)}, u32[]{:S(2)}) collective-permute-start(bf16[2,160,256]{2,1,0:T(8,128)(2,1)S(1)} %slice.414), channel_id=1, source_target_pairs={{0,8},{1,9},{2,10},{3,11},{4,12},{5,13},{6,14},{7,15},{8,0},{9,1},... | collective-permute-start | bytes 491528 | tf_op jit(solution)/shard_map/ppermute | solution.py:80
  373.9 8.0 %collective-permute-start.105 = (bf16[352,256]{1,0:T(8,128)(2,1)S(1)}, bf16[352,256]{1,0:T(8,128)(2,1)S(1)}, u32[]{:S(2)}, u32[]{:S(2)}) collective-permute-start(bf16[352,256]{1,0:T(8,128)(2,1)S(1)} %fusion.20), channel_id=1, source_target_pairs={{0,8},{1,3},{2,10},{3,1},{4,12},{5,7},{6,14},{7,5},{8,0},{9,11},{1... | collective-permute-start | bytes 540680 | tf_op jit(solution)/shard_map/ppermute | solution.py:80
  387.9 7.5 %collective-permute-start.109 = (bf16[2,352,256]{2,1,0:T(8,128)(2,1)S(1)}, bf16[2,352,256]{2,1,0:T(8,128)(2,1)S(1)}, u32[]{:S(2)}, u32[]{:S(2)}) collective-permute-start(bf16[2,352,256]{2,1,0:T(8,128)(2,1)S(1)} %pad_maximum_fusion.17), channel_id=1, source_target_pairs={{0,2},{1,7},{2,0},{3,5},{4,6},{5,3},{6,4},{7,1},{8,10},{9,15},{10,... | collective-permute-start | bytes 1081352 | tf_op jit(solution)/shard_map/ppermute | solution.py:80
  395.5 12.6 %collective-permute-start.113 = (bf16[4,352,256]{2,1,0:T(8,128)(2,1)S(1)}, bf16[4,352,256]{2,1,0:T(8,128)(2,1)S(1)}, u32[]{:S(2)}, u32[]{:S(2)}) collective-permute-start(bf16[4,352,256]{2,1,0:T(8,128)(2,1)S(1)} %pad_maximum_fusion.12.refs_0_), channel_id=1, source_target_pairs={{0,6},{1,9},{2,4},{3,11},{4,2},{5,13},{6,0},{7,15},{8,14},{9,1},{1... | collective-permute-start | bytes 2162696 | tf_op jit(solution)/shard_map/ppermute | solution.py:80
  397.1 7.2 %collective-permute-start.114 = (bf16[4,160,256]{2,1,0:T(8,128)(2,1)S(1)}, bf16[4,160,256]{2,1,0:T(8,128)(2,1)S(1)}, u32[]{:S(2)}, u32[]{:S(2)}) collective-permute-start(bf16[4,160,256]{2,1,0:T(8,128)(2,1)S(1)} %pad_maximum_fusion.20.refs_1_), channel_id=1, source_target_pairs={{0,2},{1,3},{2,0},{3,1},{4,6},{5,7},{6,4},{7,5},{8,10},{9,11},{10,... | collective-permute-start | bytes 983048 | tf_op jit(solution)/shard_map/ppermute | solution.py:80
  398.1 12.6 %collective-permute-start.111 = (bf16[4,352,256]{2,1,0:T(8,128)(2,1)S(1)}, bf16[4,352,256]{2,1,0:T(8,128)(2,1)S(1)}, u32[]{:S(2)}, u32[]{:S(2)}) collective-permute-start(bf16[4,352,256]{2,1,0:T(8,128)(2,1)S(1)} %pad_maximum_fusion.12.refs_0_), channel_id=1, source_target_pairs={{0,1},{1,0},{2,3},{3,2},{4,5},{5,4},{6,7},{7,6},{8,9},{9,8},{10,11... | collective-permute-start | bytes 2162696 | tf_op jit(solution)/shard_map/ppermute | solution.py:63
  421.8 12.8 %collective-permute-start.119 = (bf16[4,352,256]{2,1,0:T(8,128)(2,1)S(1)}, bf16[4,352,256]{2,1,0:T(8,128)(2,1)S(1)}, u32[]{:S(2)}, u32[]{:S(2)}) collective-permute-start(bf16[4,352,256]{2,1,0:T(8,128)(2,1)S(1)} %add_convert_fusion.2), channel_id=1, source_target_pairs={{0,6},{1,9},{2,4},{3,11},{4,2},{5,13},{6,0},{7,15},{8,14},{9,1},{1... | collective-permute-start | bytes 2162696 | tf_op jit(solution)/shard_map/ppermute | solution.py:80
  424.8 9.7 %collective-permute-start.120 = (bf16[4,160,256]{2,1,0:T(8,128)(2,1)S(1)}, bf16[4,160,256]{2,1,0:T(8,128)(2,1)S(1)}, u32[]{:S(2)}, u32[]{:S(2)}) collective-permute-start(bf16[4,160,256]{2,1,0:T(8,128)(2,1)S(1)} %add_convert_fusion.5), channel_id=1, source_target_pairs={{0,2},{1,3},{2,0},{3,1},{4,6},{5,7},{6,4},{7,5},{8,10},{9,11},{10,... | collective-permute-start | bytes 983048 | tf_op jit(solution)/shard_map/ppermute | solution.py:80
  435.0 7.6 %collective-permute-start.123 = (bf16[2,352,256]{2,1,0:T(8,128)(2,1)S(1)}, bf16[2,352,256]{2,1,0:T(8,128)(2,1)S(1)}, u32[]{:S(2)}, u32[]{:S(2)}) collective-permute-start(bf16[2,352,256]{2,1,0:T(8,128)(2,1)S(1)} %slice.410), channel_id=1, source_target_pairs={{0,2},{1,7},{2,0},{3,5},{4,6},{5,3},{6,4},{7,1},{8,10},{9,15},{10,... | collective-permute-start | bytes 1081352 | tf_op jit(solution)/shard_map/ppermute | solution.py:80
  435.3 7.3 %collective-permute-start.124 = (bf16[2,160,256]{2,1,0:T(8,128)(2,1)S(1)}, bf16[2,160,256]{2,1,0:T(8,128)(2,1)S(1)}, u32[]{:S(2)}, u32[]{:S(2)}) collective-permute-start(bf16[2,160,256]{2,1,0:T(8,128)(2,1)S(1)} %slice.413), channel_id=1, source_target_pairs={{0,8},{1,9},{2,10},{3,11},{4,12},{5,13},{6,14},{7,15},{8,0},{9,1},... | collective-permute-start | bytes 491528 | tf_op jit(solution)/shard_map/ppermute | solution.py:80
  442.8 8.2 %collective-permute-start.125 = (bf16[352,256]{1,0:T(8,128)(2,1)S(1)}, bf16[352,256]{1,0:T(8,128)(2,1)S(1)}, u32[]{:S(2)}, u32[]{:S(2)}) collective-permute-start(bf16[352,256]{1,0:T(8,128)(2,1)S(1)} %fusion.21), channel_id=1, source_target_pairs={{0,8},{1,3},{2,10},{3,1},{4,12},{5,7},{6,14},{7,5},{8,0},{9,11},{1... | collective-permute-start | bytes 540680 | tf_op jit(solution)/shard_map/ppermute | solution.py:80
  451.0 6.6 %collective-permute-start.127 = (bf16[256,256]{1,0:T(8,128)(2,1)S(1)}, bf16[256,256]{1,0:T(8,128)(2,1)S(1)}, u32[]{:S(2)}, u32[]{:S(2)}) collective-permute-start(bf16[256,256]{1,0:T(8,128)(2,1)S(1)} %slice.288), channel_id=1, source_target_pairs={{0,64},{64,0},{1,65},{65,1},{2,66},{66,2},{3,67},{67,3},{4,68},{68... | collective-permute-start | bytes 393224 | tf_op jit(solution)/shard_map/ppermute | solution.py:67
  (59 other events, 523.1 us)
